TPU v7x, 32 devices: a whole 2x2x4 slice. The times are simulated.
32 devices in a mesh: tower: 4 (over y, x), dp: 8 (over z, core).
Axes of the slice: x: 2, y: 2, z: 4, core: 2. Of those that a mesh axis runs over, the one named last changes fastest.
Arguments:
- query_hidden: bfloat16 [1536, 2304], P('dp'), may hold values from -6 to 6
- passage_hidden: bfloat16 [1536, 3072], P(('tower', 'dp')), may hold values from -6 to 6
- pool_hidden: bfloat16 [16384, 3072], P(('tower', 'dp')), may hold values from -6 to 6
- query_proj: bfloat16 [2304, 768], replicated, may hold values from -0.125 to 0.125
- passage_proj: bfloat16 [3072, 768], replicated, may hold values from -0.109375 to 0.109375
- negative_ids: int32 [1536, 8], P('dp'), may hold values from 0 to 16383, as said below
Outputs:
- query_grad: bfloat16 [1536, 768], P(('dp', 'tower'))
- passage_grad: bfloat16 [1536, 768], P(('tower', 'dp'))
- negative_grad: bfloat16 [16384, 768], P(('tower', 'dp'))
Inputs may be any that keep to these rules, and one draw needn't show every extreme that they name: `negative_ids`: the owner of pool row r is the device with index r // 512 along tower+dp. Among the 1536 ids of one index of dp, at most 96 have one owner, and in every draw some owner gets exactly 96 of them; ids may repeat.
All inputs are finite; a program needn't handle non-finite values.
Results may differ from a plain program's by a relative error of at most 0.015.
Values may be sent and summed in bfloat16 or wider, within the bound.
No kernel may reach another device: no remote copies, remote signals or barrier semaphores. Data moves between devices by JAX's collectives and lax.ppermute only.
A program may use at most 128 MiB of HBM per device.

v0:
```python
import jax
import jax.numpy as jnp
from jax import lax
from jax.sharding import PartitionSpec as P

logit_scale = 50.0


def unit_rows(hidden, weight):
    projected = jnp.dot(hidden, weight, preferred_element_type=jnp.float32)
    length = jnp.sqrt(jnp.sum(projected * projected, axis=1, keepdims=True) + 1e-06)
    return (projected / length).astype(jnp.bfloat16)


def shards(query_hidden, passage_hidden, pool_hidden, query_proj, passage_proj, negative_ids):
    tower_count = lax.axis_size("tower")
    dp_size = lax.axis_size("dp")
    tower_index = lax.axis_index("tower")
    dp_index = lax.axis_index("dp")
    query_count = query_hidden.shape[0]
    neg_count = negative_ids.shape[1]
    pool_rows = pool_hidden.shape[0]
    own_rows = passage_hidden.shape[0]
    block_rows = own_rows * dp_size
    cap_slots = 2 * query_count * neg_count // (tower_count * dp_size)
    slot_total = dp_size * cap_slots
    query_unit = unit_rows(query_hidden, query_proj)
    passage_unit = unit_rows(passage_hidden, passage_proj)
    pool_unit = unit_rows(pool_hidden, passage_proj)
    emb_width = query_unit.shape[1]
    passage_block = lax.all_gather(passage_unit, "dp", axis=0, tiled=True)
    scores = logit_scale * lax.dot_general(
        query_unit, passage_block, (((1,), (1,)), ((), ())), preferred_element_type=jnp.float32
    )
    exp_scores = jnp.exp(scores)
    pos_offset = dp_index * query_count - tower_index * block_rows
    has_pos = (pos_offset >= 0) & (pos_offset < block_rows)
    pos_start = jnp.clip(pos_offset, 0, block_rows - query_count)
    positives = lax.dynamic_slice_in_dim(passage_block, pos_start, query_count, 0)
    query_wide = query_unit.astype(jnp.float32)
    pos_score = logit_scale * jnp.sum(query_wide * positives.astype(jnp.float32), axis=1)
    pos_exp = jnp.where(has_pos, jnp.exp(pos_score), 0.0)
    flat_ids = negative_ids.reshape(-1)
    owner_index = flat_ids // pool_rows
    local_row = flat_ids % pool_rows
    in_tower = owner_index // dp_size == tower_index
    owner_rank = owner_index % dp_size
    member = ((owner_rank[:, None] == jnp.arange(dp_size)[None, :]) & in_tower[:, None]).astype(
        jnp.int32
    )
    before = jnp.cumsum(member, axis=0) - member
    slot_index = jnp.sum(before * member, axis=1)
    position = jnp.where(in_tower, owner_rank * cap_slots + slot_index, slot_total)
    requests = (
        jnp.zeros((slot_total,), jnp.int32)
        .at[position]
        .set(local_row, mode="drop")
        .reshape(dp_size, cap_slots)
    )
    asked_ids = lax.all_to_all(requests, "dp", split_axis=0, concat_axis=0, tiled=True)
    fetched = lax.all_to_all(pool_unit[asked_ids], "dp", split_axis=0, concat_axis=0, tiled=True)
    flat_fetched = fetched.reshape(slot_total, emb_width)
    entry_rows = flat_fetched[jnp.minimum(position, slot_total - 1)].reshape(
        query_count, neg_count, emb_width
    )
    neg_score = logit_scale * jnp.einsum(
        "qe,qke->qk", query_unit, entry_rows, preferred_element_type=jnp.float32
    )
    neg_exp = jnp.where(in_tower.reshape(query_count, neg_count), jnp.exp(neg_score), 0.0)
    batch_total, hard_total = lax.psum(
        (jnp.sum(exp_scores, axis=1), pos_exp + jnp.sum(neg_exp, axis=1)), "tower"
    )
    weights = (exp_scores / batch_total[:, None]).astype(jnp.bfloat16)
    pos_weight = pos_exp / hard_total
    hard_weight = neg_exp / hard_total[:, None]
    pos_coef = jnp.where(has_pos, pos_weight - 2.0, 0.0)
    query_term = logit_scale * (
        jnp.dot(weights, passage_block, preferred_element_type=jnp.float32)
        + pos_coef[:, None] * positives.astype(jnp.float32)
        + jnp.einsum("qk,qke->qe", hard_weight, entry_rows, preferred_element_type=jnp.float32)
    )
    query_grad = lax.psum_scatter(
        query_term.astype(jnp.bfloat16), "tower", scatter_dimension=0, tiled=True
    )
    pos_rows_coef = pos_coef[:, None] * query_wide
    product = lax.dot_general(
        weights, query_unit, (((0,), (0,)), ((), ())), preferred_element_type=jnp.float32
    )
    offsets = jnp.arange(own_rows * lax.axis_size("dp")) - pos_offset
    inside = (offsets >= 0) & (offsets < query_count)
    extra_rows = jnp.where(
        inside[:, None], pos_rows_coef[jnp.clip(offsets, 0, query_count - 1)], 0.0
    )
    passage_grad = lax.psum_scatter(
        logit_scale * (product + extra_rows), "dp", scatter_dimension=0, tiled=True
    ).astype(jnp.bfloat16)
    entry_grad = (logit_scale * hard_weight[:, :, None] * query_wide[:, None, :]).reshape(
        query_count * neg_count, emb_width
    )
    slot_grad = (
        jnp.zeros((slot_total, emb_width), jnp.float32)
        .at[position]
        .add(entry_grad, mode="drop")
        .reshape(dp_size, cap_slots, emb_width)
    )
    returned = lax.all_to_all(
        slot_grad.astype(jnp.bfloat16), "dp", split_axis=0, concat_axis=0, tiled=True
    ).astype(slot_grad.dtype)
    pool_grad = (
        jnp.zeros((pool_rows, emb_width), jnp.float32)
        .at[asked_ids.reshape(-1)]
        .add(returned.reshape(slot_total, emb_width))
    )
    return (query_grad, passage_grad, pool_grad.astype(jnp.bfloat16))


def solution(mesh):
    placed = (
        P("dp", None),
        P(("tower", "dp"), None),
        P(("tower", "dp"), None),
        P(),
        P(),
        P("dp", None),
    )
    return jax.shard_map(
        shards,
        mesh=mesh,
        in_specs=placed,
        out_specs=(P(("dp", "tower"), None), P(("tower", "dp"), None), P(("tower", "dp"), None)),
        check_vma=False,
    )
```

profile of v0, /device:TPU:0, one launch (start us, length us, event | category | flops | bytes accessed | tf_op | source)
XLA Modules:
  0.0 213.8 jit_solution(854755675412122011)
XLA Ops:
  15.5 5.1 %reduce-window.6 = s32[8,12,128]{2,1,0:T(8,128)} reduce-window(s32[8,12,128]{2,1,0:T(8,128)} %fusion.19, s32[]{:T(128)} %constant.86.clone.1), window={size=1x1x128 pad=0_0x0_0x127_0}, to_apply=%region_6.7 | reduce-window | flops 1560576 | bytes 98308 | tf_op jit(solution)/shard_map/reduce-window
  26.1 6.3 %scatter_custom_fusion = s32[768]{0:T(1024)S(1)} fusion(s32[1536]{0:T(1024)S(1)} %get-tuple-element.4, s32[1536]{0:T(1024)} %get-tuple-element.11, s32[]{:T(128)} %constant.86.clone.1), kind=kCustom, calls=%fused_computation.129 | custom fusion | bytes 3584 | tf_op jit(solution)/shard_map/scatter | solution.py:57
  33.1 6.3 %all-to-all-start = ((s32[8,1,96]{2,1,0:T(1,128)}), s32[8,1,96]{2,1,0:T(1,128)S(1)}, u32[]{:S(2)}, u32[]{:S(2)}) async-start(s32[8,1,96]{2,1,0:T(1,128)} %all_to_all.14), calls=%async_computation | async-start | bytes 8192 | tf_op jit(solution)/shard_map/all_to_all | solution.py:60
  39.5 4.2 %multiply_reduce_fusion.2 = (f32[48]{0:T(128)S(1)}, f32[48,768]{1,0:T(8,128)}) fusion(bf16[48,3072]{1,0:T(8,128)(2,1)} %param.7, bf16[3072,768]{1,0:T(8,128)(2,1)} %param.10), kind=kOutput, calls=%fused_computation.37 | convolution fusion | flops 226566096 | bytes 5161152 | tf_op jit(solution)/shard_map/dot_general | solution.py:10
  43.7 5.7 %multiply_reduce_fusion = (f32[512]{0:T(512)S(1)}, f32[512,768]{1,0:T(8,128)}) fusion(bf16[512,3072]{1,0:T(8,128)(2,1)} %param.8, bf16[3072,768]{1,0:T(8,128)(2,1)S(1)} %copy-done.2), kind=kOutput, calls=%fused_computation.17 | convolution fusion | flops 2416705024 | bytes 9439232 | tf_op jit(solution)/shard_map/dot_general | solution.py:10
  49.4 2.5 %divide_convert_fusion = bf16[512,768]{1,0:T(8,128)(2,1)} fusion(f32[512,768]{1,0:T(8,128)} %get-tuple-element.16, f32[512]{0:T(512)S(1)} %add_sqrt_fusion), kind=kLoop, calls=%fused_computation.16 | loop fusion | flops 786432 | bytes 2361344 | tf_op jit(solution)/shard_map/convert_element_type | solution.py:12
  52.6 5.2 %gather_fusion = bf16[768,768]{1,0:T(8,128)(2,1)} fusion(bf16[512,768]{1,0:T(8,128)(2,1)} %divide_convert_fusion, s32[1024]{0:T(1024)S(1)} %pad_clamp_fusion.2), kind=kCustom, calls=%fused_computation | custom fusion | bytes 2362368 | tf_op jit(solution)/shard_map/gather | solution.py:61
  57.8 5.1 %all-to-all-start.1 = ((bf16[8,96,768]{2,1,0:T(8,128)(2,1)}), bf16[8,96,768]{2,1,0:T(8,128)(2,1)}, u32[]{:S(2)}, u32[]{:S(2)}) async-start(bf16[8,96,768]{2,1,0:T(8,128)(2,1)} %bitcast.59), calls=%async_computation.1 | async-start | bytes 2359296 | tf_op jit(solution)/shard_map/all_to_all | solution.py:61
  64.2 2.2 %multiply_reduce_fusion.1 = (f32[192]{0:T(256)S(1)}, f32[192,768]{1,0:T(8,128)S(1)}) fusion(bf16[192,2304]{1,0:T(8,128)(2,1)} %param.6, bf16[2304,768]{1,0:T(8,128)(2,1)S(1)} %copy-done), kind=kOutput, calls=%fused_computation.33 | convolution fusion | flops 679771968 | bytes 5014272 | tf_op jit(solution)/shard_map/dot_general | solution.py:10
  66.5 34.2 %all_gather.3 = bf16[384,768]{1,0:T(8,128)(2,1)S(1)} all-gather(bf16[48,768]{1,0:T(8,128)(2,1)S(1)} %divide_convert_fusion.3), channel_id=1, replica_groups=mesh['tower'=4,'dp'=8] {'dp'}, dimensions={0}, use_global_device_ids=true | all-gather | bytes 663552 | tf_op jit(solution)/shard_map/all_gather | solution.py:31
  104.1 8.1 %gather_fusion.1 = bf16[1536,768]{1,0:T(8,128)(2,1)} fusion(bf16[768,768]{1,0:T(8,128)(2,1)} %bitcast.4, s32[2048]{0:T(1024)S(1)} %pad_clamp_fusion), kind=kCustom, calls=%fused_computation.1 | custom fusion | bytes 4724736 | tf_op jit(solution)/shard_map/gather | solution.py:63
  112.2 3.6 %fusion.5 = f32[192,1,8]{2,1,0:T(1,128)} fusion(bf16[1536,768]{1,0:T(8,128)(2,1)} %gather_fusion.1, bf16[192,768,1]{1,0,2:T(8,128)(2,1)} %bitcast.58), kind=kOutput, calls=%fused_computation.12 | convolution fusion | flops 2359296 | bytes 2660352 | tf_op jit(solution)/shard_map/qe,qke->qk/dot_general | solution.py:66
  118.8 10.8 %all-reduce = (f32[192]{0:T(256)}, f32[192]{0:T(256)}) all-reduce(f32[192]{0:T(256)} %fusion.53, f32[192]{0:T(256)} %get-tuple-element.19), channel_id=1, replica_groups=mesh['tower'=4,'dp'=8] {'tower'}, use_global_device_ids=true, to_apply=%region_11.12 | all-reduce | flops 384 | bytes 3072 | tf_op jit(solution)/shard_map/psum | solution.py:70
  130.8 1.9 broadcast_multiply_fusion
  132.7 4.3 %gather_fusion.2 = f32[384,768]{1,0:T(8,128)} fusion(f32[192,768]{1,0:T(8,128)} %broadcast_multiply_fusion, s32[1024]{0:T(1024)} %pad_clamp_fusion.1), kind=kCustom, calls=%fused_computation.2 | custom fusion | bytes 2360832 | tf_op jit(solution)/shard_map/gather | solution.py:92
  137.0 2.9 %fusion.9 = f32[384,768]{1,0:T(8,128)} fusion(bf16[192,768]{1,0:T(8,128)(2,1)} %copy-done.1, f32[384,768]{1,0:T(8,128)} %gather_fusion.2, pred[384]{0:T(512)(128)(4,1)} %fusion.51, f32[192,384]{1,0:T(8,128)} %get-tuple-element.20, f32[192]{0:T(256)} %get-tuple-element.6), kind=kOutput, calls=%fused_computation.19 | convolution fusion | flops 114278400 | bytes 2950272 | tf_op jit(solution)/shard_map/dot_general | solution.py:86
  143.5 13.0 %scatter_custom_fusion.1 = f32[768,768]{1,0:T(8,128)} fusion(s32[1536]{0:T(1024)} %copy-done.8, f32[192,768]{1,0:T(8,128)} %get-tuple-element.7, f32[1536]{0:T(1024)} %mul.128, f32[]{:T(128)} %constant.79.clone.1), kind=kCustom, calls=%fused_computation.7 | custom fusion | flops 2359296 | bytes 2957824 | tf_op jit(solution)/shard_map/scatter-add | solution.py:103
  156.5 2.9 %convert_element_type.52 = bf16[768,768]{1,0:T(8,128)(2,1)} convert(f32[768,768]{1,0:T(8,128)} %scatter_custom_fusion.1) | non-fusion elementwise | flops 589824 | bytes 3538944 | tf_op jit(solution)/shard_map/convert_element_type | solution.py:107
  159.4 4.3 %all-to-all-start.2 = ((bf16[8,96,768]{2,1,0:T(8,128)(2,1)}), bf16[8,96,768]{2,1,0:T(8,128)(2,1)}, u32[]{:S(2)}, u32[]{:S(2)}) async-start(bf16[8,96,768]{2,1,0:T(8,128)(2,1)} %bitcast.60), calls=%async_computation.4 | async-start | bytes 2359296 | tf_op jit(solution)/shard_map/all_to_all | solution.py:106
  165.2 2.6 %fusion.3 = f32[192,1,768]{2,1,0:T(1,128)S(1)} fusion(bf16[192,8,1]{1,2,0:T(2,128)(2,1)} %copy.15, bf16[1536,768]{1,0:T(8,128)(2,1)} %gather_fusion.1), kind=kOutput, calls=%fused_computation.10 | convolution fusion | flops 2359296 | bytes 2952192 | tf_op jit(solution)/shard_map/qk,qke->qe/dot_general | solution.py:80
  167.8 1.8 fusion.12
  170.8 23.0 %all-to-all-done.2 = bf16[8,96,768]{2,1,0:T(8,128)(2,1)} async-done(((bf16[8,96,768]{2,1,0:T(8,128)(2,1)}), bf16[8,96,768]{2,1,0:T(8,128)(2,1)}, u32[]{:S(2)}, u32[]{:S(2)}) %all-to-all-start.2) | async-done | bytes 1179680 | tf_op jit(solution)/shard_map/all_to_all | solution.py:106
  193.9 9.2 %scatter_custom_fusion.2 = f32[512,768]{1,0:T(8,128)} fusion(s32[768]{0:T(1024)S(1)} %fusion.45, bf16[768,768]{1,0:T(8,128)(2,1)} %bitcast.12, f32[]{:T(128)} %constant.79.clone.1), kind=kCustom, calls=%fused_computation.8 | custom fusion | flops 1179648 | bytes 2752516 | tf_op jit(solution)/shard_map/scatter-add | solution.py:112
  203.1 2.4 %convert_element_type.54 = bf16[512,768]{1,0:T(8,128)(2,1)} convert(f32[512,768]{1,0:T(8,128)} %scatter_custom_fusion.2) | non-fusion elementwise | flops 393216 | bytes 2359296 | tf_op jit(solution)/shard_map/convert_element_type | solution.py:114
  (71 shorter events, 32.2 us)
Async XLA Ops:
  7.2 57.0 %copy-start = (bf16[2304,768]{1,0:T(8,128)(2,1)S(1)}, bf16[2304,768]{1,0:T(8,128)(2,1)}, u32[]{:S(2)}) copy-start(bf16[2304,768]{1,0:T(8,128)(2,1)} %param.9) | copy-start | bytes 10616836
  26.1 7.0 %copy-start.8 = (s32[1536]{0:T(1024)}, s32[1536]{0:T(1024)S(1)}, u32[]{:S(2)}) copy-start(s32[1536]{0:T(1024)S(1)} %get-tuple-element.4) | copy-start | bytes 18436
  33.1 19.3 %all-to-all-start = ((s32[8,1,96]{2,1,0:T(1,128)}), s32[8,1,96]{2,1,0:T(1,128)S(1)}, u32[]{:S(2)}, u32[]{:S(2)}) async-start(s32[8,1,96]{2,1,0:T(1,128)} %all_to_all.14), calls=%async_computation | async-start | bytes 8192 | tf_op jit(solution)/shard_map/all_to_all | solution.py:60
  39.5 4.2 %copy-start.2 = (bf16[3072,768]{1,0:T(8,128)(2,1)S(1)}, bf16[3072,768]{1,0:T(8,128)(2,1)}, u32[]{:S(2)}) copy-start(bf16[3072,768]{1,0:T(8,128)(2,1)} %param.10) | copy-start | bytes 14155780
  57.8 46.3 %all-to-all-start.1 = ((bf16[8,96,768]{2,1,0:T(8,128)(2,1)}), bf16[8,96,768]{2,1,0:T(8,128)(2,1)}, u32[]{:S(2)}, u32[]{:S(2)}) async-start(bf16[8,96,768]{2,1,0:T(8,128)(2,1)} %bitcast.59), calls=%async_computation.1 | async-start | bytes 2359296 | tf_op jit(solution)/shard_map/all_to_all | solution.py:61
  62.9 142.6 %reduce-scatter.5.cloned.1.call-start = ((), (), s32[]{:S(2)}) async-start(), calls=%async_computation.6 | async-start | bytes 1327104 | tf_op jit(solution)/shard_map/reduce_scatter | solution.py:94
  64.2 2.2 %copy-start.6 = (f32[48,768]{1,0:T(8,128)S(1)}, f32[48,768]{1,0:T(8,128)}, u32[]{:S(2)}) copy-start(f32[48,768]{1,0:T(8,128)} %get-tuple-element.14) | copy-start | bytes 442372
  100.7 1.2 copy-start.3
  101.7 0.7 copy-start.1
  130.2 0.6 copy-start.9
  137.0 2.9 %copy-start.7 = (f32[192]{0:T(256)S(1)}, f32[192]{0:T(256)}, u32[]{:S(2)}) copy-start(f32[192]{0:T(256)} %get-tuple-element.5) | copy-start | bytes 2308
  159.4 34.5 %all-to-all-start.2 = ((bf16[8,96,768]{2,1,0:T(8,128)(2,1)}), bf16[8,96,768]{2,1,0:T(8,128)(2,1)}, u32[]{:S(2)}, u32[]{:S(2)}) async-start(bf16[8,96,768]{2,1,0:T(8,128)(2,1)} %bitcast.60), calls=%async_computation.4 | async-start | bytes 2359296 | tf_op jit(solution)/shard_map/all_to_all | solution.py:106
  163.7 43.3 %reduce-scatter.3.cloned.1.call-start = ((), (), s32[]{:S(2)}) async-start(), calls=%async_computation.5 | async-start | bytes 368640 | tf_op jit(solution)/shard_map/reduce_scatter | solution.py:82
  165.2 2.6 %copy-start.4 = (bf16[384,768]{1,0:T(8,128)(2,1)S(1)}, bf16[384,768]{1,0:T(8,128)(2,1)}, u32[]{:S(2)}) copy-start(bf16[384,768]{1,0:T(8,128)(2,1)} %copy-done.3) | copy-start | bytes 1769476
  165.2 2.6 %copy-start.5 = (f32[192,384]{1,0:T(8,128)S(1)}, f32[192,384]{1,0:T(8,128)}, u32[]{:S(2)}) copy-start(f32[192,384]{1,0:T(8,128)} %get-tuple-element.20) | copy-start | bytes 884740
Sparse Core Ops, SparseCore 0:
  140.0 32.4 reduce-scatter.4
  175.9 24.0 reduce-scatter.2
where the time goes:
time: 215 us; the launch traced here: 214 us
  other arithmetic  53.1 us (25%)
  blocking collectives  44.9 us (21%)
  local copies, waits for them, and re-layouts  38.1 us (18%)
  matrix products  24.6 us (11%)
  waiting for transfers between devices  23.1 us (11%)
  starting transfers between devices  15.8 us (7%)
  between operations  14.2 us (7%)
    all_gather x1, blocking collectives, shards(): passage_block = lax.all_gather(passage_unit, 'dp', axis=0, tiled=True)  34.2 us
    all_to_all x1, waiting for transfers between devices, shards(): lax.all_to_all(slot_grad.astype(jnp.bfloat16), 'dp', split_axis=0, concat...  23 us
    scatter-add x1, other arithmetic, shards(): slot_grad = jnp.zeros((slot_total, emb_width), jnp.float32).at[position]....  13 us
    dot_general x3, matrix products, unit_rows(): projected = jnp.dot(hidden, weight, preferred_element_type=jnp.float32)  12.1 us
    psum x1, blocking collectives, shards(): lax.psum((jnp.sum(exp_scores, axis=1), pos_exp + jnp.sum(neg_exp, axis=1)...  10.8 us
    scatter-add x1, other arithmetic, shards(): pool_grad = jnp.zeros((pool_rows, emb_width), jnp.float32).at[asked_ids.r...  9.21 us
    gather x1, local copies, waits for them, and re-layouts, shards(): flat_fetched[jnp.minimum(position, slot_total - 1)]  8.14 us
    another operation x2, other arithmetic  6.56 us
  transfers between devices with their start and end apart: 5, of which 1 were waited for; matrix products, arithmetic and copies ran while one was open for 28% of the time, Pallas kernels for 0%

commit v1 on v0

v1 whole, which is shorter than its diff:
```python
import jax
import jax.numpy as jnp
from jax import lax
from jax.sharding import PartitionSpec as P

logit_scale = 50.0
axes = ("tower", "dp")


def unit_rows(hidden, weight):
    projected = jnp.dot(hidden, weight, preferred_element_type=jnp.float32)
    length = jnp.sqrt(jnp.sum(projected * projected, axis=1, keepdims=True) + 1e-06)
    return (projected / length).astype(jnp.bfloat16)


def shards(query_hidden, passage_hidden, pool_hidden, query_proj, passage_proj, negative_ids):
    f32 = jnp.float32
    bf16 = jnp.bfloat16
    tower_count = lax.axis_size("tower")
    dp_size = lax.axis_size("dp")
    chips = dp_size // 2
    tower = lax.axis_index("tower")
    dp = lax.axis_index("dp")
    core = dp % 2
    place = dp // 2
    query_rows = query_hidden.shape[0]
    part_rows = query_rows // tower_count
    neg_count = negative_ids.shape[1]
    pool_rows = pool_hidden.shape[0]
    own_rows = passage_hidden.shape[0]
    width = query_proj.shape[1]

    def moved(x, tower_step=0, place_step=0, core_step=0):
        pairs = []
        for source in range(tower_count * dp_size):
            t, d = divmod(source, dp_size)
            target = ((d // 2) ^ place_step) * 2 + ((d % 2) ^ core_step)
            pairs.append((source, (t ^ tower_step) * dp_size + target))
        return lax.ppermute(x, axes, pairs)

    turned = tower ^ jnp.arange(tower_count)
    id_blocks = jnp.stack(
        [negative_ids] + [moved(negative_ids, place_step=s) for s in range(1, chips)]
    ).reshape(chips, tower_count, part_rows, neg_count)
    named = jnp.take(id_blocks, turned, axis=1).reshape(-1, neg_count)

    query_unit = unit_rows(query_hidden, query_proj)
    parts = jnp.take(query_unit.reshape(tower_count, part_rows, width), turned, axis=0)
    far = [moved(parts[0], place_step=s) for s in range(1, chips)]
    far = jnp.stack(far)
    spread = jnp.stack([far] + [moved(far, tower_step=s) for s in range(1, tower_count)], axis=1)
    queries = jnp.concatenate([parts[None], spread], axis=0).reshape(-1, width)

    passage_unit = unit_rows(passage_hidden, passage_proj)
    pool_unit = unit_rows(pool_hidden, passage_proj)
    items_own = jnp.concatenate([pool_unit, passage_unit], axis=0)
    items_other = moved(items_own, core_step=1)
    pool_all = jnp.concatenate([pool_unit, items_other[:pool_rows]], axis=0)
    passage_all = jnp.concatenate([passage_unit, items_other[pool_rows:]], axis=0)

    own_block = tower * dp_size + dp
    other_block = tower * dp_size + (dp ^ 1)
    pool_index = jnp.concatenate(
        [own_block * pool_rows + jnp.arange(pool_rows), other_block * pool_rows + jnp.arange(pool_rows)]
    )
    passage_index = jnp.concatenate(
        [own_block * own_rows + jnp.arange(own_rows), other_block * own_rows + jnp.arange(own_rows)]
    )
    query_index = (
        (((place ^ jnp.arange(chips)) * 2 + core) * query_rows)[:, None, None]
        + (turned * part_rows)[None, :, None]
        + jnp.arange(part_rows)[None, None, :]
    ).reshape(-1)
    count = jnp.sum((named[:, :, None] == pool_index[None, None, :]).astype(f32), axis=1)
    is_pos = query_index[:, None] == passage_index[None, :]

    contract = (((1,), (1,)), ((), ()))
    pool_exp = count * jnp.exp(
        logit_scale * lax.dot_general(queries, pool_all, contract, preferred_element_type=f32)
    )
    batch_exp = jnp.exp(
        logit_scale * lax.dot_general(queries, passage_all, contract, preferred_element_type=f32)
    )
    pos_exp = jnp.where(is_pos, batch_exp, 0.0)
    totals = jnp.stack(
        [jnp.sum(batch_exp, axis=1), jnp.sum(pool_exp, axis=1) + jnp.sum(pos_exp, axis=1)]
    )
    totals = totals.reshape(2, chips, tower_count, part_rows)
    line = totals
    for s in range(1, chips):
        line = line + moved(totals, place_step=s)[:, [k ^ s for k in range(chips)]]
    whole = line
    for s in range(1, tower_count):
        whole = whole + moved(line, tower_step=s)[:, :, [k ^ s for k in range(tower_count)]]
    batch_total = whole[0].reshape(-1, 1)
    hard_total = whole[1].reshape(-1, 1)
    pool_weight = (pool_exp / hard_total).astype(bf16)
    batch_weight = (
        batch_exp / batch_total + jnp.where(is_pos, pos_exp / hard_total - 2.0, 0.0)
    ).astype(bf16)
    query_term = logit_scale * (
        jnp.dot(pool_weight, pool_all, preferred_element_type=f32)
        + jnp.dot(batch_weight, passage_all, preferred_element_type=f32)
    )
    blocks = query_term.astype(bf16).reshape(chips, tower_count, part_rows, width)
    line_sum = blocks[:, 0].astype(f32)
    for s in range(1, tower_count):
        line_sum = line_sum + moved(blocks[:, s], tower_step=s).astype(f32)
    line_sum = line_sum.astype(bf16)
    query_grad = line_sum[0].astype(f32)
    for s in range(1, chips):
        query_grad = query_grad + moved(line_sum[s], place_step=s).astype(f32)

    across = (((0,), (0,)), ((), ()))
    pool_grad = logit_scale * lax.dot_general(pool_weight, queries, across, preferred_element_type=f32)
    passage_grad = logit_scale * lax.dot_general(
        batch_weight, queries, across, preferred_element_type=f32
    )
    given = jnp.concatenate([pool_grad[pool_rows:], passage_grad[own_rows:]], axis=0).astype(bf16)
    taken = moved(given, core_step=1).astype(f32)
    pool_grad = pool_grad[:pool_rows] + taken[:pool_rows]
    passage_grad = passage_grad[:own_rows] + taken[pool_rows:]
    return (query_grad.astype(bf16), passage_grad.astype(bf16), pool_grad.astype(bf16))


def solution(mesh):
    placed = (
        P("dp", None),
        P(("tower", "dp"), None),
        P(("tower", "dp"), None),
        P(),
        P(),
        P("dp", None),
    )
    return jax.shard_map(
        shards,
        mesh=mesh,
        in_specs=placed,
        out_specs=(P(("dp", "tower"), None), P(("tower", "dp"), None), P(("tower", "dp"), None)),
        check_vma=False,
    )
```

time: 215 us -> 147 us (0.68)
  blocking collectives: 44.9 us -> 0 us
  other arithmetic: 53.1 us -> 30.5 us
  starting transfers between devices: 15.8 us -> 29.5 us
  between operations: 14.2 us -> 1.15 us
  waiting for transfers between devices: 23.1 us -> 17.5 us
  local copies, waits for them, and re-layouts: 38.1 us -> 42.6 us
    all_gather x1 -> x0, blocking collectives: 34.2 us -> none  [shards(): passage_block = lax.all_gather(passage_unit, 'dp', axis=0, tiled=True)]
    ppermute x0 -> x23, starting transfers between devices: none -> 29.5 us  [moved(): return lax.ppermute(x, axes, pairs)]
    all_to_all x3 -> x0, waiting for transfers between devices: 23 us -> none  [the longest x1 23 us: shards(): lax.all_to_all(slot_grad.astype(jnp.bfloat16), 'dp', split_axis=0, concat...]
    scatter-add x2 -> x0, other arithmetic: 22.2 us -> none  [the longest x1 13 us: shards(): slot_grad = jnp.zeros((slot_total, emb_width), jnp.float32).at[position]....]
    ppermute x0 -> x23, waiting for transfers between devices: none -> 17.5 us  [moved(): return lax.ppermute(x, axes, pairs)]
    all_to_all x3 -> x0, starting transfers between devices: 15.7 us -> none  [the longest x1 6.33 us: shards(): lax.all_to_all(requests, 'dp', split_axis=0, concat_axis=0, tiled=True)]
    psum x1 -> x0, blocking collectives: 10.8 us -> none  [shards(): lax.psum((jnp.sum(exp_scores, axis=1), pos_exp + jnp.sum(neg_exp, axis=1)...]
    reduce_sum x3 -> x1, other arithmetic: 1.64 us -> 9 us  [shards(): jnp.sum((named[:, :, None] == pool_index[None, None, :]).astype(f32), axi...]
  transfers between devices with their start and end apart: 5 -> 23, of which waited for: 1 -> 9; matrix products, arithmetic and copies ran while one was open for 28% -> 41% of each run, Pallas kernels for 0% -> 0%
where the time goes in v1:
time: 147 us; the launch traced here: 145 us
  local copies, waits for them, and re-layouts  42.6 us (29%)
  other arithmetic  30.5 us (21%)
  starting transfers between devices  29.5 us (20%)
  matrix products  23.5 us (16%)
  waiting for transfers between devices  17.5 us (12%)
    ppermute x23, starting transfers between devices, moved(): return lax.ppermute(x, axes, pairs)  29.5 us
    ppermute x23, waiting for transfers between devices, moved(): return lax.ppermute(x, axes, pairs)  17.5 us
    dot_general x3, matrix products, unit_rows(): projected = jnp.dot(hidden, weight, preferred_element_type=jnp.float32)  12.1 us
    reduce_sum x1, other arithmetic, shards(): jnp.sum((named[:, :, None] == pool_index[None, None, :]).astype(f32), axi...  9 us
    ppermute x6, local copies, waits for them, and re-layouts, moved(): return lax.ppermute(x, axes, pairs)  6.49 us
    gather x3, local copies, waits for them, and re-layouts, shards(): line = line + moved(totals, place_step=s)[:, [k ^ s for k in range(chips)]]  6 us
    gather x3, local copies, waits for them, and re-layouts, shards(): moved(line, tower_step=s)[:, :, [k ^ s for k in range(tower_count)]]  5.41 us
    gather x3, local copies, waits for them, and re-layouts, shards(): named = jnp.take(id_blocks, turned, axis=1).reshape(-1, neg_count)  5.18 us
  transfers between devices with their start and end apart: 23, of which 9 were waited for; matrix products, arithmetic and copies ran while one was open for 41% of the time, Pallas kernels for 0%

profile of v1, /device:TPU:0, one launch (start us, length us, event | category | flops | bytes accessed | tf_op | source)
XLA Modules:
  0.0 144.7 jit_solution(9224984306676617152)
XLA Ops:
  0.7 2.0 %copy-done = bf16[2304,768]{1,0:T(8,128)(2,1)S(1)} copy-done((bf16[2304,768]{1,0:T(8,128)(2,1)S(1)}, bf16[2304,768]{1,0:T(8,128)(2,1)}, u32[]{:S(2)}) %copy-start) | copy-done | bytes 3538968
  2.6 2.1 %multiply_reduce_fusion.1 = (f32[192]{0:T(256)S(1)}, f32[192,768]{1,0:T(8,128)S(1)}) fusion(bf16[192,2304]{1,0:T(8,128)(2,1)} %param.12, bf16[2304,768]{1,0:T(8,128)(2,1)S(1)} %copy-done), kind=kOutput, calls=%fused_computation.30 | convolution fusion | flops 679771968 | bytes 5014272 | tf_op jit(solution)/shard_map/dot_general | solution.py:11
  5.6 2.2 %gather_fusion.1 = bf16[4,48,768]{2,1,0:T(8,128)(2,1)} fusion(bf16[4,48,768]{2,1,0:T(8,128)(2,1)} %bitcast.108, s32[1024]{0:T(1024)S(1)} %pad_clamp_fusion.3), kind=kCustom, calls=%fused_computation.1 | custom fusion | bytes 589840 | tf_op jit(solution)/shard_map/jit(_take)/gather | solution.py:48
  9.4 5.0 %collective-permute-start.5 = (bf16[48,768]{1,0:T(8,128)(2,1)}, bf16[48,768]{1,0:T(8,128)(2,1)}, u32[]{:S(2)}, u32[]{:S(2)}) collective-permute-start(bf16[48,768]{1,0:T(8,128)(2,1)} %fusion.13), channel_id=1, source_target_pairs={{0,6},{1,7},{2,4},{3,5},{4,2},{5,3},{6,0},{7,1},{8,14},{9,15},{10,... | collective-permute-start | bytes 221192 | tf_op jit(solution)/shard_map/ppermute | solution.py:39
  14.5 1.9 %collective-permute-start.2 = (s32[192,8]{0,1:T(8,128)}, s32[192,8]{0,1:T(8,128)}, u32[]{:S(2)}, u32[]{:S(2)}) collective-permute-start(s32[192,8]{0,1:T(8,128)} %param.17), channel_id=1, source_target_pairs={{0,6},{1,7},{2,4},{3,5},{4,2},{5,3},{6,0},{7,1},{8,14},{9,15},{10,... | collective-permute-start | bytes 18440 | tf_op jit(solution)/shard_map/ppermute | solution.py:39
  20.6 4.2 %multiply_reduce_fusion.2 = (f32[48]{0:T(128)S(1)}, f32[48,768]{1,0:T(8,128)}) fusion(bf16[48,3072]{1,0:T(8,128)(2,1)} %param.13, bf16[3072,768]{1,0:T(8,128)(2,1)} %param.16), kind=kOutput, calls=%fused_computation.51 | convolution fusion | flops 226566096 | bytes 5161152 | tf_op jit(solution)/shard_map/dot_general | solution.py:11
  24.9 5.7 %multiply_reduce_fusion = (f32[512]{0:T(512)S(1)}, f32[512,768]{1,0:T(8,128)}) fusion(bf16[512,3072]{1,0:T(8,128)(2,1)} %param.14, bf16[3072,768]{1,0:T(8,128)(2,1)S(1)} %copy-done.1), kind=kOutput, calls=%fused_computation.18 | convolution fusion | flops 2416705024 | bytes 9439232 | tf_op jit(solution)/shard_map/dot_general | solution.py:11
  47.9 2.1 %gather_fusion = s32[4,4,48,8]{2,3,1,0:T(8,128)} fusion(s32[4,4,48,8]{2,3,1,0:T(8,128)} %pad_add_fusion, s32[1024]{0:T(1024)} %copy-done.20), kind=kCustom, calls=%fused_computation | custom fusion | bytes 49168 | tf_op jit(solution)/shard_map/jit(_take)/gather | solution.py:45
  57.1 2.5 %collective-permute-start.8 = (bf16[3,48,768]{2,1,0:T(8,128)(2,1)S(1)}, bf16[3,48,768]{2,1,0:T(8,128)(2,1)S(1)}, u32[]{:S(2)}, u32[]{:S(2)}) collective-permute-start(bf16[3,48,768]{2,1,0:T(8,128)(2,1)S(1)} %get-tuple-element.12), channel_id=1, source_target_pairs={{0,24},{1,25},{2,26},{3,27},{4,28},{5,29},{6,30},{7,31},{8,16},{9,... | collective-permute-start | bytes 663560 | tf_op jit(solution)/shard_map/ppermute | solution.py:39
  60.7 9.0 %convert_reduce_fusion = f32[768,1024]{1,0:T(8,128)S(1)} fusion(s32[1024]{0:T(1024)S(1)} %copy-done.19, s32[768,8]{1,0:T(8,128)} %copy.62), kind=kLoop, calls=%fused_computation.8 | loop fusion | flops 18087936 | bytes 3174400 | tf_op jit(solution)/shard_map/reduce_sum | solution.py:74
  72.7 3.2 %fusion.25 = (f32[768]{0:T(1024)S(1)}, f32[768,1024]{1,0:T(8,128)}) fusion(f32[768,1024]{1,0:T(8,128)S(1)} %convert_reduce_fusion, bf16[768,768]{1,0:T(8,128)(2,1)S(1)} %bitcast.102, bf16[512,768]{1,0:T(8,128)(2,1)S(1)} %slice.98, bf16[512,768]{1,0:T(8,128)(2,1)S(1)} %copy-done.3), kind=kOutput, calls=%fused_computation.97 | convolution fusion | flops 1213463808 | bytes 9047040 | tf_op jit(solution)/shard_map/dot_general | solution.py:79
  76.8 1.8 %fusion.23 = (f32[768]{0:T(1024)}, f32[768]{0:T(1024)S(1)}, f32[768,96]{0,1:T(8,128)}) fusion(s32[96]{0:T(128)S(1)} %copy-done.22, s32[768]{0:T(1024)S(1)} %copy-done.16, bf16[768,768]{1,0:T(8,128)(2,1)S(1)} %bitcast.103, bf16[48,768]{1,0:T(8,128)(2,1)S(1)} %slice.99, bf16[48,768]{1,0:T(8,128)(2,1)S(1)} %copy-done.11), kind=kOutput, calls=%fused_computation.95 | convolution fusion | flops 113908224 | bytes 1631616 | tf_op jit(solution)/shard_map/dot_general | solution.py:82
  80.1 2.9 %collective-permute-start.12 = (f32[2,4,4,48]{3,2,0,1:T(4,128)}, f32[2,4,4,48]{3,2,0,1:T(4,128)S(1)}, u32[]{:S(2)}, u32[]{:S(2)}) collective-permute-start(f32[2,4,4,48]{3,2,0,1:T(4,128)} %pad_maximum_fusion.9), channel_id=1, source_target_pairs={{0,6},{1,7},{2,4},{3,5},{4,2},{5,3},{6,0},{7,1},{8,14},{9,15},{10,... | collective-permute-start | bytes 18440 | tf_op jit(solution)/shard_map/ppermute | solution.py:39
  86.4 2.0 %gather_fusion.4 = f32[4,2,4,48]{3,2,1,0:T(4,128)} fusion(f32[2,4,4,48]{3,2,1,0:T(4,128)} %copy.70, s32[1024]{0:T(1024)} %pad_clamp_fusion), kind=kCustom, calls=%fused_computation.4 | custom fusion | bytes 12304 | tf_op jit(solution)/shard_map/gather | solution.py:91
  89.8 2.0 %gather_fusion.3 = f32[4,2,4,48]{3,2,1,0:T(4,128)} fusion(f32[2,4,4,48]{3,2,1,0:T(4,128)} %copy.69, s32[1024]{0:T(1024)} %pad_clamp_fusion.1), kind=kCustom, calls=%fused_computation.3 | custom fusion | bytes 12304 | tf_op jit(solution)/shard_map/gather | solution.py:91
  93.1 2.0 %gather_fusion.2 = f32[4,2,4,48]{3,2,1,0:T(4,128)} fusion(f32[2,4,4,48]{3,2,1,0:T(4,128)} %copy.68, s32[1024]{0:T(1024)} %pad_clamp_fusion.2), kind=kCustom, calls=%fused_computation.2 | custom fusion | bytes 12304 | tf_op jit(solution)/shard_map/gather | solution.py:91
  104.6 2.0 %gather_fusion.6 = f32[4,2,4,48]{3,2,1,0:T(4,128)} fusion(f32[2,4,4,48]{3,1,2,0:T(4,128)} %copy.73, s32[1024]{0:T(1024)} %pad_clamp_fusion.1), kind=kCustom, calls=%fused_computation.6 | custom fusion | bytes 12304 | tf_op jit(solution)/shard_map/gather | solution.py:94
  108.0 2.0 %gather_fusion.5 = f32[4,2,4,48]{3,2,1,0:T(4,128)} fusion(f32[2,4,4,48]{3,1,2,0:T(4,128)} %copy.71, s32[1024]{0:T(1024)} %pad_clamp_fusion.2), kind=kCustom, calls=%fused_computation.5 | custom fusion | bytes 12304 | tf_op jit(solution)/shard_map/gather | solution.py:94
  111.6 3.9 %convolution_multiply_fusion = f32[1024,768]{1,0:T(8,128)S(1)} fusion(bf16[768,768]{1,0:T(8,128)(2,1)} %bitcast.104, f32[768,1024]{1,0:T(8,128)} %get-tuple-element.22, f32[768]{0:T(1024)} %div.69), kind=kOutput, calls=%fused_computation.12 | convolution fusion | flops 1210318848 | bytes 7474176 | tf_op jit(solution)/shard_map/dot_general | solution.py:115
  122.6 6.7 %collective-permute-done.18 = bf16[4,48,768]{2,1,0:T(8,128)(2,1)S(1)} collective-permute-done((bf16[4,48,768]{2,1,0:T(8,128)(2,1)S(1)}, bf16[4,48,768]{2,1,0:T(8,128)(2,1)S(1)}, u32[]{:S(2)}, u32[]{:S(2)}) %collective-permute-start.18) | collective-permute-done | bytes 294944 | tf_op jit(solution)/shard_map/ppermute | solution.py:39
  129.4 3.1 %collective-permute-done.17 = bf16[4,48,768]{2,1,0:T(8,128)(2,1)S(1)} collective-permute-done((bf16[4,48,768]{2,1,0:T(8,128)(2,1)S(1)}, bf16[4,48,768]{2,1,0:T(8,128)(2,1)S(1)}, u32[]{:S(2)}, u32[]{:S(2)}) %collective-permute-start.17) | collective-permute-done | bytes 294944 | tf_op jit(solution)/shard_map/ppermute | solution.py:39
  132.8 3.0 %collective-permute-start.21 = (bf16[48,768]{1,0:T(8,128)(2,1)S(1)}, bf16[48,768]{1,0:T(8,128)(2,1)S(1)}, u32[]{:S(2)}, u32[]{:S(2)}) collective-permute-start(bf16[48,768]{1,0:T(8,128)(2,1)S(1)} %get-tuple-element.9), channel_id=1, source_target_pairs={{0,6},{1,7},{2,4},{3,5},{4,2},{5,3},{6,0},{7,1},{8,14},{9,15},{10,... | collective-permute-start | bytes 221192 | tf_op jit(solution)/shard_map/ppermute | solution.py:39
  137.2 2.1 %collective-permute-done.21 = bf16[48,768]{1,0:T(8,128)(2,1)S(1)} collective-permute-done((bf16[48,768]{1,0:T(8,128)(2,1)S(1)}, bf16[48,768]{1,0:T(8,128)(2,1)S(1)}, u32[]{:S(2)}, u32[]{:S(2)}) %collective-permute-start.21) | collective-permute-done | bytes 73760 | tf_op jit(solution)/shard_map/ppermute | solution.py:39
  139.4 2.9 %collective-permute-done.20 = bf16[48,768]{1,0:T(8,128)(2,1)S(1)} collective-permute-done((bf16[48,768]{1,0:T(8,128)(2,1)S(1)}, bf16[48,768]{1,0:T(8,128)(2,1)S(1)}, u32[]{:S(2)}, u32[]{:S(2)}) %collective-permute-start.20) | collective-permute-done | bytes 73760 | tf_op jit(solution)/shard_map/ppermute | solution.py:39
  (161 shorter events, 67.0 us)
Async XLA Ops:
  4.8 20.1 %copy-start.20 = (s32[1024]{0:T(1024)}, s32[1024]{0:T(1024)S(1)}, u32[]{:S(2)}) copy-start(s32[1024]{0:T(1024)S(1)} %pad_clamp_fusion.3) | copy-start | bytes 12292
  9.4 46.7 %collective-permute-start.5 = (bf16[48,768]{1,0:T(8,128)(2,1)}, bf16[48,768]{1,0:T(8,128)(2,1)}, u32[]{:S(2)}, u32[]{:S(2)}) collective-permute-start(bf16[48,768]{1,0:T(8,128)(2,1)} %fusion.13), channel_id=1, source_target_pairs={{0,6},{1,7},{2,4},{3,5},{4,2},{5,3},{6,0},{7,1},{8,14},{9,15},{10,... | collective-permute-start | bytes 221192 | tf_op jit(solution)/shard_map/ppermute | solution.py:39
  14.5 41.6 %collective-permute-start.4 = (bf16[48,768]{1,0:T(8,128)(2,1)}, bf16[48,768]{1,0:T(8,128)(2,1)}, u32[]{:S(2)}, u32[]{:S(2)}) collective-permute-start(bf16[48,768]{1,0:T(8,128)(2,1)} %fusion.13), channel_id=1, source_target_pairs={{0,4},{1,5},{2,6},{3,7},{4,0},{5,1},{6,2},{7,3},{8,12},{9,13},{10,... | collective-permute-start | bytes 221192 | tf_op jit(solution)/shard_map/ppermute | solution.py:39
  14.5 28.0 %collective-permute-start.2 = (s32[192,8]{0,1:T(8,128)}, s32[192,8]{0,1:T(8,128)}, u32[]{:S(2)}, u32[]{:S(2)}) collective-permute-start(s32[192,8]{0,1:T(8,128)} %param.17), channel_id=1, source_target_pairs={{0,6},{1,7},{2,4},{3,5},{4,2},{5,3},{6,0},{7,1},{8,14},{9,15},{10,... | collective-permute-start | bytes 18440 | tf_op jit(solution)/shard_map/ppermute | solution.py:39
  16.4 28.0 %collective-permute-start.1 = (s32[192,8]{0,1:T(8,128)}, s32[192,8]{0,1:T(8,128)}, u32[]{:S(2)}, u32[]{:S(2)}) collective-permute-start(s32[192,8]{0,1:T(8,128)} %param.17), channel_id=1, source_target_pairs={{0,4},{1,5},{2,6},{3,7},{4,0},{5,1},{6,2},{7,3},{8,12},{9,13},{10,... | collective-permute-start | bytes 18440 | tf_op jit(solution)/shard_map/ppermute | solution.py:39
  17.4 28.4 %collective-permute-start = (s32[192,8]{0,1:T(8,128)}, s32[192,8]{0,1:T(8,128)}, u32[]{:S(2)}, u32[]{:S(2)}) collective-permute-start(s32[192,8]{0,1:T(8,128)} %param.17), channel_id=1, source_target_pairs={{0,2},{1,3},{2,0},{3,1},{4,6},{5,7},{6,4},{7,5},{8,10},{9,11},{10,... | collective-permute-start | bytes 18440 | tf_op jit(solution)/shard_map/ppermute | solution.py:39
  42.4 13.7 %collective-permute-start.3 = (bf16[48,768]{1,0:T(8,128)(2,1)}, bf16[48,768]{1,0:T(8,128)(2,1)}, u32[]{:S(2)}, u32[]{:S(2)}) collective-permute-start(bf16[48,768]{1,0:T(8,128)(2,1)} %fusion.13), channel_id=1, source_target_pairs={{0,2},{1,3},{2,0},{3,1},{4,6},{5,7},{6,4},{7,5},{8,10},{9,11},{10,... | collective-permute-start | bytes 221192 | tf_op jit(solution)/shard_map/ppermute | solution.py:39
  44.4 26.6 %collective-permute-start.9 = (bf16[560,768]{1,0:T(8,128)(2,1)}, bf16[560,768]{1,0:T(8,128)(2,1)}, u32[]{:S(2)}, u32[]{:S(2)}) collective-permute-start(bf16[560,768]{1,0:T(8,128)(2,1)} %pad_maximum_fusion.3), channel_id=1, source_target_pairs={{0,1},{1,0},{2,3},{3,2},{4,5},{5,4},{6,7},{7,6},{8,9},{9,8},{10,11... | collective-permute-start | bytes 2580488 | tf_op jit(solution)/shard_map/ppermute | solution.py:39
  57.1 12.6 %collective-permute-start.8 = (bf16[3,48,768]{2,1,0:T(8,128)(2,1)S(1)}, bf16[3,48,768]{2,1,0:T(8,128)(2,1)S(1)}, u32[]{:S(2)}, u32[]{:S(2)}) collective-permute-start(bf16[3,48,768]{2,1,0:T(8,128)(2,1)S(1)} %get-tuple-element.12), channel_id=1, source_target_pairs={{0,24},{1,25},{2,26},{3,27},{4,28},{5,29},{6,30},{7,31},{8,16},{9,... | collective-permute-start | bytes 663560 | tf_op jit(solution)/shard_map/ppermute | solution.py:39
  59.6 11.0 %collective-permute-start.7 = (bf16[3,48,768]{2,1,0:T(8,128)(2,1)S(1)}, bf16[3,48,768]{2,1,0:T(8,128)(2,1)S(1)}, u32[]{:S(2)}, u32[]{:S(2)}) collective-permute-start(bf16[3,48,768]{2,1,0:T(8,128)(2,1)S(1)} %get-tuple-element.12), channel_id=1, source_target_pairs={{0,16},{1,17},{2,18},{3,19},{4,20},{5,21},{6,22},{7,23},{8,24},{9,... | collective-permute-start | bytes 663560 | tf_op jit(solution)/shard_map/ppermute | solution.py:39
  60.1 10.6 %collective-permute-start.6 = (bf16[3,48,768]{2,1,0:T(8,128)(2,1)S(1)}, bf16[3,48,768]{2,1,0:T(8,128)(2,1)S(1)}, u32[]{:S(2)}, u32[]{:S(2)}) collective-permute-start(bf16[3,48,768]{2,1,0:T(8,128)(2,1)S(1)} %get-tuple-element.12), channel_id=1, source_target_pairs={{0,8},{1,9},{2,10},{3,11},{4,12},{5,13},{6,14},{7,15},{8,0},{9,1},... | collective-permute-start | bytes 663560 | tf_op jit(solution)/shard_map/ppermute | solution.py:39
  80.1 5.7 %collective-permute-start.12 = (f32[2,4,4,48]{3,2,0,1:T(4,128)}, f32[2,4,4,48]{3,2,0,1:T(4,128)S(1)}, u32[]{:S(2)}, u32[]{:S(2)}) collective-permute-start(f32[2,4,4,48]{3,2,0,1:T(4,128)} %pad_maximum_fusion.9), channel_id=1, source_target_pairs={{0,6},{1,7},{2,4},{3,5},{4,2},{5,3},{6,0},{7,1},{8,14},{9,15},{10,... | collective-permute-start | bytes 18440 | tf_op jit(solution)/shard_map/ppermute | solution.py:39
  83.0 5.4 %collective-permute-start.11 = (f32[2,4,4,48]{3,2,0,1:T(4,128)}, f32[2,4,4,48]{3,2,0,1:T(4,128)}, u32[]{:S(2)}, u32[]{:S(2)}) collective-permute-start(f32[2,4,4,48]{3,2,0,1:T(4,128)} %pad_maximum_fusion.9), channel_id=1, source_target_pairs={{0,4},{1,5},{2,6},{3,7},{4,0},{5,1},{6,2},{7,3},{8,12},{9,13},{10,... | collective-permute-start | bytes 18440 | tf_op jit(solution)/shard_map/ppermute | solution.py:39
  83.0 8.8 %collective-permute-start.10 = (f32[2,4,4,48]{3,2,0,1:T(4,128)}, f32[2,4,4,48]{3,2,0,1:T(4,128)}, u32[]{:S(2)}, u32[]{:S(2)}) collective-permute-start(f32[2,4,4,48]{3,2,0,1:T(4,128)} %pad_maximum_fusion.9), channel_id=1, source_target_pairs={{0,2},{1,3},{2,0},{3,1},{4,6},{5,7},{6,4},{7,5},{8,10},{9,11},{10,... | collective-permute-start | bytes 18440 | tf_op jit(solution)/shard_map/ppermute | solution.py:39
  96.4 4.8 %collective-permute-start.15 = (f32[2,4,4,48]{3,2,0,1:T(4,128)}, f32[2,4,4,48]{3,2,0,1:T(4,128)S(1)}, u32[]{:S(2)}, u32[]{:S(2)}) collective-permute-start(f32[2,4,4,48]{3,2,0,1:T(4,128)} %bitcast_add_fusion.3), channel_id=1, source_target_pairs={{0,24},{1,25},{2,26},{3,27},{4,28},{5,29},{6,30},{7,31},{8,16},{9,... | collective-permute-start | bytes 18440 | tf_op jit(solution)/shard_map/ppermute | solution.py:39
  98.1 5.2 %collective-permute-start.14 = (f32[2,4,4,48]{3,2,0,1:T(4,128)}, f32[2,4,4,48]{3,2,0,1:T(4,128)}, u32[]{:S(2)}, u32[]{:S(2)}) collective-permute-start(f32[2,4,4,48]{3,2,0,1:T(4,128)} %bitcast_add_fusion.3), channel_id=1, source_target_pairs={{0,16},{1,17},{2,18},{3,19},{4,20},{5,21},{6,22},{7,23},{8,24},{9,... | collective-permute-start | bytes 18440 | tf_op jit(solution)/shard_map/ppermute | solution.py:39
  99.4 7.3 %collective-permute-start.13 = (f32[2,4,4,48]{3,2,0,1:T(4,128)}, f32[2,4,4,48]{3,2,0,1:T(4,128)}, u32[]{:S(2)}, u32[]{:S(2)}) collective-permute-start(f32[2,4,4,48]{3,2,0,1:T(4,128)} %bitcast_add_fusion.3), channel_id=1, source_target_pairs={{0,8},{1,9},{2,10},{3,11},{4,12},{5,13},{6,14},{7,15},{8,0},{9,1},... | collective-permute-start | bytes 18440 | tf_op jit(solution)/shard_map/ppermute | solution.py:39
  118.5 10.9 %collective-permute-start.18 = (bf16[4,48,768]{2,1,0:T(8,128)(2,1)S(1)}, bf16[4,48,768]{2,1,0:T(8,128)(2,1)S(1)}, u32[]{:S(2)}, u32[]{:S(2)}) collective-permute-start(bf16[4,48,768]{2,1,0:T(8,128)(2,1)S(1)} %get-tuple-element.7), channel_id=1, source_target_pairs={{0,24},{1,25},{2,26},{3,27},{4,28},{5,29},{6,30},{7,31},{8,16},{9,... | collective-permute-start | bytes 884744 | tf_op jit(solution)/shard_map/ppermute | solution.py:39
  120.2 12.4 %collective-permute-start.17 = (bf16[4,48,768]{2,1,0:T(8,128)(2,1)S(1)}, bf16[4,48,768]{2,1,0:T(8,128)(2,1)S(1)}, u32[]{:S(2)}, u32[]{:S(2)}) collective-permute-start(bf16[4,48,768]{2,1,0:T(8,128)(2,1)S(1)} %get-tuple-element.6), channel_id=1, source_target_pairs={{0,16},{1,17},{2,18},{3,19},{4,20},{5,21},{6,22},{7,23},{8,24},{9,... | collective-permute-start | bytes 884744 | tf_op jit(solution)/shard_map/ppermute | solution.py:39
  121.5 11.1 %collective-permute-start.16 = (bf16[4,48,768]{2,1,0:T(8,128)(2,1)S(1)}, bf16[4,48,768]{2,1,0:T(8,128)(2,1)S(1)}, u32[]{:S(2)}, u32[]{:S(2)}) collective-permute-start(bf16[4,48,768]{2,1,0:T(8,128)(2,1)S(1)} %get-tuple-element.5), channel_id=1, source_target_pairs={{0,8},{1,9},{2,10},{3,11},{4,12},{5,13},{6,14},{7,15},{8,0},{9,1},... | collective-permute-start | bytes 884744 | tf_op jit(solution)/shard_map/ppermute | solution.py:39
  122.6 20.3 %collective-permute-start.22 = (bf16[560,768]{1,0:T(8,128)(2,1)S(1)}, bf16[560,768]{1,0:T(8,128)(2,1)S(1)}, u32[]{:S(2)}, u32[]{:S(2)}) collective-permute-start(bf16[560,768]{1,0:T(8,128)(2,1)S(1)} %pad_maximum_fusion.4), channel_id=1, source_target_pairs={{0,1},{1,0},{2,3},{3,2},{4,5},{5,4},{6,7},{7,6},{8,9},{9,8},{10,11... | collective-permute-start | bytes 2580488 | tf_op jit(solution)/shard_map/ppermute | solution.py:39
  132.8 6.6 %collective-permute-start.21 = (bf16[48,768]{1,0:T(8,128)(2,1)S(1)}, bf16[48,768]{1,0:T(8,128)(2,1)S(1)}, u32[]{:S(2)}, u32[]{:S(2)}) collective-permute-start(bf16[48,768]{1,0:T(8,128)(2,1)S(1)} %get-tuple-element.9), channel_id=1, source_target_pairs={{0,6},{1,7},{2,4},{3,5},{4,2},{5,3},{6,0},{7,1},{8,14},{9,15},{10,... | collective-permute-start | bytes 221192 | tf_op jit(solution)/shard_map/ppermute | solution.py:39
  135.8 6.5 %collective-permute-start.20 = (bf16[48,768]{1,0:T(8,128)(2,1)S(1)}, bf16[48,768]{1,0:T(8,128)(2,1)S(1)}, u32[]{:S(2)}, u32[]{:S(2)}) collective-permute-start(bf16[48,768]{1,0:T(8,128)(2,1)S(1)} %get-tuple-element.10), channel_id=1, source_target_pairs={{0,4},{1,5},{2,6},{3,7},{4,0},{5,1},{6,2},{7,3},{8,12},{9,13},{10,... | collective-permute-start | bytes 221192 | tf_op jit(solution)/shard_map/ppermute | solution.py:39
  135.8 6.5 %collective-permute-start.19 = (bf16[48,768]{1,0:T(8,128)(2,1)S(1)}, bf16[48,768]{1,0:T(8,128)(2,1)S(1)}, u32[]{:S(2)}, u32[]{:S(2)}) collective-permute-start(bf16[48,768]{1,0:T(8,128)(2,1)S(1)} %get-tuple-element.8), channel_id=1, source_target_pairs={{0,2},{1,3},{2,0},{3,1},{4,6},{5,7},{6,4},{7,5},{8,10},{9,11},{10,... | collective-permute-start | bytes 221192 | tf_op jit(solution)/shard_map/ppermute | solution.py:39
  (26 other events, 128.4 us)

commit v2 on v1

v2 whole, which is shorter than its diff:
```python
import functools

import jax
import jax.numpy as jnp
from jax import lax
from jax.experimental import pallas as pl
from jax.experimental.pallas import tpu as pltpu
from jax.sharding import PartitionSpec as P

logit_scale = 50.0
axes = ("tower", "dp")
group = 4
f32 = jnp.float32
bf16 = jnp.bfloat16
last_last = (((1,), (1,)), ((), ()))
first_first = (((0,), (0,)), ((), ()))


def params(mib):
    return pltpu.CompilerParams(vmem_limit_bytes=mib * 2**20)


def normalized(projected):
    squares = jnp.sum(projected * projected, axis=1, keepdims=True)
    return (projected * lax.rsqrt(squares + 1e-06)).astype(bf16)


def query_kernel(steps, part_rows, hidden_ref, weight_ref, unit_ref, part_ref, total):
    step = pl.program_id(0)
    product = jnp.dot(hidden_ref[...], weight_ref[...], preferred_element_type=f32)

    @pl.when(step == 0)
    def _():
        total[...] = product

    @pl.when(step > 0)
    def _():
        total[...] += product

    @pl.when(step == steps - 1)
    def _():
        unit_ref[...] = normalized(total[...])
        start = pl.multiple_of(lax.axis_index("tower") * part_rows, 16)
        part_ref[...] = unit_ref[pl.ds(start, part_rows), :]


def project_queries(hidden, weight, part_rows):
    rows, depth = hidden.shape
    width = weight.shape[1]
    steps = 6
    chunk = depth // steps
    return pl.pallas_call(
        functools.partial(query_kernel, steps, part_rows),
        grid=(steps,),
        in_specs=[
            pl.BlockSpec((rows, chunk), lambda k: (0, k)),
            pl.BlockSpec((chunk, width), lambda k: (k, 0)),
        ],
        out_specs=[
            pl.BlockSpec((rows, width), lambda k: (0, 0)),
            pl.BlockSpec((part_rows, width), lambda k: (0, 0)),
        ],
        out_shape=[
            jax.ShapeDtypeStruct((rows, width), bf16),
            jax.ShapeDtypeStruct((part_rows, width), bf16),
        ],
        scratch_shapes=[pltpu.VMEM((rows, width), f32)],
        compiler_params=params(24),
        cost_estimate=pl.CostEstimate(
            flops=2 * rows * depth * width,
            bytes_accessed=2 * depth * (rows + width),
            transcendentals=0,
        ),
        name="query_units",
    )(hidden, weight)


def item_kernel(steps, pool_ref, passage_ref, weight_ref, unit_ref, total):
    step = pl.program_id(0)
    hidden = jnp.concatenate([pool_ref[...], passage_ref[...]], axis=0)
    product = jnp.dot(hidden, weight_ref[...], preferred_element_type=f32)

    @pl.when(step == 0)
    def _():
        total[...] = product

    @pl.when(step > 0)
    def _():
        total[...] += product

    @pl.when(step == steps - 1)
    def _():
        unit_ref[...] = normalized(total[...])


def project_items(pool, passage, weight):
    depth, width = weight.shape
    rows = pool.shape[0] + passage.shape[0]
    steps = 6
    chunk = depth // steps
    return pl.pallas_call(
        functools.partial(item_kernel, steps),
        grid=(steps,),
        in_specs=[
            pl.BlockSpec((pool.shape[0], chunk), lambda k: (0, k)),
            pl.BlockSpec((passage.shape[0], chunk), lambda k: (0, k)),
            pl.BlockSpec((chunk, width), lambda k: (k, 0)),
        ],
        out_specs=pl.BlockSpec((rows, width), lambda k: (0, 0)),
        out_shape=jax.ShapeDtypeStruct((rows, width), bf16),
        scratch_shapes=[pltpu.VMEM((rows, width), f32)],
        compiler_params=params(24),
        cost_estimate=pl.CostEstimate(
            flops=2 * rows * depth * width,
            bytes_accessed=2 * depth * (rows + width),
            transcendentals=0,
        ),
        name="item_units",
    )(pool, passage, weight)


def count_kernel(pool_rows, ids_ref, count_ref):
    own = lax.axis_index("tower") * lax.axis_size("dp") + lax.axis_index("dp")
    ids = ids_ref[...]
    neg_count, queries = ids.shape
    chunk = 64

    for half in range(2):
        base = (own ^ half) * pool_rows
        local = ids - base

        @pl.loop(0, pool_rows // chunk)
        def _(step):
            rows = lax.broadcasted_iota(jnp.int32, (chunk, queries), 0) + step * chunk
            count = jnp.zeros((chunk, queries), f32)
            for k in range(neg_count):
                count += jnp.where(rows == local[k : k + 1, :], 1.0, 0.0)
            start = pl.multiple_of(half * pool_rows + step * chunk, chunk)
            count_ref[pl.ds(start, chunk), :] = count.astype(bf16)


def count_names(ids, pool_rows, block):
    neg_count, queries = ids.shape
    return pl.pallas_call(
        functools.partial(count_kernel, pool_rows),
        grid=(queries // block,),
        in_specs=[pl.BlockSpec((neg_count, block), lambda g: (0, g))],
        out_specs=pl.BlockSpec((2 * pool_rows, block), lambda g: (0, g)),
        out_shape=jax.ShapeDtypeStruct((2 * pool_rows, queries), bf16),
        compiler_params=params(16),
        cost_estimate=pl.CostEstimate(
            flops=6 * queries * neg_count * pool_rows,
            bytes_accessed=4 * pool_rows * queries,
            transcendentals=0,
        ),
        name="name_counts",
    )(ids)


def positive_mask(query_rows, own_rows, half):
    block = group * query_rows
    dp_size = lax.axis_size("dp")
    tower, dp = lax.axis_index("tower"), lax.axis_index("dp")
    lane = lax.broadcasted_iota(jnp.int32, (1, block), 1)
    query = jnp.zeros((1, block), jnp.int32)
    for k in range(group):
        step = pl.program_id(0) * group + k
        start = (((dp // 2) ^ step) * 2 + dp % 2) * query_rows
        query = jnp.where(
            (lane >= k * query_rows) & (lane < (k + 1) * query_rows),
            start + lane - k * query_rows,
            query,
        )
    first = (tower * dp_size + (dp ^ half)) * own_rows
    passage = lax.broadcasted_iota(jnp.int32, (own_rows, block), 0) + first
    return passage == query


def placed_totals(totals, query_rows):
    place = (lax.axis_index("dp") // 2) % group
    out = totals
    for k in range(1, group):
        turned = jnp.concatenate(
            [
                totals[:, (j ^ k) * query_rows : ((j ^ k) + 1) * query_rows]
                for j in range(group)
            ],
            axis=1,
        )
        out = jnp.where(place == k, turned, out)
    return out


def score_kernel(joined, copies, query_rows, pool_rows, own_rows, part_rows, towers, *refs):
    if joined:
        queries_ref, *refs = refs
    else:
        unit_ref, *refs = refs
        far_refs, refs = refs[:towers], refs[towers:]
    own_ref, other_ref, count_ref, exp_ref, totals_ref, *refs = refs
    if not joined:
        (queries_ref,) = refs
        tower = lax.axis_index("tower")
        queries_ref[:query_rows, :] = unit_ref[...]
        for d in range(towers):
            for s in range(1, group):
                start = pl.multiple_of(s * query_rows + (tower ^ d) * part_rows, 16)
                queries_ref[pl.ds(start, part_rows), :] = far_refs[d][
                    (s - 1) * part_rows : s * part_rows, :
                ]
    queries = queries_ref[...]
    block = queries.shape[0]
    hard = jnp.zeros((1, block), f32)
    batch = jnp.zeros((1, block), f32)
    passage_start = 2 * pool_rows
    chunk = 128
    for half, items_ref in enumerate((own_ref, other_ref)):
        for start in range(0, pool_rows, chunk):
            scores = lax.dot_general(
                items_ref[start : start + chunk, :], queries, last_last, preferred_element_type=f32
            )
            row = half * pool_rows + start
            exps = jnp.exp(logit_scale * scores) * count_ref[row : row + chunk, :].astype(f32)
            hard += jnp.sum(exps, axis=0, keepdims=True)
            exp_ref[row : row + chunk, :] = exps.astype(bf16)
        scores = lax.dot_general(
            items_ref[pool_rows:, :], queries, last_last, preferred_element_type=f32
        )
        exps = jnp.exp(logit_scale * scores)
        batch += jnp.sum(exps, axis=0, keepdims=True)
        mask = positive_mask(query_rows, own_rows, half)
        hard += jnp.sum(jnp.where(mask, exps, 0.0), axis=0, keepdims=True)
        row = passage_start + half * own_rows
        exp_ref[row : row + own_rows, :] = exps.astype(bf16)
    totals = placed_totals(jnp.concatenate([batch, hard], axis=0), query_rows)
    for k in range(copies):
        totals_ref[k] = totals


def score_items(pieces, items, other, count, query_rows, pool_rows, part_rows, towers, copies):
    joined = len(pieces) == 1
    queries = count.shape[1]
    block = group * query_rows
    rows, width = items.shape
    own_rows = rows - pool_rows
    whole = lambda x: pl.BlockSpec(x.shape, lambda g: (0, 0))
    if joined:
        piece_specs = [pl.BlockSpec((block, width), lambda g: (g, 0))]
    else:
        piece_specs = [whole(x) for x in pieces]
    out_specs = [
        pl.BlockSpec((2 * rows, block), lambda g: (0, g)),
        pl.BlockSpec((copies, 2, block), lambda g: (0, 0, g)),
    ]
    out_shape = [
        jax.ShapeDtypeStruct((2 * rows, queries), bf16),
        jax.ShapeDtypeStruct((copies, 2, queries), f32),
    ]
    if not joined:
        out_specs.append(pl.BlockSpec((block, width), lambda g: (g, 0)))
        out_shape.append(jax.ShapeDtypeStruct((queries, width), bf16))
    out = pl.pallas_call(
        functools.partial(
            score_kernel, joined, copies, query_rows, pool_rows, own_rows, part_rows, towers
        ),
        grid=(queries // block,),
        in_specs=piece_specs
        + [whole(items), whole(other), pl.BlockSpec((2 * pool_rows, block), lambda g: (0, g))],
        out_specs=out_specs,
        out_shape=out_shape,
        compiler_params=params(40),
        cost_estimate=pl.CostEstimate(
            flops=4 * rows * queries * width,
            bytes_accessed=8 * rows * queries,
            transcendentals=2 * rows * queries,
        ),
        name="scores",
    )(*pieces, items, other, count)
    return out if not joined else (*out, pieces[0])


def weight_kernel(query_rows, pool_rows, own_rows, part_rows, towers, *refs):
    totals_ref, exp_ref, own_ref, other_ref, weight_ref, *send_refs = refs
    totals = placed_totals(jnp.sum(totals_ref[...], axis=0), query_rows)
    scale = 1.0 / totals
    batch, hard = scale[0:1, :], scale[1:2, :]
    pools = 2 * pool_rows
    weight_ref[:pools, :] = (exp_ref[:pools, :].astype(f32) * hard).astype(bf16)
    for half in range(2):
        row = pools + half * own_rows
        exps = exp_ref[row : row + own_rows, :].astype(f32)
        mask = positive_mask(query_rows, own_rows, half)
        weight_ref[row : row + own_rows, :] = (
            exps * batch + jnp.where(mask, exps * hard - 2.0, 0.0)
        ).astype(bf16)
    tower = lax.axis_index("tower")
    items = jnp.concatenate(
        [
            own_ref[:pool_rows, :],
            other_ref[:pool_rows, :],
            own_ref[pool_rows:, :],
            other_ref[pool_rows:, :],
        ],
        axis=0,
    )
    grad = logit_scale * lax.dot_general(
        weight_ref[...], items, first_first, preferred_element_type=f32
    )
    width = grad.shape[1]
    grad = grad.astype(bf16).reshape(group, towers, part_rows, width)
    for t in range(towers):
        for d in range(towers):

            @pl.when((tower ^ d) == t)
            def _(t=t, d=d):
                send_refs[d][...] = grad[:, t]


def weigh(totals, exps, items, other, query_rows, pool_rows, part_rows, towers):
    rows, width = items.shape
    queries = exps.shape[1]
    block = group * query_rows
    whole = lambda x: pl.BlockSpec(x.shape, lambda g: (0, 0))
    tall = pl.BlockSpec((2 * rows, block), lambda g: (0, g))
    sent = (queries // query_rows, part_rows, width)
    return pl.pallas_call(
        functools.partial(
            weight_kernel, query_rows, pool_rows, rows - pool_rows, part_rows, towers
        ),
        grid=(queries // block,),
        in_specs=[
            pl.BlockSpec((totals.shape[0], 2, block), lambda g: (0, 0, g)),
            tall,
            whole(items),
            whole(other),
        ],
        out_specs=[tall]
        + [pl.BlockSpec((group, part_rows, width), lambda g: (g, 0, 0))] * towers,
        out_shape=[jax.ShapeDtypeStruct((2 * rows, queries), bf16)]
        + [jax.ShapeDtypeStruct(sent, bf16)] * towers,
        compiler_params=params(40),
        cost_estimate=pl.CostEstimate(
            flops=4 * rows * queries * width,
            bytes_accessed=8 * rows * queries,
            transcendentals=0,
        ),
        name="weights",
    )(totals, exps, items, other)


def gradient_kernel(steps, pool_rows, own_rows, weight_ref, queries_ref, own_ref, sent_ref, total):
    step = pl.program_id(0)
    product = jnp.dot(weight_ref[...], queries_ref[...], preferred_element_type=f32)

    @pl.when(step == 0)
    def _():
        total[...] = product

    @pl.when(step > 0)
    def _():
        total[...] += product

    @pl.when(step == steps - 1)
    def _():
        pools = 2 * pool_rows
        own_ref[:pool_rows, :] = logit_scale * total[:pool_rows, :]
        own_ref[pool_rows:, :] = logit_scale * total[pools : pools + own_rows, :]
        sent_ref[:pool_rows, :] = (logit_scale * total[pool_rows:pools, :]).astype(bf16)
        sent_ref[pool_rows:, :] = (logit_scale * total[pools + own_rows :, :]).astype(bf16)


def item_gradients(weights, queries, query_rows, pool_rows):
    rows = weights.shape[0]
    half = rows // 2
    total, width = queries.shape
    block = group * query_rows
    fixed = pl.BlockSpec((half, width), lambda g: (0, 0))
    return pl.pallas_call(
        functools.partial(gradient_kernel, total // block, pool_rows, half - pool_rows),
        grid=(total // block,),
        in_specs=[
            pl.BlockSpec((rows, block), lambda g: (0, g)),
            pl.BlockSpec((block, width), lambda g: (g, 0)),
        ],
        out_specs=[fixed, fixed],
        out_shape=[
            jax.ShapeDtypeStruct((half, width), f32),
            jax.ShapeDtypeStruct((half, width), bf16),
        ],
        scratch_shapes=[pltpu.VMEM((rows, width), f32)],
        compiler_params=params(40),
        cost_estimate=pl.CostEstimate(
            flops=2 * rows * total * width, bytes_accessed=6 * rows * width, transcendentals=0
        ),
        name="item_gradients",
    )(weights, queries)


def shards(query_hidden, passage_hidden, pool_hidden, query_proj, passage_proj, negative_ids):
    towers = lax.axis_size("tower")
    dp_size = lax.axis_size("dp")
    chips = dp_size // 2
    query_rows = query_hidden.shape[0]
    part_rows = query_rows // towers
    pool_rows = pool_hidden.shape[0]
    width = query_proj.shape[1]

    def moved(x, tower_step=0, place_step=0, core_step=0):
        pairs = []
        for source in range(towers * dp_size):
            t, d = divmod(source, dp_size)
            target = ((d // 2) ^ place_step) * 2 + ((d % 2) ^ core_step)
            pairs.append((source, (t ^ tower_step) * dp_size + target))
        return lax.ppermute(x, axes, pairs)

    query_unit, part = project_queries(query_hidden, query_proj, part_rows)
    far = jnp.concatenate([moved(part, place_step=s) for s in range(1, chips)], axis=0)
    ids = jnp.transpose(negative_ids)
    ids = jnp.concatenate([ids] + [moved(ids, place_step=s) for s in range(1, chips)], axis=1)
    spread = [far] + [moved(far, tower_step=d) for d in range(1, towers)]
    items = project_items(pool_hidden, passage_hidden, passage_proj)
    other = moved(items, core_step=1)
    count = count_names(ids, pool_rows, group * query_rows)

    if chips == group:
        pieces = [query_unit] + spread
    else:
        tower = lax.axis_index("tower")
        near = query_unit.reshape(1, towers, part_rows, width)
        blocks = jnp.stack([x.reshape(chips - 1, part_rows, width) for x in spread], axis=1)
        blocks = jnp.take(blocks, tower ^ jnp.arange(towers), axis=1)
        pieces = [jnp.concatenate([near, blocks], axis=0).reshape(-1, width)]
    copies = towers * chips
    exps, totals, queries = score_items(
        pieces, items, other, count, query_rows, pool_rows, part_rows, towers, copies
    )
    if chips != group:
        shift = lax.axis_index("dp") // 2 // group
        turned = shift ^ jnp.arange(chips // group)
        totals = totals.reshape(copies, 2, chips // group, -1)
        totals = jnp.take(totals, turned, axis=2).reshape(copies, 2, -1)
    same_core = [
        [t * dp_size + 2 * z + c for t in range(towers) for z in range(chips)] for c in range(2)
    ]
    totals = lax.all_to_all(totals, axes, 0, 0, axis_index_groups=same_core)
    if chips != group:
        totals = totals.reshape(copies, 2, chips // group, -1)
        totals = jnp.take(totals, turned, axis=2).reshape(copies, 2, -1)
    weights, *sends = weigh(
        totals, exps, items, other, query_rows, pool_rows, part_rows, towers
    )
    line = sends[0].astype(f32)
    for d in range(1, towers):
        line = line + moved(sends[d], tower_step=d).astype(f32)
    line = line.astype(bf16)
    query_grad = line[0].astype(f32)
    for s in range(1, chips):
        query_grad = query_grad + moved(line[s], place_step=s).astype(f32)

    own_grad, sent_grad = item_gradients(weights, queries, query_rows, pool_rows)
    own_grad = own_grad + moved(sent_grad, core_step=1).astype(f32)
    pool_grad = own_grad[:pool_rows].astype(bf16)
    passage_grad = own_grad[pool_rows:].astype(bf16)
    return (query_grad.astype(bf16), passage_grad, pool_grad)


def solution(mesh):
    placed = (
        P("dp", None),
        P(("tower", "dp"), None),
        P(("tower", "dp"), None),
        P(),
        P(),
        P("dp", None),
    )
    return jax.shard_map(
        shards,
        mesh=mesh,
        in_specs=placed,
        out_specs=(P(("dp", "tower"), None), P(("tower", "dp"), None), P(("tower", "dp"), None)),
        check_vma=False,
    )
```

time: 147 us -> 88.1 us (0.60); the launches traced: 145 us -> 87.9 us
  local copies, waits for them, and re-layouts: 42.6 us -> 6.88 us
  other arithmetic: 30.5 us -> 1.11 us
  matrix products: 23.5 us -> 0 us
  Pallas kernels: 0 us -> 18 us
  blocking collectives: 0 us -> 13.4 us
  waiting for transfers between devices: 17.5 us -> 28.2 us
  starting transfers between devices: 29.5 us -> 19.5 us
    dot_general x9 -> x0, matrix products: 23.5 us -> none  [the longest x3 12.1 us: unit_rows(): projected = jnp.dot(hidden, weight, preferred_element_type=jnp.float32)]
    gather x10 -> x0, local copies, waits for them, and re-layouts: 18.8 us -> none  [the longest x3 6 us: shards(): line = line + moved(totals, place_step=s)[:, [k ^ s for k in range(chips)]]]
    pallas_call x0 -> x6, Pallas kernels: none -> 18 us  [the longest x1 5.1 us: project_items(): pl.pallas_call(functools.partial(item_kernel, steps), grid=(steps,), in_s...]
    all_to_all x0 -> x1, blocking collectives: none -> 13.4 us  [shards(): totals = lax.all_to_all(totals, axes, 0, 0, axis_index_groups=same_core)]
    ppermute x23 -> x17, waiting for transfers between devices: 17.5 us -> 28.2 us  [moved(): return lax.ppermute(x, axes, pairs)]
    ppermute x23 -> x17, starting transfers between devices: 29.5 us -> 19.5 us  [moved(): return lax.ppermute(x, axes, pairs)]
    reduce_sum x1 -> x0, other arithmetic: 9 us -> none  [shards(): jnp.sum((named[:, :, None] == pool_index[None, None, :]).astype(f32), axi...]
    ppermute x6 -> x0, local copies, waits for them, and re-layouts: 6.49 us -> none  [moved(): return lax.ppermute(x, axes, pairs)]
  transfers between devices with their start and end apart: 23 -> 17, of which waited for: 9 -> 10; matrix products, arithmetic and copies ran while one was open for 41% -> 1% of each run, Pallas kernels for 0% -> 8%
where the time goes in v2:
time: 88.1 us; the launch traced here: 87.9 us
  waiting for transfers between devices  28.2 us (32%)
  starting transfers between devices  19.5 us (22%)
  Pallas kernels  18 us (20%)
  blocking collectives  13.4 us (15%)
  local copies, waits for them, and re-layouts  6.88 us (8%)
  other arithmetic  1.11 us (1%)
    ppermute x17, waiting for transfers between devices, moved(): return lax.ppermute(x, axes, pairs)  28.2 us
    ppermute x17, starting transfers between devices, moved(): return lax.ppermute(x, axes, pairs)  19.5 us
    all_to_all x1, blocking collectives, shards(): totals = lax.all_to_all(totals, axes, 0, 0, axis_index_groups=same_core)  13.4 us
    unnamed x14, local copies, waits for them, and re-layouts  5.28 us
    pallas_call x1, Pallas kernels, project_items(): pl.pallas_call(functools.partial(item_kernel, steps), grid=(steps,), in_s...  5.1 us
    pallas_call x1, Pallas kernels, score_items(): pl.pallas_call(functools.partial(score_kernel, joined, copies, query_rows...  4.1 us
    pallas_call x1, Pallas kernels, count_names(): pl.pallas_call(functools.partial(count_kernel, pool_rows), grid=(queries...  2.6 us
    pallas_call x1, Pallas kernels, project_queries(): pl.pallas_call(functools.partial(query_kernel, steps, part_rows), grid=(s...  2.54 us
  transfers between devices with their start and end apart: 17, of which 10 were waited for; matrix products, arithmetic and copies ran while one was open for 1% of the time, Pallas kernels for 8%

profile of v2, /device:TPU:0, one launch (start us, length us, event | category | flops | bytes accessed | tf_op | source)
XLA Modules:
  0.0 87.9 jit_solution(3514998859014270475)
XLA Ops:
  0.7 2.4 %copy-done.2 = bf16[3072,768]{1,0:T(8,128)(2,1)S(1)} copy-done((bf16[3072,768]{1,0:T(8,128)(2,1)S(1)}, bf16[3072,768]{1,0:T(8,128)(2,1)}, u32[]{:S(2)}) %copy-start.2) | copy-done | bytes 4718616
  3.1 1.9 %copy-done.3 = bf16[512,3072]{1,0:T(8,128)(2,1)S(1)} copy-done((bf16[512,3072]{1,0:T(8,128)(2,1)S(1)}, bf16[512,3072]{1,0:T(8,128)(2,1)}, u32[]{:S(2)}) %copy-start.3) | copy-done | bytes 3145752
  5.9 5.1 %item_units.1.refs_5_.refs_2_ = bf16[560,768]{1,0:T(8,128)(2,1)S(1)} custom-call(bf16[512,3072]{1,0:T(8,128)(2,1)S(1)} %copy-done.3, bf16[48,3072]{1,0:T(8,128)(2,1)S(1)} %copy-done.4, bf16[3072,768]{1,0:T(8,128)(2,1)S(1)} %copy-done.2), custom_call_target="tpu_custom_call" | custom-call | flops 2642411520 | bytes 8159232 | tf_op jit(solution)/shard_map/item_units/pallas_call | solution.py:101
  11.6 2.5 %query_units.1 = (bf16[192,768]{1,0:T(8,128)(2,1)S(1)}, bf16[48,768]{1,0:T(8,128)(2,1)S(1)}) custom-call(bf16[192,2304]{1,0:T(8,128)(2,1)S(1)} %copy-done.1, bf16[2304,768]{1,0:T(8,128)(2,1)S(1)} %copy-done), custom_call_target="tpu_custom_call" | custom-call | flops 679477248 | bytes 4423680 | tf_op jit(solution)/shard_map/query_units/pallas_call | solution.py:52
  14.1 2.7 %collective-permute-start = (bf16[48,768]{1,0:T(8,128)(2,1)S(1)}, bf16[48,768]{1,0:T(8,128)(2,1)S(1)}, u32[]{:S(2)}, u32[]{:S(2)}) collective-permute-start(bf16[48,768]{1,0:T(8,128)(2,1)S(1)} %get-tuple-element.16), channel_id=1, source_target_pairs={{0,2},{1,3},{2,0},{3,1},{4,6},{5,7},{6,4},{7,5},{8,10},{9,11},{10,... | collective-permute-start | bytes 221192 | tf_op jit(solution)/shard_map/ppermute | solution.py:414
  16.8 2.5 %collective-permute-start.2 = (bf16[48,768]{1,0:T(8,128)(2,1)S(1)}, bf16[48,768]{1,0:T(8,128)(2,1)S(1)}, u32[]{:S(2)}, u32[]{:S(2)}) collective-permute-start(bf16[48,768]{1,0:T(8,128)(2,1)S(1)} %get-tuple-element.16), channel_id=1, source_target_pairs={{0,6},{1,7},{2,4},{3,5},{4,2},{5,3},{6,0},{7,1},{8,14},{9,15},{10,... | collective-permute-start | bytes 221192 | tf_op jit(solution)/shard_map/ppermute | solution.py:414
  19.7 7.0 %collective-permute-done.1 = bf16[48,768]{1,0:T(8,128)(2,1)S(1)} collective-permute-done((bf16[48,768]{1,0:T(8,128)(2,1)S(1)}, bf16[48,768]{1,0:T(8,128)(2,1)S(1)}, u32[]{:S(2)}, u32[]{:S(2)}) %collective-permute-start.1) | collective-permute-done | bytes 73760 | tf_op jit(solution)/shard_map/ppermute | solution.py:414
  26.7 2.5 %collective-permute-start.5 = (bf16[144,768]{1,0:T(8,128)(2,1)S(1)}, bf16[144,768]{1,0:T(8,128)(2,1)S(1)}, u32[]{:S(2)}, u32[]{:S(2)}) collective-permute-start(bf16[144,768]{1,0:T(8,128)(2,1)S(1)} %constant_dynamic-update-slice_fusion.refs_1_), channel_id=1, source_target_pairs={{0,24},{1,25},{2,26},{3,27},{4,28},{5,29},{6,30},{7,31},{8,16},{9,... | collective-permute-start | bytes 663560 | tf_op jit(solution)/shard_map/ppermute | solution.py:414
  30.3 2.7 %collective-permute-start.9 = (s32[8,192]{1,0:T(8,128)S(1)}, s32[8,192]{1,0:T(8,128)S(1)}, u32[]{:S(2)}, u32[]{:S(2)}) collective-permute-start(s32[8,192]{1,0:T(8,128)S(1)} %bitcast.12), channel_id=1, source_target_pairs={{0,6},{1,7},{2,4},{3,5},{4,2},{5,3},{6,0},{7,1},{8,14},{9,15},{10,... | collective-permute-start | bytes 18440 | tf_op jit(solution)/shard_map/ppermute | solution.py:414
  33.0 2.8 %collective-permute-done.9 = s32[8,192]{1,0:T(8,128)S(1)} collective-permute-done((s32[8,192]{1,0:T(8,128)S(1)}, s32[8,192]{1,0:T(8,128)S(1)}, u32[]{:S(2)}, u32[]{:S(2)}) %collective-permute-start.9) | collective-permute-done | bytes 6176 | tf_op jit(solution)/shard_map/ppermute | solution.py:414
  35.7 4.5 %collective-permute-done.8 = s32[8,192]{1,0:T(8,128)S(1)} collective-permute-done((s32[8,192]{1,0:T(8,128)S(1)}, s32[8,192]{1,0:T(8,128)S(1)}, u32[]{:S(2)}, u32[]{:S(2)}) %collective-permute-start.8) | collective-permute-done | bytes 6176 | tf_op jit(solution)/shard_map/ppermute | solution.py:414
  40.6 3.3 %collective-permute-done.7 = s32[8,192]{1,0:T(8,128)S(1)} collective-permute-done((s32[8,192]{1,0:T(8,128)S(1)}, s32[8,192]{1,0:T(8,128)S(1)}, u32[]{:S(2)}, u32[]{:S(2)}) %collective-permute-start.7) | collective-permute-done | bytes 6176 | tf_op jit(solution)/shard_map/ppermute | solution.py:414
  44.0 2.6 %name_counts.1.refs_7_ = bf16[1024,768]{1,0:T(8,128)(2,1)S(1)} custom-call(s32[8,768]{1,0:T(8,128)S(1)} %pad_add_fusion.ids_ref), custom_call_target="tpu_custom_call" | custom-call | flops 18874368 | bytes 1572864 | tf_op jit(solution)/shard_map/name_counts/pallas_call | solution.py:144
  46.6 4.1 %scores.1 = (bf16[1120,768]{1,0:T(8,128)(2,1)S(1)}, f32[16,2,768]{2,1,0:T(2,128)S(1)}, bf16[768,768]{1,0:T(8,128)(2,1)S(1)}) custom-call(bf16[192,768]{1,0:T(8,128)(2,1)S(1)} %get-tuple-element.15.refs_0_, bf16[144,768]{1,0:T(8,128)(2,1)S(1)} %constant_dynamic-update-slice_fusion.refs_1_, bf16[144,768]{1,0:T(8,128)(2,1)S(1)} %collective-permute-done.3.refs_2_, ...), custom_call_target="tpu_custom_call" | custom-call | flops 1321205760 | bytes 3440640 | tf_op jit(solution)/shard_map/scores/pallas_call | solution.py:262
  50.7 13.4 %all_to_all.5.refs_0_ = f32[16,2,768]{2,1,0:T(2,128)S(1)} all-to-all(f32[16,2,768]{2,1,0:T(2,128)S(1)} %get-tuple-element.17), channel_id=1, replica_groups={{0,2,4,6,8,10,12,14,16,18,20,22,24,26,28,30},{1,3,5,7,9,11,13,15,17,19,..., dimensions={0} | all-to-all | bytes 196608 | tf_op jit(solution)/shard_map/all_to_all | solution.py:445
  64.1 2.2 %weights.1 = (bf16[1120,768]{1,0:T(8,128)(2,1)S(1)}, bf16[4,48,768]{2,1,0:T(8,128)(2,1)S(1)}, bf16[4,48,768]{2,1,0:T(8,128)(2,1)S(1)}, bf16[4,48,768]{2,1,0:T(8,128)(2,1)S(1)}, bf16[4,48,768]{2,1,0:T(8,128)(2,1)S(1)}) custom-call(f32[16,2,768]{2,1,0:T(2,128)S(1)} %all_to_all.5.refs_0_, bf16[1120,768]{1,0:T(8,128)(2,1)S(1)} %get-tuple-element.18.refs_1_, ...), custom_call_target="tpu_custom_call" | custom-call | flops 1321205760 | bytes 3440640 | tf_op jit(solution)/shard_map/weights/pallas_call | solution.py:326
  67.8 2.1 %collective-permute-start.12 = (bf16[4,48,768]{2,1,0:T(8,128)(2,1)S(1)}, bf16[4,48,768]{2,1,0:T(8,128)(2,1)S(1)}, u32[]{:S(2)}, u32[]{:S(2)}) collective-permute-start(bf16[4,48,768]{2,1,0:T(8,128)(2,1)S(1)} %get-tuple-element.22), channel_id=1, source_target_pairs={{0,24},{1,25},{2,26},{3,27},{4,28},{5,29},{6,30},{7,31},{8,16},{9,... | collective-permute-start | bytes 884744 | tf_op jit(solution)/shard_map/ppermute | solution.py:414
  69.9 1.5 %item_gradients.1 = (f32[560,768]{1,0:T(8,128)S(1)}, bf16[560,768]{1,0:T(8,128)(2,1)S(1)}) custom-call(bf16[1120,768]{1,0:T(8,128)(2,1)S(1)} %get-tuple-element.23.weight_ref, bf16[768,768]{1,0:T(8,128)(2,1)S(1)} %get-tuple-element.24.queries_ref), custom_call_target="tpu_custom_call" | custom-call | flops 1321205760 | bytes 5160960 | tf_op jit(solution)/shard_map/item_gradients/pallas_call | solution.py:378
  71.5 1.6 %collective-permute-done.10 = bf16[4,48,768]{2,1,0:T(8,128)(2,1)S(1)} collective-permute-done((bf16[4,48,768]{2,1,0:T(8,128)(2,1)S(1)}, bf16[4,48,768]{2,1,0:T(8,128)(2,1)S(1)}, u32[]{:S(2)}, u32[]{:S(2)}) %collective-permute-start.10) | collective-permute-done | bytes 294944 | tf_op jit(solution)/shard_map/ppermute | solution.py:414
  73.1 3.9 %collective-permute-done.11 = bf16[4,48,768]{2,1,0:T(8,128)(2,1)S(1)} collective-permute-done((bf16[4,48,768]{2,1,0:T(8,128)(2,1)S(1)}, bf16[4,48,768]{2,1,0:T(8,128)(2,1)S(1)}, u32[]{:S(2)}, u32[]{:S(2)}) %collective-permute-start.11) | collective-permute-done | bytes 294944 | tf_op jit(solution)/shard_map/ppermute | solution.py:414
  77.7 1.7 %collective-permute-start.15 = (bf16[48,768]{1,0:T(8,128)(2,1)S(1)}, bf16[48,768]{1,0:T(8,128)(2,1)S(1)}, u32[]{:S(2)}, u32[]{:S(2)}) collective-permute-start(bf16[48,768]{1,0:T(8,128)(2,1)S(1)} %get-tuple-element.28), channel_id=1, source_target_pairs={{0,6},{1,7},{2,4},{3,5},{4,2},{5,3},{6,0},{7,1},{8,14},{9,15},{10,... | collective-permute-start | bytes 221192 | tf_op jit(solution)/shard_map/ppermute | solution.py:414
  79.3 1.4 %collective-permute-start.14 = (bf16[48,768]{1,0:T(8,128)(2,1)S(1)}, bf16[48,768]{1,0:T(8,128)(2,1)S(1)}, u32[]{:S(2)}, u32[]{:S(2)}) collective-permute-start(bf16[48,768]{1,0:T(8,128)(2,1)S(1)} %get-tuple-element.29), channel_id=1, source_target_pairs={{0,4},{1,5},{2,6},{3,7},{4,0},{5,1},{6,2},{7,3},{8,12},{9,13},{10,... | collective-permute-start | bytes 221192 | tf_op jit(solution)/shard_map/ppermute | solution.py:414
  81.6 2.3 %collective-permute-done.15 = bf16[48,768]{1,0:T(8,128)(2,1)S(1)} collective-permute-done((bf16[48,768]{1,0:T(8,128)(2,1)S(1)}, bf16[48,768]{1,0:T(8,128)(2,1)S(1)}, u32[]{:S(2)}, u32[]{:S(2)}) %collective-permute-start.15) | collective-permute-done | bytes 73760 | tf_op jit(solution)/shard_map/ppermute | solution.py:414
  83.9 1.6 %collective-permute-done.14 = bf16[48,768]{1,0:T(8,128)(2,1)S(1)} collective-permute-done((bf16[48,768]{1,0:T(8,128)(2,1)S(1)}, bf16[48,768]{1,0:T(8,128)(2,1)S(1)}, u32[]{:S(2)}, u32[]{:S(2)}) %collective-permute-start.14) | collective-permute-done | bytes 73760 | tf_op jit(solution)/shard_map/ppermute | solution.py:414
  (39 shorter events, 8.9 us)
Async XLA Ops:
  0.6 10.9 %copy-start.1 = (bf16[192,2304]{1,0:T(8,128)(2,1)S(1)}, bf16[192,2304]{1,0:T(8,128)(2,1)}, u32[]{:S(2)}) copy-start(bf16[192,2304]{1,0:T(8,128)(2,1)} %hidden_ref.1) | copy-start | bytes 2654212
  0.6 2.4 %copy-start.2 = (bf16[3072,768]{1,0:T(8,128)(2,1)S(1)}, bf16[3072,768]{1,0:T(8,128)(2,1)}, u32[]{:S(2)}) copy-start(bf16[3072,768]{1,0:T(8,128)(2,1)} %weight_ref.3) | copy-start | bytes 14155780
  3.1 1.9 %copy-start.3 = (bf16[512,3072]{1,0:T(8,128)(2,1)S(1)}, bf16[512,3072]{1,0:T(8,128)(2,1)}, u32[]{:S(2)}) copy-start(bf16[512,3072]{1,0:T(8,128)(2,1)} %pool_ref.1) | copy-start | bytes 9437188
  4.9 1.0 %copy-start.4 = (bf16[48,3072]{1,0:T(8,128)(2,1)S(1)}, bf16[48,3072]{1,0:T(8,128)(2,1)}, u32[]{:S(2)}) copy-start(bf16[48,3072]{1,0:T(8,128)(2,1)} %passage_ref.1) | copy-start | bytes 884740
  5.9 5.6 %copy-start = (bf16[2304,768]{1,0:T(8,128)(2,1)S(1)}, bf16[2304,768]{1,0:T(8,128)(2,1)}, u32[]{:S(2)}) copy-start(bf16[2304,768]{1,0:T(8,128)(2,1)} %weight_ref.2) | copy-start | bytes 10616836
  11.0 19.2 %copy-start.5 = (s32[192,8]{0,1:T(8,128)S(1)}, s32[192,8]{0,1:T(8,128)}, u32[]{:S(2)}) copy-start(s32[192,8]{0,1:T(8,128)} %param.11) | copy-start | bytes 18436
  11.0 35.6 %collective-permute-start.6 = (bf16[560,768]{1,0:T(8,128)(2,1)S(1)}, bf16[560,768]{1,0:T(8,128)(2,1)S(1)}, u32[]{:S(2)}, u32[]{:S(2)}) collective-permute-start(bf16[560,768]{1,0:T(8,128)(2,1)S(1)} %item_units.1.refs_5_.refs_2_), channel_id=1, source_target_pairs={{0,1},{1,0},{2,3},{3,2},{4,5},{5,4},{6,7},{7,6},{8,9},{9,8},{10,11... | collective-permute-start | bytes 2580488 | tf_op jit(solution)/shard_map/ppermute | solution.py:414
  14.1 5.6 %collective-permute-start = (bf16[48,768]{1,0:T(8,128)(2,1)S(1)}, bf16[48,768]{1,0:T(8,128)(2,1)S(1)}, u32[]{:S(2)}, u32[]{:S(2)}) collective-permute-start(bf16[48,768]{1,0:T(8,128)(2,1)S(1)} %get-tuple-element.16), channel_id=1, source_target_pairs={{0,2},{1,3},{2,0},{3,1},{4,6},{5,7},{6,4},{7,5},{8,10},{9,11},{10,... | collective-permute-start | bytes 221192 | tf_op jit(solution)/shard_map/ppermute | solution.py:414
  16.8 9.9 %collective-permute-start.2 = (bf16[48,768]{1,0:T(8,128)(2,1)S(1)}, bf16[48,768]{1,0:T(8,128)(2,1)S(1)}, u32[]{:S(2)}, u32[]{:S(2)}) collective-permute-start(bf16[48,768]{1,0:T(8,128)(2,1)S(1)} %get-tuple-element.16), channel_id=1, source_target_pairs={{0,6},{1,7},{2,4},{3,5},{4,2},{5,3},{6,0},{7,1},{8,14},{9,15},{10,... | collective-permute-start | bytes 221192 | tf_op jit(solution)/shard_map/ppermute | solution.py:414
  19.3 7.4 %collective-permute-start.1 = (bf16[48,768]{1,0:T(8,128)(2,1)S(1)}, bf16[48,768]{1,0:T(8,128)(2,1)S(1)}, u32[]{:S(2)}, u32[]{:S(2)}) collective-permute-start(bf16[48,768]{1,0:T(8,128)(2,1)S(1)} %get-tuple-element.16), channel_id=1, source_target_pairs={{0,4},{1,5},{2,6},{3,7},{4,0},{5,1},{6,2},{7,3},{8,12},{9,13},{10,... | collective-permute-start | bytes 221192 | tf_op jit(solution)/shard_map/ppermute | solution.py:414
  26.7 19.9 %collective-permute-start.5 = (bf16[144,768]{1,0:T(8,128)(2,1)S(1)}, bf16[144,768]{1,0:T(8,128)(2,1)S(1)}, u32[]{:S(2)}, u32[]{:S(2)}) collective-permute-start(bf16[144,768]{1,0:T(8,128)(2,1)S(1)} %constant_dynamic-update-slice_fusion.refs_1_), channel_id=1, source_target_pairs={{0,24},{1,25},{2,26},{3,27},{4,28},{5,29},{6,30},{7,31},{8,16},{9,... | collective-permute-start | bytes 663560 | tf_op jit(solution)/shard_map/ppermute | solution.py:414
  29.2 17.4 %collective-permute-start.4 = (bf16[144,768]{1,0:T(8,128)(2,1)S(1)}, bf16[144,768]{1,0:T(8,128)(2,1)S(1)}, u32[]{:S(2)}, u32[]{:S(2)}) collective-permute-start(bf16[144,768]{1,0:T(8,128)(2,1)S(1)} %constant_dynamic-update-slice_fusion.refs_1_), channel_id=1, source_target_pairs={{0,16},{1,17},{2,18},{3,19},{4,20},{5,21},{6,22},{7,23},{8,24},{9,... | collective-permute-start | bytes 663560 | tf_op jit(solution)/shard_map/ppermute | solution.py:414
  29.7 16.9 %collective-permute-start.3 = (bf16[144,768]{1,0:T(8,128)(2,1)S(1)}, bf16[144,768]{1,0:T(8,128)(2,1)S(1)}, u32[]{:S(2)}, u32[]{:S(2)}) collective-permute-start(bf16[144,768]{1,0:T(8,128)(2,1)S(1)} %constant_dynamic-update-slice_fusion.refs_1_), channel_id=1, source_target_pairs={{0,8},{1,9},{2,10},{3,11},{4,12},{5,13},{6,14},{7,15},{8,0},{9,1},... | collective-permute-start | bytes 663560 | tf_op jit(solution)/shard_map/ppermute | solution.py:414
  30.3 5.4 %collective-permute-start.9 = (s32[8,192]{1,0:T(8,128)S(1)}, s32[8,192]{1,0:T(8,128)S(1)}, u32[]{:S(2)}, u32[]{:S(2)}) collective-permute-start(s32[8,192]{1,0:T(8,128)S(1)} %bitcast.12), channel_id=1, source_target_pairs={{0,6},{1,7},{2,4},{3,5},{4,2},{5,3},{6,0},{7,1},{8,14},{9,15},{10,... | collective-permute-start | bytes 18440 | tf_op jit(solution)/shard_map/ppermute | solution.py:414
  35.7 4.5 %collective-permute-start.8 = (s32[8,192]{1,0:T(8,128)S(1)}, s32[8,192]{1,0:T(8,128)S(1)}, u32[]{:S(2)}, u32[]{:S(2)}) collective-permute-start(s32[8,192]{1,0:T(8,128)S(1)} %bitcast.13), channel_id=1, source_target_pairs={{0,4},{1,5},{2,6},{3,7},{4,0},{5,1},{6,2},{7,3},{8,12},{9,13},{10,... | collective-permute-start | bytes 18440 | tf_op jit(solution)/shard_map/ppermute | solution.py:414
  40.3 3.7 %collective-permute-start.7 = (s32[8,192]{1,0:T(8,128)S(1)}, s32[8,192]{1,0:T(8,128)S(1)}, u32[]{:S(2)}, u32[]{:S(2)}) collective-permute-start(s32[8,192]{1,0:T(8,128)S(1)} %bitcast.14), channel_id=1, source_target_pairs={{0,2},{1,3},{2,0},{3,1},{4,6},{5,7},{6,4},{7,5},{8,10},{9,11},{10,... | collective-permute-start | bytes 18440 | tf_op jit(solution)/shard_map/ppermute | solution.py:414
  66.3 6.8 %collective-permute-start.10 = (bf16[4,48,768]{2,1,0:T(8,128)(2,1)S(1)}, bf16[4,48,768]{2,1,0:T(8,128)(2,1)S(1)}, u32[]{:S(2)}, u32[]{:S(2)}) collective-permute-start(bf16[4,48,768]{2,1,0:T(8,128)(2,1)S(1)} %get-tuple-element.20), channel_id=1, source_target_pairs={{0,8},{1,9},{2,10},{3,11},{4,12},{5,13},{6,14},{7,15},{8,0},{9,1},... | collective-permute-start | bytes 884744 | tf_op jit(solution)/shard_map/ppermute | solution.py:414
  67.2 9.9 %collective-permute-start.11 = (bf16[4,48,768]{2,1,0:T(8,128)(2,1)S(1)}, bf16[4,48,768]{2,1,0:T(8,128)(2,1)S(1)}, u32[]{:S(2)}, u32[]{:S(2)}) collective-permute-start(bf16[4,48,768]{2,1,0:T(8,128)(2,1)S(1)} %get-tuple-element.21), channel_id=1, source_target_pairs={{0,16},{1,17},{2,18},{3,19},{4,20},{5,21},{6,22},{7,23},{8,24},{9,... | collective-permute-start | bytes 884744 | tf_op jit(solution)/shard_map/ppermute | solution.py:414
  67.8 9.2 %collective-permute-start.12 = (bf16[4,48,768]{2,1,0:T(8,128)(2,1)S(1)}, bf16[4,48,768]{2,1,0:T(8,128)(2,1)S(1)}, u32[]{:S(2)}, u32[]{:S(2)}) collective-permute-start(bf16[4,48,768]{2,1,0:T(8,128)(2,1)S(1)} %get-tuple-element.22), channel_id=1, source_target_pairs={{0,24},{1,25},{2,26},{3,27},{4,28},{5,29},{6,30},{7,31},{8,16},{9,... | collective-permute-start | bytes 884744 | tf_op jit(solution)/shard_map/ppermute | solution.py:414
  71.4 14.7 %collective-permute-start.16 = (bf16[560,768]{1,0:T(8,128)(2,1)S(1)}, bf16[560,768]{1,0:T(8,128)(2,1)S(1)}, u32[]{:S(2)}, u32[]{:S(2)}) collective-permute-start(bf16[560,768]{1,0:T(8,128)(2,1)S(1)} %get-tuple-element.26), channel_id=1, source_target_pairs={{0,1},{1,0},{2,3},{3,2},{4,5},{5,4},{6,7},{7,6},{8,9},{9,8},{10,11... | collective-permute-start | bytes 2580488 | tf_op jit(solution)/shard_map/ppermute | solution.py:414
  77.2 4.4 %collective-permute-start.13 = (bf16[48,768]{1,0:T(8,128)(2,1)S(1)}, bf16[48,768]{1,0:T(8,128)(2,1)S(1)}, u32[]{:S(2)}, u32[]{:S(2)}) collective-permute-start(bf16[48,768]{1,0:T(8,128)(2,1)S(1)} %get-tuple-element.27), channel_id=1, source_target_pairs={{0,2},{1,3},{2,0},{3,1},{4,6},{5,7},{6,4},{7,5},{8,10},{9,11},{10,... | collective-permute-start | bytes 221192 | tf_op jit(solution)/shard_map/ppermute | solution.py:414
  77.7 6.2 %collective-permute-start.15 = (bf16[48,768]{1,0:T(8,128)(2,1)S(1)}, bf16[48,768]{1,0:T(8,128)(2,1)S(1)}, u32[]{:S(2)}, u32[]{:S(2)}) collective-permute-start(bf16[48,768]{1,0:T(8,128)(2,1)S(1)} %get-tuple-element.28), channel_id=1, source_target_pairs={{0,6},{1,7},{2,4},{3,5},{4,2},{5,3},{6,0},{7,1},{8,14},{9,15},{10,... | collective-permute-start | bytes 221192 | tf_op jit(solution)/shard_map/ppermute | solution.py:414
  79.3 6.1 %collective-permute-start.14 = (bf16[48,768]{1,0:T(8,128)(2,1)S(1)}, bf16[48,768]{1,0:T(8,128)(2,1)S(1)}, u32[]{:S(2)}, u32[]{:S(2)}) collective-permute-start(bf16[48,768]{1,0:T(8,128)(2,1)S(1)} %get-tuple-element.29), channel_id=1, source_target_pairs={{0,4},{1,5},{2,6},{3,7},{4,0},{5,1},{6,2},{7,3},{8,12},{9,13},{10,... | collective-permute-start | bytes 221192 | tf_op jit(solution)/shard_map/ppermute | solution.py:414

commit v3 on v2

v3 whole, which is shorter than its diff:
```python
import functools

import jax
import jax.numpy as jnp
from jax import lax
from jax.experimental import pallas as pl
from jax.experimental.pallas import tpu as pltpu
from jax.sharding import PartitionSpec as P

logit_scale = 50.0
axes = ("tower", "dp")
group = 4
f32 = jnp.float32
bf16 = jnp.bfloat16
last_last = (((1,), (1,)), ((), ()))
first_first = (((0,), (0,)), ((), ()))


def params(mib):
    return pltpu.CompilerParams(vmem_limit_bytes=int(mib * 2**20))


def normalized(projected):
    squares = jnp.sum(projected * projected, axis=1, keepdims=True)
    return (projected * lax.rsqrt(squares + 1e-06)).astype(bf16)


def query_kernel(steps, part_rows, hidden_ref, weight_ref, ids_ref, unit_ref, part_ref, digits_ref, hidden, weight, ids_near, sems, ids_sem):
    depth = weight.shape[0] // steps
    copies = []
    for k in range(steps):
        span = pl.ds(k * depth, depth)
        copies.append(
            (
                pltpu.make_async_copy(hidden_ref.at[:, span], hidden.at[:, span], sems.at[0, k]),
                pltpu.make_async_copy(weight_ref.at[span, :], weight.at[span, :], sems.at[1, k]),
            )
        )
    ids_copy = pltpu.make_async_copy(ids_ref, ids_near, ids_sem)
    ids_copy.start()
    for pair in copies:
        for copy in pair:
            copy.start()
    ids_copy.wait()
    ids = ids_near[...]
    neg_count, rows = ids.shape
    width = weight.shape[1]
    room = -(-rows // 128) * 128
    gap = jnp.zeros((neg_count, room - rows), f32)
    digits = jnp.concatenate(
        [
            ((ids >> 8) - 256).astype(f32),
            gap,
            (ids & 255).astype(f32),
            gap,
            jnp.zeros((neg_count, width - 2 * room), f32),
        ],
        axis=1,
    )
    extra = part_ref.shape[0] - part_rows
    digits = jnp.concatenate([digits, jnp.zeros((extra - neg_count, width), f32)], axis=0)
    digits = digits.astype(bf16)
    part_ref[part_rows:, :] = digits
    digits_ref[...] = digits
    total = None
    for k, pair in enumerate(copies):
        for copy in pair:
            copy.wait()
        span = slice(k * depth, (k + 1) * depth)
        product = jnp.dot(hidden[:, span], weight[span, :], preferred_element_type=f32)
        total = product if total is None else total + product
    unit_ref[...] = normalized(total)
    start = pl.multiple_of(lax.axis_index("tower") * part_rows, 16)
    part_ref[:part_rows, :] = unit_ref[pl.ds(start, part_rows), :]


def project_queries(hidden, weight, ids, part_rows):
    rows, depth = hidden.shape
    width = weight.shape[1]
    steps = 3
    extra = -(-ids.shape[0] // 16) * 16
    far = pl.BlockSpec(memory_space=pltpu.HBM)
    near = pl.BlockSpec(memory_space=pltpu.VMEM)
    return pl.pallas_call(
        functools.partial(query_kernel, steps, part_rows),
        in_specs=[far, far, far],
        out_specs=[near, near, near],
        out_shape=[
            jax.ShapeDtypeStruct((rows, width), bf16),
            jax.ShapeDtypeStruct((part_rows + extra, width), bf16),
            jax.ShapeDtypeStruct((extra, width), bf16),
        ],
        scratch_shapes=[
            pltpu.VMEM((rows, depth), bf16),
            pltpu.VMEM((depth, width), bf16),
            pltpu.VMEM(ids.shape, jnp.int32),
            pltpu.SemaphoreType.DMA((2, steps)),
            pltpu.SemaphoreType.DMA,
        ],
        compiler_params=params(62),
        cost_estimate=pl.CostEstimate(
            flops=2 * rows * depth * width,
            bytes_accessed=2 * depth * (rows + width),
            transcendentals=0,
        ),
        name="query_units",
    )(hidden, weight, ids)


def item_kernel(steps, pool_ref, passage_ref, weight_ref, unit_ref, hidden, weight, sems):
    depth = weight.shape[0] // steps
    pool_rows = pool_ref.shape[0]
    copies = []
    for k in range(steps):
        span = pl.ds(k * depth, depth)
        copies.append(
            (
                pltpu.make_async_copy(
                    pool_ref.at[:, span], hidden.at[pl.ds(0, pool_rows), span], sems.at[0, k]
                ),
                pltpu.make_async_copy(
                    passage_ref.at[:, span],
                    hidden.at[pl.ds(pool_rows, passage_ref.shape[0]), span],
                    sems.at[1, k],
                ),
                pltpu.make_async_copy(weight_ref.at[span, :], weight.at[span, :], sems.at[2, k]),
            )
        )
    for batch in copies:
        for copy in batch:
            copy.start()
    total = None
    for k, batch in enumerate(copies):
        for copy in batch:
            copy.wait()
        span = slice(k * depth, (k + 1) * depth)
        product = jnp.dot(hidden[:, span], weight[span, :], preferred_element_type=f32)
        total = product if total is None else total + product
    unit_ref[...] = normalized(total)


def project_items(pool, passage, weight):
    depth, width = weight.shape
    rows = pool.shape[0] + passage.shape[0]
    steps = 4
    far = pl.BlockSpec(memory_space=pltpu.HBM)
    return pl.pallas_call(
        functools.partial(item_kernel, steps),
        in_specs=[far, far, far],
        out_specs=pl.BlockSpec(memory_space=pltpu.VMEM),
        out_shape=jax.ShapeDtypeStruct((rows, width), bf16),
        scratch_shapes=[
            pltpu.VMEM((rows, depth), bf16),
            pltpu.VMEM((depth, width), bf16),
            pltpu.SemaphoreType.DMA((3, steps)),
        ],
        compiler_params=params(60),
        cost_estimate=pl.CostEstimate(
            flops=2 * rows * depth * width,
            bytes_accessed=2 * depth * (rows + width),
            transcendentals=0,
        ),
        name="item_units",
    )(pool, passage, weight)


def count_kernel(pool_rows, extra, *refs):
    ids_ref, *digit_refs, count_ref = refs
    own = lax.axis_index("tower") * lax.axis_size("dp") + lax.axis_index("dp")
    ids = [ids_ref[...]]
    for ref in digit_refs:
        digits = ref[-extra:, :].astype(f32).astype(jnp.int32)[: ids[0].shape[0]]
        rows = ids[0].shape[1]
        room = -(-rows // 128) * 128
        ids.append(((digits[:, :rows] + 256) << 8) + digits[:, room : room + rows])
    ids = jnp.concatenate(ids, axis=1)
    neg_count, queries = ids.shape
    chunk = 64

    for half in range(2):
        base = (own ^ half) * pool_rows
        local = ids - base

        @pl.loop(0, pool_rows // chunk)
        def _(step):
            rows = lax.broadcasted_iota(jnp.int32, (chunk, queries), 0) + step * chunk
            count = jnp.zeros((chunk, queries), f32)
            for k in range(neg_count):
                count += jnp.where(rows == local[k : k + 1, :], 1.0, 0.0)
            start = pl.multiple_of(half * pool_rows + step * chunk, chunk)
            count_ref[pl.ds(start, chunk), :] = count.astype(bf16)


def count_names(pieces, pool_rows, block):
    neg_count, queries = pieces[0].shape
    if len(pieces) == 1:
        specs = [pl.BlockSpec((neg_count, block), lambda g: (0, g))]
    else:
        queries *= len(pieces)
        specs = [pl.BlockSpec(x.shape, lambda g: (0, 0)) for x in pieces]
    return pl.pallas_call(
        functools.partial(count_kernel, pool_rows, -(-neg_count // 16) * 16),
        grid=(queries // block,),
        in_specs=specs,
        out_specs=pl.BlockSpec((2 * pool_rows, block), lambda g: (0, g)),
        out_shape=jax.ShapeDtypeStruct((2 * pool_rows, queries), bf16),
        compiler_params=params(16),
        cost_estimate=pl.CostEstimate(
            flops=6 * queries * neg_count * pool_rows,
            bytes_accessed=4 * pool_rows * queries,
            transcendentals=0,
        ),
        name="name_counts",
    )(*pieces)


def positive_mask(query_rows, own_rows, half, first_lane, block):
    dp_size = lax.axis_size("dp")
    tower, dp = lax.axis_index("tower"), lax.axis_index("dp")
    lane = lax.broadcasted_iota(jnp.int32, (1, block), 1) + first_lane
    query = jnp.zeros((1, block), jnp.int32)
    for k in range(group):
        step = pl.program_id(0) * group + k
        start = (((dp // 2) ^ step) * 2 + dp % 2) * query_rows
        query = jnp.where(
            (lane >= k * query_rows) & (lane < (k + 1) * query_rows),
            start + lane - k * query_rows,
            query,
        )
    first = (tower * dp_size + (dp ^ half)) * own_rows
    passage = lax.broadcasted_iota(jnp.int32, (own_rows, block), 0) + first
    return passage == query


def placed_totals(totals, query_rows):
    place = (lax.axis_index("dp") // 2) % group
    out = totals
    for k in range(1, group):
        turned = jnp.concatenate(
            [
                totals[:, (j ^ k) * query_rows : ((j ^ k) + 1) * query_rows]
                for j in range(group)
            ],
            axis=1,
        )
        out = jnp.where(place == k, turned, out)
    return out


def score_tile(items_refs, queries, count_ref, exp_ref, start, offset, query_rows, pool_rows):
    chunk = queries.shape[0]
    own_rows = items_refs[0].shape[0] - pool_rows
    lanes = slice(start, start + chunk)
    hard = jnp.zeros((1, chunk), f32)
    batch = jnp.zeros((1, chunk), f32)
    for half, items_ref in enumerate(items_refs):
        scores = lax.dot_general(items_ref[...], queries, last_last, preferred_element_type=f32)
        exps = jnp.exp(logit_scale * scores)
        rows = slice(half * pool_rows, (half + 1) * pool_rows)
        named = exps[:pool_rows] * count_ref[
            rows, offset + start : offset + start + chunk
        ].astype(f32)
        hard += jnp.sum(named, axis=0, keepdims=True)
        exp_ref[rows, lanes] = named.astype(bf16)
        mask = positive_mask(query_rows, own_rows, half, offset + start, chunk)
        hard += jnp.sum(jnp.where(mask, exps[pool_rows:], 0.0), axis=0, keepdims=True)
        batch += jnp.sum(exps[pool_rows:], axis=0, keepdims=True)
        row = 2 * pool_rows + half * own_rows
        exp_ref[row : row + own_rows, lanes] = exps[pool_rows:].astype(bf16)
    return jnp.concatenate([batch, hard], axis=0)


def score_tiles(items_refs, queries_ref, count_ref, exp_ref, offset, query_rows, pool_rows):
    block = queries_ref.shape[0]
    chunk = 256 if block % 256 == 0 else 128
    sums = []
    for start in range(0, block, chunk):
        queries = queries_ref[start : start + chunk, :]
        sums.append(
            score_tile(
                items_refs, queries, count_ref, exp_ref, start, offset, query_rows, pool_rows
            )
        )
    return jnp.concatenate(sums, axis=1)


def joined_kernel(copies, query_rows, pool_rows, queries_ref, own_ref, other_ref, count_ref, *outs):
    exp_ref, totals_ref = outs
    totals = score_tiles(
        (own_ref, other_ref), queries_ref, count_ref, exp_ref, 0, query_rows, pool_rows
    )
    totals = placed_totals(totals, query_rows)
    for k in range(copies):
        totals_ref[k] = totals


def pieces_kernel(copies, query_rows, pool_rows, part_rows, towers, *refs):
    unit_ref, next_ref, *refs = refs
    far_refs, refs = refs[:towers], refs[towers:]
    own_ref, other_ref, count_ref, exp_ref, totals_ref, queries_ref = refs
    tower = lax.axis_index("tower")
    queries_ref[:query_rows, :] = unit_ref[...]
    queries_ref[query_rows : 2 * query_rows, :] = next_ref[...]
    for d in range(towers):
        for s in range(2, group):
            start = pl.multiple_of(s * query_rows + (tower ^ d) * part_rows, 16)
            queries_ref[pl.ds(start, part_rows), :] = far_refs[d][
                (s - 2) * part_rows : (s - 1) * part_rows, :
            ]
    totals = score_tiles(
        (own_ref, other_ref), queries_ref, count_ref, exp_ref, 0, query_rows, pool_rows
    )
    totals = placed_totals(totals, query_rows)
    for k in range(copies):
        totals_ref[k] = totals


def score_cost(rows, queries, width):
    return pl.CostEstimate(
        flops=2 * rows * queries * width,
        bytes_accessed=4 * rows * queries,
        transcendentals=rows * queries,
    )


def score_joined(queries, items, other, count, query_rows, pool_rows, copies):
    total, width = queries.shape
    block = group * query_rows
    rows = 2 * items.shape[0]
    whole = lambda x: pl.BlockSpec(x.shape, lambda g: (0, 0))
    return pl.pallas_call(
        functools.partial(joined_kernel, copies, query_rows, pool_rows),
        grid=(total // block,),
        in_specs=[
            pl.BlockSpec((block, width), lambda g: (g, 0)),
            whole(items),
            whole(other),
            pl.BlockSpec((2 * pool_rows, block), lambda g: (0, g)),
        ],
        out_specs=[
            pl.BlockSpec((rows, block), lambda g: (0, g)),
            pl.BlockSpec((copies, 2, block), lambda g: (0, 0, g)),
        ],
        out_shape=[
            jax.ShapeDtypeStruct((rows, total), bf16),
            jax.ShapeDtypeStruct((copies, 2, total), f32),
        ],
        compiler_params=params(40),
        cost_estimate=score_cost(rows, total, width),
        name="scores",
    )(queries, items, other, count)


def score_pieces(pieces, items, other, count, query_rows, pool_rows, part_rows, copies):
    rows, width = 2 * items.shape[0], items.shape[1]
    queries = group * query_rows
    towers = len(pieces) - 2
    return pl.pallas_call(
        functools.partial(pieces_kernel, copies, query_rows, pool_rows, part_rows, towers),
        grid=(1,),
        out_shape=[
            jax.ShapeDtypeStruct((rows, queries), bf16),
            jax.ShapeDtypeStruct((copies, 2, queries), f32),
            jax.ShapeDtypeStruct((queries, width), bf16),
        ],
        compiler_params=params(32),
        cost_estimate=score_cost(rows, queries, width),
        name="scores",
    )(*pieces, items, other, count)


def weight_kernel(near_far, query_rows, pool_rows, own_rows, part_rows, towers, *refs):
    totals_ref, exp_ref, own_ref, other_ref, weight_ref, *grad_refs = refs
    totals = placed_totals(jnp.sum(totals_ref[...], axis=0), query_rows)
    scale = 1.0 / totals
    pools = 2 * pool_rows
    batch, hard = scale[0:1, :], scale[1:2, :]
    weight_ref[:pools, :] = (exp_ref[:pools, :].astype(f32) * hard).astype(bf16)
    for half in range(2):
        row = pools + half * own_rows
        exps = exp_ref[row : row + own_rows, :].astype(f32)
        mask = positive_mask(query_rows, own_rows, half, 0, exp_ref.shape[1])
        weight_ref[row : row + own_rows, :] = (
            exps * batch + jnp.where(mask, exps * hard - 2.0, 0.0)
        ).astype(bf16)
    tower = lax.axis_index("tower")
    items = jnp.concatenate(
        [
            own_ref[:pool_rows, :],
            other_ref[:pool_rows, :],
            own_ref[pool_rows:, :],
            other_ref[pool_rows:, :],
        ],
        axis=0,
    )
    grad = logit_scale * lax.dot_general(
        weight_ref[...], items, first_first, preferred_element_type=f32
    )
    grad = grad.astype(bf16)
    if near_far:
        near_ref, next_ref, *grad_refs = grad_refs
        near_ref[...] = grad[:query_rows]
        next_ref[...] = grad[query_rows : 2 * query_rows]
        grad = grad[2 * query_rows :]
    grad = grad.reshape(-1, towers, part_rows, grad.shape[1])
    for t in range(towers):
        for d in range(towers):

            @pl.when((tower ^ d) == t)
            def _(t=t, d=d):
                grad_refs[d][...] = grad[:, t]


def weigh(near_far, totals, exps, items, other, query_rows, pool_rows, part_rows, towers):
    rows, width = items.shape
    queries = exps.shape[1]
    block = group * query_rows
    whole = lambda x: pl.BlockSpec(x.shape, lambda g: (0, 0))
    tall = pl.BlockSpec((2 * rows, block), lambda g: (0, g))
    near = pl.BlockSpec((query_rows, width), lambda g: (0, 0))
    if not near_far:
        out_specs, out_shape, sent = [], [], group
    else:
        out_specs = [near, near]
        out_shape = [jax.ShapeDtypeStruct((query_rows, width), bf16)] * 2
        sent = group - 2
    blocks = queries // block
    return pl.pallas_call(
        functools.partial(
            weight_kernel, near_far, query_rows, pool_rows, rows - pool_rows, part_rows, towers
        ),
        grid=(blocks,),
        in_specs=[
            pl.BlockSpec((totals.shape[0], 2, block), lambda g: (0, 0, g)),
            tall,
            whole(items),
            whole(other),
        ],
        out_specs=[tall]
        + out_specs
        + [pl.BlockSpec((sent, part_rows, width), lambda g: (g, 0, 0))] * towers,
        out_shape=[jax.ShapeDtypeStruct((2 * rows, queries), bf16)]
        + out_shape
        + [jax.ShapeDtypeStruct((sent * blocks, part_rows, width), bf16)] * towers,
        compiler_params=params(40),
        cost_estimate=pl.CostEstimate(
            flops=4 * rows * queries * width,
            bytes_accessed=8 * rows * queries,
            transcendentals=0,
        ),
        name="weights",
    )(totals, exps, items, other)


def gradient_kernel(steps, pool_rows, own_rows, weight_ref, queries_ref, own_ref, sent_ref, total):
    step = pl.program_id(0)
    product = jnp.dot(weight_ref[...], queries_ref[...], preferred_element_type=f32)

    @pl.when(step == 0)
    def _():
        total[...] = product

    @pl.when(step > 0)
    def _():
        total[...] += product

    @pl.when(step == steps - 1)
    def _():
        pools = 2 * pool_rows
        own_ref[:pool_rows, :] = logit_scale * total[:pool_rows, :]
        own_ref[pool_rows:, :] = logit_scale * total[pools : pools + own_rows, :]
        sent_ref[:pool_rows, :] = (logit_scale * total[pool_rows:pools, :]).astype(bf16)
        sent_ref[pool_rows:, :] = (logit_scale * total[pools + own_rows :, :]).astype(bf16)


def item_gradients(weights, queries, query_rows, pool_rows):
    rows, total = weights.shape
    half = rows // 2
    width = queries.shape[1]
    block = group * query_rows
    fixed = pl.BlockSpec((half, width), lambda g: (0, 0))
    return pl.pallas_call(
        functools.partial(gradient_kernel, total // block, pool_rows, half - pool_rows),
        grid=(total // block,),
        in_specs=[
            pl.BlockSpec((rows, block), lambda g: (0, g)),
            pl.BlockSpec((block, width), lambda g: (g, 0)),
        ],
        out_specs=[fixed, fixed],
        out_shape=[
            jax.ShapeDtypeStruct((half, width), f32),
            jax.ShapeDtypeStruct((half, width), bf16),
        ],
        scratch_shapes=[pltpu.VMEM((rows, width), f32)],
        compiler_params=params(40),
        cost_estimate=pl.CostEstimate(
            flops=2 * rows * total * width, bytes_accessed=6 * rows * width, transcendentals=0
        ),
        name="item_gradients",
    )(weights, queries)


def join_kernel(pool_rows, own_ref, taken_ref, pool_ref, passage_ref):
    grad = (own_ref[...] + taken_ref[...].astype(f32)).astype(bf16)
    pool_ref[...] = grad[:pool_rows]
    passage_ref[...] = grad[pool_rows:]


def join_gradients(own, taken, pool_rows):
    rows, width = own.shape
    return pl.pallas_call(
        functools.partial(join_kernel, pool_rows),
        out_shape=[
            jax.ShapeDtypeStruct((pool_rows, width), bf16),
            jax.ShapeDtypeStruct((rows - pool_rows, width), bf16),
        ],
        compiler_params=params(16),
        cost_estimate=pl.CostEstimate(
            flops=rows * width, bytes_accessed=8 * rows * width, transcendentals=0
        ),
        name="join_item_gradients",
    )(own, taken)


def line_kernel(towers, part_rows, near_far, *refs):
    ins, refs = refs[:towers], refs[towers:]
    if near_far:
        near_ref, arrived_ref, *refs = refs
        plane_refs, refs = refs[:towers], refs[towers:]
        tower = lax.axis_index("tower")
        for d, out_ref in enumerate(plane_refs):
            rows = pl.ds(pl.multiple_of((tower ^ d) * part_rows, 16), part_rows)
            total = near_ref[rows, :].astype(f32) + arrived_ref[rows, :].astype(f32)
            out_ref[...] = total.astype(bf16)
    for s, out_ref in enumerate(refs):
        total = ins[0][s].astype(f32)
        for ref in ins[1:]:
            total += ref[s].astype(f32)
        out_ref[...] = total.astype(bf16)


def sum_lines(pieces, near=()):
    chips, rows, width = pieces[0].shape
    towers = len(pieces)
    outs = chips + (towers if near else 0)
    out = pl.pallas_call(
        functools.partial(line_kernel, towers, rows, len(near) > 0),
        out_shape=[jax.ShapeDtypeStruct((rows, width), bf16)] * outs,
        compiler_params=params(32),
        cost_estimate=pl.CostEstimate(
            flops=4 * outs * rows * width,
            bytes_accessed=10 * outs * rows * width,
            transcendentals=0,
        ),
        name="partial_sums",
    )(*pieces, *near)
    return (out[:towers], out[towers:]) if near else out


def shards(query_hidden, passage_hidden, pool_hidden, query_proj, passage_proj, negative_ids):
    towers = lax.axis_size("tower")
    dp_size = lax.axis_size("dp")
    chips = dp_size // 2
    query_rows = query_hidden.shape[0]
    part_rows = query_rows // towers
    pool_rows = pool_hidden.shape[0]
    width = query_proj.shape[1]

    def moved(x, tower_step=0, place_step=0, core_step=0):
        pairs = []
        for source in range(towers * dp_size):
            t, d = divmod(source, dp_size)
            target = ((d // 2) ^ place_step) * 2 + ((d % 2) ^ core_step)
            pairs.append((source, (t ^ tower_step) * dp_size + target))
        return lax.ppermute(x, axes, pairs)

    ids = jnp.transpose(negative_ids)
    near_far = chips == group
    copies = towers * chips
    query_unit, part, digits = project_queries(query_hidden, query_proj, ids, part_rows)
    parts = [moved(part, place_step=s) for s in range(2 if near_far else 1, chips)]
    far = jnp.concatenate([x[:part_rows] for x in parts], axis=0)
    if near_far:
        next_digits = moved(digits, place_step=1)
        far, next_digits = lax.optimization_barrier((far, next_digits))
    spread = [far] + [moved(far, tower_step=d) for d in range(1, towers)]
    pool_hidden, part = lax.optimization_barrier((pool_hidden, part))
    items = project_items(pool_hidden, passage_hidden, passage_proj)
    sent_items, _ = lax.optimization_barrier((items, far))
    other = moved(sent_items, core_step=1)
    if near_far:
        sent_unit, _ = lax.optimization_barrier((query_unit, far))
        next_unit = moved(sent_unit, place_step=1)
        count = count_names([ids, next_digits] + parts, pool_rows, group * query_rows)
        exps, totals, queries = score_pieces(
            [query_unit, next_unit] + spread,
            items,
            other,
            count,
            query_rows,
            pool_rows,
            part_rows,
            copies,
        )
    else:
        neg_count = ids.shape[0]
        room = -(-query_rows // 128) * 128
        ids = [ids]
        for x in parts:
            digits = x[part_rows : part_rows + neg_count].astype(f32).astype(jnp.int32)
            ids.append(
                ((digits[:, :query_rows] + 256) << 8) + digits[:, room : room + query_rows]
            )
        count = count_names([jnp.concatenate(ids, axis=1)], pool_rows, group * query_rows)
        tower = lax.axis_index("tower")
        near = query_unit.reshape(1, towers, part_rows, width)
        blocks = jnp.stack([x.reshape(chips - 1, part_rows, width) for x in spread], axis=1)
        blocks = jnp.take(blocks, tower ^ jnp.arange(towers), axis=1)
        queries = jnp.concatenate([near, blocks], axis=0).reshape(-1, width)
        exps, totals = score_joined(
            queries, items, other, count, query_rows, pool_rows, copies
        )
        shift = lax.axis_index("dp") // 2 // group
        turned = shift ^ jnp.arange(chips // group)
        totals = totals.reshape(copies, 2, chips // group, -1)
        totals = jnp.take(totals, turned, axis=2).reshape(copies, 2, -1)
    same_core = [
        [t * dp_size + 2 * z + c for t in range(towers) for z in range(chips)] for c in range(2)
    ]
    totals = lax.all_to_all(totals, axes, 0, 0, axis_index_groups=same_core)
    if not near_far:
        totals = totals.reshape(copies, 2, chips // group, -1)
        totals = jnp.take(totals, turned, axis=2).reshape(copies, 2, -1)
    weights, *grads = weigh(
        near_far, totals, exps, items, other, query_rows, pool_rows, part_rows, towers
    )
    own_grad, sent_grad = item_gradients(weights, queries, query_rows, pool_rows)
    if near_far:
        near_grad, next_grad, *grads = grads
    sums = [grads[0]] + [moved(grads[d], tower_step=d) for d in range(1, towers)]
    if near_far:
        plane, line = sum_lines(sums, (near_grad, moved(next_grad, place_step=1)))
        arrived = [moved(line[s - 2], place_step=s) for s in range(2, chips)]
        arrived += [moved(plane[d], tower_step=d) for d in range(1, towers)]
        own_line = plane[0]
    else:
        line = sum_lines(sums)
        arrived = [moved(line[s], place_step=s) for s in range(1, chips)]
        own_line = line[0]
    sent_grad, own_line = lax.optimization_barrier((sent_grad, own_line))
    taken_grad = moved(sent_grad, core_step=1)
    pool_grad, passage_grad = join_gradients(own_grad, taken_grad, pool_rows)
    own_line, pool_grad = lax.optimization_barrier((own_line, pool_grad))
    query_grad = own_line.astype(f32)
    for x in arrived:
        query_grad = query_grad + x.astype(f32)
    return (query_grad.astype(bf16), passage_grad, pool_grad)


def solution(mesh):
    placed = (
        P("dp", None),
        P(("tower", "dp"), None),
        P(("tower", "dp"), None),
        P(),
        P(),
        P("dp", None),
    )
    return jax.shard_map(
        shards,
        mesh=mesh,
        in_specs=placed,
        out_specs=(P(("dp", "tower"), None), P(("tower", "dp"), None), P(("tower", "dp"), None)),
        check_vma=False,
    )
```

time: 88.1 us -> 66.8 us (0.76)
  waiting for transfers between devices: 28.2 us -> 9.61 us
  local copies, waits for them, and re-layouts: 6.88 us -> 0.02 us
  starting transfers between devices: 19.5 us -> 22.5 us
  Pallas kernels: 18 us -> 20.4 us
    ppermute x17 -> x18, waiting for transfers between devices: 28.2 us -> 9.61 us  [moved(): return lax.ppermute(x, axes, pairs)]
    unnamed x14 -> x6, local copies, waits for them, and re-layouts: 5.28 us -> 0.01 us
    ppermute x17 -> x18, starting transfers between devices: 19.5 us -> 22.5 us  [moved(): return lax.ppermute(x, axes, pairs)]
    pallas_call x5 -> x7, Pallas kernels: 16.5 us -> 18.8 us  [the longest x1 7.22 us: project_items(): pl.pallas_call(functools.partial(item_kernel, steps), in_specs=[far, far,...]
    slice x2, local copies, waits for them, and re-layouts: 1.57 us -> 0.01 us  [shards(): far = jnp.concatenate([x[:part_rows] for x in parts], axis=0)]
  transfers between devices with their start and end apart: 17 -> 18, of which waited for: 10 -> 9; matrix products, arithmetic and copies ran while one was open for 1% -> 0% of each run, Pallas kernels for 8% -> 19%
where the time goes in v3:
time: 66.8 us; the launch traced here: 66.7 us
  starting transfers between devices  22.5 us (34%)
  Pallas kernels  20.4 us (31%)
  blocking collectives  12.7 us (19%)
  waiting for transfers between devices  9.61 us (14%)
  between operations  0.76 us (1%)
  other arithmetic  0.71 us (1%)
    ppermute x18, starting transfers between devices, moved(): return lax.ppermute(x, axes, pairs)  22.5 us
    all_to_all x1, blocking collectives, shards(): totals = lax.all_to_all(totals, axes, 0, 0, axis_index_groups=same_core)  12.7 us
    ppermute x18, waiting for transfers between devices, moved(): return lax.ppermute(x, axes, pairs)  9.61 us
    pallas_call x1, Pallas kernels, project_items(): pl.pallas_call(functools.partial(item_kernel, steps), in_specs=[far, far,...  7.22 us
    pallas_call x1, Pallas kernels, project_queries(): pl.pallas_call(functools.partial(query_kernel, steps, part_rows), in_spec...  3.72 us
    pallas_call x1, Pallas kernels, count_names(): pl.pallas_call(functools.partial(count_kernel, pool_rows, -(-neg_count //...  2.67 us
    pallas_call x1, Pallas kernels, weigh(): pl.pallas_call(functools.partial(weight_kernel, near_far, query_rows, poo...  2.12 us
    pallas_call x1, Pallas kernels, score_pieces(): pl.pallas_call(functools.partial(pieces_kernel, copies, query_rows, pool_...  1.93 us
  transfers between devices with their start and end apart: 18, of which 9 were waited for; matrix products, arithmetic and copies ran while one was open for 0% of the time, Pallas kernels for 19%

profile of v3, /device:TPU:0, one launch (start us, length us, event | category | flops | bytes accessed | tf_op | source)
XLA Modules:
  0.0 66.7 jit_solution(15899848552810173149)
XLA Ops:
  0.6 3.7 %query_units.1 = (bf16[192,768]{1,0:T(8,128)(2,1)}, bf16[64,768]{1,0:T(8,128)(2,1)}, bf16[16,768]{1,0:T(8,128)(2,1)}) custom-call(bf16[192,2304]{1,0:T(8,128)(2,1)} %hidden_ref.1, bf16[2304,768]{1,0:T(8,128)(2,1)} %weight_ref.2, s32[8,192]{1,0:T(8,128)} %bitcast.1), custom_call_target="tpu_custom_call" | custom-call | flops 679477248 | bytes 4423680 | tf_op jit(solution)/shard_map/query_units/pallas_call | solution.py:84
  4.4 5.1 %collective-permute-start.1 = (bf16[64,768]{1,0:T(8,128)(2,1)}, bf16[64,768]{1,0:T(8,128)(2,1)S(1)}, u32[]{:S(2)}, u32[]{:S(2)}) collective-permute-start(bf16[64,768]{1,0:T(8,128)(2,1)} %get-tuple-element.36), channel_id=1, source_target_pairs={{0,6},{1,7},{2,4},{3,5},{4,2},{5,3},{6,0},{7,1},{8,14},{9,15},{10,... | collective-permute-start | bytes 294920 | tf_op jit(solution)/shard_map/ppermute | solution.py:575
  10.1 7.2 %item_units.1.refs_6_.refs_2_ = bf16[560,768]{1,0:T(8,128)(2,1)} custom-call(bf16[512,3072]{1,0:T(8,128)(2,1)} %pool_ref, bf16[48,3072]{1,0:T(8,128)(2,1)} %passage_ref.1, bf16[3072,768]{1,0:T(8,128)(2,1)} %weight_ref.3), custom_call_target="tpu_custom_call" | custom-call | flops 2642411520 | bytes 8159232 | tf_op jit(solution)/shard_map/item_units/pallas_call | solution.py:147
  18.1 0.9 %collective-permute-start.3 = (bf16[192,768]{1,0:T(8,128)(2,1)S(1)}, bf16[192,768]{1,0:T(8,128)(2,1)S(1)}, u32[]{:S(2)}, u32[]{:S(2)}) collective-permute-start(bf16[192,768]{1,0:T(8,128)(2,1)S(1)} %copy-done.2), channel_id=1, source_target_pairs={{0,2},{1,3},{2,0},{3,1},{4,6},{5,7},{6,4},{7,5},{8,10},{9,11},{10,... | collective-permute-start | bytes 884744 | tf_op jit(solution)/shard_map/ppermute | solution.py:575
  19.0 2.4 %collective-permute-start.6 = (bf16[96,768]{1,0:T(8,128)(2,1)S(1)}, bf16[96,768]{1,0:T(8,128)(2,1)S(1)}, u32[]{:S(2)}, u32[]{:S(2)}) collective-permute-start(bf16[96,768]{1,0:T(8,128)(2,1)S(1)} %pad_maximum_fusion.refs_2_), channel_id=1, source_target_pairs={{0,24},{1,25},{2,26},{3,27},{4,28},{5,29},{6,30},{7,31},{8,16},{9,... | collective-permute-start | bytes 442376 | tf_op jit(solution)/shard_map/ppermute | solution.py:575
  22.5 2.7 %name_counts.1.refs_8_ = bf16[1024,768]{1,0:T(8,128)(2,1)S(1)} custom-call(s32[8,192]{1,0:T(8,128)S(1)} %bitcast.2, bf16[16,768]{1,0:T(8,128)(2,1)S(1)} %collective-permute-done.2.refs_1_, bf16[64,768]{1,0:T(8,128)(2,1)S(1)} %collective-permute-done.refs_2_, bf16[64,768]{1,0:T(8,128)(2,1)S(1)} %collective-permute-done.1.refs_3_), custom_call_target="tpu_custom_call" | custom-call | flops 18874368 | bytes 1572864 | tf_op jit(solution)/shard_map/name_counts/pallas_call | solution.py:201
  25.2 1.3 %collective-permute-done.6.refs_5_ = bf16[96,768]{1,0:T(8,128)(2,1)S(1)} collective-permute-done((bf16[96,768]{1,0:T(8,128)(2,1)S(1)}, bf16[96,768]{1,0:T(8,128)(2,1)S(1)}, u32[]{:S(2)}, u32[]{:S(2)}) %collective-permute-start.6) | collective-permute-done | bytes 147488 | tf_op jit(solution)/shard_map/ppermute | solution.py:575
  26.4 2.5 %collective-permute-done.5.refs_4_ = bf16[96,768]{1,0:T(8,128)(2,1)S(1)} collective-permute-done((bf16[96,768]{1,0:T(8,128)(2,1)S(1)}, bf16[96,768]{1,0:T(8,128)(2,1)S(1)}, u32[]{:S(2)}, u32[]{:S(2)}) %collective-permute-start.5) | collective-permute-done | bytes 147488 | tf_op jit(solution)/shard_map/ppermute | solution.py:575
  29.1 1.9 %scores.1 = (bf16[1120,768]{1,0:T(8,128)(2,1)S(1)}, f32[16,2,768]{2,1,0:T(2,128)S(1)}, bf16[768,768]{1,0:T(8,128)(2,1)S(1)}) custom-call(bf16[192,768]{1,0:T(8,128)(2,1)S(1)} %copy-done.2, bf16[192,768]{1,0:T(8,128)(2,1)S(1)} %collective-permute-done.3.refs_1_, bf16[96,768]{1,0:T(8,128)(2,1)S(1)} %pad_maximum_fusion.refs_2_, ...), custom_call_target="tpu_custom_call" | custom-call | flops 1321205760 | bytes 3440640 | tf_op jit(solution)/shard_map/scores/pallas_call | solution.py:358
  31.0 12.7 %all_to_all.5.refs_0_ = f32[16,2,768]{2,1,0:T(2,128)S(1)} all-to-all(f32[16,2,768]{2,1,0:T(2,128)S(1)} %get-tuple-element.43), channel_id=1, replica_groups={{0,2,4,6,8,10,12,14,16,18,20,22,24,26,28,30},{1,3,5,7,9,11,13,15,17,19,..., dimensions={0} | all-to-all | bytes 196608 | tf_op jit(solution)/shard_map/all_to_all | solution.py:630
  43.7 2.1 %weights.1 = (bf16[1120,768]{1,0:T(8,128)(2,1)S(1)}, bf16[192,768]{1,0:T(8,128)(2,1)S(1)}, bf16[192,768]{1,0:T(8,128)(2,1)S(1)}, bf16[2,48,768]{2,1,0:T(8,128)(2...) custom-call(f32[16,2,768]{2,1,0:T(2,128)S(1)} %all_to_all.5.refs_0_, ...), custom_call_target="tpu_custom_call" | custom-call | flops 1321205760 | bytes 3440640 | tf_op jit(solution)/shard_map/weights/pallas_call | solution.py:428
  45.9 1.2 %collective-permute-start.11 = (bf16[192,768]{1,0:T(8,128)(2,1)S(1)}, bf16[192,768]{1,0:T(8,128)(2,1)S(1)}, u32[]{:S(2)}, u32[]{:S(2)}) collective-permute-start(bf16[192,768]{1,0:T(8,128)(2,1)S(1)} %get-tuple-element.53), channel_id=1, source_target_pairs={{0,2},{1,3},{2,0},{3,1},{4,6},{5,7},{6,4},{7,5},{8,10},{9,11},{10,... | collective-permute-start | bytes 884744 | tf_op jit(solution)/shard_map/ppermute | solution.py:575
  47.0 1.1 %collective-permute-start.9 = (bf16[2,48,768]{2,1,0:T(8,128)(2,1)S(1)}, bf16[2,48,768]{2,1,0:T(8,128)(2,1)S(1)}, u32[]{:S(2)}, u32[]{:S(2)}) collective-permute-start(bf16[2,48,768]{2,1,0:T(8,128)(2,1)S(1)} %get-tuple-element.50), channel_id=1, source_target_pairs={{0,16},{1,17},{2,18},{3,19},{4,20},{5,21},{6,22},{7,23},{8,24},{9,... | collective-permute-start | bytes 442376 | tf_op jit(solution)/shard_map/ppermute | solution.py:575
  48.1 2.4 %collective-permute-start.10 = (bf16[2,48,768]{2,1,0:T(8,128)(2,1)S(1)}, bf16[2,48,768]{2,1,0:T(8,128)(2,1)S(1)}, u32[]{:S(2)}, u32[]{:S(2)}) collective-permute-start(bf16[2,48,768]{2,1,0:T(8,128)(2,1)S(1)} %get-tuple-element.51), channel_id=1, source_target_pairs={{0,24},{1,25},{2,26},{3,27},{4,28},{5,29},{6,30},{7,31},{8,16},{9,... | collective-permute-start | bytes 442376 | tf_op jit(solution)/shard_map/ppermute | solution.py:575
  50.5 1.5 %item_gradients.1 = (f32[560,768]{1,0:T(8,128)S(1)}, bf16[560,768]{1,0:T(8,128)(2,1)S(1)}) custom-call(bf16[1120,768]{1,0:T(8,128)(2,1)S(1)} %get-tuple-element.45.weight_ref, bf16[768,768]{1,0:T(8,128)(2,1)S(1)} %get-tuple-element.46.queries_ref), custom_call_target="tpu_custom_call" | custom-call | flops 1321205760 | bytes 5160960 | tf_op jit(solution)/shard_map/item_gradients/pallas_call | solution.py:482
  52.5 1.7 %collective-permute-done.10.refs_3_ = bf16[2,48,768]{2,1,0:T(8,128)(2,1)S(1)} collective-permute-done((bf16[2,48,768]{2,1,0:T(8,128)(2,1)S(1)}, bf16[2,48,768]{2,1,0:T(8,128)(2,1)S(1)}, u32[]{:S(2)}, u32[]{:S(2)}) %collective-permute-start.10) | collective-permute-done | bytes 147488 | tf_op jit(solution)/shard_map/ppermute | solution.py:575
  54.4 1.2 %collective-permute-start.13 = (bf16[48,768]{1,0:T(8,128)(2,1)S(1)}, bf16[48,768]{1,0:T(8,128)(2,1)S(1)}, u32[]{:S(2)}, u32[]{:S(2)}) collective-permute-start(bf16[48,768]{1,0:T(8,128)(2,1)S(1)} %get-tuple-element.60), channel_id=1, source_target_pairs={{0,4},{1,5},{2,6},{3,7},{4,0},{5,1},{6,2},{7,3},{8,12},{9,13},{10,... | collective-permute-start | bytes 221192 | tf_op jit(solution)/shard_map/ppermute | solution.py:575
  55.6 2.9 %collective-permute-start.14 = (bf16[48,768]{1,0:T(8,128)(2,1)S(1)}, bf16[48,768]{1,0:T(8,128)(2,1)S(1)}, u32[]{:S(2)}, u32[]{:S(2)}) collective-permute-start(bf16[48,768]{1,0:T(8,128)(2,1)S(1)} %get-tuple-element.61), channel_id=1, source_target_pairs={{0,6},{1,7},{2,4},{3,5},{4,2},{5,3},{6,0},{7,1},{8,14},{9,15},{10,... | collective-permute-start | bytes 221192 | tf_op jit(solution)/shard_map/ppermute | solution.py:575
  58.5 1.3 %collective-permute-start.15 = (bf16[48,768]{1,0:T(8,128)(2,1)S(1)}, bf16[48,768]{1,0:T(8,128)(2,1)S(1)}, u32[]{:S(2)}, u32[]{:S(2)}) collective-permute-start(bf16[48,768]{1,0:T(8,128)(2,1)S(1)} %get-tuple-element.62), channel_id=1, source_target_pairs={{0,8},{1,9},{2,10},{3,11},{4,12},{5,13},{6,14},{7,15},{8,0},{9,1},... | collective-permute-start | bytes 221192 | tf_op jit(solution)/shard_map/ppermute | solution.py:575
  59.8 0.9 %collective-permute-start.16 = (bf16[48,768]{1,0:T(8,128)(2,1)S(1)}, bf16[48,768]{1,0:T(8,128)(2,1)S(1)}, u32[]{:S(2)}, u32[]{:S(2)}) collective-permute-start(bf16[48,768]{1,0:T(8,128)(2,1)S(1)} %get-tuple-element.63), channel_id=1, source_target_pairs={{0,16},{1,17},{2,18},{3,19},{4,20},{5,21},{6,22},{7,23},{8,24},{9,... | collective-permute-start | bytes 221192 | tf_op jit(solution)/shard_map/ppermute | solution.py:575
  60.7 1.2 %collective-permute-start.17 = (bf16[48,768]{1,0:T(8,128)(2,1)S(1)}, bf16[48,768]{1,0:T(8,128)(2,1)S(1)}, u32[]{:S(2)}, u32[]{:S(2)}) collective-permute-start(bf16[48,768]{1,0:T(8,128)(2,1)S(1)} %get-tuple-element.64), channel_id=1, source_target_pairs={{0,24},{1,25},{2,26},{3,27},{4,28},{5,29},{6,30},{7,31},{8,16},{9,... | collective-permute-start | bytes 221192 | tf_op jit(solution)/shard_map/ppermute | solution.py:575
  62.0 1.0 %join_item_gradients.1 = (bf16[512,768]{1,0:T(8,128)(2,1)}, bf16[48,768]{1,0:T(8,128)(2,1)}) custom-call(f32[560,768]{1,0:T(8,128)S(1)} %get-tuple-element.56.own_ref, bf16[560,768]{1,0:T(8,128)(2,1)S(1)} %collective-permute-done.12.taken_ref), custom_call_target="tpu_custom_call" | custom-call | flops 430080 | bytes 3440640 | tf_op jit(solution)/shard_map/join_item_gradients/pallas_call | solution.py:511
  63.6 1.3 %collective-permute-done.16 = bf16[48,768]{1,0:T(8,128)(2,1)S(1)} collective-permute-done((bf16[48,768]{1,0:T(8,128)(2,1)S(1)}, bf16[48,768]{1,0:T(8,128)(2,1)S(1)}, u32[]{:S(2)}, u32[]{:S(2)}) %collective-permute-start.16) | collective-permute-done | bytes 73760 | tf_op jit(solution)/shard_map/ppermute | solution.py:575
  64.9 1.1 %collective-permute-done.17 = bf16[48,768]{1,0:T(8,128)(2,1)S(1)} collective-permute-done((bf16[48,768]{1,0:T(8,128)(2,1)S(1)}, bf16[48,768]{1,0:T(8,128)(2,1)S(1)}, u32[]{:S(2)}, u32[]{:S(2)}) %collective-permute-start.17) | collective-permute-done | bytes 73760 | tf_op jit(solution)/shard_map/ppermute | solution.py:575
  (31 shorter events, 4.5 us)
Async XLA Ops:
  4.4 13.0 %collective-permute-start.1 = (bf16[64,768]{1,0:T(8,128)(2,1)}, bf16[64,768]{1,0:T(8,128)(2,1)S(1)}, u32[]{:S(2)}, u32[]{:S(2)}) collective-permute-start(bf16[64,768]{1,0:T(8,128)(2,1)} %get-tuple-element.36), channel_id=1, source_target_pairs={{0,6},{1,7},{2,4},{3,5},{4,2},{5,3},{6,0},{7,1},{8,14},{9,15},{10,... | collective-permute-start | bytes 294920 | tf_op jit(solution)/shard_map/ppermute | solution.py:575
  9.5 8.5 %collective-permute-start = (bf16[64,768]{1,0:T(8,128)(2,1)}, bf16[64,768]{1,0:T(8,128)(2,1)S(1)}, u32[]{:S(2)}, u32[]{:S(2)}) collective-permute-start(bf16[64,768]{1,0:T(8,128)(2,1)} %get-tuple-element.36), channel_id=1, source_target_pairs={{0,4},{1,5},{2,6},{3,7},{4,0},{5,1},{6,2},{7,3},{8,12},{9,13},{10,... | collective-permute-start | bytes 294920 | tf_op jit(solution)/shard_map/ppermute | solution.py:575
  9.5 8.6 %copy-start.2 = (bf16[192,768]{1,0:T(8,128)(2,1)S(1)}, bf16[192,768]{1,0:T(8,128)(2,1)}, u32[]{:S(2)}) copy-start(bf16[192,768]{1,0:T(8,128)(2,1)} %get-tuple-element.39.refs_0_) | copy-start | bytes 884740
  9.5 13.0 %copy-start = (s32[192,8]{0,1:T(8,128)S(1)}, s32[192,8]{0,1:T(8,128)}, u32[]{:S(2)}) copy-start(s32[192,8]{0,1:T(8,128)} %param.11) | copy-start | bytes 18436
  9.5 8.5 %collective-permute-start.2 = (bf16[16,768]{1,0:T(8,128)(2,1)}, bf16[16,768]{1,0:T(8,128)(2,1)S(1)}, u32[]{:S(2)}, u32[]{:S(2)}) collective-permute-start(bf16[16,768]{1,0:T(8,128)(2,1)} %get-tuple-element.37), channel_id=1, source_target_pairs={{0,2},{1,3},{2,0},{3,1},{4,6},{5,7},{6,4},{7,5},{8,10},{9,11},{10,... | collective-permute-start | bytes 73736 | tf_op jit(solution)/shard_map/ppermute | solution.py:575
  17.3 11.7 %copy-start.1 = (bf16[560,768]{1,0:T(8,128)(2,1)S(1)}, bf16[560,768]{1,0:T(8,128)(2,1)}, u32[]{:S(2)}) copy-start(bf16[560,768]{1,0:T(8,128)(2,1)} %item_units.1.refs_6_.refs_2_) | copy-start | bytes 2580484
  18.0 11.1 %collective-permute-start.7 = (bf16[560,768]{1,0:T(8,128)(2,1)}, bf16[560,768]{1,0:T(8,128)(2,1)S(1)}, u32[]{:S(2)}, u32[]{:S(2)}) collective-permute-start(bf16[560,768]{1,0:T(8,128)(2,1)} %item_units.1.refs_6_.refs_2_), channel_id=1, source_target_pairs={{0,1},{1,0},{2,3},{3,2},{4,5},{5,4},{6,7},{7,6},{8,9},{9,8},{10,11... | collective-permute-start | bytes 2580488 | tf_op jit(solution)/shard_map/ppermute | solution.py:575
  18.1 11.0 %collective-permute-start.3 = (bf16[192,768]{1,0:T(8,128)(2,1)S(1)}, bf16[192,768]{1,0:T(8,128)(2,1)S(1)}, u32[]{:S(2)}, u32[]{:S(2)}) collective-permute-start(bf16[192,768]{1,0:T(8,128)(2,1)S(1)} %copy-done.2), channel_id=1, source_target_pairs={{0,2},{1,3},{2,0},{3,1},{4,6},{5,7},{6,4},{7,5},{8,10},{9,11},{10,... | collective-permute-start | bytes 884744 | tf_op jit(solution)/shard_map/ppermute | solution.py:575
  19.0 7.5 %collective-permute-start.6 = (bf16[96,768]{1,0:T(8,128)(2,1)S(1)}, bf16[96,768]{1,0:T(8,128)(2,1)S(1)}, u32[]{:S(2)}, u32[]{:S(2)}) collective-permute-start(bf16[96,768]{1,0:T(8,128)(2,1)S(1)} %pad_maximum_fusion.refs_2_), channel_id=1, source_target_pairs={{0,24},{1,25},{2,26},{3,27},{4,28},{5,29},{6,30},{7,31},{8,16},{9,... | collective-permute-start | bytes 442376 | tf_op jit(solution)/shard_map/ppermute | solution.py:575
  21.4 7.5 %collective-permute-start.5 = (bf16[96,768]{1,0:T(8,128)(2,1)S(1)}, bf16[96,768]{1,0:T(8,128)(2,1)S(1)}, u32[]{:S(2)}, u32[]{:S(2)}) collective-permute-start(bf16[96,768]{1,0:T(8,128)(2,1)S(1)} %pad_maximum_fusion.refs_2_), channel_id=1, source_target_pairs={{0,16},{1,17},{2,18},{3,19},{4,20},{5,21},{6,22},{7,23},{8,24},{9,... | collective-permute-start | bytes 442376 | tf_op jit(solution)/shard_map/ppermute | solution.py:575
  21.9 7.1 %collective-permute-start.4 = (bf16[96,768]{1,0:T(8,128)(2,1)S(1)}, bf16[96,768]{1,0:T(8,128)(2,1)S(1)}, u32[]{:S(2)}, u32[]{:S(2)}) collective-permute-start(bf16[96,768]{1,0:T(8,128)(2,1)S(1)} %pad_maximum_fusion.refs_2_), channel_id=1, source_target_pairs={{0,8},{1,9},{2,10},{3,11},{4,12},{5,13},{6,14},{7,15},{8,0},{9,1},... | collective-permute-start | bytes 442376 | tf_op jit(solution)/shard_map/ppermute | solution.py:575
  45.9 8.3 %collective-permute-start.11 = (bf16[192,768]{1,0:T(8,128)(2,1)S(1)}, bf16[192,768]{1,0:T(8,128)(2,1)S(1)}, u32[]{:S(2)}, u32[]{:S(2)}) collective-permute-start(bf16[192,768]{1,0:T(8,128)(2,1)S(1)} %get-tuple-element.53), channel_id=1, source_target_pairs={{0,2},{1,3},{2,0},{3,1},{4,6},{5,7},{6,4},{7,5},{8,10},{9,11},{10,... | collective-permute-start | bytes 884744 | tf_op jit(solution)/shard_map/ppermute | solution.py:575
  47.0 5.4 %collective-permute-start.8 = (bf16[2,48,768]{2,1,0:T(8,128)(2,1)S(1)}, bf16[2,48,768]{2,1,0:T(8,128)(2,1)S(1)}, u32[]{:S(2)}, u32[]{:S(2)}) collective-permute-start(bf16[2,48,768]{2,1,0:T(8,128)(2,1)S(1)} %get-tuple-element.49), channel_id=1, source_target_pairs={{0,8},{1,9},{2,10},{3,11},{4,12},{5,13},{6,14},{7,15},{8,0},{9,1},... | collective-permute-start | bytes 442376 | tf_op jit(solution)/shard_map/ppermute | solution.py:575
  47.0 5.4 %collective-permute-start.9 = (bf16[2,48,768]{2,1,0:T(8,128)(2,1)S(1)}, bf16[2,48,768]{2,1,0:T(8,128)(2,1)S(1)}, u32[]{:S(2)}, u32[]{:S(2)}) collective-permute-start(bf16[2,48,768]{2,1,0:T(8,128)(2,1)S(1)} %get-tuple-element.50), channel_id=1, source_target_pairs={{0,16},{1,17},{2,18},{3,19},{4,20},{5,21},{6,22},{7,23},{8,24},{9,... | collective-permute-start | bytes 442376 | tf_op jit(solution)/shard_map/ppermute | solution.py:575
  48.1 6.0 %collective-permute-start.10 = (bf16[2,48,768]{2,1,0:T(8,128)(2,1)S(1)}, bf16[2,48,768]{2,1,0:T(8,128)(2,1)S(1)}, u32[]{:S(2)}, u32[]{:S(2)}) collective-permute-start(bf16[2,48,768]{2,1,0:T(8,128)(2,1)S(1)} %get-tuple-element.51), channel_id=1, source_target_pairs={{0,24},{1,25},{2,26},{3,27},{4,28},{5,29},{6,30},{7,31},{8,16},{9,... | collective-permute-start | bytes 442376 | tf_op jit(solution)/shard_map/ppermute | solution.py:575
  54.3 6.4 %collective-permute-start.12 = (bf16[560,768]{1,0:T(8,128)(2,1)S(1)}, bf16[560,768]{1,0:T(8,128)(2,1)S(1)}, u32[]{:S(2)}, u32[]{:S(2)}) collective-permute-start(bf16[560,768]{1,0:T(8,128)(2,1)S(1)} %get-tuple-element.57), channel_id=1, source_target_pairs={{0,1},{1,0},{2,3},{3,2},{4,5},{5,4},{6,7},{7,6},{8,9},{9,8},{10,11... | collective-permute-start | bytes 2580488 | tf_op jit(solution)/shard_map/ppermute | solution.py:575
  54.4 9.2 %collective-permute-start.13 = (bf16[48,768]{1,0:T(8,128)(2,1)S(1)}, bf16[48,768]{1,0:T(8,128)(2,1)S(1)}, u32[]{:S(2)}, u32[]{:S(2)}) collective-permute-start(bf16[48,768]{1,0:T(8,128)(2,1)S(1)} %get-tuple-element.60), channel_id=1, source_target_pairs={{0,4},{1,5},{2,6},{3,7},{4,0},{5,1},{6,2},{7,3},{8,12},{9,13},{10,... | collective-permute-start | bytes 221192 | tf_op jit(solution)/shard_map/ppermute | solution.py:575
  55.6 8.0 %collective-permute-start.14 = (bf16[48,768]{1,0:T(8,128)(2,1)S(1)}, bf16[48,768]{1,0:T(8,128)(2,1)S(1)}, u32[]{:S(2)}, u32[]{:S(2)}) collective-permute-start(bf16[48,768]{1,0:T(8,128)(2,1)S(1)} %get-tuple-element.61), channel_id=1, source_target_pairs={{0,6},{1,7},{2,4},{3,5},{4,2},{5,3},{6,0},{7,1},{8,14},{9,15},{10,... | collective-permute-start | bytes 221192 | tf_op jit(solution)/shard_map/ppermute | solution.py:575
  58.5 5.2 %collective-permute-start.15 = (bf16[48,768]{1,0:T(8,128)(2,1)S(1)}, bf16[48,768]{1,0:T(8,128)(2,1)S(1)}, u32[]{:S(2)}, u32[]{:S(2)}) collective-permute-start(bf16[48,768]{1,0:T(8,128)(2,1)S(1)} %get-tuple-element.62), channel_id=1, source_target_pairs={{0,8},{1,9},{2,10},{3,11},{4,12},{5,13},{6,14},{7,15},{8,0},{9,1},... | collective-permute-start | bytes 221192 | tf_op jit(solution)/shard_map/ppermute | solution.py:575
  59.8 5.1 %collective-permute-start.16 = (bf16[48,768]{1,0:T(8,128)(2,1)S(1)}, bf16[48,768]{1,0:T(8,128)(2,1)S(1)}, u32[]{:S(2)}, u32[]{:S(2)}) collective-permute-start(bf16[48,768]{1,0:T(8,128)(2,1)S(1)} %get-tuple-element.63), channel_id=1, source_target_pairs={{0,16},{1,17},{2,18},{3,19},{4,20},{5,21},{6,22},{7,23},{8,24},{9,... | collective-permute-start | bytes 221192 | tf_op jit(solution)/shard_map/ppermute | solution.py:575
  60.7 5.3 %collective-permute-start.17 = (bf16[48,768]{1,0:T(8,128)(2,1)S(1)}, bf16[48,768]{1,0:T(8,128)(2,1)S(1)}, u32[]{:S(2)}, u32[]{:S(2)}) collective-permute-start(bf16[48,768]{1,0:T(8,128)(2,1)S(1)} %get-tuple-element.64), channel_id=1, source_target_pairs={{0,24},{1,25},{2,26},{3,27},{4,28},{5,29},{6,30},{7,31},{8,16},{9,... | collective-permute-start | bytes 221192 | tf_op jit(solution)/shard_map/ppermute | solution.py:575

commit v4 on v3

--- a/solution.py
+++ b/solution.py
@@ -57,8 +57,6 @@
         ],
         axis=1,
     )
-    extra = part_ref.shape[0] - part_rows
-    digits = jnp.concatenate([digits, jnp.zeros((extra - neg_count, width), f32)], axis=0)
     digits = digits.astype(bf16)
     part_ref[part_rows:, :] = digits
     digits_ref[...] = digits
@@ -78,7 +76,7 @@
     rows, depth = hidden.shape
     width = weight.shape[1]
     steps = 3
-    extra = -(-ids.shape[0] // 16) * 16
+    extra = ids.shape[0]
     far = pl.BlockSpec(memory_space=pltpu.HBM)
     near = pl.BlockSpec(memory_space=pltpu.VMEM)
     return pl.pallas_call(
@@ -97,64 +95,34 @@
             pltpu.SemaphoreType.DMA((2, steps)),
             pltpu.SemaphoreType.DMA,
         ],
-        compiler_params=params(62),
+        compiler_params=params(24),
         cost_estimate=pl.CostEstimate(
             flops=2 * rows * depth * width,
             bytes_accessed=2 * depth * (rows + width),
             transcendentals=0,
         ),
         name="query_units",
-    )(hidden, weight, ids)
-
-
-def item_kernel(steps, pool_ref, passage_ref, weight_ref, unit_ref, hidden, weight, sems):
-    depth = weight.shape[0] // steps
-    pool_rows = pool_ref.shape[0]
-    copies = []
-    for k in range(steps):
-        span = pl.ds(k * depth, depth)
-        copies.append(
-            (
-                pltpu.make_async_copy(
-                    pool_ref.at[:, span], hidden.at[pl.ds(0, pool_rows), span], sems.at[0, k]
-                ),
-                pltpu.make_async_copy(
-                    passage_ref.at[:, span],
-                    hidden.at[pl.ds(pool_rows, passage_ref.shape[0]), span],
-                    sems.at[1, k],
-                ),
-                pltpu.make_async_copy(weight_ref.at[span, :], weight.at[span, :], sems.at[2, k]),
-            )
-        )
-    for batch in copies:
-        for copy in batch:
-            copy.start()
-    total = None
-    for k, batch in enumerate(copies):
-        for copy in batch:
-            copy.wait()
-        span = slice(k * depth, (k + 1) * depth)
-        product = jnp.dot(hidden[:, span], weight[span, :], preferred_element_type=f32)
-        total = product if total is None else total + product
-    unit_ref[...] = normalized(total)
+    )(
+        pltpu.with_memory_space_constraint(hidden, pltpu.HBM),
+        pltpu.with_memory_space_constraint(weight, pltpu.HBM),
+        pltpu.with_memory_space_constraint(ids, pltpu.HBM),
+    )
+
+
+def item_kernel(pool_ref, passage_ref, weight_ref, unit_ref):
+    hidden = jnp.concatenate([pool_ref[...], passage_ref[...]], axis=0)
+    unit_ref[...] = normalized(
+        jnp.dot(hidden, weight_ref[...], preferred_element_type=f32)
+    )
 
 
 def project_items(pool, passage, weight):
     depth, width = weight.shape
     rows = pool.shape[0] + passage.shape[0]
-    steps = 4
-    far = pl.BlockSpec(memory_space=pltpu.HBM)
-    return pl.pallas_call(
-        functools.partial(item_kernel, steps),
-        in_specs=[far, far, far],
-        out_specs=pl.BlockSpec(memory_space=pltpu.VMEM),
+    return pl.pallas_call(
+        item_kernel,
         out_shape=jax.ShapeDtypeStruct((rows, width), bf16),
-        scratch_shapes=[
-            pltpu.VMEM((rows, depth), bf16),
-            pltpu.VMEM((depth, width), bf16),
-            pltpu.SemaphoreType.DMA((3, steps)),
-        ],
-        compiler_params=params(60),
+        compiler_params=params(24),
         cost_estimate=pl.CostEstimate(
             flops=2 * rows * depth * width,
             bytes_accessed=2 * depth * (rows + width),
@@ -199,7 +167,7 @@
         queries *= len(pieces)
         specs = [pl.BlockSpec(x.shape, lambda g: (0, 0)) for x in pieces]
     return pl.pallas_call(
-        functools.partial(count_kernel, pool_rows, -(-neg_count // 16) * 16),
+        functools.partial(count_kernel, pool_rows, neg_count),
         grid=(queries // block,),
         in_specs=specs,
         out_specs=pl.BlockSpec((2 * pool_rows, block), lambda g: (0, g)),

time: 66.8 us -> 64.5 us (0.966)
  Pallas kernels: 20.4 us -> 15.5 us
  local copies, waits for them, and re-layouts: 0.02 us -> 2.36 us
  waiting for transfers between devices: 9.61 us -> 10.4 us
  starting transfers between devices: 22.5 us -> 21.8 us
    pallas_call x2, Pallas kernels: 9.89 us -> 5.61 us  [the longest x1 2.94 us: project_items(): pl.pallas_call(item_kernel, out_shape=jax.ShapeDtypeStruct((rows, width),...]
    unnamed x6 -> x8, local copies, waits for them, and re-layouts: 0.01 us -> 2.35 us
    ppermute x18, waiting for transfers between devices: 9.61 us -> 10.4 us  [moved(): return lax.ppermute(x, axes, pairs)]
    ppermute x18, starting transfers between devices: 22.5 us -> 21.8 us  [moved(): return lax.ppermute(x, axes, pairs)]
  transfers between devices with their start and end apart: 18 -> 18, of which waited for: 9 -> 9; matrix products, arithmetic and copies ran while one was open for 0% -> 0% of each run, Pallas kernels for 19% -> 13%
where the time goes in v4:
time: 64.5 us; the launch traced here: 64.3 us
  starting transfers between devices  21.8 us (34%)
  Pallas kernels  15.5 us (24%)
  blocking collectives  12.8 us (20%)
  waiting for transfers between devices  10.4 us (16%)
  local copies, waits for them, and re-layouts  2.36 us (4%)
  between operations  0.76 us (1%)
  other arithmetic  0.71 us (1%)
    ppermute x18, starting transfers between devices, moved(): return lax.ppermute(x, axes, pairs)  21.8 us
    all_to_all x1, blocking collectives, shards(): totals = lax.all_to_all(totals, axes, 0, 0, axis_index_groups=same_core)  12.8 us
    ppermute x18, waiting for transfers between devices, moved(): return lax.ppermute(x, axes, pairs)  10.4 us
    pallas_call x1, Pallas kernels, project_queries(): pl.pallas_call(functools.partial(query_kernel, steps, part_rows), in_spec...  3.13 us
    pallas_call x1, Pallas kernels, project_items(): pl.pallas_call(item_kernel, out_shape=jax.ShapeDtypeStruct((rows, width),...  2.94 us
    pallas_call x1, Pallas kernels, count_names(): pl.pallas_call(functools.partial(count_kernel, pool_rows, neg_count), gri...  2.67 us
    unnamed x8, local copies, waits for them, and re-layouts  2.35 us
    pallas_call x1, Pallas kernels, weigh(): pl.pallas_call(functools.partial(weight_kernel, near_far, query_rows, poo...  2.12 us
  transfers between devices with their start and end apart: 18, of which 9 were waited for; matrix products, arithmetic and copies ran while one was open for 0% of the time, Pallas kernels for 13%

profile of v4, /device:TPU:0, one launch (start us, length us, event | category | flops | bytes accessed | tf_op | source)
XLA Modules:
  0.0 64.3 jit_solution(13948181173902722522)
XLA Ops:
  0.7 3.1 %query_units.1 = (bf16[192,768]{1,0:T(8,128)(2,1)S(1)}, bf16[56,768]{1,0:T(8,128)(2,1)S(1)}, bf16[8,768]{1,0:T(8,128)(2,1)S(1)}) custom-call(bf16[192,2304]{1,0:T(8,128)(2,1)} %hidden_ref.1, bf16[2304,768]{1,0:T(8,128)(2,1)} %weight_ref.2, s32[8,192]{1,0:T(8,128)} %bitcast.1), custom_call_target="tpu_custom_call" | custom-call | flops 679477248 | bytes 4423680 | tf_op jit(solution)/shard_map/query_units/pallas_call | solution.py:82
  3.8 5.1 %collective-permute-start.1 = (bf16[56,768]{1,0:T(8,128)(2,1)S(1)}, bf16[56,768]{1,0:T(8,128)(2,1)S(1)}, u32[]{:S(2)}, u32[]{:S(2)}) collective-permute-start(bf16[56,768]{1,0:T(8,128)(2,1)S(1)} %get-tuple-element.36), channel_id=1, source_target_pairs={{0,6},{1,7},{2,4},{3,5},{4,2},{5,3},{6,0},{7,1},{8,14},{9,15},{10,... | collective-permute-start | bytes 258056 | tf_op jit(solution)/shard_map/ppermute | solution.py:543
  9.6 2.3 %copy-done.1 = bf16[3072,768]{1,0:T(8,128)(2,1)S(1)} copy-done((bf16[3072,768]{1,0:T(8,128)(2,1)S(1)}, bf16[3072,768]{1,0:T(8,128)(2,1)}, u32[]{:S(2)}) %copy-start.1) | copy-done | bytes 4718616
  11.9 2.9 %item_units.1.refs_6_.refs_2_ = bf16[560,768]{1,0:T(8,128)(2,1)S(1)} custom-call(bf16[512,3072]{1,0:T(8,128)(2,1)S(1)} %copy-done.2, bf16[48,3072]{1,0:T(8,128)(2,1)S(1)} %copy-done.3, bf16[3072,768]{1,0:T(8,128)(2,1)S(1)} %copy-done.1), custom_call_target="tpu_custom_call" | custom-call | flops 2642411520 | bytes 8159232 | tf_op jit(solution)/shard_map/item_units/pallas_call | solution.py:122
  14.9 1.3 %collective-permute-done.refs_2_ = bf16[56,768]{1,0:T(8,128)(2,1)S(1)} collective-permute-done((bf16[56,768]{1,0:T(8,128)(2,1)S(1)}, bf16[56,768]{1,0:T(8,128)(2,1)S(1)}, u32[]{:S(2)}, u32[]{:S(2)}) %collective-permute-start) | collective-permute-done | bytes 86048 | tf_op jit(solution)/shard_map/ppermute | solution.py:543
  16.4 2.5 %collective-permute-start.6 = (bf16[96,768]{1,0:T(8,128)(2,1)S(1)}, bf16[96,768]{1,0:T(8,128)(2,1)S(1)}, u32[]{:S(2)}, u32[]{:S(2)}) collective-permute-start(bf16[96,768]{1,0:T(8,128)(2,1)S(1)} %pad_maximum_fusion.refs_2_), channel_id=1, source_target_pairs={{0,24},{1,25},{2,26},{3,27},{4,28},{5,29},{6,30},{7,31},{8,16},{9,... | collective-permute-start | bytes 442376 | tf_op jit(solution)/shard_map/ppermute | solution.py:543
  19.9 2.7 %name_counts.1.refs_8_ = bf16[1024,768]{1,0:T(8,128)(2,1)S(1)} custom-call(s32[8,192]{1,0:T(8,128)S(1)} %bitcast.2, bf16[8,768]{1,0:T(8,128)(2,1)S(1)} %collective-permute-done.2.refs_1_, bf16[56,768]{1,0:T(8,128)(2,1)S(1)} %collective-permute-done.refs_2_, bf16[56,768]{1,0:T(8,128)(2,1)S(1)} %collective-permute-done.1.refs_3_), custom_call_target="tpu_custom_call" | custom-call | flops 18874368 | bytes 1572864 | tf_op jit(solution)/shard_map/name_counts/pallas_call | solution.py:169
  22.6 1.4 %collective-permute-done.6.refs_5_ = bf16[96,768]{1,0:T(8,128)(2,1)S(1)} collective-permute-done((bf16[96,768]{1,0:T(8,128)(2,1)S(1)}, bf16[96,768]{1,0:T(8,128)(2,1)S(1)}, u32[]{:S(2)}, u32[]{:S(2)}) %collective-permute-start.6) | collective-permute-done | bytes 147488 | tf_op jit(solution)/shard_map/ppermute | solution.py:543
  24.0 2.5 %collective-permute-done.5.refs_4_ = bf16[96,768]{1,0:T(8,128)(2,1)S(1)} collective-permute-done((bf16[96,768]{1,0:T(8,128)(2,1)S(1)}, bf16[96,768]{1,0:T(8,128)(2,1)S(1)}, u32[]{:S(2)}, u32[]{:S(2)}) %collective-permute-start.5) | collective-permute-done | bytes 147488 | tf_op jit(solution)/shard_map/ppermute | solution.py:543
  26.6 1.9 %scores.1 = (bf16[1120,768]{1,0:T(8,128)(2,1)S(1)}, f32[16,2,768]{2,1,0:T(2,128)S(1)}, bf16[768,768]{1,0:T(8,128)(2,1)S(1)}) custom-call(bf16[192,768]{1,0:T(8,128)(2,1)S(1)} %get-tuple-element.39.refs_0_, bf16[192,768]{1,0:T(8,128)(2,1)S(1)} %collective-permute-done.3.refs_1_, bf16[96,768]{1,0:T(8,128)(2,1)S(1)} %pad_maximum_fusion.refs_2_, ...), custom_call_target="tpu_custom_call" | custom-call | flops 1321205760 | bytes 3440640 | tf_op jit(solution)/shard_map/scores/pallas_call | solution.py:326
  28.6 12.8 %all_to_all.5.refs_0_ = f32[16,2,768]{2,1,0:T(2,128)S(1)} all-to-all(f32[16,2,768]{2,1,0:T(2,128)S(1)} %get-tuple-element.43), channel_id=1, replica_groups={{0,2,4,6,8,10,12,14,16,18,20,22,24,26,28,30},{1,3,5,7,9,11,13,15,17,19,..., dimensions={0} | all-to-all | bytes 196608 | tf_op jit(solution)/shard_map/all_to_all | solution.py:598
  41.3 2.1 %weights.1 = (bf16[1120,768]{1,0:T(8,128)(2,1)S(1)}, bf16[192,768]{1,0:T(8,128)(2,1)S(1)}, bf16[192,768]{1,0:T(8,128)(2,1)S(1)}, bf16[2,48,768]{2,1,0:T(8,128)(2...) custom-call(f32[16,2,768]{2,1,0:T(2,128)S(1)} %all_to_all.5.refs_0_, ...), custom_call_target="tpu_custom_call" | custom-call | flops 1321205760 | bytes 3440640 | tf_op jit(solution)/shard_map/weights/pallas_call | solution.py:396
  43.5 1.2 %collective-permute-start.11 = (bf16[192,768]{1,0:T(8,128)(2,1)S(1)}, bf16[192,768]{1,0:T(8,128)(2,1)S(1)}, u32[]{:S(2)}, u32[]{:S(2)}) collective-permute-start(bf16[192,768]{1,0:T(8,128)(2,1)S(1)} %get-tuple-element.53), channel_id=1, source_target_pairs={{0,2},{1,3},{2,0},{3,1},{4,6},{5,7},{6,4},{7,5},{8,10},{9,11},{10,... | collective-permute-start | bytes 884744 | tf_op jit(solution)/shard_map/ppermute | solution.py:543
  44.6 1.1 %collective-permute-start.9 = (bf16[2,48,768]{2,1,0:T(8,128)(2,1)S(1)}, bf16[2,48,768]{2,1,0:T(8,128)(2,1)S(1)}, u32[]{:S(2)}, u32[]{:S(2)}) collective-permute-start(bf16[2,48,768]{2,1,0:T(8,128)(2,1)S(1)} %get-tuple-element.50), channel_id=1, source_target_pairs={{0,16},{1,17},{2,18},{3,19},{4,20},{5,21},{6,22},{7,23},{8,24},{9,... | collective-permute-start | bytes 442376 | tf_op jit(solution)/shard_map/ppermute | solution.py:543
  45.7 2.4 %collective-permute-start.10 = (bf16[2,48,768]{2,1,0:T(8,128)(2,1)S(1)}, bf16[2,48,768]{2,1,0:T(8,128)(2,1)S(1)}, u32[]{:S(2)}, u32[]{:S(2)}) collective-permute-start(bf16[2,48,768]{2,1,0:T(8,128)(2,1)S(1)} %get-tuple-element.51), channel_id=1, source_target_pairs={{0,24},{1,25},{2,26},{3,27},{4,28},{5,29},{6,30},{7,31},{8,16},{9,... | collective-permute-start | bytes 442376 | tf_op jit(solution)/shard_map/ppermute | solution.py:543
  48.1 1.5 %item_gradients.1 = (f32[560,768]{1,0:T(8,128)S(1)}, bf16[560,768]{1,0:T(8,128)(2,1)S(1)}) custom-call(bf16[1120,768]{1,0:T(8,128)(2,1)S(1)} %get-tuple-element.45.weight_ref, bf16[768,768]{1,0:T(8,128)(2,1)S(1)} %get-tuple-element.46.queries_ref), custom_call_target="tpu_custom_call" | custom-call | flops 1321205760 | bytes 5160960 | tf_op jit(solution)/shard_map/item_gradients/pallas_call | solution.py:450
  50.1 1.7 %collective-permute-done.10.refs_3_ = bf16[2,48,768]{2,1,0:T(8,128)(2,1)S(1)} collective-permute-done((bf16[2,48,768]{2,1,0:T(8,128)(2,1)S(1)}, bf16[2,48,768]{2,1,0:T(8,128)(2,1)S(1)}, u32[]{:S(2)}, u32[]{:S(2)}) %collective-permute-start.10) | collective-permute-done | bytes 147488 | tf_op jit(solution)/shard_map/ppermute | solution.py:543
  52.0 1.2 %collective-permute-start.13 = (bf16[48,768]{1,0:T(8,128)(2,1)S(1)}, bf16[48,768]{1,0:T(8,128)(2,1)S(1)}, u32[]{:S(2)}, u32[]{:S(2)}) collective-permute-start(bf16[48,768]{1,0:T(8,128)(2,1)S(1)} %get-tuple-element.60), channel_id=1, source_target_pairs={{0,4},{1,5},{2,6},{3,7},{4,0},{5,1},{6,2},{7,3},{8,12},{9,13},{10,... | collective-permute-start | bytes 221192 | tf_op jit(solution)/shard_map/ppermute | solution.py:543
  53.2 2.9 %collective-permute-start.14 = (bf16[48,768]{1,0:T(8,128)(2,1)S(1)}, bf16[48,768]{1,0:T(8,128)(2,1)S(1)}, u32[]{:S(2)}, u32[]{:S(2)}) collective-permute-start(bf16[48,768]{1,0:T(8,128)(2,1)S(1)} %get-tuple-element.61), channel_id=1, source_target_pairs={{0,6},{1,7},{2,4},{3,5},{4,2},{5,3},{6,0},{7,1},{8,14},{9,15},{10,... | collective-permute-start | bytes 221192 | tf_op jit(solution)/shard_map/ppermute | solution.py:543
  56.1 1.3 %collective-permute-start.15 = (bf16[48,768]{1,0:T(8,128)(2,1)S(1)}, bf16[48,768]{1,0:T(8,128)(2,1)S(1)}, u32[]{:S(2)}, u32[]{:S(2)}) collective-permute-start(bf16[48,768]{1,0:T(8,128)(2,1)S(1)} %get-tuple-element.62), channel_id=1, source_target_pairs={{0,8},{1,9},{2,10},{3,11},{4,12},{5,13},{6,14},{7,15},{8,0},{9,1},... | collective-permute-start | bytes 221192 | tf_op jit(solution)/shard_map/ppermute | solution.py:543
  58.3 1.2 %collective-permute-start.17 = (bf16[48,768]{1,0:T(8,128)(2,1)S(1)}, bf16[48,768]{1,0:T(8,128)(2,1)S(1)}, u32[]{:S(2)}, u32[]{:S(2)}) collective-permute-start(bf16[48,768]{1,0:T(8,128)(2,1)S(1)} %get-tuple-element.64), channel_id=1, source_target_pairs={{0,24},{1,25},{2,26},{3,27},{4,28},{5,29},{6,30},{7,31},{8,16},{9,... | collective-permute-start | bytes 221192 | tf_op jit(solution)/shard_map/ppermute | solution.py:543
  59.6 1.0 %join_item_gradients.1 = (bf16[512,768]{1,0:T(8,128)(2,1)}, bf16[48,768]{1,0:T(8,128)(2,1)}) custom-call(f32[560,768]{1,0:T(8,128)S(1)} %get-tuple-element.56.own_ref, bf16[560,768]{1,0:T(8,128)(2,1)S(1)} %collective-permute-done.12.taken_ref), custom_call_target="tpu_custom_call" | custom-call | flops 430080 | bytes 3440640 | tf_op jit(solution)/shard_map/join_item_gradients/pallas_call | solution.py:479
  61.2 1.3 %collective-permute-done.16 = bf16[48,768]{1,0:T(8,128)(2,1)S(1)} collective-permute-done((bf16[48,768]{1,0:T(8,128)(2,1)S(1)}, bf16[48,768]{1,0:T(8,128)(2,1)S(1)}, u32[]{:S(2)}, u32[]{:S(2)}) %collective-permute-start.16) | collective-permute-done | bytes 73760 | tf_op jit(solution)/shard_map/ppermute | solution.py:543
  62.5 1.1 %collective-permute-done.17 = bf16[48,768]{1,0:T(8,128)(2,1)S(1)} collective-permute-done((bf16[48,768]{1,0:T(8,128)(2,1)S(1)}, bf16[48,768]{1,0:T(8,128)(2,1)S(1)}, u32[]{:S(2)}, u32[]{:S(2)}) %collective-permute-start.17) | collective-permute-done | bytes 73760 | tf_op jit(solution)/shard_map/ppermute | solution.py:543
  (33 shorter events, 5.0 us)
Async XLA Ops:
  0.6 8.9 %copy-start.2 = (bf16[512,3072]{1,0:T(8,128)(2,1)S(1)}, bf16[512,3072]{1,0:T(8,128)(2,1)}, u32[]{:S(2)}) copy-start(bf16[512,3072]{1,0:T(8,128)(2,1)} %pool_ref) | copy-start | bytes 9437188
  0.6 8.9 %copy-start.3 = (bf16[48,3072]{1,0:T(8,128)(2,1)S(1)}, bf16[48,3072]{1,0:T(8,128)(2,1)}, u32[]{:S(2)}) copy-start(bf16[48,3072]{1,0:T(8,128)(2,1)} %passage_ref.1) | copy-start | bytes 884740
  3.8 11.1 %collective-permute-start.1 = (bf16[56,768]{1,0:T(8,128)(2,1)S(1)}, bf16[56,768]{1,0:T(8,128)(2,1)S(1)}, u32[]{:S(2)}, u32[]{:S(2)}) collective-permute-start(bf16[56,768]{1,0:T(8,128)(2,1)S(1)} %get-tuple-element.36), channel_id=1, source_target_pairs={{0,6},{1,7},{2,4},{3,5},{4,2},{5,3},{6,0},{7,1},{8,14},{9,15},{10,... | collective-permute-start | bytes 258056 | tf_op jit(solution)/shard_map/ppermute | solution.py:543
  8.9 7.2 %collective-permute-start = (bf16[56,768]{1,0:T(8,128)(2,1)S(1)}, bf16[56,768]{1,0:T(8,128)(2,1)S(1)}, u32[]{:S(2)}, u32[]{:S(2)}) collective-permute-start(bf16[56,768]{1,0:T(8,128)(2,1)S(1)} %get-tuple-element.36), channel_id=1, source_target_pairs={{0,4},{1,5},{2,6},{3,7},{4,0},{5,1},{6,2},{7,3},{8,12},{9,13},{10,... | collective-permute-start | bytes 258056 | tf_op jit(solution)/shard_map/ppermute | solution.py:543
  8.9 11.0 %copy-start = (s32[192,8]{0,1:T(8,128)S(1)}, s32[192,8]{0,1:T(8,128)}, u32[]{:S(2)}) copy-start(s32[192,8]{0,1:T(8,128)} %param.11) | copy-start | bytes 18436
  8.9 7.2 %collective-permute-start.2 = (bf16[8,768]{1,0:T(8,128)(2,1)S(1)}, bf16[8,768]{1,0:T(8,128)(2,1)S(1)}, u32[]{:S(2)}, u32[]{:S(2)}) collective-permute-start(bf16[8,768]{1,0:T(8,128)(2,1)S(1)} %get-tuple-element.37), channel_id=1, source_target_pairs={{0,2},{1,3},{2,0},{3,1},{4,6},{5,7},{6,4},{7,5},{8,10},{9,11},{10,... | collective-permute-start | bytes 36872 | tf_op jit(solution)/shard_map/ppermute | solution.py:543
  9.6 2.3 %copy-start.1 = (bf16[3072,768]{1,0:T(8,128)(2,1)S(1)}, bf16[3072,768]{1,0:T(8,128)(2,1)}, u32[]{:S(2)}) copy-start(bf16[3072,768]{1,0:T(8,128)(2,1)} %weight_ref.3) | copy-start | bytes 14155780
  16.1 10.5 %collective-permute-start.7 = (bf16[560,768]{1,0:T(8,128)(2,1)S(1)}, bf16[560,768]{1,0:T(8,128)(2,1)S(1)}, u32[]{:S(2)}, u32[]{:S(2)}) collective-permute-start(bf16[560,768]{1,0:T(8,128)(2,1)S(1)} %item_units.1.refs_6_.refs_2_), channel_id=1, source_target_pairs={{0,1},{1,0},{2,3},{3,2},{4,5},{5,4},{6,7},{7,6},{8,9},{9,8},{10,11... | collective-permute-start | bytes 2580488 | tf_op jit(solution)/shard_map/ppermute | solution.py:543
  16.2 10.4 %collective-permute-start.3 = (bf16[192,768]{1,0:T(8,128)(2,1)S(1)}, bf16[192,768]{1,0:T(8,128)(2,1)S(1)}, u32[]{:S(2)}, u32[]{:S(2)}) collective-permute-start(bf16[192,768]{1,0:T(8,128)(2,1)S(1)} %get-tuple-element.39.refs_0_), channel_id=1, source_target_pairs={{0,2},{1,3},{2,0},{3,1},{4,6},{5,7},{6,4},{7,5},{8,10},{9,11},{10,... | collective-permute-start | bytes 884744 | tf_op jit(solution)/shard_map/ppermute | solution.py:543
  16.4 7.6 %collective-permute-start.6 = (bf16[96,768]{1,0:T(8,128)(2,1)S(1)}, bf16[96,768]{1,0:T(8,128)(2,1)S(1)}, u32[]{:S(2)}, u32[]{:S(2)}) collective-permute-start(bf16[96,768]{1,0:T(8,128)(2,1)S(1)} %pad_maximum_fusion.refs_2_), channel_id=1, source_target_pairs={{0,24},{1,25},{2,26},{3,27},{4,28},{5,29},{6,30},{7,31},{8,16},{9,... | collective-permute-start | bytes 442376 | tf_op jit(solution)/shard_map/ppermute | solution.py:543
  18.9 7.6 %collective-permute-start.5 = (bf16[96,768]{1,0:T(8,128)(2,1)S(1)}, bf16[96,768]{1,0:T(8,128)(2,1)S(1)}, u32[]{:S(2)}, u32[]{:S(2)}) collective-permute-start(bf16[96,768]{1,0:T(8,128)(2,1)S(1)} %pad_maximum_fusion.refs_2_), channel_id=1, source_target_pairs={{0,16},{1,17},{2,18},{3,19},{4,20},{5,21},{6,22},{7,23},{8,24},{9,... | collective-permute-start | bytes 442376 | tf_op jit(solution)/shard_map/ppermute | solution.py:543
  19.4 7.2 %collective-permute-start.4 = (bf16[96,768]{1,0:T(8,128)(2,1)S(1)}, bf16[96,768]{1,0:T(8,128)(2,1)S(1)}, u32[]{:S(2)}, u32[]{:S(2)}) collective-permute-start(bf16[96,768]{1,0:T(8,128)(2,1)S(1)} %pad_maximum_fusion.refs_2_), channel_id=1, source_target_pairs={{0,8},{1,9},{2,10},{3,11},{4,12},{5,13},{6,14},{7,15},{8,0},{9,1},... | collective-permute-start | bytes 442376 | tf_op jit(solution)/shard_map/ppermute | solution.py:543
  43.5 8.3 %collective-permute-start.11 = (bf16[192,768]{1,0:T(8,128)(2,1)S(1)}, bf16[192,768]{1,0:T(8,128)(2,1)S(1)}, u32[]{:S(2)}, u32[]{:S(2)}) collective-permute-start(bf16[192,768]{1,0:T(8,128)(2,1)S(1)} %get-tuple-element.53), channel_id=1, source_target_pairs={{0,2},{1,3},{2,0},{3,1},{4,6},{5,7},{6,4},{7,5},{8,10},{9,11},{10,... | collective-permute-start | bytes 884744 | tf_op jit(solution)/shard_map/ppermute | solution.py:543
  44.6 5.4 %collective-permute-start.8 = (bf16[2,48,768]{2,1,0:T(8,128)(2,1)S(1)}, bf16[2,48,768]{2,1,0:T(8,128)(2,1)S(1)}, u32[]{:S(2)}, u32[]{:S(2)}) collective-permute-start(bf16[2,48,768]{2,1,0:T(8,128)(2,1)S(1)} %get-tuple-element.49), channel_id=1, source_target_pairs={{0,8},{1,9},{2,10},{3,11},{4,12},{5,13},{6,14},{7,15},{8,0},{9,1},... | collective-permute-start | bytes 442376 | tf_op jit(solution)/shard_map/ppermute | solution.py:543
  44.6 5.4 %collective-permute-start.9 = (bf16[2,48,768]{2,1,0:T(8,128)(2,1)S(1)}, bf16[2,48,768]{2,1,0:T(8,128)(2,1)S(1)}, u32[]{:S(2)}, u32[]{:S(2)}) collective-permute-start(bf16[2,48,768]{2,1,0:T(8,128)(2,1)S(1)} %get-tuple-element.50), channel_id=1, source_target_pairs={{0,16},{1,17},{2,18},{3,19},{4,20},{5,21},{6,22},{7,23},{8,24},{9,... | collective-permute-start | bytes 442376 | tf_op jit(solution)/shard_map/ppermute | solution.py:543
  45.7 6.0 %collective-permute-start.10 = (bf16[2,48,768]{2,1,0:T(8,128)(2,1)S(1)}, bf16[2,48,768]{2,1,0:T(8,128)(2,1)S(1)}, u32[]{:S(2)}, u32[]{:S(2)}) collective-permute-start(bf16[2,48,768]{2,1,0:T(8,128)(2,1)S(1)} %get-tuple-element.51), channel_id=1, source_target_pairs={{0,24},{1,25},{2,26},{3,27},{4,28},{5,29},{6,30},{7,31},{8,16},{9,... | collective-permute-start | bytes 442376 | tf_op jit(solution)/shard_map/ppermute | solution.py:543
  51.9 6.4 %collective-permute-start.12 = (bf16[560,768]{1,0:T(8,128)(2,1)S(1)}, bf16[560,768]{1,0:T(8,128)(2,1)S(1)}, u32[]{:S(2)}, u32[]{:S(2)}) collective-permute-start(bf16[560,768]{1,0:T(8,128)(2,1)S(1)} %get-tuple-element.57), channel_id=1, source_target_pairs={{0,1},{1,0},{2,3},{3,2},{4,5},{5,4},{6,7},{7,6},{8,9},{9,8},{10,11... | collective-permute-start | bytes 2580488 | tf_op jit(solution)/shard_map/ppermute | solution.py:543
  52.0 9.2 %collective-permute-start.13 = (bf16[48,768]{1,0:T(8,128)(2,1)S(1)}, bf16[48,768]{1,0:T(8,128)(2,1)S(1)}, u32[]{:S(2)}, u32[]{:S(2)}) collective-permute-start(bf16[48,768]{1,0:T(8,128)(2,1)S(1)} %get-tuple-element.60), channel_id=1, source_target_pairs={{0,4},{1,5},{2,6},{3,7},{4,0},{5,1},{6,2},{7,3},{8,12},{9,13},{10,... | collective-permute-start | bytes 221192 | tf_op jit(solution)/shard_map/ppermute | solution.py:543
  53.2 8.0 %collective-permute-start.14 = (bf16[48,768]{1,0:T(8,128)(2,1)S(1)}, bf16[48,768]{1,0:T(8,128)(2,1)S(1)}, u32[]{:S(2)}, u32[]{:S(2)}) collective-permute-start(bf16[48,768]{1,0:T(8,128)(2,1)S(1)} %get-tuple-element.61), channel_id=1, source_target_pairs={{0,6},{1,7},{2,4},{3,5},{4,2},{5,3},{6,0},{7,1},{8,14},{9,15},{10,... | collective-permute-start | bytes 221192 | tf_op jit(solution)/shard_map/ppermute | solution.py:543
  56.1 5.1 %collective-permute-start.15 = (bf16[48,768]{1,0:T(8,128)(2,1)S(1)}, bf16[48,768]{1,0:T(8,128)(2,1)S(1)}, u32[]{:S(2)}, u32[]{:S(2)}) collective-permute-start(bf16[48,768]{1,0:T(8,128)(2,1)S(1)} %get-tuple-element.62), channel_id=1, source_target_pairs={{0,8},{1,9},{2,10},{3,11},{4,12},{5,13},{6,14},{7,15},{8,0},{9,1},... | collective-permute-start | bytes 221192 | tf_op jit(solution)/shard_map/ppermute | solution.py:543
  57.4 5.1 %collective-permute-start.16 = (bf16[48,768]{1,0:T(8,128)(2,1)S(1)}, bf16[48,768]{1,0:T(8,128)(2,1)S(1)}, u32[]{:S(2)}, u32[]{:S(2)}) collective-permute-start(bf16[48,768]{1,0:T(8,128)(2,1)S(1)} %get-tuple-element.63), channel_id=1, source_target_pairs={{0,16},{1,17},{2,18},{3,19},{4,20},{5,21},{6,22},{7,23},{8,24},{9,... | collective-permute-start | bytes 221192 | tf_op jit(solution)/shard_map/ppermute | solution.py:543
  58.3 5.3 %collective-permute-start.17 = (bf16[48,768]{1,0:T(8,128)(2,1)S(1)}, bf16[48,768]{1,0:T(8,128)(2,1)S(1)}, u32[]{:S(2)}, u32[]{:S(2)}) collective-permute-start(bf16[48,768]{1,0:T(8,128)(2,1)S(1)} %get-tuple-element.64), channel_id=1, source_target_pairs={{0,24},{1,25},{2,26},{3,27},{4,28},{5,29},{6,30},{7,31},{8,16},{9,... | collective-permute-start | bytes 221192 | tf_op jit(solution)/shard_map/ppermute | solution.py:543

commit v5 on v4

--- a/solution.py
+++ b/solution.py
@@ -16,6 +16,16 @@
 first_first = (((0,), (0,)), ((), ()))
 
 
+def block_step(blocks):
+    return pl.program_id(0) if blocks > 1 else 0
+
+
+def grid_of(blocks, in_specs, out_specs):
+    if blocks == 1:
+        return {}
+    return {"grid": (blocks,), "in_specs": in_specs, "out_specs": out_specs}
+
+
 def params(mib):
     return pltpu.CompilerParams(vmem_limit_bytes=int(mib * 2**20))
 
@@ -23,6 +33,25 @@
 def normalized(projected):
     squares = jnp.sum(projected * projected, axis=1, keepdims=True)
     return (projected * lax.rsqrt(squares + 1e-06)).astype(bf16)
+
+
+def digits_of(ids):
+    rows = ids.shape[1]
+    full = rows // 128 * 128
+    assert rows - full == 64 and full == 128
+    high = ((ids >> 8) - 256).astype(f32)
+    low = (ids & 255).astype(f32)
+    last = jnp.concatenate([high[:, full:], low[:, full:]], axis=1)
+    return jnp.concatenate([high[:, :full], low[:, :full], last], axis=0).astype(bf16)
+
+
+def ids_of(digits):
+    digits = digits.astype(f32).astype(jnp.int32)
+    count = digits.shape[0] // 3
+    last = digits[2 * count :]
+    high = jnp.concatenate([digits[:count], last[:, :64]], axis=1)
+    low = jnp.concatenate([digits[count : 2 * count], last[:, 64:]], axis=1)
+    return ((high + 256) << 8) + low
 
 
 def query_kernel(steps, part_rows, hidden_ref, weight_ref, ids_ref, unit_ref, part_ref, digits_ref, hidden, weight, ids_near, sems, ids_sem):
@@ -42,23 +71,9 @@
         for copy in pair:
             copy.start()
     ids_copy.wait()
-    ids = ids_near[...]
-    neg_count, rows = ids.shape
-    width = weight.shape[1]
-    room = -(-rows // 128) * 128
-    gap = jnp.zeros((neg_count, room - rows), f32)
-    digits = jnp.concatenate(
-        [
-            ((ids >> 8) - 256).astype(f32),
-            gap,
-            (ids & 255).astype(f32),
-            gap,
-            jnp.zeros((neg_count, width - 2 * room), f32),
-        ],
-        axis=1,
-    )
-    digits = digits.astype(bf16)
-    part_ref[part_rows:, :] = digits
+    digits = digits_of(ids_near[...])
+    slabs = weight.shape[1] // 128
+    part_ref[slabs * part_rows :, :] = digits
     digits_ref[...] = digits
     total = None
     for k, pair in enumerate(copies):
@@ -69,14 +84,17 @@
         total = product if total is None else total + product
     unit_ref[...] = normalized(total)
     start = pl.multiple_of(lax.axis_index("tower") * part_rows, 16)
-    part_ref[:part_rows, :] = unit_ref[pl.ds(start, part_rows), :]
+    for k in range(slabs):
+        part_ref[k * part_rows : (k + 1) * part_rows, :] = unit_ref[
+            pl.ds(start, part_rows), k * 128 : (k + 1) * 128
+        ]
 
 
 def project_queries(hidden, weight, ids, part_rows):
     rows, depth = hidden.shape
     width = weight.shape[1]
     steps = 3
-    extra = ids.shape[0]
+    extra = 3 * ids.shape[0]
     far = pl.BlockSpec(memory_space=pltpu.HBM)
     near = pl.BlockSpec(memory_space=pltpu.VMEM)
     return pl.pallas_call(
@@ -85,8 +103,8 @@
         out_specs=[near, near, near],
         out_shape=[
             jax.ShapeDtypeStruct((rows, width), bf16),
-            jax.ShapeDtypeStruct((part_rows + extra, width), bf16),
-            jax.ShapeDtypeStruct((extra, width), bf16),
+            jax.ShapeDtypeStruct((part_rows * width // 128 + extra, 128), bf16),
+            jax.ShapeDtypeStruct((extra, 128), bf16),
         ],
         scratch_shapes=[
             pltpu.VMEM((rows, depth), bf16),
@@ -97,8 +115,8 @@
         ],
         compiler_params=params(24),
         cost_estimate=pl.CostEstimate(
-            flops=2 * rows * depth * width,
-            bytes_accessed=2 * depth * (rows + width),
+            flops=16 * rows * depth * width,
+            bytes_accessed=12 * depth * (rows + width),
             transcendentals=0,
         ),
         name="query_units",
@@ -137,10 +155,7 @@
     own = lax.axis_index("tower") * lax.axis_size("dp") + lax.axis_index("dp")
     ids = [ids_ref[...]]
     for ref in digit_refs:
-        digits = ref[-extra:, :].astype(f32).astype(jnp.int32)[: ids[0].shape[0]]
-        rows = ids[0].shape[1]
-        room = -(-rows // 128) * 128
-        ids.append(((digits[:, :rows] + 256) << 8) + digits[:, room : room + rows])
+        ids.append(ids_of(ref[-extra:, :]))
     ids = jnp.concatenate(ids, axis=1)
     neg_count, queries = ids.shape
     chunk = 64
@@ -167,11 +182,11 @@
         queries *= len(pieces)
         specs = [pl.BlockSpec(x.shape, lambda g: (0, 0)) for x in pieces]
     return pl.pallas_call(
-        functools.partial(count_kernel, pool_rows, neg_count),
-        grid=(queries // block,),
-        in_specs=specs,
-        out_specs=pl.BlockSpec((2 * pool_rows, block), lambda g: (0, g)),
+        functools.partial(count_kernel, pool_rows, 3 * neg_count),
         out_shape=jax.ShapeDtypeStruct((2 * pool_rows, queries), bf16),
+        **grid_of(
+            queries // block, specs, pl.BlockSpec((2 * pool_rows, block), lambda g: (0, g))
+        ),
         compiler_params=params(16),
         cost_estimate=pl.CostEstimate(
             flops=6 * queries * neg_count * pool_rows,
@@ -182,13 +197,13 @@
     )(*pieces)
 
 
-def positive_mask(query_rows, own_rows, half, first_lane, block):
+def positive_mask(query_rows, own_rows, half, first_lane, block, blocks):
     dp_size = lax.axis_size("dp")
     tower, dp = lax.axis_index("tower"), lax.axis_index("dp")
     lane = lax.broadcasted_iota(jnp.int32, (1, block), 1) + first_lane
     query = jnp.zeros((1, block), jnp.int32)
     for k in range(group):
-        step = pl.program_id(0) * group + k
+        step = block_step(blocks) * group + k
         start = (((dp // 2) ^ step) * 2 + dp % 2) * query_rows
         query = jnp.where(
             (lane >= k * query_rows) & (lane < (k + 1) * query_rows),
@@ -215,7 +230,9 @@
     return out
 
 
-def score_tile(items_refs, queries, count_ref, exp_ref, start, offset, query_rows, pool_rows):
+def score_tile(
+    items_refs, queries, count_ref, exp_ref, start, offset, query_rows, pool_rows, blocks
+):
     chunk = queries.shape[0]
     own_rows = items_refs[0].shape[0] - pool_rows
     lanes = slice(start, start + chunk)
@@ -230,7 +247,7 @@
         ].astype(f32)
         hard += jnp.sum(named, axis=0, keepdims=True)
         exp_ref[rows, lanes] = named.astype(bf16)
-        mask = positive_mask(query_rows, own_rows, half, offset + start, chunk)
+        mask = positive_mask(query_rows, own_rows, half, offset + start, chunk, blocks)
         hard += jnp.sum(jnp.where(mask, exps[pool_rows:], 0.0), axis=0, keepdims=True)
         batch += jnp.sum(exps[pool_rows:], axis=0, keepdims=True)
         row = 2 * pool_rows + half * own_rows
@@ -238,49 +255,68 @@
     return jnp.concatenate([batch, hard], axis=0)
 
 
-def score_tiles(items_refs, queries_ref, count_ref, exp_ref, offset, query_rows, pool_rows):
+def score_tiles(
+    items_refs, queries_ref, count_ref, exp_ref, offset, query_rows, pool_rows, blocks
+):
     block = queries_ref.shape[0]
-    chunk = 256 if block % 256 == 0 else 128
+    chunk = 256 if block % 256 == 0 else block
     sums = []
     for start in range(0, block, chunk):
         queries = queries_ref[start : start + chunk, :]
         sums.append(
             score_tile(
-                items_refs, queries, count_ref, exp_ref, start, offset, query_rows, pool_rows
+                items_refs,
+                queries,
+                count_ref,
+                exp_ref,
+                start,
+                offset,
+                query_rows,
+                pool_rows,
+                blocks,
             )
         )
     return jnp.concatenate(sums, axis=1)
 
 
-def joined_kernel(copies, query_rows, pool_rows, queries_ref, own_ref, other_ref, count_ref, *outs):
+def joined_kernel(blocks, copies, query_rows, pool_rows, queries_ref, own_ref, other_ref, count_ref, *outs):
     exp_ref, totals_ref = outs
     totals = score_tiles(
-        (own_ref, other_ref), queries_ref, count_ref, exp_ref, 0, query_rows, pool_rows
+        (own_ref, other_ref), queries_ref, count_ref, exp_ref, 0, query_rows, pool_rows, blocks
     )
     totals = placed_totals(totals, query_rows)
     for k in range(copies):
         totals_ref[k] = totals
 
 
-def pieces_kernel(copies, query_rows, pool_rows, part_rows, towers, *refs):
-    unit_ref, next_ref, *refs = refs
+def far_kernel(copies, query_rows, pool_rows, part_rows, towers, *refs):
     far_refs, refs = refs[:towers], refs[towers:]
-    own_ref, other_ref, count_ref, exp_ref, totals_ref, queries_ref = refs
+    own_ref, other_ref, count_ref, near_ref, exp_ref, totals_ref, queries_ref = refs
     tower = lax.axis_index("tower")
-    queries_ref[:query_rows, :] = unit_ref[...]
-    queries_ref[query_rows : 2 * query_rows, :] = next_ref[...]
+    slabs = queries_ref.shape[1] // 128
     for d in range(towers):
-        for s in range(2, group):
+        for s in range(queries_ref.shape[0] // query_rows):
             start = pl.multiple_of(s * query_rows + (tower ^ d) * part_rows, 16)
-            queries_ref[pl.ds(start, part_rows), :] = far_refs[d][
-                (s - 2) * part_rows : (s - 1) * part_rows, :
-            ]
+            for k in range(slabs):
+                queries_ref[pl.ds(start, part_rows), k * 128 : (k + 1) * 128] = far_refs[d][
+                    (s * slabs + k) * part_rows : (s * slabs + k + 1) * part_rows, :
+                ]
+    items = (own_ref, other_ref)
     totals = score_tiles(
-        (own_ref, other_ref), queries_ref, count_ref, exp_ref, 0, query_rows, pool_rows
-    )
-    totals = placed_totals(totals, query_rows)
+        items, queries_ref, count_ref, exp_ref, 2 * query_rows, query_rows, pool_rows, 1
+    )
+    totals = placed_totals(jnp.concatenate([near_ref[...], totals], axis=1), query_rows)
     for k in range(copies):
         totals_ref[k] = totals
+
+
+def near_kernel(query_rows, pool_rows, *refs):
+    unit_ref, next_ref, own_ref, other_ref, count_ref, exp_ref, totals_ref, queries = refs
+    queries[:query_rows, :] = unit_ref[...]
+    queries[query_rows:, :] = next_ref[...]
+    totals_ref[...] = score_tiles(
+        (own_ref, other_ref), queries, count_ref, exp_ref, 0, query_rows, pool_rows, 1
+    )
 
 
 def score_cost(rows, queries, width):
@@ -297,7 +333,7 @@
     rows = 2 * items.shape[0]
     whole = lambda x: pl.BlockSpec(x.shape, lambda g: (0, 0))
     return pl.pallas_call(
-        functools.partial(joined_kernel, copies, query_rows, pool_rows),
+        functools.partial(joined_kernel, total // block, copies, query_rows, pool_rows),
         grid=(total // block,),
         in_specs=[
             pl.BlockSpec((block, width), lambda g: (g, 0)),
@@ -319,38 +355,59 @@
     )(queries, items, other, count)
 
 
-def score_pieces(pieces, items, other, count, query_rows, pool_rows, part_rows, copies):
+def score_far(spread, items, other, count, near, query_rows, pool_rows, part_rows, copies):
     rows, width = 2 * items.shape[0], items.shape[1]
-    queries = group * query_rows
-    towers = len(pieces) - 2
-    return pl.pallas_call(
-        functools.partial(pieces_kernel, copies, query_rows, pool_rows, part_rows, towers),
-        grid=(1,),
+    queries = (group - 2) * query_rows
+    return pl.pallas_call(
+        functools.partial(far_kernel, copies, query_rows, pool_rows, part_rows, len(spread)),
         out_shape=[
             jax.ShapeDtypeStruct((rows, queries), bf16),
-            jax.ShapeDtypeStruct((copies, 2, queries), f32),
+            jax.ShapeDtypeStruct((copies, 2, group * query_rows), f32),
             jax.ShapeDtypeStruct((queries, width), bf16),
         ],
         compiler_params=params(32),
         cost_estimate=score_cost(rows, queries, width),
-        name="scores",
-    )(*pieces, items, other, count)
-
-
-def weight_kernel(near_far, query_rows, pool_rows, own_rows, part_rows, towers, *refs):
-    totals_ref, exp_ref, own_ref, other_ref, weight_ref, *grad_refs = refs
+        name="far_scores",
+    )(*spread, items, other, count, near)
+
+
+def score_near(unit, next_unit, items, other, count, query_rows, pool_rows):
+    rows, width = 2 * items.shape[0], items.shape[1]
+    queries = 2 * query_rows
+    return pl.pallas_call(
+        functools.partial(near_kernel, query_rows, pool_rows),
+        out_shape=[
+            jax.ShapeDtypeStruct((rows, queries), bf16),
+            jax.ShapeDtypeStruct((2, queries), f32),
+        ],
+        scratch_shapes=[pltpu.VMEM((queries, width), bf16)],
+        compiler_params=params(32),
+        cost_estimate=score_cost(rows, queries, width),
+        name="near_scores",
+    )(unit, next_unit, items, other, count)
+
+
+def weight_kernel(blocks, exp_count, query_rows, pool_rows, own_rows, part_rows, towers, *refs):
+    totals_ref, refs = refs[0], refs[1:]
+    exp_refs, refs = refs[:exp_count], refs[exp_count:]
+    own_ref, other_ref, weight_ref, *grad_refs = refs
     totals = placed_totals(jnp.sum(totals_ref[...], axis=0), query_rows)
     scale = 1.0 / totals
     pools = 2 * pool_rows
-    batch, hard = scale[0:1, :], scale[1:2, :]
-    weight_ref[:pools, :] = (exp_ref[:pools, :].astype(f32) * hard).astype(bf16)
-    for half in range(2):
-        row = pools + half * own_rows
-        exps = exp_ref[row : row + own_rows, :].astype(f32)
-        mask = positive_mask(query_rows, own_rows, half, 0, exp_ref.shape[1])
-        weight_ref[row : row + own_rows, :] = (
-            exps * batch + jnp.where(mask, exps * hard - 2.0, 0.0)
-        ).astype(bf16)
+    first = 0
+    for exp_ref in exp_refs:
+        block = exp_ref.shape[1]
+        lanes = slice(first, first + block)
+        batch, hard = scale[0:1, lanes], scale[1:2, lanes]
+        weight_ref[:pools, lanes] = (exp_ref[:pools, :].astype(f32) * hard).astype(bf16)
+        for half in range(2):
+            row = pools + half * own_rows
+            exps = exp_ref[row : row + own_rows, :].astype(f32)
+            mask = positive_mask(query_rows, own_rows, half, first, block, blocks)
+            weight_ref[row : row + own_rows, lanes] = (
+                exps * batch + jnp.where(mask, exps * hard - 2.0, 0.0)
+            ).astype(bf16)
+        first += block
     tower = lax.axis_index("tower")
     items = jnp.concatenate(
         [
@@ -365,7 +422,7 @@
         weight_ref[...], items, first_first, preferred_element_type=f32
     )
     grad = grad.astype(bf16)
-    if near_far:
+    if exp_count == 2:
         near_ref, next_ref, *grad_refs = grad_refs
         near_ref[...] = grad[:query_rows]
         next_ref[...] = grad[query_rows : 2 * query_rows]
@@ -379,34 +436,41 @@
                 grad_refs[d][...] = grad[:, t]
 
 
-def weigh(near_far, totals, exps, items, other, query_rows, pool_rows, part_rows, towers):
+def weigh(totals, exps, items, other, query_rows, pool_rows, part_rows, towers):
     rows, width = items.shape
-    queries = exps.shape[1]
+    queries = sum(x.shape[1] for x in exps)
     block = group * query_rows
     whole = lambda x: pl.BlockSpec(x.shape, lambda g: (0, 0))
     tall = pl.BlockSpec((2 * rows, block), lambda g: (0, g))
     near = pl.BlockSpec((query_rows, width), lambda g: (0, 0))
-    if not near_far:
-        out_specs, out_shape, sent = [], [], group
+    if len(exps) == 1:
+        exp_specs, out_specs, out_shape, sent = [tall], [], [], group
     else:
+        exp_specs = [whole(x) for x in exps]
         out_specs = [near, near]
         out_shape = [jax.ShapeDtypeStruct((query_rows, width), bf16)] * 2
         sent = group - 2
     blocks = queries // block
     return pl.pallas_call(
         functools.partial(
-            weight_kernel, near_far, query_rows, pool_rows, rows - pool_rows, part_rows, towers
-        ),
-        grid=(blocks,),
-        in_specs=[
-            pl.BlockSpec((totals.shape[0], 2, block), lambda g: (0, 0, g)),
-            tall,
-            whole(items),
-            whole(other),
-        ],
-        out_specs=[tall]
-        + out_specs
-        + [pl.BlockSpec((sent, part_rows, width), lambda g: (g, 0, 0))] * towers,
+            weight_kernel,
+            blocks,
+            len(exps),
+            query_rows,
+            pool_rows,
+            rows - pool_rows,
+            part_rows,
+            towers,
+        ),
+        **grid_of(
+            blocks,
+            [pl.BlockSpec((totals.shape[0], 2, block), lambda g: (0, 0, g))]
+            + exp_specs
+            + [whole(items), whole(other)],
+            [tall]
+            + out_specs
+            + [pl.BlockSpec((sent, part_rows, width), lambda g: (g, 0, 0))] * towers,
+        ),
         out_shape=[jax.ShapeDtypeStruct((2 * rows, queries), bf16)]
         + out_shape
         + [jax.ShapeDtypeStruct((sent * blocks, part_rows, width), bf16)] * towers,
@@ -417,55 +481,78 @@
             transcendentals=0,
         ),
         name="weights",
-    )(totals, exps, items, other)
-
-
-def gradient_kernel(steps, pool_rows, own_rows, weight_ref, queries_ref, own_ref, sent_ref, total):
-    step = pl.program_id(0)
-    product = jnp.dot(weight_ref[...], queries_ref[...], preferred_element_type=f32)
-
-    @pl.when(step == 0)
-    def _():
-        total[...] = product
-
-    @pl.when(step > 0)
-    def _():
-        total[...] += product
-
-    @pl.when(step == steps - 1)
-    def _():
+    )(totals, *exps, items, other)
+
+
+def gradient_kernel(steps, query_count, pool_rows, own_rows, weight_ref, *refs):
+    query_refs, refs = refs[:query_count], refs[query_count:]
+    own_ref, sent_ref, *scratch = refs
+    step = block_step(steps)
+    if len(query_refs) == 1:
+        queries = query_refs[0][...]
+    else:
+        unit_ref, next_ref, far_ref = query_refs
+        queries = jnp.concatenate(
+            [unit_ref[...], next_ref[...], far_ref[...]], axis=0
+        )
+    product = jnp.dot(weight_ref[...], queries, preferred_element_type=f32)
+
+    def finish(total):
         pools = 2 * pool_rows
         own_ref[:pool_rows, :] = logit_scale * total[:pool_rows, :]
         own_ref[pool_rows:, :] = logit_scale * total[pools : pools + own_rows, :]
         sent_ref[:pool_rows, :] = (logit_scale * total[pool_rows:pools, :]).astype(bf16)
         sent_ref[pool_rows:, :] = (logit_scale * total[pools + own_rows :, :]).astype(bf16)
 
+    if steps == 1:
+        finish(product)
+        return
+    (total,) = scratch
+
+    @pl.when(step == 0)
+    def _():
+        total[...] = product
+
+    @pl.when(step > 0)
+    def _():
+        total[...] += product
+
+    @pl.when(step == steps - 1)
+    def _():
+        finish(total[...])
+
 
 def item_gradients(weights, queries, query_rows, pool_rows):
     rows, total = weights.shape
     half = rows // 2
-    width = queries.shape[1]
+    width = queries[0].shape[1]
     block = group * query_rows
+    blocks = total // block
     fixed = pl.BlockSpec((half, width), lambda g: (0, 0))
-    return pl.pallas_call(
-        functools.partial(gradient_kernel, total // block, pool_rows, half - pool_rows),
-        grid=(total // block,),
-        in_specs=[
-            pl.BlockSpec((rows, block), lambda g: (0, g)),
-            pl.BlockSpec((block, width), lambda g: (g, 0)),
-        ],
-        out_specs=[fixed, fixed],
+    if len(queries) == 1:
+        query_specs = [pl.BlockSpec((block, width), lambda g: (g, 0))]
+    else:
+        query_specs = [pl.BlockSpec(x.shape, lambda g: (0, 0)) for x in queries]
+    return pl.pallas_call(
+        functools.partial(
+            gradient_kernel, blocks, len(queries), pool_rows, half - pool_rows
+        ),
+        **grid_of(
+            blocks,
+            [pl.BlockSpec((rows, block), lambda g: (0, g))] + query_specs,
+            [fixed, fixed],
+        ),
         out_shape=[
             jax.ShapeDtypeStruct((half, width), f32),
             jax.ShapeDtypeStruct((half, width), bf16),
         ],
-        scratch_shapes=[pltpu.VMEM((rows, width), f32)],
+        scratch_shapes=[pltpu.VMEM((rows, width), f32)] if blocks > 1 else [],
         compiler_params=params(40),
         cost_estimate=pl.CostEstimate(
             flops=2 * rows * total * width, bytes_accessed=6 * rows * width, transcendentals=0
         ),
         name="item_gradients",
-    )(weights, queries)
+    )(weights, *queries)
 
 
 def join_kernel(pool_rows, own_ref, taken_ref, pool_ref, passage_ref):
@@ -547,7 +634,8 @@
     copies = towers * chips
     query_unit, part, digits = project_queries(query_hidden, query_proj, ids, part_rows)
     parts = [moved(part, place_step=s) for s in range(2 if near_far else 1, chips)]
-    far = jnp.concatenate([x[:part_rows] for x in parts], axis=0)
+    slabs = width // 128
+    far = jnp.concatenate([x[: slabs * part_rows] for x in parts], axis=0)
     if near_far:
         next_digits = moved(digits, place_step=1)
         far, next_digits = lax.optimization_barrier((far, next_digits))
@@ -560,34 +648,35 @@
         sent_unit, _ = lax.optimization_barrier((query_unit, far))
         next_unit = moved(sent_unit, place_step=1)
         count = count_names([ids, next_digits] + parts, pool_rows, group * query_rows)
-        exps, totals, queries = score_pieces(
-            [query_unit, next_unit] + spread,
-            items,
-            other,
-            count,
-            query_rows,
-            pool_rows,
-            part_rows,
-            copies,
-        )
+        exps, near_totals = score_near(
+            query_unit, next_unit, items, other, count, query_rows, pool_rows
+        )
+        far_exps, totals, far_queries = score_far(
+            spread, items, other, count, near_totals, query_rows, pool_rows, part_rows, copies
+        )
+        exps = [exps, far_exps]
+        queries = [query_unit, next_unit, far_queries]
     else:
-        neg_count = ids.shape[0]
-        room = -(-query_rows // 128) * 128
-        ids = [ids]
-        for x in parts:
-            digits = x[part_rows : part_rows + neg_count].astype(f32).astype(jnp.int32)
-            ids.append(
-                ((digits[:, :query_rows] + 256) << 8) + digits[:, room : room + query_rows]
-            )
+        ids = [ids] + [ids_of(x[slabs * part_rows :]) for x in parts]
         count = count_names([jnp.concatenate(ids, axis=1)], pool_rows, group * query_rows)
         tower = lax.axis_index("tower")
         near = query_unit.reshape(1, towers, part_rows, width)
-        blocks = jnp.stack([x.reshape(chips - 1, part_rows, width) for x in spread], axis=1)
+        blocks = jnp.stack(
+            [
+                jnp.moveaxis(x.reshape(chips - 1, slabs, part_rows, 128), 1, 2).reshape(
+                    chips - 1, part_rows, width
+                )
+                for x in spread
+            ],
+            axis=1,
+        )
         blocks = jnp.take(blocks, tower ^ jnp.arange(towers), axis=1)
         queries = jnp.concatenate([near, blocks], axis=0).reshape(-1, width)
         exps, totals = score_joined(
             queries, items, other, count, query_rows, pool_rows, copies
         )
+        exps = [exps]
+        queries = [queries]
         shift = lax.axis_index("dp") // 2 // group
         turned = shift ^ jnp.arange(chips // group)
         totals = totals.reshape(copies, 2, chips // group, -1)
@@ -600,7 +689,7 @@
         totals = totals.reshape(copies, 2, chips // group, -1)
         totals = jnp.take(totals, turned, axis=2).reshape(copies, 2, -1)
     weights, *grads = weigh(
-        near_far, totals, exps, items, other, query_rows, pool_rows, part_rows, towers
+        totals, exps, items, other, query_rows, pool_rows, part_rows, towers
     )
     own_grad, sent_grad = item_gradients(weights, queries, query_rows, pool_rows)
     if near_far:

time: 64.5 us -> 64 us (level)
  local copies, waits for them, and re-layouts: 2.36 us -> 0.03 us
  waiting for transfers between devices: 10.4 us -> 11.4 us
    unnamed x8, local copies, waits for them, and re-layouts: 2.35 us -> 0.02 us
    ppermute x18, waiting for transfers between devices: 10.4 us -> 11.4 us  [moved(): return lax.ppermute(x, axes, pairs)]
    pallas_call x4 -> x5, Pallas kernels: 8.24 us -> 8.79 us  [the longest x1 2.74 us: count_names(): pl.pallas_call(functools.partial(count_kernel, pool_rows, 3 * neg_count),...]
  transfers between devices with their start and end apart: 18 -> 18, of which waited for: 9 -> 7; matrix products, arithmetic and copies ran while one was open for 0% -> 0% of each run, Pallas kernels for 13% -> 15%
where the time goes in v5:
time: 64 us; the launch traced here: 63.9 us
  starting transfers between devices  21.6 us (34%)
  Pallas kernels  16.1 us (25%)
  blocking collectives  13.3 us (21%)
  waiting for transfers between devices  11.4 us (18%)
  between operations  0.8 us (1%)
  other arithmetic  0.71 us (1%)
    ppermute x18, starting transfers between devices, moved(): return lax.ppermute(x, axes, pairs)  21.6 us
    all_to_all x1, blocking collectives, shards(): totals = lax.all_to_all(totals, axes, 0, 0, axis_index_groups=same_core)  13.3 us
    ppermute x18, waiting for transfers between devices, moved(): return lax.ppermute(x, axes, pairs)  11.4 us
    pallas_call x1, Pallas kernels, project_queries(): pl.pallas_call(functools.partial(query_kernel, steps, part_rows), in_spec...  3.17 us
    pallas_call x1, Pallas kernels, project_items(): pl.pallas_call(item_kernel, out_shape=jax.ShapeDtypeStruct((rows, width),...  2.95 us
    pallas_call x1, Pallas kernels, count_names(): pl.pallas_call(functools.partial(count_kernel, pool_rows, 3 * neg_count),...  2.74 us
    pallas_call x1, Pallas kernels, weigh(): pl.pallas_call(functools.partial(weight_kernel, blocks, len(exps), query_...  2.08 us
    pallas_call x1, Pallas kernels, item_gradients(): pl.pallas_call(functools.partial(gradient_kernel, blocks, len(queries), p...  1.52 us
  transfers between devices with their start and end apart: 18, of which 7 were waited for; matrix products, arithmetic and copies ran while one was open for 0% of the time, Pallas kernels for 15%

profile of v5, /device:TPU:0, one launch (start us, length us, event | category | flops | bytes accessed | tf_op | source)
XLA Modules:
  0.0 63.9 jit_solution(8952894908499982447)
XLA Ops:
  0.7 3.2 %query_units.1 = (bf16[192,768]{1,0:T(8,128)(2,1)S(1)}, bf16[312,128]{1,0:T(8,128)(2,1)S(1)}, bf16[24,128]{1,0:T(8,128)(2,1)S(1)}) custom-call(bf16[192,2304]{1,0:T(8,128)(2,1)} %hidden_ref.1, bf16[2304,768]{1,0:T(8,128)(2,1)} %weight_ref.2, s32[8,192]{1,0:T(8,128)} %bitcast.1), custom_call_target="tpu_custom_call" | custom-call | flops 5435817984 | bytes 26542080 | tf_op jit(solution)/shard_map/query_units/pallas_call | solution.py:100
  3.8 5.1 %collective-permute-start.1 = (bf16[312,128]{1,0:T(8,128)(2,1)S(1)}, bf16[312,128]{1,0:T(8,128)(2,1)S(1)}, u32[]{:S(2)}, u32[]{:S(2)}) collective-permute-start(bf16[312,128]{1,0:T(8,128)(2,1)S(1)} %get-tuple-element.37), channel_id=1, source_target_pairs={{0,6},{1,7},{2,4},{3,5},{4,2},{5,3},{6,0},{7,1},{8,14},{9,15},{10,... | collective-permute-start | bytes 239624 | tf_op jit(solution)/shard_map/ppermute | solution.py:630
  9.6 2.9 %item_units.1.refs_2_.refs_4_.refs_3_ = bf16[560,768]{1,0:T(8,128)(2,1)S(1)} custom-call(bf16[512,3072]{1,0:T(8,128)(2,1)S(1)} %copy-done.2, bf16[48,3072]{1,0:T(8,128)(2,1)S(1)} %copy-done.3, bf16[3072,768]{1,0:T(8,128)(2,1)S(1)} %copy-done.1), custom_call_target="tpu_custom_call" | custom-call | flops 2642411520 | bytes 8159232 | tf_op jit(solution)/shard_map/item_units/pallas_call | solution.py:140
  12.6 3.1 %collective-permute-done.refs_2_ = bf16[312,128]{1,0:T(8,128)(2,1)S(1)} collective-permute-done((bf16[312,128]{1,0:T(8,128)(2,1)S(1)}, bf16[312,128]{1,0:T(8,128)(2,1)S(1)}, u32[]{:S(2)}, u32[]{:S(2)}) %collective-permute-start) | collective-permute-done | bytes 79904 | tf_op jit(solution)/shard_map/ppermute | solution.py:630
  15.8 2.5 %collective-permute-start.5 = (bf16[576,128]{1,0:T(8,128)(2,1)S(1)}, bf16[576,128]{1,0:T(8,128)(2,1)S(1)}, u32[]{:S(2)}, u32[]{:S(2)}) collective-permute-start(bf16[576,128]{1,0:T(8,128)(2,1)S(1)} %pad_maximum_fusion.refs_0_), channel_id=1, source_target_pairs={{0,24},{1,25},{2,26},{3,27},{4,28},{5,29},{6,30},{7,31},{8,16},{9,... | collective-permute-start | bytes 442376 | tf_op jit(solution)/shard_map/ppermute | solution.py:630
  19.4 2.7 %name_counts.1.refs_4_.refs_6_ = bf16[1024,768]{1,0:T(8,128)(2,1)S(1)} custom-call(s32[8,192]{1,0:T(8,128)S(1)} %bitcast.2, bf16[24,128]{1,0:T(8,128)(2,1)S(1)} %collective-permute-done.2.refs_1_, bf16[312,128]{1,0:T(8,128)(2,1)S(1)} %collective-permute-done.refs_2_, bf16[312,128]{1,0:T(8,128)(2,1)S(1)} %collective-permute-done.1.refs_3_), custom_call_target="tpu_custom_call" | custom-call | flops 18874368 | bytes 1572864 | tf_op jit(solution)/shard_map/name_counts/pallas_call | solution.py:184
  22.1 3.0 %collective-permute-done.7.refs_1_ = bf16[192,768]{1,0:T(8,128)(2,1)S(1)} collective-permute-done((bf16[192,768]{1,0:T(8,128)(2,1)S(1)}, bf16[192,768]{1,0:T(8,128)(2,1)S(1)}, u32[]{:S(2)}, u32[]{:S(2)}) %collective-permute-start.7) | collective-permute-done | bytes 294944 | tf_op jit(solution)/shard_map/ppermute | solution.py:630
  25.2 1.1 %near_scores.1 = (bf16[1120,384]{1,0:T(8,128)(2,1)S(1)}, f32[2,384]{1,0:T(2,128)S(1)}) custom-call(bf16[192,768]{1,0:T(8,128)(2,1)S(1)} %get-tuple-element.44.refs_0_, bf16[192,768]{1,0:T(8,128)(2,1)S(1)} %collective-permute-done.7.refs_1_, bf16[560,768]{1,0:T(8,128)(2,1)S(1)} %item_units.1.refs_2_.refs_4_.refs_3_, ...), custom_call_target="tpu_custom_call" | custom-call | flops 660602880 | bytes 1720320 | tf_op jit(solution)/shard_map/near_scores/pallas_call | solution.py:377
  26.4 1.3 %far_scores.1 = (bf16[1120,384]{1,0:T(8,128)(2,1)S(1)}, f32[16,2,768]{2,1,0:T(2,128)S(1)}, bf16[384,768]{1,0:T(8,128)(2,1)S(1)}) custom-call(bf16[576,128]{1,0:T(8,128)(2,1)S(1)} %pad_maximum_fusion.refs_0_, bf16[576,128]{1,0:T(8,128)(2,1)S(1)} %collective-permute-done.3.refs_1_, bf16[576,128]{1,0:T(8,128)(2,1)S(1)} %collective-permute-done.4.refs_2_, ...), custom_call_target="tpu_custom_call" | custom-call | flops 660602880 | bytes 1720320 | tf_op jit(solution)/shard_map/far_scores/pallas_call | solution.py:361
  27.7 13.3 %all_to_all.5.refs_0_ = f32[16,2,768]{2,1,0:T(2,128)S(1)} all-to-all(f32[16,2,768]{2,1,0:T(2,128)S(1)} %get-tuple-element.46), channel_id=1, replica_groups={{0,2,4,6,8,10,12,14,16,18,20,22,24,26,28,30},{1,3,5,7,9,11,13,15,17,19,..., dimensions={0} | all-to-all | bytes 196608 | tf_op jit(solution)/shard_map/all_to_all | solution.py:687
  41.0 2.1 %weights.1 = (bf16[1120,768]{1,0:T(8,128)(2,1)S(1)}, bf16[192,768]{1,0:T(8,128)(2,1)S(1)}, bf16[192,768]{1,0:T(8,128)(2,1)S(1)}, bf16[2,48,768]{2,1,0:T(8,128)(2...) custom-call(f32[16,2,768]{2,1,0:T(2,128)S(1)} %all_to_all.5.refs_0_, ...), custom_call_target="tpu_custom_call" | custom-call | flops 1321205760 | bytes 3440640 | tf_op jit(solution)/shard_map/weights/pallas_call | solution.py:454
  43.1 1.2 %collective-permute-start.11 = (bf16[192,768]{1,0:T(8,128)(2,1)S(1)}, bf16[192,768]{1,0:T(8,128)(2,1)S(1)}, u32[]{:S(2)}, u32[]{:S(2)}) collective-permute-start(bf16[192,768]{1,0:T(8,128)(2,1)S(1)} %get-tuple-element.57), channel_id=1, source_target_pairs={{0,2},{1,3},{2,0},{3,1},{4,6},{5,7},{6,4},{7,5},{8,10},{9,11},{10,... | collective-permute-start | bytes 884744 | tf_op jit(solution)/shard_map/ppermute | solution.py:630
  44.2 1.1 %collective-permute-start.9 = (bf16[2,48,768]{2,1,0:T(8,128)(2,1)S(1)}, bf16[2,48,768]{2,1,0:T(8,128)(2,1)S(1)}, u32[]{:S(2)}, u32[]{:S(2)}) collective-permute-start(bf16[2,48,768]{2,1,0:T(8,128)(2,1)S(1)} %get-tuple-element.54), channel_id=1, source_target_pairs={{0,16},{1,17},{2,18},{3,19},{4,20},{5,21},{6,22},{7,23},{8,24},{9,... | collective-permute-start | bytes 442376 | tf_op jit(solution)/shard_map/ppermute | solution.py:630
  45.3 2.4 %collective-permute-start.10 = (bf16[2,48,768]{2,1,0:T(8,128)(2,1)S(1)}, bf16[2,48,768]{2,1,0:T(8,128)(2,1)S(1)}, u32[]{:S(2)}, u32[]{:S(2)}) collective-permute-start(bf16[2,48,768]{2,1,0:T(8,128)(2,1)S(1)} %get-tuple-element.55), channel_id=1, source_target_pairs={{0,24},{1,25},{2,26},{3,27},{4,28},{5,29},{6,30},{7,31},{8,16},{9,... | collective-permute-start | bytes 442376 | tf_op jit(solution)/shard_map/ppermute | solution.py:630
  47.7 1.5 %item_gradients.1 = (f32[560,768]{1,0:T(8,128)S(1)}, bf16[560,768]{1,0:T(8,128)(2,1)S(1)}) custom-call(bf16[1120,768]{1,0:T(8,128)(2,1)S(1)} %get-tuple-element.49.weight_ref, bf16[192,768]{1,0:T(8,128)(2,1)S(1)} %get-tuple-element.44.refs_0_, bf16[192,768]{1,0:T(8,128)(2,1)S(1)} %collective-permute-done.7.refs_1_, ...), custom_call_target="tpu_custom_call" | custom-call | flops 1321205760 | bytes 5160960 | tf_op jit(solution)/shard_map/item_gradients/pallas_call | solution.py:536
  49.6 1.8 %collective-permute-done.10.refs_3_ = bf16[2,48,768]{2,1,0:T(8,128)(2,1)S(1)} collective-permute-done((bf16[2,48,768]{2,1,0:T(8,128)(2,1)S(1)}, bf16[2,48,768]{2,1,0:T(8,128)(2,1)S(1)}, u32[]{:S(2)}, u32[]{:S(2)}) %collective-permute-start.10) | collective-permute-done | bytes 147488 | tf_op jit(solution)/shard_map/ppermute | solution.py:630
  51.6 1.1 %collective-permute-start.13 = (bf16[48,768]{1,0:T(8,128)(2,1)S(1)}, bf16[48,768]{1,0:T(8,128)(2,1)S(1)}, u32[]{:S(2)}, u32[]{:S(2)}) collective-permute-start(bf16[48,768]{1,0:T(8,128)(2,1)S(1)} %get-tuple-element.64), channel_id=1, source_target_pairs={{0,4},{1,5},{2,6},{3,7},{4,0},{5,1},{6,2},{7,3},{8,12},{9,13},{10,... | collective-permute-start | bytes 221192 | tf_op jit(solution)/shard_map/ppermute | solution.py:630
  52.7 2.8 %collective-permute-start.14 = (bf16[48,768]{1,0:T(8,128)(2,1)S(1)}, bf16[48,768]{1,0:T(8,128)(2,1)S(1)}, u32[]{:S(2)}, u32[]{:S(2)}) collective-permute-start(bf16[48,768]{1,0:T(8,128)(2,1)S(1)} %get-tuple-element.65), channel_id=1, source_target_pairs={{0,6},{1,7},{2,4},{3,5},{4,2},{5,3},{6,0},{7,1},{8,14},{9,15},{10,... | collective-permute-start | bytes 221192 | tf_op jit(solution)/shard_map/ppermute | solution.py:630
  55.5 1.3 %collective-permute-start.15 = (bf16[48,768]{1,0:T(8,128)(2,1)S(1)}, bf16[48,768]{1,0:T(8,128)(2,1)S(1)}, u32[]{:S(2)}, u32[]{:S(2)}) collective-permute-start(bf16[48,768]{1,0:T(8,128)(2,1)S(1)} %get-tuple-element.66), channel_id=1, source_target_pairs={{0,8},{1,9},{2,10},{3,11},{4,12},{5,13},{6,14},{7,15},{8,0},{9,1},... | collective-permute-start | bytes 221192 | tf_op jit(solution)/shard_map/ppermute | solution.py:630
  56.8 1.1 %collective-permute-start.16 = (bf16[48,768]{1,0:T(8,128)(2,1)S(1)}, bf16[48,768]{1,0:T(8,128)(2,1)S(1)}, u32[]{:S(2)}, u32[]{:S(2)}) collective-permute-start(bf16[48,768]{1,0:T(8,128)(2,1)S(1)} %get-tuple-element.67), channel_id=1, source_target_pairs={{0,16},{1,17},{2,18},{3,19},{4,20},{5,21},{6,22},{7,23},{8,24},{9,... | collective-permute-start | bytes 221192 | tf_op jit(solution)/shard_map/ppermute | solution.py:630
  57.9 1.1 %collective-permute-start.17 = (bf16[48,768]{1,0:T(8,128)(2,1)S(1)}, bf16[48,768]{1,0:T(8,128)(2,1)S(1)}, u32[]{:S(2)}, u32[]{:S(2)}) collective-permute-start(bf16[48,768]{1,0:T(8,128)(2,1)S(1)} %get-tuple-element.68), channel_id=1, source_target_pairs={{0,24},{1,25},{2,26},{3,27},{4,28},{5,29},{6,30},{7,31},{8,16},{9,... | collective-permute-start | bytes 221192 | tf_op jit(solution)/shard_map/ppermute | solution.py:630
  59.0 1.0 %join_item_gradients.1 = (bf16[512,768]{1,0:T(8,128)(2,1)}, bf16[48,768]{1,0:T(8,128)(2,1)}) custom-call(f32[560,768]{1,0:T(8,128)S(1)} %get-tuple-element.60.own_ref, bf16[560,768]{1,0:T(8,128)(2,1)S(1)} %collective-permute-done.12.taken_ref), custom_call_target="tpu_custom_call" | custom-call | flops 430080 | bytes 3440640 | tf_op jit(solution)/shard_map/join_item_gradients/pallas_call | solution.py:566
  60.8 1.2 %collective-permute-done.16 = bf16[48,768]{1,0:T(8,128)(2,1)S(1)} collective-permute-done((bf16[48,768]{1,0:T(8,128)(2,1)S(1)}, bf16[48,768]{1,0:T(8,128)(2,1)S(1)}, u32[]{:S(2)}, u32[]{:S(2)}) %collective-permute-start.16) | collective-permute-done | bytes 73760 | tf_op jit(solution)/shard_map/ppermute | solution.py:630
  62.0 1.2 %collective-permute-done.17 = bf16[48,768]{1,0:T(8,128)(2,1)S(1)} collective-permute-done((bf16[48,768]{1,0:T(8,128)(2,1)S(1)}, bf16[48,768]{1,0:T(8,128)(2,1)S(1)}, u32[]{:S(2)}, u32[]{:S(2)}) %collective-permute-start.17) | collective-permute-done | bytes 73760 | tf_op jit(solution)/shard_map/ppermute | solution.py:630
  (34 shorter events, 3.9 us)
Async XLA Ops:
  0.6 9.0 %copy-start.1 = (bf16[3072,768]{1,0:T(8,128)(2,1)S(1)}, bf16[3072,768]{1,0:T(8,128)(2,1)}, u32[]{:S(2)}) copy-start(bf16[3072,768]{1,0:T(8,128)(2,1)} %weight_ref.3) | copy-start | bytes 14155780
  0.6 9.0 %copy-start.2 = (bf16[512,3072]{1,0:T(8,128)(2,1)S(1)}, bf16[512,3072]{1,0:T(8,128)(2,1)}, u32[]{:S(2)}) copy-start(bf16[512,3072]{1,0:T(8,128)(2,1)} %pool_ref) | copy-start | bytes 9437188
  0.7 9.0 %copy-start.3 = (bf16[48,3072]{1,0:T(8,128)(2,1)S(1)}, bf16[48,3072]{1,0:T(8,128)(2,1)}, u32[]{:S(2)}) copy-start(bf16[48,3072]{1,0:T(8,128)(2,1)} %passage_ref.1) | copy-start | bytes 884740
  3.8 8.7 %collective-permute-start.1 = (bf16[312,128]{1,0:T(8,128)(2,1)S(1)}, bf16[312,128]{1,0:T(8,128)(2,1)S(1)}, u32[]{:S(2)}, u32[]{:S(2)}) collective-permute-start(bf16[312,128]{1,0:T(8,128)(2,1)S(1)} %get-tuple-element.37), channel_id=1, source_target_pairs={{0,6},{1,7},{2,4},{3,5},{4,2},{5,3},{6,0},{7,1},{8,14},{9,15},{10,... | collective-permute-start | bytes 239624 | tf_op jit(solution)/shard_map/ppermute | solution.py:630
  9.0 6.7 %collective-permute-start = (bf16[312,128]{1,0:T(8,128)(2,1)S(1)}, bf16[312,128]{1,0:T(8,128)(2,1)S(1)}, u32[]{:S(2)}, u32[]{:S(2)}) collective-permute-start(bf16[312,128]{1,0:T(8,128)(2,1)S(1)} %get-tuple-element.37), channel_id=1, source_target_pairs={{0,4},{1,5},{2,6},{3,7},{4,0},{5,1},{6,2},{7,3},{8,12},{9,13},{10,... | collective-permute-start | bytes 239624 | tf_op jit(solution)/shard_map/ppermute | solution.py:630
  9.0 10.4 %copy-start = (s32[192,8]{0,1:T(8,128)S(1)}, s32[192,8]{0,1:T(8,128)}, u32[]{:S(2)}) copy-start(s32[192,8]{0,1:T(8,128)} %param.11) | copy-start | bytes 18436
  9.0 6.7 %collective-permute-start.2 = (bf16[24,128]{1,0:T(8,128)(2,1)S(1)}, bf16[24,128]{1,0:T(8,128)(2,1)S(1)}, u32[]{:S(2)}, u32[]{:S(2)}) collective-permute-start(bf16[24,128]{1,0:T(8,128)(2,1)S(1)} %get-tuple-element.38), channel_id=1, source_target_pairs={{0,2},{1,3},{2,0},{3,1},{4,6},{5,7},{6,4},{7,5},{8,10},{9,11},{10,... | collective-permute-start | bytes 18440 | tf_op jit(solution)/shard_map/ppermute | solution.py:630
  15.7 9.5 %collective-permute-start.6 = (bf16[560,768]{1,0:T(8,128)(2,1)S(1)}, bf16[560,768]{1,0:T(8,128)(2,1)S(1)}, u32[]{:S(2)}, u32[]{:S(2)}) collective-permute-start(bf16[560,768]{1,0:T(8,128)(2,1)S(1)} %item_units.1.refs_2_.refs_4_.refs_3_), channel_id=1, source_target_pairs={{0,1},{1,0},{2,3},{3,2},{4,5},{5,4},{6,7},{7,6},{8,9},{9,8},{10,11... | collective-permute-start | bytes 2580488 | tf_op jit(solution)/shard_map/ppermute | solution.py:630
  15.8 9.4 %collective-permute-start.7 = (bf16[192,768]{1,0:T(8,128)(2,1)S(1)}, bf16[192,768]{1,0:T(8,128)(2,1)S(1)}, u32[]{:S(2)}, u32[]{:S(2)}) collective-permute-start(bf16[192,768]{1,0:T(8,128)(2,1)S(1)} %get-tuple-element.44.refs_0_), channel_id=1, source_target_pairs={{0,2},{1,3},{2,0},{3,1},{4,6},{5,7},{6,4},{7,5},{8,10},{9,11},{10,... | collective-permute-start | bytes 884744 | tf_op jit(solution)/shard_map/ppermute | solution.py:630
  15.8 10.5 %collective-permute-start.5 = (bf16[576,128]{1,0:T(8,128)(2,1)S(1)}, bf16[576,128]{1,0:T(8,128)(2,1)S(1)}, u32[]{:S(2)}, u32[]{:S(2)}) collective-permute-start(bf16[576,128]{1,0:T(8,128)(2,1)S(1)} %pad_maximum_fusion.refs_0_), channel_id=1, source_target_pairs={{0,24},{1,25},{2,26},{3,27},{4,28},{5,29},{6,30},{7,31},{8,16},{9,... | collective-permute-start | bytes 442376 | tf_op jit(solution)/shard_map/ppermute | solution.py:630
  18.3 8.0 %collective-permute-start.4 = (bf16[576,128]{1,0:T(8,128)(2,1)S(1)}, bf16[576,128]{1,0:T(8,128)(2,1)S(1)}, u32[]{:S(2)}, u32[]{:S(2)}) collective-permute-start(bf16[576,128]{1,0:T(8,128)(2,1)S(1)} %pad_maximum_fusion.refs_0_), channel_id=1, source_target_pairs={{0,16},{1,17},{2,18},{3,19},{4,20},{5,21},{6,22},{7,23},{8,24},{9,... | collective-permute-start | bytes 442376 | tf_op jit(solution)/shard_map/ppermute | solution.py:630
  18.9 7.5 %collective-permute-start.3 = (bf16[576,128]{1,0:T(8,128)(2,1)S(1)}, bf16[576,128]{1,0:T(8,128)(2,1)S(1)}, u32[]{:S(2)}, u32[]{:S(2)}) collective-permute-start(bf16[576,128]{1,0:T(8,128)(2,1)S(1)} %pad_maximum_fusion.refs_0_), channel_id=1, source_target_pairs={{0,8},{1,9},{2,10},{3,11},{4,12},{5,13},{6,14},{7,15},{8,0},{9,1},... | collective-permute-start | bytes 442376 | tf_op jit(solution)/shard_map/ppermute | solution.py:630
  43.1 8.3 %collective-permute-start.11 = (bf16[192,768]{1,0:T(8,128)(2,1)S(1)}, bf16[192,768]{1,0:T(8,128)(2,1)S(1)}, u32[]{:S(2)}, u32[]{:S(2)}) collective-permute-start(bf16[192,768]{1,0:T(8,128)(2,1)S(1)} %get-tuple-element.57), channel_id=1, source_target_pairs={{0,2},{1,3},{2,0},{3,1},{4,6},{5,7},{6,4},{7,5},{8,10},{9,11},{10,... | collective-permute-start | bytes 884744 | tf_op jit(solution)/shard_map/ppermute | solution.py:630
  44.2 5.4 %collective-permute-start.8 = (bf16[2,48,768]{2,1,0:T(8,128)(2,1)S(1)}, bf16[2,48,768]{2,1,0:T(8,128)(2,1)S(1)}, u32[]{:S(2)}, u32[]{:S(2)}) collective-permute-start(bf16[2,48,768]{2,1,0:T(8,128)(2,1)S(1)} %get-tuple-element.53), channel_id=1, source_target_pairs={{0,8},{1,9},{2,10},{3,11},{4,12},{5,13},{6,14},{7,15},{8,0},{9,1},... | collective-permute-start | bytes 442376 | tf_op jit(solution)/shard_map/ppermute | solution.py:630
  44.2 5.4 %collective-permute-start.9 = (bf16[2,48,768]{2,1,0:T(8,128)(2,1)S(1)}, bf16[2,48,768]{2,1,0:T(8,128)(2,1)S(1)}, u32[]{:S(2)}, u32[]{:S(2)}) collective-permute-start(bf16[2,48,768]{2,1,0:T(8,128)(2,1)S(1)} %get-tuple-element.54), channel_id=1, source_target_pairs={{0,16},{1,17},{2,18},{3,19},{4,20},{5,21},{6,22},{7,23},{8,24},{9,... | collective-permute-start | bytes 442376 | tf_op jit(solution)/shard_map/ppermute | solution.py:630
  45.3 6.0 %collective-permute-start.10 = (bf16[2,48,768]{2,1,0:T(8,128)(2,1)S(1)}, bf16[2,48,768]{2,1,0:T(8,128)(2,1)S(1)}, u32[]{:S(2)}, u32[]{:S(2)}) collective-permute-start(bf16[2,48,768]{2,1,0:T(8,128)(2,1)S(1)} %get-tuple-element.55), channel_id=1, source_target_pairs={{0,24},{1,25},{2,26},{3,27},{4,28},{5,29},{6,30},{7,31},{8,16},{9,... | collective-permute-start | bytes 442376 | tf_op jit(solution)/shard_map/ppermute | solution.py:630
  51.5 6.4 %collective-permute-start.12 = (bf16[560,768]{1,0:T(8,128)(2,1)S(1)}, bf16[560,768]{1,0:T(8,128)(2,1)S(1)}, u32[]{:S(2)}, u32[]{:S(2)}) collective-permute-start(bf16[560,768]{1,0:T(8,128)(2,1)S(1)} %get-tuple-element.61), channel_id=1, source_target_pairs={{0,1},{1,0},{2,3},{3,2},{4,5},{5,4},{6,7},{7,6},{8,9},{9,8},{10,11... | collective-permute-start | bytes 2580488 | tf_op jit(solution)/shard_map/ppermute | solution.py:630
  51.6 9.2 %collective-permute-start.13 = (bf16[48,768]{1,0:T(8,128)(2,1)S(1)}, bf16[48,768]{1,0:T(8,128)(2,1)S(1)}, u32[]{:S(2)}, u32[]{:S(2)}) collective-permute-start(bf16[48,768]{1,0:T(8,128)(2,1)S(1)} %get-tuple-element.64), channel_id=1, source_target_pairs={{0,4},{1,5},{2,6},{3,7},{4,0},{5,1},{6,2},{7,3},{8,12},{9,13},{10,... | collective-permute-start | bytes 221192 | tf_op jit(solution)/shard_map/ppermute | solution.py:630
  52.7 8.1 %collective-permute-start.14 = (bf16[48,768]{1,0:T(8,128)(2,1)S(1)}, bf16[48,768]{1,0:T(8,128)(2,1)S(1)}, u32[]{:S(2)}, u32[]{:S(2)}) collective-permute-start(bf16[48,768]{1,0:T(8,128)(2,1)S(1)} %get-tuple-element.65), channel_id=1, source_target_pairs={{0,6},{1,7},{2,4},{3,5},{4,2},{5,3},{6,0},{7,1},{8,14},{9,15},{10,... | collective-permute-start | bytes 221192 | tf_op jit(solution)/shard_map/ppermute | solution.py:630
  55.5 5.3 %collective-permute-start.15 = (bf16[48,768]{1,0:T(8,128)(2,1)S(1)}, bf16[48,768]{1,0:T(8,128)(2,1)S(1)}, u32[]{:S(2)}, u32[]{:S(2)}) collective-permute-start(bf16[48,768]{1,0:T(8,128)(2,1)S(1)} %get-tuple-element.66), channel_id=1, source_target_pairs={{0,8},{1,9},{2,10},{3,11},{4,12},{5,13},{6,14},{7,15},{8,0},{9,1},... | collective-permute-start | bytes 221192 | tf_op jit(solution)/shard_map/ppermute | solution.py:630
  56.8 5.1 %collective-permute-start.16 = (bf16[48,768]{1,0:T(8,128)(2,1)S(1)}, bf16[48,768]{1,0:T(8,128)(2,1)S(1)}, u32[]{:S(2)}, u32[]{:S(2)}) collective-permute-start(bf16[48,768]{1,0:T(8,128)(2,1)S(1)} %get-tuple-element.67), channel_id=1, source_target_pairs={{0,16},{1,17},{2,18},{3,19},{4,20},{5,21},{6,22},{7,23},{8,24},{9,... | collective-permute-start | bytes 221192 | tf_op jit(solution)/shard_map/ppermute | solution.py:630
  57.9 5.3 %collective-permute-start.17 = (bf16[48,768]{1,0:T(8,128)(2,1)S(1)}, bf16[48,768]{1,0:T(8,128)(2,1)S(1)}, u32[]{:S(2)}, u32[]{:S(2)}) collective-permute-start(bf16[48,768]{1,0:T(8,128)(2,1)S(1)} %get-tuple-element.68), channel_id=1, source_target_pairs={{0,24},{1,25},{2,26},{3,27},{4,28},{5,29},{6,30},{7,31},{8,16},{9,... | collective-permute-start | bytes 221192 | tf_op jit(solution)/shard_map/ppermute | solution.py:630

commit v6 on v5

--- a/solution.py
+++ b/solution.py
@@ -633,13 +633,18 @@
     near_far = chips == group
     copies = towers * chips
     query_unit, part, digits = project_queries(query_hidden, query_proj, ids, part_rows)
-    parts = [moved(part, place_step=s) for s in range(2 if near_far else 1, chips)]
+    if near_far:
+        parts = {s: moved(part, place_step=s) for s in [2, 3]}
+        parts = [parts[s] for s in range(2, chips)]
+    else:
+        parts = [moved(part, place_step=s) for s in range(1, chips)]
     slabs = width // 128
     far = jnp.concatenate([x[: slabs * part_rows] for x in parts], axis=0)
     if near_far:
         next_digits = moved(digits, place_step=1)
         far, next_digits = lax.optimization_barrier((far, next_digits))
-    spread = [far] + [moved(far, tower_step=d) for d in range(1, towers)]
+    spread = {d: moved(far, tower_step=d) for d in [1, 2, 3]}
+    spread = [far] + [spread[d] for d in range(1, towers)]
     pool_hidden, part = lax.optimization_barrier((pool_hidden, part))
     items = project_items(pool_hidden, passage_hidden, passage_proj)
     sent_items, _ = lax.optimization_barrier((items, far))
@@ -694,11 +699,12 @@
     own_grad, sent_grad = item_gradients(weights, queries, query_rows, pool_rows)
     if near_far:
         near_grad, next_grad, *grads = grads
-    sums = [grads[0]] + [moved(grads[d], tower_step=d) for d in range(1, towers)]
+    far_sums = [moved(grads[d], tower_step=d) for d in [3, 2, 1]]
+    sums = [grads[0]] + far_sums
     if near_far:
         plane, line = sum_lines(sums, (near_grad, moved(next_grad, place_step=1)))
-        arrived = [moved(line[s - 2], place_step=s) for s in range(2, chips)]
-        arrived += [moved(plane[d], tower_step=d) for d in range(1, towers)]
+        arrived = [moved(line[s - 2], place_step=s) for s in [3, 2]]
+        arrived += [moved(plane[d], tower_step=d) for d in [3, 2, 1]]
         own_line = plane[0]
     else:
         line = sum_lines(sums)

time: 64 us -> 62.9 us (0.983)
  starting transfers between devices: 21.6 us -> 20.6 us
    ppermute x18, starting transfers between devices: 21.6 us -> 20.6 us  [moved(): return lax.ppermute(x, axes, pairs)]
  transfers between devices with their start and end apart: 18 -> 18, of which waited for: 7 -> 5; matrix products, arithmetic and copies ran while one was open for 0% -> 0% of each run, Pallas kernels for 15% -> 15%
where the time goes in v6:
time: 62.9 us; the launch traced here: 62.7 us
  starting transfers between devices  20.6 us (33%)
  Pallas kernels  16.1 us (26%)
  blocking collectives  13.3 us (21%)
  waiting for transfers between devices  11.2 us (18%)
  between operations  0.81 us (1%)
  other arithmetic  0.71 us (1%)
    ppermute x18, starting transfers between devices, moved(): return lax.ppermute(x, axes, pairs)  20.6 us
    all_to_all x1, blocking collectives, shards(): totals = lax.all_to_all(totals, axes, 0, 0, axis_index_groups=same_core)  13.3 us
    ppermute x18, waiting for transfers between devices, moved(): return lax.ppermute(x, axes, pairs)  11.2 us
    pallas_call x1, Pallas kernels, project_queries(): pl.pallas_call(functools.partial(query_kernel, steps, part_rows), in_spec...  3.17 us
    pallas_call x1, Pallas kernels, project_items(): pl.pallas_call(item_kernel, out_shape=jax.ShapeDtypeStruct((rows, width),...  2.95 us
    pallas_call x1, Pallas kernels, count_names(): pl.pallas_call(functools.partial(count_kernel, pool_rows, 3 * neg_count),...  2.74 us
    pallas_call x1, Pallas kernels, weigh(): pl.pallas_call(functools.partial(weight_kernel, blocks, len(exps), query_...  2.08 us
    pallas_call x1, Pallas kernels, item_gradients(): pl.pallas_call(functools.partial(gradient_kernel, blocks, len(queries), p...  1.52 us
  transfers between devices with their start and end apart: 18, of which 5 were waited for; matrix products, arithmetic and copies ran while one was open for 0% of the time, Pallas kernels for 15%

profile of v6, /device:TPU:0, one launch (start us, length us, event | category | flops | bytes accessed | tf_op | source)
XLA Modules:
  0.0 62.7 jit_solution(4985816501832494024)
XLA Ops:
  0.7 3.2 %query_units.1 = (bf16[192,768]{1,0:T(8,128)(2,1)S(1)}, bf16[312,128]{1,0:T(8,128)(2,1)S(1)}, bf16[24,128]{1,0:T(8,128)(2,1)S(1)}) custom-call(bf16[192,2304]{1,0:T(8,128)(2,1)} %hidden_ref.1, bf16[2304,768]{1,0:T(8,128)(2,1)} %weight_ref.2, s32[8,192]{1,0:T(8,128)} %bitcast.1), custom_call_target="tpu_custom_call" | custom-call | flops 5435817984 | bytes 26542080 | tf_op jit(solution)/shard_map/query_units/pallas_call | solution.py:100
  3.8 5.1 %collective-permute-start.1 = (bf16[312,128]{1,0:T(8,128)(2,1)S(1)}, bf16[312,128]{1,0:T(8,128)(2,1)S(1)}, u32[]{:S(2)}, u32[]{:S(2)}) collective-permute-start(bf16[312,128]{1,0:T(8,128)(2,1)S(1)} %get-tuple-element.37), channel_id=1, source_target_pairs={{0,6},{1,7},{2,4},{3,5},{4,2},{5,3},{6,0},{7,1},{8,14},{9,15},{10,... | collective-permute-start | bytes 239624 | tf_op jit(solution)/shard_map/ppermute | solution.py:630
  9.6 2.9 %item_units.1.refs_2_.refs_4_.refs_3_ = bf16[560,768]{1,0:T(8,128)(2,1)S(1)} custom-call(bf16[512,3072]{1,0:T(8,128)(2,1)S(1)} %copy-done.2, bf16[48,3072]{1,0:T(8,128)(2,1)S(1)} %copy-done.3, bf16[3072,768]{1,0:T(8,128)(2,1)S(1)} %copy-done.1), custom_call_target="tpu_custom_call" | custom-call | flops 2642411520 | bytes 8159232 | tf_op jit(solution)/shard_map/item_units/pallas_call | solution.py:140
  12.6 3.1 %collective-permute-done.refs_2_ = bf16[312,128]{1,0:T(8,128)(2,1)S(1)} collective-permute-done((bf16[312,128]{1,0:T(8,128)(2,1)S(1)}, bf16[312,128]{1,0:T(8,128)(2,1)S(1)}, u32[]{:S(2)}, u32[]{:S(2)}) %collective-permute-start) | collective-permute-done | bytes 79904 | tf_op jit(solution)/shard_map/ppermute | solution.py:630
  15.8 2.5 %collective-permute-start.5 = (bf16[576,128]{1,0:T(8,128)(2,1)S(1)}, bf16[576,128]{1,0:T(8,128)(2,1)S(1)}, u32[]{:S(2)}, u32[]{:S(2)}) collective-permute-start(bf16[576,128]{1,0:T(8,128)(2,1)S(1)} %pad_maximum_fusion.refs_0_), channel_id=1, source_target_pairs={{0,24},{1,25},{2,26},{3,27},{4,28},{5,29},{6,30},{7,31},{8,16},{9,... | collective-permute-start | bytes 442376 | tf_op jit(solution)/shard_map/ppermute | solution.py:630
  19.4 2.7 %name_counts.1.refs_4_.refs_6_ = bf16[1024,768]{1,0:T(8,128)(2,1)S(1)} custom-call(s32[8,192]{1,0:T(8,128)S(1)} %bitcast.2, bf16[24,128]{1,0:T(8,128)(2,1)S(1)} %collective-permute-done.2.refs_1_, bf16[312,128]{1,0:T(8,128)(2,1)S(1)} %collective-permute-done.refs_2_, bf16[312,128]{1,0:T(8,128)(2,1)S(1)} %collective-permute-done.1.refs_3_), custom_call_target="tpu_custom_call" | custom-call | flops 18874368 | bytes 1572864 | tf_op jit(solution)/shard_map/name_counts/pallas_call | solution.py:184
  22.1 3.0 %collective-permute-done.7.refs_1_ = bf16[192,768]{1,0:T(8,128)(2,1)S(1)} collective-permute-done((bf16[192,768]{1,0:T(8,128)(2,1)S(1)}, bf16[192,768]{1,0:T(8,128)(2,1)S(1)}, u32[]{:S(2)}, u32[]{:S(2)}) %collective-permute-start.7) | collective-permute-done | bytes 294944 | tf_op jit(solution)/shard_map/ppermute | solution.py:630
  25.2 1.1 %near_scores.1 = (bf16[1120,384]{1,0:T(8,128)(2,1)S(1)}, f32[2,384]{1,0:T(2,128)S(1)}) custom-call(bf16[192,768]{1,0:T(8,128)(2,1)S(1)} %get-tuple-element.44.refs_0_, bf16[192,768]{1,0:T(8,128)(2,1)S(1)} %collective-permute-done.7.refs_1_, bf16[560,768]{1,0:T(8,128)(2,1)S(1)} %item_units.1.refs_2_.refs_4_.refs_3_, ...), custom_call_target="tpu_custom_call" | custom-call | flops 660602880 | bytes 1720320 | tf_op jit(solution)/shard_map/near_scores/pallas_call | solution.py:377
  26.4 1.3 %far_scores.1 = (bf16[1120,384]{1,0:T(8,128)(2,1)S(1)}, f32[16,2,768]{2,1,0:T(2,128)S(1)}, bf16[384,768]{1,0:T(8,128)(2,1)S(1)}) custom-call(bf16[576,128]{1,0:T(8,128)(2,1)S(1)} %pad_maximum_fusion.refs_0_, bf16[576,128]{1,0:T(8,128)(2,1)S(1)} %collective-permute-done.3.refs_1_, bf16[576,128]{1,0:T(8,128)(2,1)S(1)} %collective-permute-done.4.refs_2_, ...), custom_call_target="tpu_custom_call" | custom-call | flops 660602880 | bytes 1720320 | tf_op jit(solution)/shard_map/far_scores/pallas_call | solution.py:361
  27.7 13.3 %all_to_all.5.refs_0_ = f32[16,2,768]{2,1,0:T(2,128)S(1)} all-to-all(f32[16,2,768]{2,1,0:T(2,128)S(1)} %get-tuple-element.46), channel_id=1, replica_groups={{0,2,4,6,8,10,12,14,16,18,20,22,24,26,28,30},{1,3,5,7,9,11,13,15,17,19,..., dimensions={0} | all-to-all | bytes 196608 | tf_op jit(solution)/shard_map/all_to_all | solution.py:692
  41.0 2.1 %weights.1 = (bf16[1120,768]{1,0:T(8,128)(2,1)S(1)}, bf16[192,768]{1,0:T(8,128)(2,1)S(1)}, bf16[192,768]{1,0:T(8,128)(2,1)S(1)}, bf16[2,48,768]{2,1,0:T(8,128)(2...) custom-call(f32[16,2,768]{2,1,0:T(2,128)S(1)} %all_to_all.5.refs_0_, ...), custom_call_target="tpu_custom_call" | custom-call | flops 1321205760 | bytes 3440640 | tf_op jit(solution)/shard_map/weights/pallas_call | solution.py:454
  43.1 1.2 %collective-permute-start.11 = (bf16[192,768]{1,0:T(8,128)(2,1)S(1)}, bf16[192,768]{1,0:T(8,128)(2,1)S(1)}, u32[]{:S(2)}, u32[]{:S(2)}) collective-permute-start(bf16[192,768]{1,0:T(8,128)(2,1)S(1)} %get-tuple-element.57), channel_id=1, source_target_pairs={{0,2},{1,3},{2,0},{3,1},{4,6},{5,7},{6,4},{7,5},{8,10},{9,11},{10,... | collective-permute-start | bytes 884744 | tf_op jit(solution)/shard_map/ppermute | solution.py:630
  44.8 0.8 %collective-permute-start.9 = (bf16[2,48,768]{2,1,0:T(8,128)(2,1)S(1)}, bf16[2,48,768]{2,1,0:T(8,128)(2,1)S(1)}, u32[]{:S(2)}, u32[]{:S(2)}) collective-permute-start(bf16[2,48,768]{2,1,0:T(8,128)(2,1)S(1)} %get-tuple-element.54), channel_id=1, source_target_pairs={{0,16},{1,17},{2,18},{3,19},{4,20},{5,21},{6,22},{7,23},{8,24},{9,... | collective-permute-start | bytes 442376 | tf_op jit(solution)/shard_map/ppermute | solution.py:630
  45.6 2.1 %collective-permute-start.10 = (bf16[2,48,768]{2,1,0:T(8,128)(2,1)S(1)}, bf16[2,48,768]{2,1,0:T(8,128)(2,1)S(1)}, u32[]{:S(2)}, u32[]{:S(2)}) collective-permute-start(bf16[2,48,768]{2,1,0:T(8,128)(2,1)S(1)} %get-tuple-element.55), channel_id=1, source_target_pairs={{0,8},{1,9},{2,10},{3,11},{4,12},{5,13},{6,14},{7,15},{8,0},{9,1},... | collective-permute-start | bytes 442376 | tf_op jit(solution)/shard_map/ppermute | solution.py:630
  47.7 1.5 %item_gradients.1 = (f32[560,768]{1,0:T(8,128)S(1)}, bf16[560,768]{1,0:T(8,128)(2,1)S(1)}) custom-call(bf16[1120,768]{1,0:T(8,128)(2,1)S(1)} %get-tuple-element.49.weight_ref, bf16[192,768]{1,0:T(8,128)(2,1)S(1)} %get-tuple-element.44.refs_0_, bf16[192,768]{1,0:T(8,128)(2,1)S(1)} %collective-permute-done.7.refs_1_, ...), custom_call_target="tpu_custom_call" | custom-call | flops 1321205760 | bytes 5160960 | tf_op jit(solution)/shard_map/item_gradients/pallas_call | solution.py:536
  49.2 1.4 %collective-permute-done.8.refs_1_ = bf16[2,48,768]{2,1,0:T(8,128)(2,1)S(1)} collective-permute-done((bf16[2,48,768]{2,1,0:T(8,128)(2,1)S(1)}, bf16[2,48,768]{2,1,0:T(8,128)(2,1)S(1)}, u32[]{:S(2)}, u32[]{:S(2)}) %collective-permute-start.8) | collective-permute-done | bytes 147488 | tf_op jit(solution)/shard_map/ppermute | solution.py:630
  50.7 0.8 %collective-permute-done.9.refs_2_ = bf16[2,48,768]{2,1,0:T(8,128)(2,1)S(1)} collective-permute-done((bf16[2,48,768]{2,1,0:T(8,128)(2,1)S(1)}, bf16[2,48,768]{2,1,0:T(8,128)(2,1)S(1)}, u32[]{:S(2)}, u32[]{:S(2)}) %collective-permute-start.9) | collective-permute-done | bytes 147488 | tf_op jit(solution)/shard_map/ppermute | solution.py:630
  51.7 1.6 %collective-permute-start.13 = (bf16[48,768]{1,0:T(8,128)(2,1)S(1)}, bf16[48,768]{1,0:T(8,128)(2,1)S(1)}, u32[]{:S(2)}, u32[]{:S(2)}) collective-permute-start(bf16[48,768]{1,0:T(8,128)(2,1)S(1)} %get-tuple-element.64), channel_id=1, source_target_pairs={{0,6},{1,7},{2,4},{3,5},{4,2},{5,3},{6,0},{7,1},{8,14},{9,15},{10,... | collective-permute-start | bytes 221192 | tf_op jit(solution)/shard_map/ppermute | solution.py:630
  53.4 1.3 %collective-permute-start.14 = (bf16[48,768]{1,0:T(8,128)(2,1)S(1)}, bf16[48,768]{1,0:T(8,128)(2,1)S(1)}, u32[]{:S(2)}, u32[]{:S(2)}) collective-permute-start(bf16[48,768]{1,0:T(8,128)(2,1)S(1)} %get-tuple-element.65), channel_id=1, source_target_pairs={{0,4},{1,5},{2,6},{3,7},{4,0},{5,1},{6,2},{7,3},{8,12},{9,13},{10,... | collective-permute-start | bytes 221192 | tf_op jit(solution)/shard_map/ppermute | solution.py:630
  54.7 1.3 %collective-permute-start.15 = (bf16[48,768]{1,0:T(8,128)(2,1)S(1)}, bf16[48,768]{1,0:T(8,128)(2,1)S(1)}, u32[]{:S(2)}, u32[]{:S(2)}) collective-permute-start(bf16[48,768]{1,0:T(8,128)(2,1)S(1)} %get-tuple-element.66), channel_id=1, source_target_pairs={{0,24},{1,25},{2,26},{3,27},{4,28},{5,29},{6,30},{7,31},{8,16},{9,... | collective-permute-start | bytes 221192 | tf_op jit(solution)/shard_map/ppermute | solution.py:630
  56.0 1.0 %collective-permute-start.16 = (bf16[48,768]{1,0:T(8,128)(2,1)S(1)}, bf16[48,768]{1,0:T(8,128)(2,1)S(1)}, u32[]{:S(2)}, u32[]{:S(2)}) collective-permute-start(bf16[48,768]{1,0:T(8,128)(2,1)S(1)} %get-tuple-element.67), channel_id=1, source_target_pairs={{0,16},{1,17},{2,18},{3,19},{4,20},{5,21},{6,22},{7,23},{8,24},{9,... | collective-permute-start | bytes 221192 | tf_op jit(solution)/shard_map/ppermute | solution.py:630
  57.0 1.2 %collective-permute-start.17 = (bf16[48,768]{1,0:T(8,128)(2,1)S(1)}, bf16[48,768]{1,0:T(8,128)(2,1)S(1)}, u32[]{:S(2)}, u32[]{:S(2)}) collective-permute-start(bf16[48,768]{1,0:T(8,128)(2,1)S(1)} %get-tuple-element.68), channel_id=1, source_target_pairs={{0,8},{1,9},{2,10},{3,11},{4,12},{5,13},{6,14},{7,15},{8,0},{9,1},... | collective-permute-start | bytes 221192 | tf_op jit(solution)/shard_map/ppermute | solution.py:630
  58.2 1.0 %join_item_gradients.1 = (bf16[512,768]{1,0:T(8,128)(2,1)}, bf16[48,768]{1,0:T(8,128)(2,1)}) custom-call(f32[560,768]{1,0:T(8,128)S(1)} %get-tuple-element.60.own_ref, bf16[560,768]{1,0:T(8,128)(2,1)S(1)} %collective-permute-done.12.taken_ref), custom_call_target="tpu_custom_call" | custom-call | flops 430080 | bytes 3440640 | tf_op jit(solution)/shard_map/join_item_gradients/pallas_call | solution.py:566
  59.2 2.8 %collective-permute-done.14 = bf16[48,768]{1,0:T(8,128)(2,1)S(1)} collective-permute-done((bf16[48,768]{1,0:T(8,128)(2,1)S(1)}, bf16[48,768]{1,0:T(8,128)(2,1)S(1)}, u32[]{:S(2)}, u32[]{:S(2)}) %collective-permute-start.14) | collective-permute-done | bytes 73760 | tf_op jit(solution)/shard_map/ppermute | solution.py:630
  (34 shorter events, 3.4 us)
Async XLA Ops:
  0.6 9.0 %copy-start.1 = (bf16[3072,768]{1,0:T(8,128)(2,1)S(1)}, bf16[3072,768]{1,0:T(8,128)(2,1)}, u32[]{:S(2)}) copy-start(bf16[3072,768]{1,0:T(8,128)(2,1)} %weight_ref.3) | copy-start | bytes 14155780
  0.6 9.0 %copy-start.2 = (bf16[512,3072]{1,0:T(8,128)(2,1)S(1)}, bf16[512,3072]{1,0:T(8,128)(2,1)}, u32[]{:S(2)}) copy-start(bf16[512,3072]{1,0:T(8,128)(2,1)} %pool_ref) | copy-start | bytes 9437188
  0.7 9.0 %copy-start.3 = (bf16[48,3072]{1,0:T(8,128)(2,1)S(1)}, bf16[48,3072]{1,0:T(8,128)(2,1)}, u32[]{:S(2)}) copy-start(bf16[48,3072]{1,0:T(8,128)(2,1)} %passage_ref.1) | copy-start | bytes 884740
  3.8 8.7 %collective-permute-start.1 = (bf16[312,128]{1,0:T(8,128)(2,1)S(1)}, bf16[312,128]{1,0:T(8,128)(2,1)S(1)}, u32[]{:S(2)}, u32[]{:S(2)}) collective-permute-start(bf16[312,128]{1,0:T(8,128)(2,1)S(1)} %get-tuple-element.37), channel_id=1, source_target_pairs={{0,6},{1,7},{2,4},{3,5},{4,2},{5,3},{6,0},{7,1},{8,14},{9,15},{10,... | collective-permute-start | bytes 239624 | tf_op jit(solution)/shard_map/ppermute | solution.py:630
  9.0 6.7 %collective-permute-start = (bf16[312,128]{1,0:T(8,128)(2,1)S(1)}, bf16[312,128]{1,0:T(8,128)(2,1)S(1)}, u32[]{:S(2)}, u32[]{:S(2)}) collective-permute-start(bf16[312,128]{1,0:T(8,128)(2,1)S(1)} %get-tuple-element.37), channel_id=1, source_target_pairs={{0,4},{1,5},{2,6},{3,7},{4,0},{5,1},{6,2},{7,3},{8,12},{9,13},{10,... | collective-permute-start | bytes 239624 | tf_op jit(solution)/shard_map/ppermute | solution.py:630
  9.0 10.4 %copy-start = (s32[192,8]{0,1:T(8,128)S(1)}, s32[192,8]{0,1:T(8,128)}, u32[]{:S(2)}) copy-start(s32[192,8]{0,1:T(8,128)} %param.11) | copy-start | bytes 18436
  9.0 6.7 %collective-permute-start.2 = (bf16[24,128]{1,0:T(8,128)(2,1)S(1)}, bf16[24,128]{1,0:T(8,128)(2,1)S(1)}, u32[]{:S(2)}, u32[]{:S(2)}) collective-permute-start(bf16[24,128]{1,0:T(8,128)(2,1)S(1)} %get-tuple-element.38), channel_id=1, source_target_pairs={{0,2},{1,3},{2,0},{3,1},{4,6},{5,7},{6,4},{7,5},{8,10},{9,11},{10,... | collective-permute-start | bytes 18440 | tf_op jit(solution)/shard_map/ppermute | solution.py:630
  15.7 9.5 %collective-permute-start.6 = (bf16[560,768]{1,0:T(8,128)(2,1)S(1)}, bf16[560,768]{1,0:T(8,128)(2,1)S(1)}, u32[]{:S(2)}, u32[]{:S(2)}) collective-permute-start(bf16[560,768]{1,0:T(8,128)(2,1)S(1)} %item_units.1.refs_2_.refs_4_.refs_3_), channel_id=1, source_target_pairs={{0,1},{1,0},{2,3},{3,2},{4,5},{5,4},{6,7},{7,6},{8,9},{9,8},{10,11... | collective-permute-start | bytes 2580488 | tf_op jit(solution)/shard_map/ppermute | solution.py:630
  15.8 9.4 %collective-permute-start.7 = (bf16[192,768]{1,0:T(8,128)(2,1)S(1)}, bf16[192,768]{1,0:T(8,128)(2,1)S(1)}, u32[]{:S(2)}, u32[]{:S(2)}) collective-permute-start(bf16[192,768]{1,0:T(8,128)(2,1)S(1)} %get-tuple-element.44.refs_0_), channel_id=1, source_target_pairs={{0,2},{1,3},{2,0},{3,1},{4,6},{5,7},{6,4},{7,5},{8,10},{9,11},{10,... | collective-permute-start | bytes 884744 | tf_op jit(solution)/shard_map/ppermute | solution.py:630
  15.8 10.5 %collective-permute-start.5 = (bf16[576,128]{1,0:T(8,128)(2,1)S(1)}, bf16[576,128]{1,0:T(8,128)(2,1)S(1)}, u32[]{:S(2)}, u32[]{:S(2)}) collective-permute-start(bf16[576,128]{1,0:T(8,128)(2,1)S(1)} %pad_maximum_fusion.refs_0_), channel_id=1, source_target_pairs={{0,24},{1,25},{2,26},{3,27},{4,28},{5,29},{6,30},{7,31},{8,16},{9,... | collective-permute-start | bytes 442376 | tf_op jit(solution)/shard_map/ppermute | solution.py:630
  18.3 8.0 %collective-permute-start.4 = (bf16[576,128]{1,0:T(8,128)(2,1)S(1)}, bf16[576,128]{1,0:T(8,128)(2,1)S(1)}, u32[]{:S(2)}, u32[]{:S(2)}) collective-permute-start(bf16[576,128]{1,0:T(8,128)(2,1)S(1)} %pad_maximum_fusion.refs_0_), channel_id=1, source_target_pairs={{0,16},{1,17},{2,18},{3,19},{4,20},{5,21},{6,22},{7,23},{8,24},{9,... | collective-permute-start | bytes 442376 | tf_op jit(solution)/shard_map/ppermute | solution.py:630
  18.9 7.5 %collective-permute-start.3 = (bf16[576,128]{1,0:T(8,128)(2,1)S(1)}, bf16[576,128]{1,0:T(8,128)(2,1)S(1)}, u32[]{:S(2)}, u32[]{:S(2)}) collective-permute-start(bf16[576,128]{1,0:T(8,128)(2,1)S(1)} %pad_maximum_fusion.refs_0_), channel_id=1, source_target_pairs={{0,8},{1,9},{2,10},{3,11},{4,12},{5,13},{6,14},{7,15},{8,0},{9,1},... | collective-permute-start | bytes 442376 | tf_op jit(solution)/shard_map/ppermute | solution.py:630
  43.1 8.4 %collective-permute-start.11 = (bf16[192,768]{1,0:T(8,128)(2,1)S(1)}, bf16[192,768]{1,0:T(8,128)(2,1)S(1)}, u32[]{:S(2)}, u32[]{:S(2)}) collective-permute-start(bf16[192,768]{1,0:T(8,128)(2,1)S(1)} %get-tuple-element.57), channel_id=1, source_target_pairs={{0,2},{1,3},{2,0},{3,1},{4,6},{5,7},{6,4},{7,5},{8,10},{9,11},{10,... | collective-permute-start | bytes 884744 | tf_op jit(solution)/shard_map/ppermute | solution.py:630
  44.2 6.4 %collective-permute-start.8 = (bf16[2,48,768]{2,1,0:T(8,128)(2,1)S(1)}, bf16[2,48,768]{2,1,0:T(8,128)(2,1)S(1)}, u32[]{:S(2)}, u32[]{:S(2)}) collective-permute-start(bf16[2,48,768]{2,1,0:T(8,128)(2,1)S(1)} %get-tuple-element.53), channel_id=1, source_target_pairs={{0,24},{1,25},{2,26},{3,27},{4,28},{5,29},{6,30},{7,31},{8,16},{9,... | collective-permute-start | bytes 442376 | tf_op jit(solution)/shard_map/ppermute | solution.py:630
  44.8 6.7 %collective-permute-start.9 = (bf16[2,48,768]{2,1,0:T(8,128)(2,1)S(1)}, bf16[2,48,768]{2,1,0:T(8,128)(2,1)S(1)}, u32[]{:S(2)}, u32[]{:S(2)}) collective-permute-start(bf16[2,48,768]{2,1,0:T(8,128)(2,1)S(1)} %get-tuple-element.54), channel_id=1, source_target_pairs={{0,16},{1,17},{2,18},{3,19},{4,20},{5,21},{6,22},{7,23},{8,24},{9,... | collective-permute-start | bytes 442376 | tf_op jit(solution)/shard_map/ppermute | solution.py:630
  45.6 5.9 %collective-permute-start.10 = (bf16[2,48,768]{2,1,0:T(8,128)(2,1)S(1)}, bf16[2,48,768]{2,1,0:T(8,128)(2,1)S(1)}, u32[]{:S(2)}, u32[]{:S(2)}) collective-permute-start(bf16[2,48,768]{2,1,0:T(8,128)(2,1)S(1)} %get-tuple-element.55), channel_id=1, source_target_pairs={{0,8},{1,9},{2,10},{3,11},{4,12},{5,13},{6,14},{7,15},{8,0},{9,1},... | collective-permute-start | bytes 442376 | tf_op jit(solution)/shard_map/ppermute | solution.py:630
  51.7 5.4 %collective-permute-start.12 = (bf16[560,768]{1,0:T(8,128)(2,1)S(1)}, bf16[560,768]{1,0:T(8,128)(2,1)S(1)}, u32[]{:S(2)}, u32[]{:S(2)}) collective-permute-start(bf16[560,768]{1,0:T(8,128)(2,1)S(1)} %get-tuple-element.61), channel_id=1, source_target_pairs={{0,1},{1,0},{2,3},{3,2},{4,5},{5,4},{6,7},{7,6},{8,9},{9,8},{10,11... | collective-permute-start | bytes 2580488 | tf_op jit(solution)/shard_map/ppermute | solution.py:630
  51.7 7.5 %collective-permute-start.13 = (bf16[48,768]{1,0:T(8,128)(2,1)S(1)}, bf16[48,768]{1,0:T(8,128)(2,1)S(1)}, u32[]{:S(2)}, u32[]{:S(2)}) collective-permute-start(bf16[48,768]{1,0:T(8,128)(2,1)S(1)} %get-tuple-element.64), channel_id=1, source_target_pairs={{0,6},{1,7},{2,4},{3,5},{4,2},{5,3},{6,0},{7,1},{8,14},{9,15},{10,... | collective-permute-start | bytes 221192 | tf_op jit(solution)/shard_map/ppermute | solution.py:630
  53.4 8.7 %collective-permute-start.14 = (bf16[48,768]{1,0:T(8,128)(2,1)S(1)}, bf16[48,768]{1,0:T(8,128)(2,1)S(1)}, u32[]{:S(2)}, u32[]{:S(2)}) collective-permute-start(bf16[48,768]{1,0:T(8,128)(2,1)S(1)} %get-tuple-element.65), channel_id=1, source_target_pairs={{0,4},{1,5},{2,6},{3,7},{4,0},{5,1},{6,2},{7,3},{8,12},{9,13},{10,... | collective-permute-start | bytes 221192 | tf_op jit(solution)/shard_map/ppermute | solution.py:630
  54.7 7.3 %collective-permute-start.15 = (bf16[48,768]{1,0:T(8,128)(2,1)S(1)}, bf16[48,768]{1,0:T(8,128)(2,1)S(1)}, u32[]{:S(2)}, u32[]{:S(2)}) collective-permute-start(bf16[48,768]{1,0:T(8,128)(2,1)S(1)} %get-tuple-element.66), channel_id=1, source_target_pairs={{0,24},{1,25},{2,26},{3,27},{4,28},{5,29},{6,30},{7,31},{8,16},{9,... | collective-permute-start | bytes 221192 | tf_op jit(solution)/shard_map/ppermute | solution.py:630
  56.0 6.0 %collective-permute-start.16 = (bf16[48,768]{1,0:T(8,128)(2,1)S(1)}, bf16[48,768]{1,0:T(8,128)(2,1)S(1)}, u32[]{:S(2)}, u32[]{:S(2)}) collective-permute-start(bf16[48,768]{1,0:T(8,128)(2,1)S(1)} %get-tuple-element.67), channel_id=1, source_target_pairs={{0,16},{1,17},{2,18},{3,19},{4,20},{5,21},{6,22},{7,23},{8,24},{9,... | collective-permute-start | bytes 221192 | tf_op jit(solution)/shard_map/ppermute | solution.py:630
  57.0 5.0 %collective-permute-start.17 = (bf16[48,768]{1,0:T(8,128)(2,1)S(1)}, bf16[48,768]{1,0:T(8,128)(2,1)S(1)}, u32[]{:S(2)}, u32[]{:S(2)}) collective-permute-start(bf16[48,768]{1,0:T(8,128)(2,1)S(1)} %get-tuple-element.68), channel_id=1, source_target_pairs={{0,8},{1,9},{2,10},{3,11},{4,12},{5,13},{6,14},{7,15},{8,0},{9,1},... | collective-permute-start | bytes 221192 | tf_op jit(solution)/shard_map/ppermute | solution.py:630

commit v7 on v6

--- a/solution.py
+++ b/solution.py
@@ -54,7 +54,7 @@
     return ((high + 256) << 8) + low
 
 
-def query_kernel(steps, part_rows, hidden_ref, weight_ref, ids_ref, unit_ref, part_ref, digits_ref, hidden, weight, ids_near, sems, ids_sem):
+def query_kernel(steps, part_rows, hidden_ref, weight_ref, ids_ref, unit_ref, part_ref, head_ref, rest_ref, hidden, weight, ids_near, sems, ids_sem):
     depth = weight.shape[0] // steps
     copies = []
     for k in range(steps):
@@ -74,7 +74,8 @@
     digits = digits_of(ids_near[...])
     slabs = weight.shape[1] // 128
     part_ref[slabs * part_rows :, :] = digits
-    digits_ref[...] = digits
+    head_rows = unit_ref.shape[0] - rest_ref.shape[0]
+    head_ref[slabs * head_rows :, :] = digits
     total = None
     for k, pair in enumerate(copies):
         for copy in pair:
@@ -84,7 +85,11 @@
         total = product if total is None else total + product
     unit_ref[...] = normalized(total)
     start = pl.multiple_of(lax.axis_index("tower") * part_rows, 16)
+    rest_ref[...] = unit_ref[head_rows:, :]
     for k in range(slabs):
+        head_ref[k * head_rows : (k + 1) * head_rows, :] = unit_ref[
+            :head_rows, k * 128 : (k + 1) * 128
+        ]
         part_ref[k * part_rows : (k + 1) * part_rows, :] = unit_ref[
             pl.ds(start, part_rows), k * 128 : (k + 1) * 128
         ]
@@ -95,16 +100,18 @@
     width = weight.shape[1]
     steps = 3
     extra = 3 * ids.shape[0]
+    head = 1 * part_rows
     far = pl.BlockSpec(memory_space=pltpu.HBM)
     near = pl.BlockSpec(memory_space=pltpu.VMEM)
     return pl.pallas_call(
         functools.partial(query_kernel, steps, part_rows),
         in_specs=[far, far, far],
-        out_specs=[near, near, near],
+        out_specs=[near, near, near, near],
         out_shape=[
             jax.ShapeDtypeStruct((rows, width), bf16),
             jax.ShapeDtypeStruct((part_rows * width // 128 + extra, 128), bf16),
-            jax.ShapeDtypeStruct((extra, 128), bf16),
+            jax.ShapeDtypeStruct((head * width // 128 + extra, 128), bf16),
+            jax.ShapeDtypeStruct((rows - head, width), bf16),
         ],
         scratch_shapes=[
             pltpu.VMEM((rows, depth), bf16),
@@ -311,9 +318,14 @@
 
 
 def near_kernel(query_rows, pool_rows, *refs):
-    unit_ref, next_ref, own_ref, other_ref, count_ref, exp_ref, totals_ref, queries = refs
+    unit_ref, head_ref, rest_ref, own_ref, other_ref, count_ref, exp_ref, totals_ref, queries = refs
     queries[:query_rows, :] = unit_ref[...]
-    queries[query_rows:, :] = next_ref[...]
+    head_rows = query_rows - rest_ref.shape[0]
+    for k in range(queries.shape[1] // 128):
+        queries[query_rows : query_rows + head_rows, k * 128 : (k + 1) * 128] = head_ref[
+            k * head_rows : (k + 1) * head_rows, :
+        ]
+    queries[query_rows + head_rows :, :] = rest_ref[...]
     totals_ref[...] = score_tiles(
         (own_ref, other_ref), queries, count_ref, exp_ref, 0, query_rows, pool_rows, 1
     )
@@ -371,7 +383,7 @@
     )(*spread, items, other, count, near)
 
 
-def score_near(unit, next_unit, items, other, count, query_rows, pool_rows):
+def score_near(unit, head, rest, items, other, count, query_rows, pool_rows):
     rows, width = 2 * items.shape[0], items.shape[1]
     queries = 2 * query_rows
     return pl.pallas_call(
@@ -379,12 +391,12 @@
         out_shape=[
             jax.ShapeDtypeStruct((rows, queries), bf16),
             jax.ShapeDtypeStruct((2, queries), f32),
-        ],
-        scratch_shapes=[pltpu.VMEM((queries, width), bf16)],
+            jax.ShapeDtypeStruct((queries, width), bf16),
+        ],
         compiler_params=params(32),
         cost_estimate=score_cost(rows, queries, width),
         name="near_scores",
-    )(unit, next_unit, items, other, count)
+    )(unit, head, rest, items, other, count)
 
 
 def weight_kernel(blocks, exp_count, query_rows, pool_rows, own_rows, part_rows, towers, *refs):
@@ -392,7 +404,7 @@
     exp_refs, refs = refs[:exp_count], refs[exp_count:]
     own_ref, other_ref, weight_ref, *grad_refs = refs
     totals = placed_totals(jnp.sum(totals_ref[...], axis=0), query_rows)
-    scale = 1.0 / totals
+    scale = logit_scale / totals
     pools = 2 * pool_rows
     first = 0
     for exp_ref in exp_refs:
@@ -405,7 +417,7 @@
             exps = exp_ref[row : row + own_rows, :].astype(f32)
             mask = positive_mask(query_rows, own_rows, half, first, block, blocks)
             weight_ref[row : row + own_rows, lanes] = (
-                exps * batch + jnp.where(mask, exps * hard - 2.0, 0.0)
+                exps * batch + jnp.where(mask, exps * hard - 2.0 * logit_scale, 0.0)
             ).astype(bf16)
         first += block
     tower = lax.axis_index("tower")
@@ -418,10 +430,9 @@
         ],
         axis=0,
     )
-    grad = logit_scale * lax.dot_general(
+    grad = lax.dot_general(
         weight_ref[...], items, first_first, preferred_element_type=f32
-    )
-    grad = grad.astype(bf16)
+    ).astype(bf16)
     if exp_count == 2:
         near_ref, next_ref, *grad_refs = grad_refs
         near_ref[...] = grad[:query_rows]
@@ -491,18 +502,15 @@
     if len(query_refs) == 1:
         queries = query_refs[0][...]
     else:
-        unit_ref, next_ref, far_ref = query_refs
-        queries = jnp.concatenate(
-            [unit_ref[...], next_ref[...], far_ref[...]], axis=0
-        )
+        queries = jnp.concatenate([ref[...] for ref in query_refs], axis=0)
     product = jnp.dot(weight_ref[...], queries, preferred_element_type=f32)
 
     def finish(total):
         pools = 2 * pool_rows
-        own_ref[:pool_rows, :] = logit_scale * total[:pool_rows, :]
-        own_ref[pool_rows:, :] = logit_scale * total[pools : pools + own_rows, :]
-        sent_ref[:pool_rows, :] = (logit_scale * total[pool_rows:pools, :]).astype(bf16)
-        sent_ref[pool_rows:, :] = (logit_scale * total[pools + own_rows :, :]).astype(bf16)
+        own_ref[:pool_rows, :] = total[:pool_rows, :]
+        own_ref[pool_rows:, :] = total[pools : pools + own_rows, :]
+        sent_ref[:pool_rows, :] = total[pool_rows:pools, :].astype(bf16)
+        sent_ref[pool_rows:, :] = total[pools + own_rows :, :].astype(bf16)
 
     if steps == 1:
         finish(product)
@@ -632,7 +640,7 @@
     ids = jnp.transpose(negative_ids)
     near_far = chips == group
     copies = towers * chips
-    query_unit, part, digits = project_queries(query_hidden, query_proj, ids, part_rows)
+    query_unit, part, head, rest = project_queries(query_hidden, query_proj, ids, part_rows)
     if near_far:
         parts = {s: moved(part, place_step=s) for s in [2, 3]}
         parts = [parts[s] for s in range(2, chips)]
@@ -641,8 +649,8 @@
     slabs = width // 128
     far = jnp.concatenate([x[: slabs * part_rows] for x in parts], axis=0)
     if near_far:
-        next_digits = moved(digits, place_step=1)
-        far, next_digits = lax.optimization_barrier((far, next_digits))
+        next_head = moved(head, place_step=1)
+        far, next_head = lax.optimization_barrier((far, next_head))
     spread = {d: moved(far, tower_step=d) for d in [1, 2, 3]}
     spread = [far] + [spread[d] for d in range(1, towers)]
     pool_hidden, part = lax.optimization_barrier((pool_hidden, part))
@@ -650,17 +658,17 @@
     sent_items, _ = lax.optimization_barrier((items, far))
     other = moved(sent_items, core_step=1)
     if near_far:
-        sent_unit, _ = lax.optimization_barrier((query_unit, far))
-        next_unit = moved(sent_unit, place_step=1)
-        count = count_names([ids, next_digits] + parts, pool_rows, group * query_rows)
-        exps, near_totals = score_near(
-            query_unit, next_unit, items, other, count, query_rows, pool_rows
+        sent_rest, _ = lax.optimization_barrier((rest, far))
+        next_rest = moved(sent_rest, place_step=1)
+        count = count_names([ids, next_head] + parts, pool_rows, group * query_rows)
+        exps, near_totals, near_queries = score_near(
+            query_unit, next_head, next_rest, items, other, count, query_rows, pool_rows
         )
         far_exps, totals, far_queries = score_far(
             spread, items, other, count, near_totals, query_rows, pool_rows, part_rows, copies
         )
         exps = [exps, far_exps]
-        queries = [query_unit, next_unit, far_queries]
+        queries = [near_queries, far_queries]
     else:
         ids = [ids] + [ids_of(x[slabs * part_rows :]) for x in parts]
         count = count_names([jnp.concatenate(ids, axis=1)], pool_rows, group * query_rows)

time: 62.9 us -> 62.3 us (level)
  blocking collectives: 13.3 us -> 12.3 us
  starting transfers between devices: 20.6 us -> 21.4 us
    all_to_all x1, blocking collectives: 13.3 us -> 12.3 us  [shards(): totals = lax.all_to_all(totals, axes, 0, 0, axis_index_groups=same_core)]
    ppermute x18, starting transfers between devices: 20.6 us -> 21.4 us  [moved(): return lax.ppermute(x, axes, pairs)]
  transfers between devices with their start and end apart: 18 -> 18, of which waited for: 5 -> 7; matrix products, arithmetic and copies ran while one was open for 0% -> 0% of each run, Pallas kernels for 15% -> 15%
where the time goes in v7:
time: 62.3 us; the launch traced here: 62.2 us
  starting transfers between devices  21.4 us (34%)
  Pallas kernels  16.1 us (26%)
  blocking collectives  12.3 us (20%)
  waiting for transfers between devices  10.9 us (17%)
  between operations  0.79 us (1%)
  other arithmetic  0.71 us (1%)
    ppermute x18, starting transfers between devices, moved(): return lax.ppermute(x, axes, pairs)  21.4 us
    all_to_all x1, blocking collectives, shards(): totals = lax.all_to_all(totals, axes, 0, 0, axis_index_groups=same_core)  12.3 us
    ppermute x18, waiting for transfers between devices, moved(): return lax.ppermute(x, axes, pairs)  10.9 us
    pallas_call x1, Pallas kernels, project_queries(): pl.pallas_call(functools.partial(query_kernel, steps, part_rows), in_spec...  3.18 us
    pallas_call x1, Pallas kernels, project_items(): pl.pallas_call(item_kernel, out_shape=jax.ShapeDtypeStruct((rows, width),...  2.95 us
    pallas_call x1, Pallas kernels, count_names(): pl.pallas_call(functools.partial(count_kernel, pool_rows, 3 * neg_count),...  2.74 us
    pallas_call x1, Pallas kernels, weigh(): pl.pallas_call(functools.partial(weight_kernel, blocks, len(exps), query_...  2.07 us
    pallas_call x1, Pallas kernels, item_gradients(): pl.pallas_call(functools.partial(gradient_kernel, blocks, len(queries), p...  1.51 us
  transfers between devices with their start and end apart: 18, of which 7 were waited for; matrix products, arithmetic and copies ran while one was open for 0% of the time, Pallas kernels for 15%

profile of v7, /device:TPU:0, one launch (start us, length us, event | category | flops | bytes accessed | tf_op | source)
XLA Modules:
  0.0 62.2 jit_solution(1873427410938563290)
XLA Ops:
  0.7 3.2 %query_units.1 = (bf16[192,768]{1,0:T(8,128)(2,1)S(1)}, bf16[312,128]{1,0:T(8,128)(2,1)S(1)}, bf16[312,128]{1,0:T(8,128)(2,1)S(1)}, bf16[144,768]{1,0:T(8,128)(2,1)S(1)}) custom-call(bf16[192,2304]{1,0:T(8,128)(2,1)} %hidden_ref.1, bf16[2304,768]{1,0:T(8,128)(2,1)} %weight_ref.2, s32[8,192]{1,0:T(8,128)} %bitcast.1), custom_call_target="tpu_custom_call" | custom-call | flops 5435817984 | bytes 26542080 | tf_op jit(solution)/shard_map/query_units/pallas_call | solution.py:106
  3.9 5.1 %collective-permute-start.1 = (bf16[312,128]{1,0:T(8,128)(2,1)S(1)}, bf16[312,128]{1,0:T(8,128)(2,1)S(1)}, u32[]{:S(2)}, u32[]{:S(2)}) collective-permute-start(bf16[312,128]{1,0:T(8,128)(2,1)S(1)} %get-tuple-element.39), channel_id=1, source_target_pairs={{0,6},{1,7},{2,4},{3,5},{4,2},{5,3},{6,0},{7,1},{8,14},{9,15},{10,... | collective-permute-start | bytes 239624 | tf_op jit(solution)/shard_map/ppermute | solution.py:638
  9.6 2.9 %item_units.1.refs_3_.refs_4_ = bf16[560,768]{1,0:T(8,128)(2,1)S(1)} custom-call(bf16[512,3072]{1,0:T(8,128)(2,1)S(1)} %copy-done.2, bf16[48,3072]{1,0:T(8,128)(2,1)S(1)} %copy-done.3, bf16[3072,768]{1,0:T(8,128)(2,1)S(1)} %copy-done.1), custom_call_target="tpu_custom_call" | custom-call | flops 2642411520 | bytes 8159232 | tf_op jit(solution)/shard_map/item_units/pallas_call | solution.py:147
  12.6 3.1 %collective-permute-done.refs_2_ = bf16[312,128]{1,0:T(8,128)(2,1)S(1)} collective-permute-done((bf16[312,128]{1,0:T(8,128)(2,1)S(1)}, bf16[312,128]{1,0:T(8,128)(2,1)S(1)}, u32[]{:S(2)}, u32[]{:S(2)}) %collective-permute-start) | collective-permute-done | bytes 79904 | tf_op jit(solution)/shard_map/ppermute | solution.py:638
  15.8 0.8 %collective-permute-start.7 = (bf16[144,768]{1,0:T(8,128)(2,1)S(1)}, bf16[144,768]{1,0:T(8,128)(2,1)S(1)}, u32[]{:S(2)}, u32[]{:S(2)}) collective-permute-start(bf16[144,768]{1,0:T(8,128)(2,1)S(1)} %get-tuple-element.47), channel_id=1, source_target_pairs={{0,2},{1,3},{2,0},{3,1},{4,6},{5,7},{6,4},{7,5},{8,10},{9,11},{10,... | collective-permute-start | bytes 663560 | tf_op jit(solution)/shard_map/ppermute | solution.py:638
  16.6 2.5 %collective-permute-start.5 = (bf16[576,128]{1,0:T(8,128)(2,1)S(1)}, bf16[576,128]{1,0:T(8,128)(2,1)S(1)}, u32[]{:S(2)}, u32[]{:S(2)}) collective-permute-start(bf16[576,128]{1,0:T(8,128)(2,1)S(1)} %pad_maximum_fusion.refs_0_), channel_id=1, source_target_pairs={{0,24},{1,25},{2,26},{3,27},{4,28},{5,29},{6,30},{7,31},{8,16},{9,... | collective-permute-start | bytes 442376 | tf_op jit(solution)/shard_map/ppermute | solution.py:638
  20.1 2.7 %name_counts.1.refs_5_.refs_6_ = bf16[1024,768]{1,0:T(8,128)(2,1)S(1)} custom-call(s32[8,192]{1,0:T(8,128)S(1)} %bitcast.2, bf16[312,128]{1,0:T(8,128)(2,1)S(1)} %collective-permute-done.2.refs_1_, bf16[312,128]{1,0:T(8,128)(2,1)S(1)} %collective-permute-done.refs_2_, bf16[312,128]{1,0:T(8,128)(2,1)S(1)} %collective-permute-done.1.refs_3_), custom_call_target="tpu_custom_call" | custom-call | flops 18874368 | bytes 1572864 | tf_op jit(solution)/shard_map/name_counts/pallas_call | solution.py:191
  23.6 1.1 %near_scores.1 = (bf16[1120,384]{1,0:T(8,128)(2,1)S(1)}, f32[2,384]{1,0:T(2,128)S(1)}, bf16[384,768]{1,0:T(8,128)(2,1)S(1)}) custom-call(bf16[192,768]{1,0:T(8,128)(2,1)S(1)} %get-tuple-element.45.refs_0_, bf16[312,128]{1,0:T(8,128)(2,1)S(1)} %collective-permute-done.2.refs_1_, bf16[144,768]{1,0:T(8,128)(2,1)S(1)} %collective-permute-done.7.refs_2_, ...), custom_call_target="tpu_custom_call" | custom-call | flops 660602880 | bytes 1720320 | tf_op jit(solution)/shard_map/near_scores/pallas_call | solution.py:389
  24.8 1.8 %collective-permute-done.4.refs_2_ = bf16[576,128]{1,0:T(8,128)(2,1)S(1)} collective-permute-done((bf16[576,128]{1,0:T(8,128)(2,1)S(1)}, bf16[576,128]{1,0:T(8,128)(2,1)S(1)}, u32[]{:S(2)}, u32[]{:S(2)}) %collective-permute-start.4) | collective-permute-done | bytes 147488 | tf_op jit(solution)/shard_map/ppermute | solution.py:638
  26.7 1.3 %far_scores.1 = (bf16[1120,384]{1,0:T(8,128)(2,1)S(1)}, f32[16,2,768]{2,1,0:T(2,128)S(1)}, bf16[384,768]{1,0:T(8,128)(2,1)S(1)}) custom-call(bf16[576,128]{1,0:T(8,128)(2,1)S(1)} %pad_maximum_fusion.refs_0_, bf16[576,128]{1,0:T(8,128)(2,1)S(1)} %collective-permute-done.3.refs_1_, bf16[576,128]{1,0:T(8,128)(2,1)S(1)} %collective-permute-done.4.refs_2_, ...), custom_call_target="tpu_custom_call" | custom-call | flops 660602880 | bytes 1720320 | tf_op jit(solution)/shard_map/far_scores/pallas_call | solution.py:373
  28.0 12.3 %all_to_all.5.refs_0_ = f32[16,2,768]{2,1,0:T(2,128)S(1)} all-to-all(f32[16,2,768]{2,1,0:T(2,128)S(1)} %get-tuple-element.49), channel_id=1, replica_groups={{0,2,4,6,8,10,12,14,16,18,20,22,24,26,28,30},{1,3,5,7,9,11,13,15,17,19,..., dimensions={0} | all-to-all | bytes 196608 | tf_op jit(solution)/shard_map/all_to_all | solution.py:700
  40.3 2.1 %weights.1 = (bf16[1120,768]{1,0:T(8,128)(2,1)S(1)}, bf16[192,768]{1,0:T(8,128)(2,1)S(1)}, bf16[192,768]{1,0:T(8,128)(2,1)S(1)}, bf16[2,48,768]{2,1,0:T(8,128)(2...) custom-call(f32[16,2,768]{2,1,0:T(2,128)S(1)} %all_to_all.5.refs_0_, ...), custom_call_target="tpu_custom_call" | custom-call | flops 1321205760 | bytes 3440640 | tf_op jit(solution)/shard_map/weights/pallas_call | solution.py:465
  42.4 1.2 %collective-permute-start.11 = (bf16[192,768]{1,0:T(8,128)(2,1)S(1)}, bf16[192,768]{1,0:T(8,128)(2,1)S(1)}, u32[]{:S(2)}, u32[]{:S(2)}) collective-permute-start(bf16[192,768]{1,0:T(8,128)(2,1)S(1)} %get-tuple-element.61), channel_id=1, source_target_pairs={{0,2},{1,3},{2,0},{3,1},{4,6},{5,7},{6,4},{7,5},{8,10},{9,11},{10,... | collective-permute-start | bytes 884744 | tf_op jit(solution)/shard_map/ppermute | solution.py:638
  44.9 2.1 %collective-permute-start.10 = (bf16[2,48,768]{2,1,0:T(8,128)(2,1)S(1)}, bf16[2,48,768]{2,1,0:T(8,128)(2,1)S(1)}, u32[]{:S(2)}, u32[]{:S(2)}) collective-permute-start(bf16[2,48,768]{2,1,0:T(8,128)(2,1)S(1)} %get-tuple-element.59), channel_id=1, source_target_pairs={{0,8},{1,9},{2,10},{3,11},{4,12},{5,13},{6,14},{7,15},{8,0},{9,1},... | collective-permute-start | bytes 442376 | tf_op jit(solution)/shard_map/ppermute | solution.py:638
  47.0 1.5 %item_gradients.1 = (f32[560,768]{1,0:T(8,128)S(1)}, bf16[560,768]{1,0:T(8,128)(2,1)S(1)}) custom-call(bf16[1120,768]{1,0:T(8,128)(2,1)S(1)} %get-tuple-element.52.weight_ref, bf16[384,768]{1,0:T(8,128)(2,1)S(1)} %get-tuple-element.53.refs_0_, bf16[384,768]{1,0:T(8,128)(2,1)S(1)} %get-tuple-element.54.refs_1_), custom_call_target="tpu_custom_call" | custom-call | flops 1321205760 | bytes 5160960 | tf_op jit(solution)/shard_map/item_gradients/pallas_call | solution.py:544
  48.5 1.5 %collective-permute-done.8.refs_1_ = bf16[2,48,768]{2,1,0:T(8,128)(2,1)S(1)} collective-permute-done((bf16[2,48,768]{2,1,0:T(8,128)(2,1)S(1)}, bf16[2,48,768]{2,1,0:T(8,128)(2,1)S(1)}, u32[]{:S(2)}, u32[]{:S(2)}) %collective-permute-start.8) | collective-permute-done | bytes 147488 | tf_op jit(solution)/shard_map/ppermute | solution.py:638
  50.0 0.8 %collective-permute-done.9.refs_2_ = bf16[2,48,768]{2,1,0:T(8,128)(2,1)S(1)} collective-permute-done((bf16[2,48,768]{2,1,0:T(8,128)(2,1)S(1)}, bf16[2,48,768]{2,1,0:T(8,128)(2,1)S(1)}, u32[]{:S(2)}, u32[]{:S(2)}) %collective-permute-start.9) | collective-permute-done | bytes 147488 | tf_op jit(solution)/shard_map/ppermute | solution.py:638
  51.1 1.7 %collective-permute-start.13 = (bf16[48,768]{1,0:T(8,128)(2,1)S(1)}, bf16[48,768]{1,0:T(8,128)(2,1)S(1)}, u32[]{:S(2)}, u32[]{:S(2)}) collective-permute-start(bf16[48,768]{1,0:T(8,128)(2,1)S(1)} %get-tuple-element.68), channel_id=1, source_target_pairs={{0,6},{1,7},{2,4},{3,5},{4,2},{5,3},{6,0},{7,1},{8,14},{9,15},{10,... | collective-permute-start | bytes 221192 | tf_op jit(solution)/shard_map/ppermute | solution.py:638
  52.8 1.3 %collective-permute-start.14 = (bf16[48,768]{1,0:T(8,128)(2,1)S(1)}, bf16[48,768]{1,0:T(8,128)(2,1)S(1)}, u32[]{:S(2)}, u32[]{:S(2)}) collective-permute-start(bf16[48,768]{1,0:T(8,128)(2,1)S(1)} %get-tuple-element.69), channel_id=1, source_target_pairs={{0,4},{1,5},{2,6},{3,7},{4,0},{5,1},{6,2},{7,3},{8,12},{9,13},{10,... | collective-permute-start | bytes 221192 | tf_op jit(solution)/shard_map/ppermute | solution.py:638
  54.1 1.2 %collective-permute-start.15 = (bf16[48,768]{1,0:T(8,128)(2,1)S(1)}, bf16[48,768]{1,0:T(8,128)(2,1)S(1)}, u32[]{:S(2)}, u32[]{:S(2)}) collective-permute-start(bf16[48,768]{1,0:T(8,128)(2,1)S(1)} %get-tuple-element.70), channel_id=1, source_target_pairs={{0,24},{1,25},{2,26},{3,27},{4,28},{5,29},{6,30},{7,31},{8,16},{9,... | collective-permute-start | bytes 221192 | tf_op jit(solution)/shard_map/ppermute | solution.py:638
  55.4 1.0 %collective-permute-start.16 = (bf16[48,768]{1,0:T(8,128)(2,1)S(1)}, bf16[48,768]{1,0:T(8,128)(2,1)S(1)}, u32[]{:S(2)}, u32[]{:S(2)}) collective-permute-start(bf16[48,768]{1,0:T(8,128)(2,1)S(1)} %get-tuple-element.71), channel_id=1, source_target_pairs={{0,16},{1,17},{2,18},{3,19},{4,20},{5,21},{6,22},{7,23},{8,24},{9,... | collective-permute-start | bytes 221192 | tf_op jit(solution)/shard_map/ppermute | solution.py:638
  56.4 1.2 %collective-permute-start.17 = (bf16[48,768]{1,0:T(8,128)(2,1)S(1)}, bf16[48,768]{1,0:T(8,128)(2,1)S(1)}, u32[]{:S(2)}, u32[]{:S(2)}) collective-permute-start(bf16[48,768]{1,0:T(8,128)(2,1)S(1)} %get-tuple-element.72), channel_id=1, source_target_pairs={{0,8},{1,9},{2,10},{3,11},{4,12},{5,13},{6,14},{7,15},{8,0},{9,1},... | collective-permute-start | bytes 221192 | tf_op jit(solution)/shard_map/ppermute | solution.py:638
  57.6 1.0 %join_item_gradients.1 = (bf16[512,768]{1,0:T(8,128)(2,1)}, bf16[48,768]{1,0:T(8,128)(2,1)}) custom-call(f32[560,768]{1,0:T(8,128)S(1)} %get-tuple-element.64.own_ref, bf16[560,768]{1,0:T(8,128)(2,1)S(1)} %collective-permute-done.12.taken_ref), custom_call_target="tpu_custom_call" | custom-call | flops 430080 | bytes 3440640 | tf_op jit(solution)/shard_map/join_item_gradients/pallas_call | solution.py:574
  58.6 2.8 %collective-permute-done.14 = bf16[48,768]{1,0:T(8,128)(2,1)S(1)} collective-permute-done((bf16[48,768]{1,0:T(8,128)(2,1)S(1)}, bf16[48,768]{1,0:T(8,128)(2,1)S(1)}, u32[]{:S(2)}, u32[]{:S(2)}) %collective-permute-start.14) | collective-permute-done | bytes 73760 | tf_op jit(solution)/shard_map/ppermute | solution.py:638
  (34 shorter events, 5.0 us)
Async XLA Ops:
  0.6 9.0 %copy-start.1 = (bf16[3072,768]{1,0:T(8,128)(2,1)S(1)}, bf16[3072,768]{1,0:T(8,128)(2,1)}, u32[]{:S(2)}) copy-start(bf16[3072,768]{1,0:T(8,128)(2,1)} %weight_ref.3) | copy-start | bytes 14155780
  0.6 9.0 %copy-start.2 = (bf16[512,3072]{1,0:T(8,128)(2,1)S(1)}, bf16[512,3072]{1,0:T(8,128)(2,1)}, u32[]{:S(2)}) copy-start(bf16[512,3072]{1,0:T(8,128)(2,1)} %pool_ref) | copy-start | bytes 9437188
  0.7 9.0 %copy-start.3 = (bf16[48,3072]{1,0:T(8,128)(2,1)S(1)}, bf16[48,3072]{1,0:T(8,128)(2,1)}, u32[]{:S(2)}) copy-start(bf16[48,3072]{1,0:T(8,128)(2,1)} %passage_ref.1) | copy-start | bytes 884740
  3.9 8.7 %collective-permute-start.1 = (bf16[312,128]{1,0:T(8,128)(2,1)S(1)}, bf16[312,128]{1,0:T(8,128)(2,1)S(1)}, u32[]{:S(2)}, u32[]{:S(2)}) collective-permute-start(bf16[312,128]{1,0:T(8,128)(2,1)S(1)} %get-tuple-element.39), channel_id=1, source_target_pairs={{0,6},{1,7},{2,4},{3,5},{4,2},{5,3},{6,0},{7,1},{8,14},{9,15},{10,... | collective-permute-start | bytes 239624 | tf_op jit(solution)/shard_map/ppermute | solution.py:638
  9.0 6.7 %collective-permute-start = (bf16[312,128]{1,0:T(8,128)(2,1)S(1)}, bf16[312,128]{1,0:T(8,128)(2,1)S(1)}, u32[]{:S(2)}, u32[]{:S(2)}) collective-permute-start(bf16[312,128]{1,0:T(8,128)(2,1)S(1)} %get-tuple-element.39), channel_id=1, source_target_pairs={{0,4},{1,5},{2,6},{3,7},{4,0},{5,1},{6,2},{7,3},{8,12},{9,13},{10,... | collective-permute-start | bytes 239624 | tf_op jit(solution)/shard_map/ppermute | solution.py:638
  9.0 11.1 %copy-start = (s32[192,8]{0,1:T(8,128)S(1)}, s32[192,8]{0,1:T(8,128)}, u32[]{:S(2)}) copy-start(s32[192,8]{0,1:T(8,128)} %param.11) | copy-start | bytes 18436
  9.0 6.7 %collective-permute-start.2 = (bf16[312,128]{1,0:T(8,128)(2,1)S(1)}, bf16[312,128]{1,0:T(8,128)(2,1)S(1)}, u32[]{:S(2)}, u32[]{:S(2)}) collective-permute-start(bf16[312,128]{1,0:T(8,128)(2,1)S(1)} %get-tuple-element.40), channel_id=1, source_target_pairs={{0,2},{1,3},{2,0},{3,1},{4,6},{5,7},{6,4},{7,5},{8,10},{9,11},{10,... | collective-permute-start | bytes 239624 | tf_op jit(solution)/shard_map/ppermute | solution.py:638
  15.7 7.9 %collective-permute-start.6 = (bf16[560,768]{1,0:T(8,128)(2,1)S(1)}, bf16[560,768]{1,0:T(8,128)(2,1)S(1)}, u32[]{:S(2)}, u32[]{:S(2)}) collective-permute-start(bf16[560,768]{1,0:T(8,128)(2,1)S(1)} %item_units.1.refs_3_.refs_4_), channel_id=1, source_target_pairs={{0,1},{1,0},{2,3},{3,2},{4,5},{5,4},{6,7},{7,6},{8,9},{9,8},{10,11... | collective-permute-start | bytes 2580488 | tf_op jit(solution)/shard_map/ppermute | solution.py:638
  15.8 7.8 %collective-permute-start.7 = (bf16[144,768]{1,0:T(8,128)(2,1)S(1)}, bf16[144,768]{1,0:T(8,128)(2,1)S(1)}, u32[]{:S(2)}, u32[]{:S(2)}) collective-permute-start(bf16[144,768]{1,0:T(8,128)(2,1)S(1)} %get-tuple-element.47), channel_id=1, source_target_pairs={{0,2},{1,3},{2,0},{3,1},{4,6},{5,7},{6,4},{7,5},{8,10},{9,11},{10,... | collective-permute-start | bytes 663560 | tf_op jit(solution)/shard_map/ppermute | solution.py:638
  16.6 8.2 %collective-permute-start.5 = (bf16[576,128]{1,0:T(8,128)(2,1)S(1)}, bf16[576,128]{1,0:T(8,128)(2,1)S(1)}, u32[]{:S(2)}, u32[]{:S(2)}) collective-permute-start(bf16[576,128]{1,0:T(8,128)(2,1)S(1)} %pad_maximum_fusion.refs_0_), channel_id=1, source_target_pairs={{0,24},{1,25},{2,26},{3,27},{4,28},{5,29},{6,30},{7,31},{8,16},{9,... | collective-permute-start | bytes 442376 | tf_op jit(solution)/shard_map/ppermute | solution.py:638
  19.0 7.6 %collective-permute-start.4 = (bf16[576,128]{1,0:T(8,128)(2,1)S(1)}, bf16[576,128]{1,0:T(8,128)(2,1)S(1)}, u32[]{:S(2)}, u32[]{:S(2)}) collective-permute-start(bf16[576,128]{1,0:T(8,128)(2,1)S(1)} %pad_maximum_fusion.refs_0_), channel_id=1, source_target_pairs={{0,16},{1,17},{2,18},{3,19},{4,20},{5,21},{6,22},{7,23},{8,24},{9,... | collective-permute-start | bytes 442376 | tf_op jit(solution)/shard_map/ppermute | solution.py:638
  19.5 7.2 %collective-permute-start.3 = (bf16[576,128]{1,0:T(8,128)(2,1)S(1)}, bf16[576,128]{1,0:T(8,128)(2,1)S(1)}, u32[]{:S(2)}, u32[]{:S(2)}) collective-permute-start(bf16[576,128]{1,0:T(8,128)(2,1)S(1)} %pad_maximum_fusion.refs_0_), channel_id=1, source_target_pairs={{0,8},{1,9},{2,10},{3,11},{4,12},{5,13},{6,14},{7,15},{8,0},{9,1},... | collective-permute-start | bytes 442376 | tf_op jit(solution)/shard_map/ppermute | solution.py:638
  42.4 8.5 %collective-permute-start.11 = (bf16[192,768]{1,0:T(8,128)(2,1)S(1)}, bf16[192,768]{1,0:T(8,128)(2,1)S(1)}, u32[]{:S(2)}, u32[]{:S(2)}) collective-permute-start(bf16[192,768]{1,0:T(8,128)(2,1)S(1)} %get-tuple-element.61), channel_id=1, source_target_pairs={{0,2},{1,3},{2,0},{3,1},{4,6},{5,7},{6,4},{7,5},{8,10},{9,11},{10,... | collective-permute-start | bytes 884744 | tf_op jit(solution)/shard_map/ppermute | solution.py:638
  43.5 6.5 %collective-permute-start.8 = (bf16[2,48,768]{2,1,0:T(8,128)(2,1)S(1)}, bf16[2,48,768]{2,1,0:T(8,128)(2,1)S(1)}, u32[]{:S(2)}, u32[]{:S(2)}) collective-permute-start(bf16[2,48,768]{2,1,0:T(8,128)(2,1)S(1)} %get-tuple-element.57), channel_id=1, source_target_pairs={{0,24},{1,25},{2,26},{3,27},{4,28},{5,29},{6,30},{7,31},{8,16},{9,... | collective-permute-start | bytes 442376 | tf_op jit(solution)/shard_map/ppermute | solution.py:638
  44.1 6.8 %collective-permute-start.9 = (bf16[2,48,768]{2,1,0:T(8,128)(2,1)S(1)}, bf16[2,48,768]{2,1,0:T(8,128)(2,1)S(1)}, u32[]{:S(2)}, u32[]{:S(2)}) collective-permute-start(bf16[2,48,768]{2,1,0:T(8,128)(2,1)S(1)} %get-tuple-element.58), channel_id=1, source_target_pairs={{0,16},{1,17},{2,18},{3,19},{4,20},{5,21},{6,22},{7,23},{8,24},{9,... | collective-permute-start | bytes 442376 | tf_op jit(solution)/shard_map/ppermute | solution.py:638
  44.9 6.0 %collective-permute-start.10 = (bf16[2,48,768]{2,1,0:T(8,128)(2,1)S(1)}, bf16[2,48,768]{2,1,0:T(8,128)(2,1)S(1)}, u32[]{:S(2)}, u32[]{:S(2)}) collective-permute-start(bf16[2,48,768]{2,1,0:T(8,128)(2,1)S(1)} %get-tuple-element.59), channel_id=1, source_target_pairs={{0,8},{1,9},{2,10},{3,11},{4,12},{5,13},{6,14},{7,15},{8,0},{9,1},... | collective-permute-start | bytes 442376 | tf_op jit(solution)/shard_map/ppermute | solution.py:638
  51.0 5.4 %collective-permute-start.12 = (bf16[560,768]{1,0:T(8,128)(2,1)S(1)}, bf16[560,768]{1,0:T(8,128)(2,1)S(1)}, u32[]{:S(2)}, u32[]{:S(2)}) collective-permute-start(bf16[560,768]{1,0:T(8,128)(2,1)S(1)} %get-tuple-element.65), channel_id=1, source_target_pairs={{0,1},{1,0},{2,3},{3,2},{4,5},{5,4},{6,7},{7,6},{8,9},{9,8},{10,11... | collective-permute-start | bytes 2580488 | tf_op jit(solution)/shard_map/ppermute | solution.py:638
  51.1 7.6 %collective-permute-start.13 = (bf16[48,768]{1,0:T(8,128)(2,1)S(1)}, bf16[48,768]{1,0:T(8,128)(2,1)S(1)}, u32[]{:S(2)}, u32[]{:S(2)}) collective-permute-start(bf16[48,768]{1,0:T(8,128)(2,1)S(1)} %get-tuple-element.68), channel_id=1, source_target_pairs={{0,6},{1,7},{2,4},{3,5},{4,2},{5,3},{6,0},{7,1},{8,14},{9,15},{10,... | collective-permute-start | bytes 221192 | tf_op jit(solution)/shard_map/ppermute | solution.py:638
  52.8 8.7 %collective-permute-start.14 = (bf16[48,768]{1,0:T(8,128)(2,1)S(1)}, bf16[48,768]{1,0:T(8,128)(2,1)S(1)}, u32[]{:S(2)}, u32[]{:S(2)}) collective-permute-start(bf16[48,768]{1,0:T(8,128)(2,1)S(1)} %get-tuple-element.69), channel_id=1, source_target_pairs={{0,4},{1,5},{2,6},{3,7},{4,0},{5,1},{6,2},{7,3},{8,12},{9,13},{10,... | collective-permute-start | bytes 221192 | tf_op jit(solution)/shard_map/ppermute | solution.py:638
  54.1 7.3 %collective-permute-start.15 = (bf16[48,768]{1,0:T(8,128)(2,1)S(1)}, bf16[48,768]{1,0:T(8,128)(2,1)S(1)}, u32[]{:S(2)}, u32[]{:S(2)}) collective-permute-start(bf16[48,768]{1,0:T(8,128)(2,1)S(1)} %get-tuple-element.70), channel_id=1, source_target_pairs={{0,24},{1,25},{2,26},{3,27},{4,28},{5,29},{6,30},{7,31},{8,16},{9,... | collective-permute-start | bytes 221192 | tf_op jit(solution)/shard_map/ppermute | solution.py:638
  55.4 6.1 %collective-permute-start.16 = (bf16[48,768]{1,0:T(8,128)(2,1)S(1)}, bf16[48,768]{1,0:T(8,128)(2,1)S(1)}, u32[]{:S(2)}, u32[]{:S(2)}) collective-permute-start(bf16[48,768]{1,0:T(8,128)(2,1)S(1)} %get-tuple-element.71), channel_id=1, source_target_pairs={{0,16},{1,17},{2,18},{3,19},{4,20},{5,21},{6,22},{7,23},{8,24},{9,... | collective-permute-start | bytes 221192 | tf_op jit(solution)/shard_map/ppermute | solution.py:638
  56.4 5.1 %collective-permute-start.17 = (bf16[48,768]{1,0:T(8,128)(2,1)S(1)}, bf16[48,768]{1,0:T(8,128)(2,1)S(1)}, u32[]{:S(2)}, u32[]{:S(2)}) collective-permute-start(bf16[48,768]{1,0:T(8,128)(2,1)S(1)} %get-tuple-element.72), channel_id=1, source_target_pairs={{0,8},{1,9},{2,10},{3,11},{4,12},{5,13},{6,14},{7,15},{8,0},{9,1},... | collective-permute-start | bytes 221192 | tf_op jit(solution)/shard_map/ppermute | solution.py:638

commit v8 on v7

--- a/solution.py
+++ b/solution.py
@@ -9,6 +9,7 @@
 
 logit_scale = 50.0
 axes = ("tower", "dp")
+rank_order = [14, 10, 8, 15, 9, 4, 13, 11, 12, 1, 0, 3, 2, 6, 5, 7]
 group = 4
 f32 = jnp.float32
 bf16 = jnp.bfloat16
@@ -694,8 +695,11 @@
         turned = shift ^ jnp.arange(chips // group)
         totals = totals.reshape(copies, 2, chips // group, -1)
         totals = jnp.take(totals, turned, axis=2).reshape(copies, 2, -1)
+    ranks = list(reversed(range(copies)))
+    if copies == len(rank_order):
+        ranks = rank_order
     same_core = [
-        [t * dp_size + 2 * z + c for t in range(towers) for z in range(chips)] for c in range(2)
+        [rank // chips * dp_size + 2 * (rank % chips) + c for rank in ranks] for c in range(2)
     ]
     totals = lax.all_to_all(totals, axes, 0, 0, axis_index_groups=same_core)
     if not near_far:

time: 62.3 us -> 60.4 us (0.970)
  blocking collectives: 12.3 us -> 9.94 us
  waiting for transfers between devices: 10.9 us -> 11.9 us
    all_to_all x1, blocking collectives: 12.3 us -> 9.94 us  [shards(): totals = lax.all_to_all(totals, axes, 0, 0, axis_index_groups=same_core)]
    ppermute x18, waiting for transfers between devices: 10.9 us -> 11.9 us  [moved(): return lax.ppermute(x, axes, pairs)]
  transfers between devices with their start and end apart: 18 -> 18, of which waited for: 7 -> 7; matrix products, arithmetic and copies ran while one was open for 0% -> 0% of each run, Pallas kernels for 15% -> 16%
where the time goes in v8:
time: 60.4 us; the launch traced here: 60.2 us
  starting transfers between devices  20.8 us (34%)
  Pallas kernels  16.1 us (27%)
  waiting for transfers between devices  11.9 us (20%)
  blocking collectives  9.94 us (16%)
  between operations  0.79 us (1%)
  other arithmetic  0.71 us (1%)
    ppermute x18, starting transfers between devices, moved(): return lax.ppermute(x, axes, pairs)  20.8 us
    ppermute x18, waiting for transfers between devices, moved(): return lax.ppermute(x, axes, pairs)  11.9 us
    all_to_all x1, blocking collectives, shards(): totals = lax.all_to_all(totals, axes, 0, 0, axis_index_groups=same_core)  9.94 us
    pallas_call x1, Pallas kernels, project_queries(): pl.pallas_call(functools.partial(query_kernel, steps, part_rows), in_spec...  3.18 us
    pallas_call x1, Pallas kernels, project_items(): pl.pallas_call(item_kernel, out_shape=jax.ShapeDtypeStruct((rows, width),...  2.95 us
    pallas_call x1, Pallas kernels, count_names(): pl.pallas_call(functools.partial(count_kernel, pool_rows, 3 * neg_count),...  2.74 us
    pallas_call x1, Pallas kernels, weigh(): pl.pallas_call(functools.partial(weight_kernel, blocks, len(exps), query_...  2.07 us
    pallas_call x1, Pallas kernels, item_gradients(): pl.pallas_call(functools.partial(gradient_kernel, blocks, len(queries), p...  1.51 us
  transfers between devices with their start and end apart: 18, of which 7 were waited for; matrix products, arithmetic and copies ran while one was open for 0% of the time, Pallas kernels for 16%

profile of v8, /device:TPU:0, one launch (start us, length us, event | category | flops | bytes accessed | tf_op | source)
XLA Modules:
  0.0 60.2 jit_solution(3544013816639728160)
XLA Ops:
  0.7 3.2 %query_units.1 = (bf16[192,768]{1,0:T(8,128)(2,1)S(1)}, bf16[312,128]{1,0:T(8,128)(2,1)S(1)}, bf16[312,128]{1,0:T(8,128)(2,1)S(1)}, bf16[144,768]{1,0:T(8,128)(2,1)S(1)}) custom-call(bf16[192,2304]{1,0:T(8,128)(2,1)} %hidden_ref.1, bf16[2304,768]{1,0:T(8,128)(2,1)} %weight_ref.2, s32[8,192]{1,0:T(8,128)} %bitcast.1), custom_call_target="tpu_custom_call" | custom-call | flops 5435817984 | bytes 26542080 | tf_op jit(solution)/shard_map/query_units/pallas_call | solution.py:107
  3.9 5.1 %collective-permute-start.1 = (bf16[312,128]{1,0:T(8,128)(2,1)S(1)}, bf16[312,128]{1,0:T(8,128)(2,1)S(1)}, u32[]{:S(2)}, u32[]{:S(2)}) collective-permute-start(bf16[312,128]{1,0:T(8,128)(2,1)S(1)} %get-tuple-element.39), channel_id=1, source_target_pairs={{0,6},{1,7},{2,4},{3,5},{4,2},{5,3},{6,0},{7,1},{8,14},{9,15},{10,... | collective-permute-start | bytes 239624 | tf_op jit(solution)/shard_map/ppermute | solution.py:639
  9.6 2.9 %item_units.1.refs_3_.refs_4_ = bf16[560,768]{1,0:T(8,128)(2,1)S(1)} custom-call(bf16[512,3072]{1,0:T(8,128)(2,1)S(1)} %copy-done.2, bf16[48,3072]{1,0:T(8,128)(2,1)S(1)} %copy-done.3, bf16[3072,768]{1,0:T(8,128)(2,1)S(1)} %copy-done.1), custom_call_target="tpu_custom_call" | custom-call | flops 2642411520 | bytes 8159232 | tf_op jit(solution)/shard_map/item_units/pallas_call | solution.py:148
  12.6 3.1 %collective-permute-done.refs_2_ = bf16[312,128]{1,0:T(8,128)(2,1)S(1)} collective-permute-done((bf16[312,128]{1,0:T(8,128)(2,1)S(1)}, bf16[312,128]{1,0:T(8,128)(2,1)S(1)}, u32[]{:S(2)}, u32[]{:S(2)}) %collective-permute-start) | collective-permute-done | bytes 79904 | tf_op jit(solution)/shard_map/ppermute | solution.py:639
  15.8 0.8 %collective-permute-start.7 = (bf16[144,768]{1,0:T(8,128)(2,1)S(1)}, bf16[144,768]{1,0:T(8,128)(2,1)S(1)}, u32[]{:S(2)}, u32[]{:S(2)}) collective-permute-start(bf16[144,768]{1,0:T(8,128)(2,1)S(1)} %get-tuple-element.47), channel_id=1, source_target_pairs={{0,2},{1,3},{2,0},{3,1},{4,6},{5,7},{6,4},{7,5},{8,10},{9,11},{10,... | collective-permute-start | bytes 663560 | tf_op jit(solution)/shard_map/ppermute | solution.py:639
  16.6 2.5 %collective-permute-start.5 = (bf16[576,128]{1,0:T(8,128)(2,1)S(1)}, bf16[576,128]{1,0:T(8,128)(2,1)S(1)}, u32[]{:S(2)}, u32[]{:S(2)}) collective-permute-start(bf16[576,128]{1,0:T(8,128)(2,1)S(1)} %pad_maximum_fusion.refs_0_), channel_id=1, source_target_pairs={{0,24},{1,25},{2,26},{3,27},{4,28},{5,29},{6,30},{7,31},{8,16},{9,... | collective-permute-start | bytes 442376 | tf_op jit(solution)/shard_map/ppermute | solution.py:639
  20.1 2.7 %name_counts.1.refs_5_.refs_6_ = bf16[1024,768]{1,0:T(8,128)(2,1)S(1)} custom-call(s32[8,192]{1,0:T(8,128)S(1)} %bitcast.2, bf16[312,128]{1,0:T(8,128)(2,1)S(1)} %collective-permute-done.2.refs_1_, bf16[312,128]{1,0:T(8,128)(2,1)S(1)} %collective-permute-done.refs_2_, bf16[312,128]{1,0:T(8,128)(2,1)S(1)} %collective-permute-done.1.refs_3_), custom_call_target="tpu_custom_call" | custom-call | flops 18874368 | bytes 1572864 | tf_op jit(solution)/shard_map/name_counts/pallas_call | solution.py:192
  22.8 0.8 %collective-permute-done.7.refs_2_ = bf16[144,768]{1,0:T(8,128)(2,1)S(1)} collective-permute-done((bf16[144,768]{1,0:T(8,128)(2,1)S(1)}, bf16[144,768]{1,0:T(8,128)(2,1)S(1)}, u32[]{:S(2)}, u32[]{:S(2)}) %collective-permute-start.7) | collective-permute-done | bytes 221216 | tf_op jit(solution)/shard_map/ppermute | solution.py:639
  23.6 1.1 %near_scores.1 = (bf16[1120,384]{1,0:T(8,128)(2,1)S(1)}, f32[2,384]{1,0:T(2,128)S(1)}, bf16[384,768]{1,0:T(8,128)(2,1)S(1)}) custom-call(bf16[192,768]{1,0:T(8,128)(2,1)S(1)} %get-tuple-element.45.refs_0_, bf16[312,128]{1,0:T(8,128)(2,1)S(1)} %collective-permute-done.2.refs_1_, bf16[144,768]{1,0:T(8,128)(2,1)S(1)} %collective-permute-done.7.refs_2_, ...), custom_call_target="tpu_custom_call" | custom-call | flops 660602880 | bytes 1720320 | tf_op jit(solution)/shard_map/near_scores/pallas_call | solution.py:390
  24.8 1.8 %collective-permute-done.4.refs_2_ = bf16[576,128]{1,0:T(8,128)(2,1)S(1)} collective-permute-done((bf16[576,128]{1,0:T(8,128)(2,1)S(1)}, bf16[576,128]{1,0:T(8,128)(2,1)S(1)}, u32[]{:S(2)}, u32[]{:S(2)}) %collective-permute-start.4) | collective-permute-done | bytes 147488 | tf_op jit(solution)/shard_map/ppermute | solution.py:639
  26.7 1.3 %far_scores.1 = (bf16[1120,384]{1,0:T(8,128)(2,1)S(1)}, f32[16,2,768]{2,1,0:T(2,128)S(1)}, bf16[384,768]{1,0:T(8,128)(2,1)S(1)}) custom-call(bf16[576,128]{1,0:T(8,128)(2,1)S(1)} %pad_maximum_fusion.refs_0_, bf16[576,128]{1,0:T(8,128)(2,1)S(1)} %collective-permute-done.3.refs_1_, bf16[576,128]{1,0:T(8,128)(2,1)S(1)} %collective-permute-done.4.refs_2_, ...), custom_call_target="tpu_custom_call" | custom-call | flops 660602880 | bytes 1720320 | tf_op jit(solution)/shard_map/far_scores/pallas_call | solution.py:374
  28.0 9.9 %all_to_all.5.refs_0_ = f32[16,2,768]{2,1,0:T(2,128)S(1)} all-to-all(f32[16,2,768]{2,1,0:T(2,128)S(1)} %get-tuple-element.49), channel_id=1, replica_groups={{28,20,16,30,18,8,26,22,24,2,0,6,4,12,10,14},{29,21,17,31,19,9,27,23,25..., dimensions={0} | all-to-all | bytes 196608 | tf_op jit(solution)/shard_map/all_to_all | solution.py:704
  38.0 2.1 %weights.1 = (bf16[1120,768]{1,0:T(8,128)(2,1)S(1)}, bf16[192,768]{1,0:T(8,128)(2,1)S(1)}, bf16[192,768]{1,0:T(8,128)(2,1)S(1)}, bf16[2,48,768]{2,1,0:T(8,128)(2...) custom-call(f32[16,2,768]{2,1,0:T(2,128)S(1)} %all_to_all.5.refs_0_, ...), custom_call_target="tpu_custom_call" | custom-call | flops 1321205760 | bytes 3440640 | tf_op jit(solution)/shard_map/weights/pallas_call | solution.py:466
  40.7 2.2 %collective-permute-start.8 = (bf16[2,48,768]{2,1,0:T(8,128)(2,1)S(1)}, bf16[2,48,768]{2,1,0:T(8,128)(2,1)S(1)}, u32[]{:S(2)}, u32[]{:S(2)}) collective-permute-start(bf16[2,48,768]{2,1,0:T(8,128)(2,1)S(1)} %get-tuple-element.57), channel_id=1, source_target_pairs={{0,24},{1,25},{2,26},{3,27},{4,28},{5,29},{6,30},{7,31},{8,16},{9,... | collective-permute-start | bytes 442376 | tf_op jit(solution)/shard_map/ppermute | solution.py:639
  43.3 0.9 %collective-permute-start.10 = (bf16[2,48,768]{2,1,0:T(8,128)(2,1)S(1)}, bf16[2,48,768]{2,1,0:T(8,128)(2,1)S(1)}, u32[]{:S(2)}, u32[]{:S(2)}) collective-permute-start(bf16[2,48,768]{2,1,0:T(8,128)(2,1)S(1)} %get-tuple-element.59), channel_id=1, source_target_pairs={{0,8},{1,9},{2,10},{3,11},{4,12},{5,13},{6,14},{7,15},{8,0},{9,1},... | collective-permute-start | bytes 442376 | tf_op jit(solution)/shard_map/ppermute | solution.py:639
  44.2 1.5 %item_gradients.1 = (f32[560,768]{1,0:T(8,128)S(1)}, bf16[560,768]{1,0:T(8,128)(2,1)S(1)}) custom-call(bf16[1120,768]{1,0:T(8,128)(2,1)S(1)} %get-tuple-element.52.weight_ref, bf16[384,768]{1,0:T(8,128)(2,1)S(1)} %get-tuple-element.53.refs_0_, bf16[384,768]{1,0:T(8,128)(2,1)S(1)} %get-tuple-element.54.refs_1_), custom_call_target="tpu_custom_call" | custom-call | flops 1321205760 | bytes 5160960 | tf_op jit(solution)/shard_map/item_gradients/pallas_call | solution.py:545
  45.7 2.1 %collective-permute-done.8.refs_1_ = bf16[2,48,768]{2,1,0:T(8,128)(2,1)S(1)} collective-permute-done((bf16[2,48,768]{2,1,0:T(8,128)(2,1)S(1)}, bf16[2,48,768]{2,1,0:T(8,128)(2,1)S(1)}, u32[]{:S(2)}, u32[]{:S(2)}) %collective-permute-start.8) | collective-permute-done | bytes 147488 | tf_op jit(solution)/shard_map/ppermute | solution.py:639
  47.8 1.1 %collective-permute-done.9.refs_2_ = bf16[2,48,768]{2,1,0:T(8,128)(2,1)S(1)} collective-permute-done((bf16[2,48,768]{2,1,0:T(8,128)(2,1)S(1)}, bf16[2,48,768]{2,1,0:T(8,128)(2,1)S(1)}, u32[]{:S(2)}, u32[]{:S(2)}) %collective-permute-start.9) | collective-permute-done | bytes 147488 | tf_op jit(solution)/shard_map/ppermute | solution.py:639
  49.2 2.5 %collective-permute-start.13 = (bf16[48,768]{1,0:T(8,128)(2,1)S(1)}, bf16[48,768]{1,0:T(8,128)(2,1)S(1)}, u32[]{:S(2)}, u32[]{:S(2)}) collective-permute-start(bf16[48,768]{1,0:T(8,128)(2,1)S(1)} %get-tuple-element.68), channel_id=1, source_target_pairs={{0,6},{1,7},{2,4},{3,5},{4,2},{5,3},{6,0},{7,1},{8,14},{9,15},{10,... | collective-permute-start | bytes 221192 | tf_op jit(solution)/shard_map/ppermute | solution.py:639
  52.2 1.6 %collective-permute-start.15 = (bf16[48,768]{1,0:T(8,128)(2,1)S(1)}, bf16[48,768]{1,0:T(8,128)(2,1)S(1)}, u32[]{:S(2)}, u32[]{:S(2)}) collective-permute-start(bf16[48,768]{1,0:T(8,128)(2,1)S(1)} %get-tuple-element.70), channel_id=1, source_target_pairs={{0,24},{1,25},{2,26},{3,27},{4,28},{5,29},{6,30},{7,31},{8,16},{9,... | collective-permute-start | bytes 221192 | tf_op jit(solution)/shard_map/ppermute | solution.py:639
  53.8 1.1 %collective-permute-start.16 = (bf16[48,768]{1,0:T(8,128)(2,1)S(1)}, bf16[48,768]{1,0:T(8,128)(2,1)S(1)}, u32[]{:S(2)}, u32[]{:S(2)}) collective-permute-start(bf16[48,768]{1,0:T(8,128)(2,1)S(1)} %get-tuple-element.71), channel_id=1, source_target_pairs={{0,16},{1,17},{2,18},{3,19},{4,20},{5,21},{6,22},{7,23},{8,24},{9,... | collective-permute-start | bytes 221192 | tf_op jit(solution)/shard_map/ppermute | solution.py:639
  54.9 0.7 %collective-permute-start.17 = (bf16[48,768]{1,0:T(8,128)(2,1)S(1)}, bf16[48,768]{1,0:T(8,128)(2,1)S(1)}, u32[]{:S(2)}, u32[]{:S(2)}) collective-permute-start(bf16[48,768]{1,0:T(8,128)(2,1)S(1)} %get-tuple-element.72), channel_id=1, source_target_pairs={{0,8},{1,9},{2,10},{3,11},{4,12},{5,13},{6,14},{7,15},{8,0},{9,1},... | collective-permute-start | bytes 221192 | tf_op jit(solution)/shard_map/ppermute | solution.py:639
  55.7 1.0 %join_item_gradients.1 = (bf16[512,768]{1,0:T(8,128)(2,1)}, bf16[48,768]{1,0:T(8,128)(2,1)}) custom-call(f32[560,768]{1,0:T(8,128)S(1)} %get-tuple-element.64.own_ref, bf16[560,768]{1,0:T(8,128)(2,1)S(1)} %collective-permute-done.12.taken_ref), custom_call_target="tpu_custom_call" | custom-call | flops 430080 | bytes 3440640 | tf_op jit(solution)/shard_map/join_item_gradients/pallas_call | solution.py:575
  56.7 2.8 %collective-permute-done.14 = bf16[48,768]{1,0:T(8,128)(2,1)S(1)} collective-permute-done((bf16[48,768]{1,0:T(8,128)(2,1)S(1)}, bf16[48,768]{1,0:T(8,128)(2,1)S(1)}, u32[]{:S(2)}, u32[]{:S(2)}) %collective-permute-start.14) | collective-permute-done | bytes 73760 | tf_op jit(solution)/shard_map/ppermute | solution.py:639
  (34 shorter events, 4.4 us)
Async XLA Ops:
  0.6 9.0 %copy-start.1 = (bf16[3072,768]{1,0:T(8,128)(2,1)S(1)}, bf16[3072,768]{1,0:T(8,128)(2,1)}, u32[]{:S(2)}) copy-start(bf16[3072,768]{1,0:T(8,128)(2,1)} %weight_ref.3) | copy-start | bytes 14155780
  0.6 9.0 %copy-start.2 = (bf16[512,3072]{1,0:T(8,128)(2,1)S(1)}, bf16[512,3072]{1,0:T(8,128)(2,1)}, u32[]{:S(2)}) copy-start(bf16[512,3072]{1,0:T(8,128)(2,1)} %pool_ref) | copy-start | bytes 9437188
  0.7 9.0 %copy-start.3 = (bf16[48,3072]{1,0:T(8,128)(2,1)S(1)}, bf16[48,3072]{1,0:T(8,128)(2,1)}, u32[]{:S(2)}) copy-start(bf16[48,3072]{1,0:T(8,128)(2,1)} %passage_ref.1) | copy-start | bytes 884740
  3.9 8.7 %collective-permute-start.1 = (bf16[312,128]{1,0:T(8,128)(2,1)S(1)}, bf16[312,128]{1,0:T(8,128)(2,1)S(1)}, u32[]{:S(2)}, u32[]{:S(2)}) collective-permute-start(bf16[312,128]{1,0:T(8,128)(2,1)S(1)} %get-tuple-element.39), channel_id=1, source_target_pairs={{0,6},{1,7},{2,4},{3,5},{4,2},{5,3},{6,0},{7,1},{8,14},{9,15},{10,... | collective-permute-start | bytes 239624 | tf_op jit(solution)/shard_map/ppermute | solution.py:639
  9.0 6.7 %collective-permute-start = (bf16[312,128]{1,0:T(8,128)(2,1)S(1)}, bf16[312,128]{1,0:T(8,128)(2,1)S(1)}, u32[]{:S(2)}, u32[]{:S(2)}) collective-permute-start(bf16[312,128]{1,0:T(8,128)(2,1)S(1)} %get-tuple-element.39), channel_id=1, source_target_pairs={{0,4},{1,5},{2,6},{3,7},{4,0},{5,1},{6,2},{7,3},{8,12},{9,13},{10,... | collective-permute-start | bytes 239624 | tf_op jit(solution)/shard_map/ppermute | solution.py:639
  9.0 11.1 %copy-start = (s32[192,8]{0,1:T(8,128)S(1)}, s32[192,8]{0,1:T(8,128)}, u32[]{:S(2)}) copy-start(s32[192,8]{0,1:T(8,128)} %param.11) | copy-start | bytes 18436
  9.0 6.7 %collective-permute-start.2 = (bf16[312,128]{1,0:T(8,128)(2,1)S(1)}, bf16[312,128]{1,0:T(8,128)(2,1)S(1)}, u32[]{:S(2)}, u32[]{:S(2)}) collective-permute-start(bf16[312,128]{1,0:T(8,128)(2,1)S(1)} %get-tuple-element.40), channel_id=1, source_target_pairs={{0,2},{1,3},{2,0},{3,1},{4,6},{5,7},{6,4},{7,5},{8,10},{9,11},{10,... | collective-permute-start | bytes 239624 | tf_op jit(solution)/shard_map/ppermute | solution.py:639
  15.7 7.9 %collective-permute-start.6 = (bf16[560,768]{1,0:T(8,128)(2,1)S(1)}, bf16[560,768]{1,0:T(8,128)(2,1)S(1)}, u32[]{:S(2)}, u32[]{:S(2)}) collective-permute-start(bf16[560,768]{1,0:T(8,128)(2,1)S(1)} %item_units.1.refs_3_.refs_4_), channel_id=1, source_target_pairs={{0,1},{1,0},{2,3},{3,2},{4,5},{5,4},{6,7},{7,6},{8,9},{9,8},{10,11... | collective-permute-start | bytes 2580488 | tf_op jit(solution)/shard_map/ppermute | solution.py:639
  15.8 7.8 %collective-permute-start.7 = (bf16[144,768]{1,0:T(8,128)(2,1)S(1)}, bf16[144,768]{1,0:T(8,128)(2,1)S(1)}, u32[]{:S(2)}, u32[]{:S(2)}) collective-permute-start(bf16[144,768]{1,0:T(8,128)(2,1)S(1)} %get-tuple-element.47), channel_id=1, source_target_pairs={{0,2},{1,3},{2,0},{3,1},{4,6},{5,7},{6,4},{7,5},{8,10},{9,11},{10,... | collective-permute-start | bytes 663560 | tf_op jit(solution)/shard_map/ppermute | solution.py:639
  16.6 8.2 %collective-permute-start.5 = (bf16[576,128]{1,0:T(8,128)(2,1)S(1)}, bf16[576,128]{1,0:T(8,128)(2,1)S(1)}, u32[]{:S(2)}, u32[]{:S(2)}) collective-permute-start(bf16[576,128]{1,0:T(8,128)(2,1)S(1)} %pad_maximum_fusion.refs_0_), channel_id=1, source_target_pairs={{0,24},{1,25},{2,26},{3,27},{4,28},{5,29},{6,30},{7,31},{8,16},{9,... | collective-permute-start | bytes 442376 | tf_op jit(solution)/shard_map/ppermute | solution.py:639
  19.0 7.6 %collective-permute-start.4 = (bf16[576,128]{1,0:T(8,128)(2,1)S(1)}, bf16[576,128]{1,0:T(8,128)(2,1)S(1)}, u32[]{:S(2)}, u32[]{:S(2)}) collective-permute-start(bf16[576,128]{1,0:T(8,128)(2,1)S(1)} %pad_maximum_fusion.refs_0_), channel_id=1, source_target_pairs={{0,16},{1,17},{2,18},{3,19},{4,20},{5,21},{6,22},{7,23},{8,24},{9,... | collective-permute-start | bytes 442376 | tf_op jit(solution)/shard_map/ppermute | solution.py:639
  19.5 7.2 %collective-permute-start.3 = (bf16[576,128]{1,0:T(8,128)(2,1)S(1)}, bf16[576,128]{1,0:T(8,128)(2,1)S(1)}, u32[]{:S(2)}, u32[]{:S(2)}) collective-permute-start(bf16[576,128]{1,0:T(8,128)(2,1)S(1)} %pad_maximum_fusion.refs_0_), channel_id=1, source_target_pairs={{0,8},{1,9},{2,10},{3,11},{4,12},{5,13},{6,14},{7,15},{8,0},{9,1},... | collective-permute-start | bytes 442376 | tf_op jit(solution)/shard_map/ppermute | solution.py:639
  40.0 8.9 %collective-permute-start.11 = (bf16[192,768]{1,0:T(8,128)(2,1)S(1)}, bf16[192,768]{1,0:T(8,128)(2,1)S(1)}, u32[]{:S(2)}, u32[]{:S(2)}) collective-permute-start(bf16[192,768]{1,0:T(8,128)(2,1)S(1)} %get-tuple-element.61), channel_id=1, source_target_pairs={{0,2},{1,3},{2,0},{3,1},{4,6},{5,7},{6,4},{7,5},{8,10},{9,11},{10,... | collective-permute-start | bytes 884744 | tf_op jit(solution)/shard_map/ppermute | solution.py:639
  40.7 7.1 %collective-permute-start.8 = (bf16[2,48,768]{2,1,0:T(8,128)(2,1)S(1)}, bf16[2,48,768]{2,1,0:T(8,128)(2,1)S(1)}, u32[]{:S(2)}, u32[]{:S(2)}) collective-permute-start(bf16[2,48,768]{2,1,0:T(8,128)(2,1)S(1)} %get-tuple-element.57), channel_id=1, source_target_pairs={{0,24},{1,25},{2,26},{3,27},{4,28},{5,29},{6,30},{7,31},{8,16},{9,... | collective-permute-start | bytes 442376 | tf_op jit(solution)/shard_map/ppermute | solution.py:639
  42.9 6.0 %collective-permute-start.9 = (bf16[2,48,768]{2,1,0:T(8,128)(2,1)S(1)}, bf16[2,48,768]{2,1,0:T(8,128)(2,1)S(1)}, u32[]{:S(2)}, u32[]{:S(2)}) collective-permute-start(bf16[2,48,768]{2,1,0:T(8,128)(2,1)S(1)} %get-tuple-element.58), channel_id=1, source_target_pairs={{0,16},{1,17},{2,18},{3,19},{4,20},{5,21},{6,22},{7,23},{8,24},{9,... | collective-permute-start | bytes 442376 | tf_op jit(solution)/shard_map/ppermute | solution.py:639
  43.3 5.6 %collective-permute-start.10 = (bf16[2,48,768]{2,1,0:T(8,128)(2,1)S(1)}, bf16[2,48,768]{2,1,0:T(8,128)(2,1)S(1)}, u32[]{:S(2)}, u32[]{:S(2)}) collective-permute-start(bf16[2,48,768]{2,1,0:T(8,128)(2,1)S(1)} %get-tuple-element.59), channel_id=1, source_target_pairs={{0,8},{1,9},{2,10},{3,11},{4,12},{5,13},{6,14},{7,15},{8,0},{9,1},... | collective-permute-start | bytes 442376 | tf_op jit(solution)/shard_map/ppermute | solution.py:639
  49.1 5.8 %collective-permute-start.12 = (bf16[560,768]{1,0:T(8,128)(2,1)S(1)}, bf16[560,768]{1,0:T(8,128)(2,1)S(1)}, u32[]{:S(2)}, u32[]{:S(2)}) collective-permute-start(bf16[560,768]{1,0:T(8,128)(2,1)S(1)} %get-tuple-element.65), channel_id=1, source_target_pairs={{0,1},{1,0},{2,3},{3,2},{4,5},{5,4},{6,7},{7,6},{8,9},{9,8},{10,11... | collective-permute-start | bytes 2580488 | tf_op jit(solution)/shard_map/ppermute | solution.py:639
  49.2 7.5 %collective-permute-start.13 = (bf16[48,768]{1,0:T(8,128)(2,1)S(1)}, bf16[48,768]{1,0:T(8,128)(2,1)S(1)}, u32[]{:S(2)}, u32[]{:S(2)}) collective-permute-start(bf16[48,768]{1,0:T(8,128)(2,1)S(1)} %get-tuple-element.68), channel_id=1, source_target_pairs={{0,6},{1,7},{2,4},{3,5},{4,2},{5,3},{6,0},{7,1},{8,14},{9,15},{10,... | collective-permute-start | bytes 221192 | tf_op jit(solution)/shard_map/ppermute | solution.py:639
  51.7 7.8 %collective-permute-start.14 = (bf16[48,768]{1,0:T(8,128)(2,1)S(1)}, bf16[48,768]{1,0:T(8,128)(2,1)S(1)}, u32[]{:S(2)}, u32[]{:S(2)}) collective-permute-start(bf16[48,768]{1,0:T(8,128)(2,1)S(1)} %get-tuple-element.69), channel_id=1, source_target_pairs={{0,4},{1,5},{2,6},{3,7},{4,0},{5,1},{6,2},{7,3},{8,12},{9,13},{10,... | collective-permute-start | bytes 221192 | tf_op jit(solution)/shard_map/ppermute | solution.py:639
  52.2 7.3 %collective-permute-start.15 = (bf16[48,768]{1,0:T(8,128)(2,1)S(1)}, bf16[48,768]{1,0:T(8,128)(2,1)S(1)}, u32[]{:S(2)}, u32[]{:S(2)}) collective-permute-start(bf16[48,768]{1,0:T(8,128)(2,1)S(1)} %get-tuple-element.70), channel_id=1, source_target_pairs={{0,24},{1,25},{2,26},{3,27},{4,28},{5,29},{6,30},{7,31},{8,16},{9,... | collective-permute-start | bytes 221192 | tf_op jit(solution)/shard_map/ppermute | solution.py:639
  53.8 5.7 %collective-permute-start.16 = (bf16[48,768]{1,0:T(8,128)(2,1)S(1)}, bf16[48,768]{1,0:T(8,128)(2,1)S(1)}, u32[]{:S(2)}, u32[]{:S(2)}) collective-permute-start(bf16[48,768]{1,0:T(8,128)(2,1)S(1)} %get-tuple-element.71), channel_id=1, source_target_pairs={{0,16},{1,17},{2,18},{3,19},{4,20},{5,21},{6,22},{7,23},{8,24},{9,... | collective-permute-start | bytes 221192 | tf_op jit(solution)/shard_map/ppermute | solution.py:639
  54.9 4.6 %collective-permute-start.17 = (bf16[48,768]{1,0:T(8,128)(2,1)S(1)}, bf16[48,768]{1,0:T(8,128)(2,1)S(1)}, u32[]{:S(2)}, u32[]{:S(2)}) collective-permute-start(bf16[48,768]{1,0:T(8,128)(2,1)S(1)} %get-tuple-element.72), channel_id=1, source_target_pairs={{0,8},{1,9},{2,10},{3,11},{4,12},{5,13},{6,14},{7,15},{8,0},{9,1},... | collective-permute-start | bytes 221192 | tf_op jit(solution)/shard_map/ppermute | solution.py:639

commit v9 on v8

--- a/solution.py
+++ b/solution.py
@@ -652,7 +652,7 @@
     if near_far:
         next_head = moved(head, place_step=1)
         far, next_head = lax.optimization_barrier((far, next_head))
-    spread = {d: moved(far, tower_step=d) for d in [1, 2, 3]}
+    spread = {d: moved(far, tower_step=d) for d in [2, 1, 3]}
     spread = [far] + [spread[d] for d in range(1, towers)]
     pool_hidden, part = lax.optimization_barrier((pool_hidden, part))
     items = project_items(pool_hidden, passage_hidden, passage_proj)

time: 60.4 us -> 60.4 us (level)
  no operation moved by 1% of the time
where the time goes in v9:
time: 60.4 us; the launch traced here: 60.2 us
  starting transfers between devices  20.8 us (34%)
  Pallas kernels  16.1 us (27%)
  waiting for transfers between devices  11.9 us (20%)
  blocking collectives  9.94 us (16%)
  between operations  0.79 us (1%)
  other arithmetic  0.71 us (1%)
    ppermute x18, starting transfers between devices, moved(): return lax.ppermute(x, axes, pairs)  20.8 us
    ppermute x18, waiting for transfers between devices, moved(): return lax.ppermute(x, axes, pairs)  11.9 us
    all_to_all x1, blocking collectives, shards(): totals = lax.all_to_all(totals, axes, 0, 0, axis_index_groups=same_core)  9.94 us
    pallas_call x1, Pallas kernels, project_queries(): pl.pallas_call(functools.partial(query_kernel, steps, part_rows), in_spec...  3.18 us
    pallas_call x1, Pallas kernels, project_items(): pl.pallas_call(item_kernel, out_shape=jax.ShapeDtypeStruct((rows, width),...  2.95 us
    pallas_call x1, Pallas kernels, count_names(): pl.pallas_call(functools.partial(count_kernel, pool_rows, 3 * neg_count),...  2.74 us
    pallas_call x1, Pallas kernels, weigh(): pl.pallas_call(functools.partial(weight_kernel, blocks, len(exps), query_...  2.07 us
    pallas_call x1, Pallas kernels, item_gradients(): pl.pallas_call(functools.partial(gradient_kernel, blocks, len(queries), p...  1.51 us
  transfers between devices with their start and end apart: 18, of which 7 were waited for; matrix products, arithmetic and copies ran while one was open for 0% of the time, Pallas kernels for 16%

profile of v9, /device:TPU:0, one launch (start us, length us, event | category | flops | bytes accessed | tf_op | source)
XLA Modules:
  0.0 60.2 jit_solution(3544013816639728160)
XLA Ops:
  0.7 3.2 %query_units.1 = (bf16[192,768]{1,0:T(8,128)(2,1)S(1)}, bf16[312,128]{1,0:T(8,128)(2,1)S(1)}, bf16[312,128]{1,0:T(8,128)(2,1)S(1)}, bf16[144,768]{1,0:T(8,128)(2,1)S(1)}) custom-call(bf16[192,2304]{1,0:T(8,128)(2,1)} %hidden_ref.1, bf16[2304,768]{1,0:T(8,128)(2,1)} %weight_ref.2, s32[8,192]{1,0:T(8,128)} %bitcast.1), custom_call_target="tpu_custom_call" | custom-call | flops 5435817984 | bytes 26542080 | tf_op jit(solution)/shard_map/query_units/pallas_call | solution.py:107
  3.9 5.1 %collective-permute-start.1 = (bf16[312,128]{1,0:T(8,128)(2,1)S(1)}, bf16[312,128]{1,0:T(8,128)(2,1)S(1)}, u32[]{:S(2)}, u32[]{:S(2)}) collective-permute-start(bf16[312,128]{1,0:T(8,128)(2,1)S(1)} %get-tuple-element.39), channel_id=1, source_target_pairs={{0,6},{1,7},{2,4},{3,5},{4,2},{5,3},{6,0},{7,1},{8,14},{9,15},{10,... | collective-permute-start | bytes 239624 | tf_op jit(solution)/shard_map/ppermute | solution.py:639
  9.6 2.9 %item_units.1.refs_3_.refs_4_ = bf16[560,768]{1,0:T(8,128)(2,1)S(1)} custom-call(bf16[512,3072]{1,0:T(8,128)(2,1)S(1)} %copy-done.2, bf16[48,3072]{1,0:T(8,128)(2,1)S(1)} %copy-done.3, bf16[3072,768]{1,0:T(8,128)(2,1)S(1)} %copy-done.1), custom_call_target="tpu_custom_call" | custom-call | flops 2642411520 | bytes 8159232 | tf_op jit(solution)/shard_map/item_units/pallas_call | solution.py:148
  12.6 3.1 %collective-permute-done.refs_2_ = bf16[312,128]{1,0:T(8,128)(2,1)S(1)} collective-permute-done((bf16[312,128]{1,0:T(8,128)(2,1)S(1)}, bf16[312,128]{1,0:T(8,128)(2,1)S(1)}, u32[]{:S(2)}, u32[]{:S(2)}) %collective-permute-start) | collective-permute-done | bytes 79904 | tf_op jit(solution)/shard_map/ppermute | solution.py:639
  15.8 0.8 %collective-permute-start.7 = (bf16[144,768]{1,0:T(8,128)(2,1)S(1)}, bf16[144,768]{1,0:T(8,128)(2,1)S(1)}, u32[]{:S(2)}, u32[]{:S(2)}) collective-permute-start(bf16[144,768]{1,0:T(8,128)(2,1)S(1)} %get-tuple-element.47), channel_id=1, source_target_pairs={{0,2},{1,3},{2,0},{3,1},{4,6},{5,7},{6,4},{7,5},{8,10},{9,11},{10,... | collective-permute-start | bytes 663560 | tf_op jit(solution)/shard_map/ppermute | solution.py:639
  16.6 2.5 %collective-permute-start.5 = (bf16[576,128]{1,0:T(8,128)(2,1)S(1)}, bf16[576,128]{1,0:T(8,128)(2,1)S(1)}, u32[]{:S(2)}, u32[]{:S(2)}) collective-permute-start(bf16[576,128]{1,0:T(8,128)(2,1)S(1)} %pad_maximum_fusion.refs_0_), channel_id=1, source_target_pairs={{0,24},{1,25},{2,26},{3,27},{4,28},{5,29},{6,30},{7,31},{8,16},{9,... | collective-permute-start | bytes 442376 | tf_op jit(solution)/shard_map/ppermute | solution.py:639
  20.1 2.7 %name_counts.1.refs_5_.refs_6_ = bf16[1024,768]{1,0:T(8,128)(2,1)S(1)} custom-call(s32[8,192]{1,0:T(8,128)S(1)} %bitcast.2, bf16[312,128]{1,0:T(8,128)(2,1)S(1)} %collective-permute-done.2.refs_1_, bf16[312,128]{1,0:T(8,128)(2,1)S(1)} %collective-permute-done.refs_2_, bf16[312,128]{1,0:T(8,128)(2,1)S(1)} %collective-permute-done.1.refs_3_), custom_call_target="tpu_custom_call" | custom-call | flops 18874368 | bytes 1572864 | tf_op jit(solution)/shard_map/name_counts/pallas_call | solution.py:192
  22.8 0.8 %collective-permute-done.7.refs_2_ = bf16[144,768]{1,0:T(8,128)(2,1)S(1)} collective-permute-done((bf16[144,768]{1,0:T(8,128)(2,1)S(1)}, bf16[144,768]{1,0:T(8,128)(2,1)S(1)}, u32[]{:S(2)}, u32[]{:S(2)}) %collective-permute-start.7) | collective-permute-done | bytes 221216 | tf_op jit(solution)/shard_map/ppermute | solution.py:639
  23.6 1.1 %near_scores.1 = (bf16[1120,384]{1,0:T(8,128)(2,1)S(1)}, f32[2,384]{1,0:T(2,128)S(1)}, bf16[384,768]{1,0:T(8,128)(2,1)S(1)}) custom-call(bf16[192,768]{1,0:T(8,128)(2,1)S(1)} %get-tuple-element.45.refs_0_, bf16[312,128]{1,0:T(8,128)(2,1)S(1)} %collective-permute-done.2.refs_1_, bf16[144,768]{1,0:T(8,128)(2,1)S(1)} %collective-permute-done.7.refs_2_, ...), custom_call_target="tpu_custom_call" | custom-call | flops 660602880 | bytes 1720320 | tf_op jit(solution)/shard_map/near_scores/pallas_call | solution.py:390
  24.8 1.8 %collective-permute-done.4.refs_2_ = bf16[576,128]{1,0:T(8,128)(2,1)S(1)} collective-permute-done((bf16[576,128]{1,0:T(8,128)(2,1)S(1)}, bf16[576,128]{1,0:T(8,128)(2,1)S(1)}, u32[]{:S(2)}, u32[]{:S(2)}) %collective-permute-start.4) | collective-permute-done | bytes 147488 | tf_op jit(solution)/shard_map/ppermute | solution.py:639
  26.7 1.3 %far_scores.1 = (bf16[1120,384]{1,0:T(8,128)(2,1)S(1)}, f32[16,2,768]{2,1,0:T(2,128)S(1)}, bf16[384,768]{1,0:T(8,128)(2,1)S(1)}) custom-call(bf16[576,128]{1,0:T(8,128)(2,1)S(1)} %pad_maximum_fusion.refs_0_, bf16[576,128]{1,0:T(8,128)(2,1)S(1)} %collective-permute-done.3.refs_1_, bf16[576,128]{1,0:T(8,128)(2,1)S(1)} %collective-permute-done.4.refs_2_, ...), custom_call_target="tpu_custom_call" | custom-call | flops 660602880 | bytes 1720320 | tf_op jit(solution)/shard_map/far_scores/pallas_call | solution.py:374
  28.0 9.9 %all_to_all.5.refs_0_ = f32[16,2,768]{2,1,0:T(2,128)S(1)} all-to-all(f32[16,2,768]{2,1,0:T(2,128)S(1)} %get-tuple-element.49), channel_id=1, replica_groups={{28,20,16,30,18,8,26,22,24,2,0,6,4,12,10,14},{29,21,17,31,19,9,27,23,25..., dimensions={0} | all-to-all | bytes 196608 | tf_op jit(solution)/shard_map/all_to_all | solution.py:704
  38.0 2.1 %weights.1 = (bf16[1120,768]{1,0:T(8,128)(2,1)S(1)}, bf16[192,768]{1,0:T(8,128)(2,1)S(1)}, bf16[192,768]{1,0:T(8,128)(2,1)S(1)}, bf16[2,48,768]{2,1,0:T(8,128)(2...) custom-call(f32[16,2,768]{2,1,0:T(2,128)S(1)} %all_to_all.5.refs_0_, ...), custom_call_target="tpu_custom_call" | custom-call | flops 1321205760 | bytes 3440640 | tf_op jit(solution)/shard_map/weights/pallas_call | solution.py:466
  40.7 2.2 %collective-permute-start.8 = (bf16[2,48,768]{2,1,0:T(8,128)(2,1)S(1)}, bf16[2,48,768]{2,1,0:T(8,128)(2,1)S(1)}, u32[]{:S(2)}, u32[]{:S(2)}) collective-permute-start(bf16[2,48,768]{2,1,0:T(8,128)(2,1)S(1)} %get-tuple-element.57), channel_id=1, source_target_pairs={{0,24},{1,25},{2,26},{3,27},{4,28},{5,29},{6,30},{7,31},{8,16},{9,... | collective-permute-start | bytes 442376 | tf_op jit(solution)/shard_map/ppermute | solution.py:639
  43.3 0.9 %collective-permute-start.10 = (bf16[2,48,768]{2,1,0:T(8,128)(2,1)S(1)}, bf16[2,48,768]{2,1,0:T(8,128)(2,1)S(1)}, u32[]{:S(2)}, u32[]{:S(2)}) collective-permute-start(bf16[2,48,768]{2,1,0:T(8,128)(2,1)S(1)} %get-tuple-element.59), channel_id=1, source_target_pairs={{0,8},{1,9},{2,10},{3,11},{4,12},{5,13},{6,14},{7,15},{8,0},{9,1},... | collective-permute-start | bytes 442376 | tf_op jit(solution)/shard_map/ppermute | solution.py:639
  44.2 1.5 %item_gradients.1 = (f32[560,768]{1,0:T(8,128)S(1)}, bf16[560,768]{1,0:T(8,128)(2,1)S(1)}) custom-call(bf16[1120,768]{1,0:T(8,128)(2,1)S(1)} %get-tuple-element.52.weight_ref, bf16[384,768]{1,0:T(8,128)(2,1)S(1)} %get-tuple-element.53.refs_0_, bf16[384,768]{1,0:T(8,128)(2,1)S(1)} %get-tuple-element.54.refs_1_), custom_call_target="tpu_custom_call" | custom-call | flops 1321205760 | bytes 5160960 | tf_op jit(solution)/shard_map/item_gradients/pallas_call | solution.py:545
  45.7 2.1 %collective-permute-done.8.refs_1_ = bf16[2,48,768]{2,1,0:T(8,128)(2,1)S(1)} collective-permute-done((bf16[2,48,768]{2,1,0:T(8,128)(2,1)S(1)}, bf16[2,48,768]{2,1,0:T(8,128)(2,1)S(1)}, u32[]{:S(2)}, u32[]{:S(2)}) %collective-permute-start.8) | collective-permute-done | bytes 147488 | tf_op jit(solution)/shard_map/ppermute | solution.py:639
  47.8 1.1 %collective-permute-done.9.refs_2_ = bf16[2,48,768]{2,1,0:T(8,128)(2,1)S(1)} collective-permute-done((bf16[2,48,768]{2,1,0:T(8,128)(2,1)S(1)}, bf16[2,48,768]{2,1,0:T(8,128)(2,1)S(1)}, u32[]{:S(2)}, u32[]{:S(2)}) %collective-permute-start.9) | collective-permute-done | bytes 147488 | tf_op jit(solution)/shard_map/ppermute | solution.py:639
  49.2 2.5 %collective-permute-start.13 = (bf16[48,768]{1,0:T(8,128)(2,1)S(1)}, bf16[48,768]{1,0:T(8,128)(2,1)S(1)}, u32[]{:S(2)}, u32[]{:S(2)}) collective-permute-start(bf16[48,768]{1,0:T(8,128)(2,1)S(1)} %get-tuple-element.68), channel_id=1, source_target_pairs={{0,6},{1,7},{2,4},{3,5},{4,2},{5,3},{6,0},{7,1},{8,14},{9,15},{10,... | collective-permute-start | bytes 221192 | tf_op jit(solution)/shard_map/ppermute | solution.py:639
  52.2 1.6 %collective-permute-start.15 = (bf16[48,768]{1,0:T(8,128)(2,1)S(1)}, bf16[48,768]{1,0:T(8,128)(2,1)S(1)}, u32[]{:S(2)}, u32[]{:S(2)}) collective-permute-start(bf16[48,768]{1,0:T(8,128)(2,1)S(1)} %get-tuple-element.70), channel_id=1, source_target_pairs={{0,24},{1,25},{2,26},{3,27},{4,28},{5,29},{6,30},{7,31},{8,16},{9,... | collective-permute-start | bytes 221192 | tf_op jit(solution)/shard_map/ppermute | solution.py:639
  53.8 1.1 %collective-permute-start.16 = (bf16[48,768]{1,0:T(8,128)(2,1)S(1)}, bf16[48,768]{1,0:T(8,128)(2,1)S(1)}, u32[]{:S(2)}, u32[]{:S(2)}) collective-permute-start(bf16[48,768]{1,0:T(8,128)(2,1)S(1)} %get-tuple-element.71), channel_id=1, source_target_pairs={{0,16},{1,17},{2,18},{3,19},{4,20},{5,21},{6,22},{7,23},{8,24},{9,... | collective-permute-start | bytes 221192 | tf_op jit(solution)/shard_map/ppermute | solution.py:639
  54.9 0.7 %collective-permute-start.17 = (bf16[48,768]{1,0:T(8,128)(2,1)S(1)}, bf16[48,768]{1,0:T(8,128)(2,1)S(1)}, u32[]{:S(2)}, u32[]{:S(2)}) collective-permute-start(bf16[48,768]{1,0:T(8,128)(2,1)S(1)} %get-tuple-element.72), channel_id=1, source_target_pairs={{0,8},{1,9},{2,10},{3,11},{4,12},{5,13},{6,14},{7,15},{8,0},{9,1},... | collective-permute-start | bytes 221192 | tf_op jit(solution)/shard_map/ppermute | solution.py:639
  55.7 1.0 %join_item_gradients.1 = (bf16[512,768]{1,0:T(8,128)(2,1)}, bf16[48,768]{1,0:T(8,128)(2,1)}) custom-call(f32[560,768]{1,0:T(8,128)S(1)} %get-tuple-element.64.own_ref, bf16[560,768]{1,0:T(8,128)(2,1)S(1)} %collective-permute-done.12.taken_ref), custom_call_target="tpu_custom_call" | custom-call | flops 430080 | bytes 3440640 | tf_op jit(solution)/shard_map/join_item_gradients/pallas_call | solution.py:575
  56.7 2.8 %collective-permute-done.14 = bf16[48,768]{1,0:T(8,128)(2,1)S(1)} collective-permute-done((bf16[48,768]{1,0:T(8,128)(2,1)S(1)}, bf16[48,768]{1,0:T(8,128)(2,1)S(1)}, u32[]{:S(2)}, u32[]{:S(2)}) %collective-permute-start.14) | collective-permute-done | bytes 73760 | tf_op jit(solution)/shard_map/ppermute | solution.py:639
  (34 shorter events, 4.4 us)
Async XLA Ops:
  0.6 9.0 %copy-start.1 = (bf16[3072,768]{1,0:T(8,128)(2,1)S(1)}, bf16[3072,768]{1,0:T(8,128)(2,1)}, u32[]{:S(2)}) copy-start(bf16[3072,768]{1,0:T(8,128)(2,1)} %weight_ref.3) | copy-start | bytes 14155780
  0.6 9.0 %copy-start.2 = (bf16[512,3072]{1,0:T(8,128)(2,1)S(1)}, bf16[512,3072]{1,0:T(8,128)(2,1)}, u32[]{:S(2)}) copy-start(bf16[512,3072]{1,0:T(8,128)(2,1)} %pool_ref) | copy-start | bytes 9437188
  0.7 9.0 %copy-start.3 = (bf16[48,3072]{1,0:T(8,128)(2,1)S(1)}, bf16[48,3072]{1,0:T(8,128)(2,1)}, u32[]{:S(2)}) copy-start(bf16[48,3072]{1,0:T(8,128)(2,1)} %passage_ref.1) | copy-start | bytes 884740
  3.9 8.7 %collective-permute-start.1 = (bf16[312,128]{1,0:T(8,128)(2,1)S(1)}, bf16[312,128]{1,0:T(8,128)(2,1)S(1)}, u32[]{:S(2)}, u32[]{:S(2)}) collective-permute-start(bf16[312,128]{1,0:T(8,128)(2,1)S(1)} %get-tuple-element.39), channel_id=1, source_target_pairs={{0,6},{1,7},{2,4},{3,5},{4,2},{5,3},{6,0},{7,1},{8,14},{9,15},{10,... | collective-permute-start | bytes 239624 | tf_op jit(solution)/shard_map/ppermute | solution.py:639
  9.0 6.7 %collective-permute-start = (bf16[312,128]{1,0:T(8,128)(2,1)S(1)}, bf16[312,128]{1,0:T(8,128)(2,1)S(1)}, u32[]{:S(2)}, u32[]{:S(2)}) collective-permute-start(bf16[312,128]{1,0:T(8,128)(2,1)S(1)} %get-tuple-element.39), channel_id=1, source_target_pairs={{0,4},{1,5},{2,6},{3,7},{4,0},{5,1},{6,2},{7,3},{8,12},{9,13},{10,... | collective-permute-start | bytes 239624 | tf_op jit(solution)/shard_map/ppermute | solution.py:639
  9.0 11.1 %copy-start = (s32[192,8]{0,1:T(8,128)S(1)}, s32[192,8]{0,1:T(8,128)}, u32[]{:S(2)}) copy-start(s32[192,8]{0,1:T(8,128)} %param.11) | copy-start | bytes 18436
  9.0 6.7 %collective-permute-start.2 = (bf16[312,128]{1,0:T(8,128)(2,1)S(1)}, bf16[312,128]{1,0:T(8,128)(2,1)S(1)}, u32[]{:S(2)}, u32[]{:S(2)}) collective-permute-start(bf16[312,128]{1,0:T(8,128)(2,1)S(1)} %get-tuple-element.40), channel_id=1, source_target_pairs={{0,2},{1,3},{2,0},{3,1},{4,6},{5,7},{6,4},{7,5},{8,10},{9,11},{10,... | collective-permute-start | bytes 239624 | tf_op jit(solution)/shard_map/ppermute | solution.py:639
  15.7 7.9 %collective-permute-start.6 = (bf16[560,768]{1,0:T(8,128)(2,1)S(1)}, bf16[560,768]{1,0:T(8,128)(2,1)S(1)}, u32[]{:S(2)}, u32[]{:S(2)}) collective-permute-start(bf16[560,768]{1,0:T(8,128)(2,1)S(1)} %item_units.1.refs_3_.refs_4_), channel_id=1, source_target_pairs={{0,1},{1,0},{2,3},{3,2},{4,5},{5,4},{6,7},{7,6},{8,9},{9,8},{10,11... | collective-permute-start | bytes 2580488 | tf_op jit(solution)/shard_map/ppermute | solution.py:639
  15.8 7.8 %collective-permute-start.7 = (bf16[144,768]{1,0:T(8,128)(2,1)S(1)}, bf16[144,768]{1,0:T(8,128)(2,1)S(1)}, u32[]{:S(2)}, u32[]{:S(2)}) collective-permute-start(bf16[144,768]{1,0:T(8,128)(2,1)S(1)} %get-tuple-element.47), channel_id=1, source_target_pairs={{0,2},{1,3},{2,0},{3,1},{4,6},{5,7},{6,4},{7,5},{8,10},{9,11},{10,... | collective-permute-start | bytes 663560 | tf_op jit(solution)/shard_map/ppermute | solution.py:639
  16.6 8.2 %collective-permute-start.5 = (bf16[576,128]{1,0:T(8,128)(2,1)S(1)}, bf16[576,128]{1,0:T(8,128)(2,1)S(1)}, u32[]{:S(2)}, u32[]{:S(2)}) collective-permute-start(bf16[576,128]{1,0:T(8,128)(2,1)S(1)} %pad_maximum_fusion.refs_0_), channel_id=1, source_target_pairs={{0,24},{1,25},{2,26},{3,27},{4,28},{5,29},{6,30},{7,31},{8,16},{9,... | collective-permute-start | bytes 442376 | tf_op jit(solution)/shard_map/ppermute | solution.py:639
  19.0 7.6 %collective-permute-start.4 = (bf16[576,128]{1,0:T(8,128)(2,1)S(1)}, bf16[576,128]{1,0:T(8,128)(2,1)S(1)}, u32[]{:S(2)}, u32[]{:S(2)}) collective-permute-start(bf16[576,128]{1,0:T(8,128)(2,1)S(1)} %pad_maximum_fusion.refs_0_), channel_id=1, source_target_pairs={{0,16},{1,17},{2,18},{3,19},{4,20},{5,21},{6,22},{7,23},{8,24},{9,... | collective-permute-start | bytes 442376 | tf_op jit(solution)/shard_map/ppermute | solution.py:639
  19.5 7.2 %collective-permute-start.3 = (bf16[576,128]{1,0:T(8,128)(2,1)S(1)}, bf16[576,128]{1,0:T(8,128)(2,1)S(1)}, u32[]{:S(2)}, u32[]{:S(2)}) collective-permute-start(bf16[576,128]{1,0:T(8,128)(2,1)S(1)} %pad_maximum_fusion.refs_0_), channel_id=1, source_target_pairs={{0,8},{1,9},{2,10},{3,11},{4,12},{5,13},{6,14},{7,15},{8,0},{9,1},... | collective-permute-start | bytes 442376 | tf_op jit(solution)/shard_map/ppermute | solution.py:639
  40.0 8.9 %collective-permute-start.11 = (bf16[192,768]{1,0:T(8,128)(2,1)S(1)}, bf16[192,768]{1,0:T(8,128)(2,1)S(1)}, u32[]{:S(2)}, u32[]{:S(2)}) collective-permute-start(bf16[192,768]{1,0:T(8,128)(2,1)S(1)} %get-tuple-element.61), channel_id=1, source_target_pairs={{0,2},{1,3},{2,0},{3,1},{4,6},{5,7},{6,4},{7,5},{8,10},{9,11},{10,... | collective-permute-start | bytes 884744 | tf_op jit(solution)/shard_map/ppermute | solution.py:639
  40.7 7.1 %collective-permute-start.8 = (bf16[2,48,768]{2,1,0:T(8,128)(2,1)S(1)}, bf16[2,48,768]{2,1,0:T(8,128)(2,1)S(1)}, u32[]{:S(2)}, u32[]{:S(2)}) collective-permute-start(bf16[2,48,768]{2,1,0:T(8,128)(2,1)S(1)} %get-tuple-element.57), channel_id=1, source_target_pairs={{0,24},{1,25},{2,26},{3,27},{4,28},{5,29},{6,30},{7,31},{8,16},{9,... | collective-permute-start | bytes 442376 | tf_op jit(solution)/shard_map/ppermute | solution.py:639
  42.9 6.0 %collective-permute-start.9 = (bf16[2,48,768]{2,1,0:T(8,128)(2,1)S(1)}, bf16[2,48,768]{2,1,0:T(8,128)(2,1)S(1)}, u32[]{:S(2)}, u32[]{:S(2)}) collective-permute-start(bf16[2,48,768]{2,1,0:T(8,128)(2,1)S(1)} %get-tuple-element.58), channel_id=1, source_target_pairs={{0,16},{1,17},{2,18},{3,19},{4,20},{5,21},{6,22},{7,23},{8,24},{9,... | collective-permute-start | bytes 442376 | tf_op jit(solution)/shard_map/ppermute | solution.py:639
  43.3 5.6 %collective-permute-start.10 = (bf16[2,48,768]{2,1,0:T(8,128)(2,1)S(1)}, bf16[2,48,768]{2,1,0:T(8,128)(2,1)S(1)}, u32[]{:S(2)}, u32[]{:S(2)}) collective-permute-start(bf16[2,48,768]{2,1,0:T(8,128)(2,1)S(1)} %get-tuple-element.59), channel_id=1, source_target_pairs={{0,8},{1,9},{2,10},{3,11},{4,12},{5,13},{6,14},{7,15},{8,0},{9,1},... | collective-permute-start | bytes 442376 | tf_op jit(solution)/shard_map/ppermute | solution.py:639
  49.1 5.8 %collective-permute-start.12 = (bf16[560,768]{1,0:T(8,128)(2,1)S(1)}, bf16[560,768]{1,0:T(8,128)(2,1)S(1)}, u32[]{:S(2)}, u32[]{:S(2)}) collective-permute-start(bf16[560,768]{1,0:T(8,128)(2,1)S(1)} %get-tuple-element.65), channel_id=1, source_target_pairs={{0,1},{1,0},{2,3},{3,2},{4,5},{5,4},{6,7},{7,6},{8,9},{9,8},{10,11... | collective-permute-start | bytes 2580488 | tf_op jit(solution)/shard_map/ppermute | solution.py:639
  49.2 7.5 %collective-permute-start.13 = (bf16[48,768]{1,0:T(8,128)(2,1)S(1)}, bf16[48,768]{1,0:T(8,128)(2,1)S(1)}, u32[]{:S(2)}, u32[]{:S(2)}) collective-permute-start(bf16[48,768]{1,0:T(8,128)(2,1)S(1)} %get-tuple-element.68), channel_id=1, source_target_pairs={{0,6},{1,7},{2,4},{3,5},{4,2},{5,3},{6,0},{7,1},{8,14},{9,15},{10,... | collective-permute-start | bytes 221192 | tf_op jit(solution)/shard_map/ppermute | solution.py:639
  51.7 7.8 %collective-permute-start.14 = (bf16[48,768]{1,0:T(8,128)(2,1)S(1)}, bf16[48,768]{1,0:T(8,128)(2,1)S(1)}, u32[]{:S(2)}, u32[]{:S(2)}) collective-permute-start(bf16[48,768]{1,0:T(8,128)(2,1)S(1)} %get-tuple-element.69), channel_id=1, source_target_pairs={{0,4},{1,5},{2,6},{3,7},{4,0},{5,1},{6,2},{7,3},{8,12},{9,13},{10,... | collective-permute-start | bytes 221192 | tf_op jit(solution)/shard_map/ppermute | solution.py:639
  52.2 7.3 %collective-permute-start.15 = (bf16[48,768]{1,0:T(8,128)(2,1)S(1)}, bf16[48,768]{1,0:T(8,128)(2,1)S(1)}, u32[]{:S(2)}, u32[]{:S(2)}) collective-permute-start(bf16[48,768]{1,0:T(8,128)(2,1)S(1)} %get-tuple-element.70), channel_id=1, source_target_pairs={{0,24},{1,25},{2,26},{3,27},{4,28},{5,29},{6,30},{7,31},{8,16},{9,... | collective-permute-start | bytes 221192 | tf_op jit(solution)/shard_map/ppermute | solution.py:639
  53.8 5.7 %collective-permute-start.16 = (bf16[48,768]{1,0:T(8,128)(2,1)S(1)}, bf16[48,768]{1,0:T(8,128)(2,1)S(1)}, u32[]{:S(2)}, u32[]{:S(2)}) collective-permute-start(bf16[48,768]{1,0:T(8,128)(2,1)S(1)} %get-tuple-element.71), channel_id=1, source_target_pairs={{0,16},{1,17},{2,18},{3,19},{4,20},{5,21},{6,22},{7,23},{8,24},{9,... | collective-permute-start | bytes 221192 | tf_op jit(solution)/shard_map/ppermute | solution.py:639
  54.9 4.6 %collective-permute-start.17 = (bf16[48,768]{1,0:T(8,128)(2,1)S(1)}, bf16[48,768]{1,0:T(8,128)(2,1)S(1)}, u32[]{:S(2)}, u32[]{:S(2)}) collective-permute-start(bf16[48,768]{1,0:T(8,128)(2,1)S(1)} %get-tuple-element.72), channel_id=1, source_target_pairs={{0,8},{1,9},{2,10},{3,11},{4,12},{5,13},{6,14},{7,15},{8,0},{9,1},... | collective-permute-start | bytes 221192 | tf_op jit(solution)/shard_map/ppermute | solution.py:639

commit v10 on v8

--- a/solution.py
+++ b/solution.py
@@ -9,7 +9,7 @@
 
 logit_scale = 50.0
 axes = ("tower", "dp")
-rank_order = [14, 10, 8, 15, 9, 4, 13, 11, 12, 1, 0, 3, 2, 6, 5, 7]
+rank_order = [14, 4, 6, 0, 8, 7, 5, 1, 10, 11, 15, 3, 2, 9, 13, 12]
 group = 4
 f32 = jnp.float32
 bf16 = jnp.bfloat16

time: 60.4 us -> 60.3 us (level)
  no operation moved by 1% of the time
where the time goes in v10:
time: 60.3 us; the launch traced here: 60.1 us
  starting transfers between devices  20.8 us (34%)
  Pallas kernels  16.1 us (27%)
  waiting for transfers between devices  11.9 us (20%)
  blocking collectives  9.87 us (16%)
  between operations  0.79 us (1%)
  other arithmetic  0.71 us (1%)
    ppermute x18, starting transfers between devices, moved(): return lax.ppermute(x, axes, pairs)  20.8 us
    ppermute x18, waiting for transfers between devices, moved(): return lax.ppermute(x, axes, pairs)  11.9 us
    all_to_all x1, blocking collectives, shards(): totals = lax.all_to_all(totals, axes, 0, 0, axis_index_groups=same_core)  9.87 us
    pallas_call x1, Pallas kernels, project_queries(): pl.pallas_call(functools.partial(query_kernel, steps, part_rows), in_spec...  3.18 us
    pallas_call x1, Pallas kernels, project_items(): pl.pallas_call(item_kernel, out_shape=jax.ShapeDtypeStruct((rows, width),...  2.95 us
    pallas_call x1, Pallas kernels, count_names(): pl.pallas_call(functools.partial(count_kernel, pool_rows, 3 * neg_count),...  2.74 us
    pallas_call x1, Pallas kernels, weigh(): pl.pallas_call(functools.partial(weight_kernel, blocks, len(exps), query_...  2.07 us
    pallas_call x1, Pallas kernels, item_gradients(): pl.pallas_call(functools.partial(gradient_kernel, blocks, len(queries), p...  1.51 us
  transfers between devices with their start and end apart: 18, of which 7 were waited for; matrix products, arithmetic and copies ran while one was open for 0% of the time, Pallas kernels for 16%

profile of v10, /device:TPU:0, one launch (start us, length us, event | category | flops | bytes accessed | tf_op | source)
XLA Modules:
  0.0 60.1 jit_solution(15574654540084784612)
XLA Ops:
  0.7 3.2 %query_units.1 = (bf16[192,768]{1,0:T(8,128)(2,1)S(1)}, bf16[312,128]{1,0:T(8,128)(2,1)S(1)}, bf16[312,128]{1,0:T(8,128)(2,1)S(1)}, bf16[144,768]{1,0:T(8,128)(2,1)S(1)}) custom-call(bf16[192,2304]{1,0:T(8,128)(2,1)} %hidden_ref.1, bf16[2304,768]{1,0:T(8,128)(2,1)} %weight_ref.2, s32[8,192]{1,0:T(8,128)} %bitcast.1), custom_call_target="tpu_custom_call" | custom-call | flops 5435817984 | bytes 26542080 | tf_op jit(solution)/shard_map/query_units/pallas_call | solution.py:107
  3.9 5.1 %collective-permute-start.1 = (bf16[312,128]{1,0:T(8,128)(2,1)S(1)}, bf16[312,128]{1,0:T(8,128)(2,1)S(1)}, u32[]{:S(2)}, u32[]{:S(2)}) collective-permute-start(bf16[312,128]{1,0:T(8,128)(2,1)S(1)} %get-tuple-element.39), channel_id=1, source_target_pairs={{0,6},{1,7},{2,4},{3,5},{4,2},{5,3},{6,0},{7,1},{8,14},{9,15},{10,... | collective-permute-start | bytes 239624 | tf_op jit(solution)/shard_map/ppermute | solution.py:639
  9.6 2.9 %item_units.1.refs_3_.refs_4_ = bf16[560,768]{1,0:T(8,128)(2,1)S(1)} custom-call(bf16[512,3072]{1,0:T(8,128)(2,1)S(1)} %copy-done.2, bf16[48,3072]{1,0:T(8,128)(2,1)S(1)} %copy-done.3, bf16[3072,768]{1,0:T(8,128)(2,1)S(1)} %copy-done.1), custom_call_target="tpu_custom_call" | custom-call | flops 2642411520 | bytes 8159232 | tf_op jit(solution)/shard_map/item_units/pallas_call | solution.py:148
  12.6 3.1 %collective-permute-done.refs_2_ = bf16[312,128]{1,0:T(8,128)(2,1)S(1)} collective-permute-done((bf16[312,128]{1,0:T(8,128)(2,1)S(1)}, bf16[312,128]{1,0:T(8,128)(2,1)S(1)}, u32[]{:S(2)}, u32[]{:S(2)}) %collective-permute-start) | collective-permute-done | bytes 79904 | tf_op jit(solution)/shard_map/ppermute | solution.py:639
  15.8 0.8 %collective-permute-start.7 = (bf16[144,768]{1,0:T(8,128)(2,1)S(1)}, bf16[144,768]{1,0:T(8,128)(2,1)S(1)}, u32[]{:S(2)}, u32[]{:S(2)}) collective-permute-start(bf16[144,768]{1,0:T(8,128)(2,1)S(1)} %get-tuple-element.47), channel_id=1, source_target_pairs={{0,2},{1,3},{2,0},{3,1},{4,6},{5,7},{6,4},{7,5},{8,10},{9,11},{10,... | collective-permute-start | bytes 663560 | tf_op jit(solution)/shard_map/ppermute | solution.py:639
  16.6 2.5 %collective-permute-start.5 = (bf16[576,128]{1,0:T(8,128)(2,1)S(1)}, bf16[576,128]{1,0:T(8,128)(2,1)S(1)}, u32[]{:S(2)}, u32[]{:S(2)}) collective-permute-start(bf16[576,128]{1,0:T(8,128)(2,1)S(1)} %pad_maximum_fusion.refs_0_), channel_id=1, source_target_pairs={{0,24},{1,25},{2,26},{3,27},{4,28},{5,29},{6,30},{7,31},{8,16},{9,... | collective-permute-start | bytes 442376 | tf_op jit(solution)/shard_map/ppermute | solution.py:639
  20.1 2.7 %name_counts.1.refs_5_.refs_6_ = bf16[1024,768]{1,0:T(8,128)(2,1)S(1)} custom-call(s32[8,192]{1,0:T(8,128)S(1)} %bitcast.2, bf16[312,128]{1,0:T(8,128)(2,1)S(1)} %collective-permute-done.2.refs_1_, bf16[312,128]{1,0:T(8,128)(2,1)S(1)} %collective-permute-done.refs_2_, bf16[312,128]{1,0:T(8,128)(2,1)S(1)} %collective-permute-done.1.refs_3_), custom_call_target="tpu_custom_call" | custom-call | flops 18874368 | bytes 1572864 | tf_op jit(solution)/shard_map/name_counts/pallas_call | solution.py:192
  22.8 0.8 %collective-permute-done.7.refs_2_ = bf16[144,768]{1,0:T(8,128)(2,1)S(1)} collective-permute-done((bf16[144,768]{1,0:T(8,128)(2,1)S(1)}, bf16[144,768]{1,0:T(8,128)(2,1)S(1)}, u32[]{:S(2)}, u32[]{:S(2)}) %collective-permute-start.7) | collective-permute-done | bytes 221216 | tf_op jit(solution)/shard_map/ppermute | solution.py:639
  23.6 1.1 %near_scores.1 = (bf16[1120,384]{1,0:T(8,128)(2,1)S(1)}, f32[2,384]{1,0:T(2,128)S(1)}, bf16[384,768]{1,0:T(8,128)(2,1)S(1)}) custom-call(bf16[192,768]{1,0:T(8,128)(2,1)S(1)} %get-tuple-element.45.refs_0_, bf16[312,128]{1,0:T(8,128)(2,1)S(1)} %collective-permute-done.2.refs_1_, bf16[144,768]{1,0:T(8,128)(2,1)S(1)} %collective-permute-done.7.refs_2_, ...), custom_call_target="tpu_custom_call" | custom-call | flops 660602880 | bytes 1720320 | tf_op jit(solution)/shard_map/near_scores/pallas_call | solution.py:390
  24.8 1.8 %collective-permute-done.4.refs_2_ = bf16[576,128]{1,0:T(8,128)(2,1)S(1)} collective-permute-done((bf16[576,128]{1,0:T(8,128)(2,1)S(1)}, bf16[576,128]{1,0:T(8,128)(2,1)S(1)}, u32[]{:S(2)}, u32[]{:S(2)}) %collective-permute-start.4) | collective-permute-done | bytes 147488 | tf_op jit(solution)/shard_map/ppermute | solution.py:639
  26.7 1.3 %far_scores.1 = (bf16[1120,384]{1,0:T(8,128)(2,1)S(1)}, f32[16,2,768]{2,1,0:T(2,128)S(1)}, bf16[384,768]{1,0:T(8,128)(2,1)S(1)}) custom-call(bf16[576,128]{1,0:T(8,128)(2,1)S(1)} %pad_maximum_fusion.refs_0_, bf16[576,128]{1,0:T(8,128)(2,1)S(1)} %collective-permute-done.3.refs_1_, bf16[576,128]{1,0:T(8,128)(2,1)S(1)} %collective-permute-done.4.refs_2_, ...), custom_call_target="tpu_custom_call" | custom-call | flops 660602880 | bytes 1720320 | tf_op jit(solution)/shard_map/far_scores/pallas_call | solution.py:374
  28.0 9.9 %all_to_all.5.refs_0_ = f32[16,2,768]{2,1,0:T(2,128)S(1)} all-to-all(f32[16,2,768]{2,1,0:T(2,128)S(1)} %get-tuple-element.49), channel_id=1, replica_groups={{28,8,12,0,16,14,10,2,20,22,30,6,4,18,26,24},{29,9,13,1,17,15,11,3,21,2..., dimensions={0} | all-to-all | bytes 196608 | tf_op jit(solution)/shard_map/all_to_all | solution.py:704
  37.9 2.1 %weights.1 = (bf16[1120,768]{1,0:T(8,128)(2,1)S(1)}, bf16[192,768]{1,0:T(8,128)(2,1)S(1)}, bf16[192,768]{1,0:T(8,128)(2,1)S(1)}, bf16[2,48,768]{2,1,0:T(8,128)(2...) custom-call(f32[16,2,768]{2,1,0:T(2,128)S(1)} %all_to_all.5.refs_0_, ...), custom_call_target="tpu_custom_call" | custom-call | flops 1321205760 | bytes 3440640 | tf_op jit(solution)/shard_map/weights/pallas_call | solution.py:466
  40.7 2.1 %collective-permute-start.8 = (bf16[2,48,768]{2,1,0:T(8,128)(2,1)S(1)}, bf16[2,48,768]{2,1,0:T(8,128)(2,1)S(1)}, u32[]{:S(2)}, u32[]{:S(2)}) collective-permute-start(bf16[2,48,768]{2,1,0:T(8,128)(2,1)S(1)} %get-tuple-element.57), channel_id=1, source_target_pairs={{0,24},{1,25},{2,26},{3,27},{4,28},{5,29},{6,30},{7,31},{8,16},{9,... | collective-permute-start | bytes 442376 | tf_op jit(solution)/shard_map/ppermute | solution.py:639
  42.8 0.8 %collective-permute-start.9 = (bf16[2,48,768]{2,1,0:T(8,128)(2,1)S(1)}, bf16[2,48,768]{2,1,0:T(8,128)(2,1)S(1)}, u32[]{:S(2)}, u32[]{:S(2)}) collective-permute-start(bf16[2,48,768]{2,1,0:T(8,128)(2,1)S(1)} %get-tuple-element.58), channel_id=1, source_target_pairs={{0,16},{1,17},{2,18},{3,19},{4,20},{5,21},{6,22},{7,23},{8,24},{9,... | collective-permute-start | bytes 442376 | tf_op jit(solution)/shard_map/ppermute | solution.py:639
  44.2 1.5 %item_gradients.1 = (f32[560,768]{1,0:T(8,128)S(1)}, bf16[560,768]{1,0:T(8,128)(2,1)S(1)}) custom-call(bf16[1120,768]{1,0:T(8,128)(2,1)S(1)} %get-tuple-element.52.weight_ref, bf16[384,768]{1,0:T(8,128)(2,1)S(1)} %get-tuple-element.53.refs_0_, bf16[384,768]{1,0:T(8,128)(2,1)S(1)} %get-tuple-element.54.refs_1_), custom_call_target="tpu_custom_call" | custom-call | flops 1321205760 | bytes 5160960 | tf_op jit(solution)/shard_map/item_gradients/pallas_call | solution.py:545
  45.7 2.1 %collective-permute-done.8.refs_1_ = bf16[2,48,768]{2,1,0:T(8,128)(2,1)S(1)} collective-permute-done((bf16[2,48,768]{2,1,0:T(8,128)(2,1)S(1)}, bf16[2,48,768]{2,1,0:T(8,128)(2,1)S(1)}, u32[]{:S(2)}, u32[]{:S(2)}) %collective-permute-start.8) | collective-permute-done | bytes 147488 | tf_op jit(solution)/shard_map/ppermute | solution.py:639
  47.9 1.1 %collective-permute-done.9.refs_2_ = bf16[2,48,768]{2,1,0:T(8,128)(2,1)S(1)} collective-permute-done((bf16[2,48,768]{2,1,0:T(8,128)(2,1)S(1)}, bf16[2,48,768]{2,1,0:T(8,128)(2,1)S(1)}, u32[]{:S(2)}, u32[]{:S(2)}) %collective-permute-start.9) | collective-permute-done | bytes 147488 | tf_op jit(solution)/shard_map/ppermute | solution.py:639
  49.2 2.4 %collective-permute-start.13 = (bf16[48,768]{1,0:T(8,128)(2,1)S(1)}, bf16[48,768]{1,0:T(8,128)(2,1)S(1)}, u32[]{:S(2)}, u32[]{:S(2)}) collective-permute-start(bf16[48,768]{1,0:T(8,128)(2,1)S(1)} %get-tuple-element.68), channel_id=1, source_target_pairs={{0,6},{1,7},{2,4},{3,5},{4,2},{5,3},{6,0},{7,1},{8,14},{9,15},{10,... | collective-permute-start | bytes 221192 | tf_op jit(solution)/shard_map/ppermute | solution.py:639
  52.0 1.6 %collective-permute-start.15 = (bf16[48,768]{1,0:T(8,128)(2,1)S(1)}, bf16[48,768]{1,0:T(8,128)(2,1)S(1)}, u32[]{:S(2)}, u32[]{:S(2)}) collective-permute-start(bf16[48,768]{1,0:T(8,128)(2,1)S(1)} %get-tuple-element.70), channel_id=1, source_target_pairs={{0,24},{1,25},{2,26},{3,27},{4,28},{5,29},{6,30},{7,31},{8,16},{9,... | collective-permute-start | bytes 221192 | tf_op jit(solution)/shard_map/ppermute | solution.py:639
  53.6 0.8 %collective-permute-start.16 = (bf16[48,768]{1,0:T(8,128)(2,1)S(1)}, bf16[48,768]{1,0:T(8,128)(2,1)S(1)}, u32[]{:S(2)}, u32[]{:S(2)}) collective-permute-start(bf16[48,768]{1,0:T(8,128)(2,1)S(1)} %get-tuple-element.71), channel_id=1, source_target_pairs={{0,16},{1,17},{2,18},{3,19},{4,20},{5,21},{6,22},{7,23},{8,24},{9,... | collective-permute-start | bytes 221192 | tf_op jit(solution)/shard_map/ppermute | solution.py:639
  54.4 1.1 %collective-permute-start.17 = (bf16[48,768]{1,0:T(8,128)(2,1)S(1)}, bf16[48,768]{1,0:T(8,128)(2,1)S(1)}, u32[]{:S(2)}, u32[]{:S(2)}) collective-permute-start(bf16[48,768]{1,0:T(8,128)(2,1)S(1)} %get-tuple-element.72), channel_id=1, source_target_pairs={{0,8},{1,9},{2,10},{3,11},{4,12},{5,13},{6,14},{7,15},{8,0},{9,1},... | collective-permute-start | bytes 221192 | tf_op jit(solution)/shard_map/ppermute | solution.py:639
  55.5 1.0 %join_item_gradients.1 = (bf16[512,768]{1,0:T(8,128)(2,1)}, bf16[48,768]{1,0:T(8,128)(2,1)}) custom-call(f32[560,768]{1,0:T(8,128)S(1)} %get-tuple-element.64.own_ref, bf16[560,768]{1,0:T(8,128)(2,1)S(1)} %collective-permute-done.12.taken_ref), custom_call_target="tpu_custom_call" | custom-call | flops 430080 | bytes 3440640 | tf_op jit(solution)/shard_map/join_item_gradients/pallas_call | solution.py:575
  56.6 2.8 %collective-permute-done.14 = bf16[48,768]{1,0:T(8,128)(2,1)S(1)} collective-permute-done((bf16[48,768]{1,0:T(8,128)(2,1)S(1)}, bf16[48,768]{1,0:T(8,128)(2,1)S(1)}, u32[]{:S(2)}, u32[]{:S(2)}) %collective-permute-start.14) | collective-permute-done | bytes 73760 | tf_op jit(solution)/shard_map/ppermute | solution.py:639
  (34 shorter events, 4.6 us)
Async XLA Ops:
  0.6 9.0 %copy-start.1 = (bf16[3072,768]{1,0:T(8,128)(2,1)S(1)}, bf16[3072,768]{1,0:T(8,128)(2,1)}, u32[]{:S(2)}) copy-start(bf16[3072,768]{1,0:T(8,128)(2,1)} %weight_ref.3) | copy-start | bytes 14155780
  0.6 9.0 %copy-start.2 = (bf16[512,3072]{1,0:T(8,128)(2,1)S(1)}, bf16[512,3072]{1,0:T(8,128)(2,1)}, u32[]{:S(2)}) copy-start(bf16[512,3072]{1,0:T(8,128)(2,1)} %pool_ref) | copy-start | bytes 9437188
  0.7 9.0 %copy-start.3 = (bf16[48,3072]{1,0:T(8,128)(2,1)S(1)}, bf16[48,3072]{1,0:T(8,128)(2,1)}, u32[]{:S(2)}) copy-start(bf16[48,3072]{1,0:T(8,128)(2,1)} %passage_ref.1) | copy-start | bytes 884740
  3.9 8.7 %collective-permute-start.1 = (bf16[312,128]{1,0:T(8,128)(2,1)S(1)}, bf16[312,128]{1,0:T(8,128)(2,1)S(1)}, u32[]{:S(2)}, u32[]{:S(2)}) collective-permute-start(bf16[312,128]{1,0:T(8,128)(2,1)S(1)} %get-tuple-element.39), channel_id=1, source_target_pairs={{0,6},{1,7},{2,4},{3,5},{4,2},{5,3},{6,0},{7,1},{8,14},{9,15},{10,... | collective-permute-start | bytes 239624 | tf_op jit(solution)/shard_map/ppermute | solution.py:639
  9.0 6.7 %collective-permute-start = (bf16[312,128]{1,0:T(8,128)(2,1)S(1)}, bf16[312,128]{1,0:T(8,128)(2,1)S(1)}, u32[]{:S(2)}, u32[]{:S(2)}) collective-permute-start(bf16[312,128]{1,0:T(8,128)(2,1)S(1)} %get-tuple-element.39), channel_id=1, source_target_pairs={{0,4},{1,5},{2,6},{3,7},{4,0},{5,1},{6,2},{7,3},{8,12},{9,13},{10,... | collective-permute-start | bytes 239624 | tf_op jit(solution)/shard_map/ppermute | solution.py:639
  9.0 11.1 %copy-start = (s32[192,8]{0,1:T(8,128)S(1)}, s32[192,8]{0,1:T(8,128)}, u32[]{:S(2)}) copy-start(s32[192,8]{0,1:T(8,128)} %param.11) | copy-start | bytes 18436
  9.0 6.7 %collective-permute-start.2 = (bf16[312,128]{1,0:T(8,128)(2,1)S(1)}, bf16[312,128]{1,0:T(8,128)(2,1)S(1)}, u32[]{:S(2)}, u32[]{:S(2)}) collective-permute-start(bf16[312,128]{1,0:T(8,128)(2,1)S(1)} %get-tuple-element.40), channel_id=1, source_target_pairs={{0,2},{1,3},{2,0},{3,1},{4,6},{5,7},{6,4},{7,5},{8,10},{9,11},{10,... | collective-permute-start | bytes 239624 | tf_op jit(solution)/shard_map/ppermute | solution.py:639
  15.7 7.9 %collective-permute-start.6 = (bf16[560,768]{1,0:T(8,128)(2,1)S(1)}, bf16[560,768]{1,0:T(8,128)(2,1)S(1)}, u32[]{:S(2)}, u32[]{:S(2)}) collective-permute-start(bf16[560,768]{1,0:T(8,128)(2,1)S(1)} %item_units.1.refs_3_.refs_4_), channel_id=1, source_target_pairs={{0,1},{1,0},{2,3},{3,2},{4,5},{5,4},{6,7},{7,6},{8,9},{9,8},{10,11... | collective-permute-start | bytes 2580488 | tf_op jit(solution)/shard_map/ppermute | solution.py:639
  15.8 7.8 %collective-permute-start.7 = (bf16[144,768]{1,0:T(8,128)(2,1)S(1)}, bf16[144,768]{1,0:T(8,128)(2,1)S(1)}, u32[]{:S(2)}, u32[]{:S(2)}) collective-permute-start(bf16[144,768]{1,0:T(8,128)(2,1)S(1)} %get-tuple-element.47), channel_id=1, source_target_pairs={{0,2},{1,3},{2,0},{3,1},{4,6},{5,7},{6,4},{7,5},{8,10},{9,11},{10,... | collective-permute-start | bytes 663560 | tf_op jit(solution)/shard_map/ppermute | solution.py:639
  16.6 8.2 %collective-permute-start.5 = (bf16[576,128]{1,0:T(8,128)(2,1)S(1)}, bf16[576,128]{1,0:T(8,128)(2,1)S(1)}, u32[]{:S(2)}, u32[]{:S(2)}) collective-permute-start(bf16[576,128]{1,0:T(8,128)(2,1)S(1)} %pad_maximum_fusion.refs_0_), channel_id=1, source_target_pairs={{0,24},{1,25},{2,26},{3,27},{4,28},{5,29},{6,30},{7,31},{8,16},{9,... | collective-permute-start | bytes 442376 | tf_op jit(solution)/shard_map/ppermute | solution.py:639
  19.0 7.6 %collective-permute-start.4 = (bf16[576,128]{1,0:T(8,128)(2,1)S(1)}, bf16[576,128]{1,0:T(8,128)(2,1)S(1)}, u32[]{:S(2)}, u32[]{:S(2)}) collective-permute-start(bf16[576,128]{1,0:T(8,128)(2,1)S(1)} %pad_maximum_fusion.refs_0_), channel_id=1, source_target_pairs={{0,16},{1,17},{2,18},{3,19},{4,20},{5,21},{6,22},{7,23},{8,24},{9,... | collective-permute-start | bytes 442376 | tf_op jit(solution)/shard_map/ppermute | solution.py:639
  19.5 7.2 %collective-permute-start.3 = (bf16[576,128]{1,0:T(8,128)(2,1)S(1)}, bf16[576,128]{1,0:T(8,128)(2,1)S(1)}, u32[]{:S(2)}, u32[]{:S(2)}) collective-permute-start(bf16[576,128]{1,0:T(8,128)(2,1)S(1)} %pad_maximum_fusion.refs_0_), channel_id=1, source_target_pairs={{0,8},{1,9},{2,10},{3,11},{4,12},{5,13},{6,14},{7,15},{8,0},{9,1},... | collective-permute-start | bytes 442376 | tf_op jit(solution)/shard_map/ppermute | solution.py:639
  40.0 9.0 %collective-permute-start.11 = (bf16[192,768]{1,0:T(8,128)(2,1)S(1)}, bf16[192,768]{1,0:T(8,128)(2,1)S(1)}, u32[]{:S(2)}, u32[]{:S(2)}) collective-permute-start(bf16[192,768]{1,0:T(8,128)(2,1)S(1)} %get-tuple-element.61), channel_id=1, source_target_pairs={{0,2},{1,3},{2,0},{3,1},{4,6},{5,7},{6,4},{7,5},{8,10},{9,11},{10,... | collective-permute-start | bytes 884744 | tf_op jit(solution)/shard_map/ppermute | solution.py:639
  40.7 7.2 %collective-permute-start.8 = (bf16[2,48,768]{2,1,0:T(8,128)(2,1)S(1)}, bf16[2,48,768]{2,1,0:T(8,128)(2,1)S(1)}, u32[]{:S(2)}, u32[]{:S(2)}) collective-permute-start(bf16[2,48,768]{2,1,0:T(8,128)(2,1)S(1)} %get-tuple-element.57), channel_id=1, source_target_pairs={{0,24},{1,25},{2,26},{3,27},{4,28},{5,29},{6,30},{7,31},{8,16},{9,... | collective-permute-start | bytes 442376 | tf_op jit(solution)/shard_map/ppermute | solution.py:639
  42.8 6.1 %collective-permute-start.9 = (bf16[2,48,768]{2,1,0:T(8,128)(2,1)S(1)}, bf16[2,48,768]{2,1,0:T(8,128)(2,1)S(1)}, u32[]{:S(2)}, u32[]{:S(2)}) collective-permute-start(bf16[2,48,768]{2,1,0:T(8,128)(2,1)S(1)} %get-tuple-element.58), channel_id=1, source_target_pairs={{0,16},{1,17},{2,18},{3,19},{4,20},{5,21},{6,22},{7,23},{8,24},{9,... | collective-permute-start | bytes 442376 | tf_op jit(solution)/shard_map/ppermute | solution.py:639
  43.6 5.3 %collective-permute-start.10 = (bf16[2,48,768]{2,1,0:T(8,128)(2,1)S(1)}, bf16[2,48,768]{2,1,0:T(8,128)(2,1)S(1)}, u32[]{:S(2)}, u32[]{:S(2)}) collective-permute-start(bf16[2,48,768]{2,1,0:T(8,128)(2,1)S(1)} %get-tuple-element.59), channel_id=1, source_target_pairs={{0,8},{1,9},{2,10},{3,11},{4,12},{5,13},{6,14},{7,15},{8,0},{9,1},... | collective-permute-start | bytes 442376 | tf_op jit(solution)/shard_map/ppermute | solution.py:639
  49.1 5.3 %collective-permute-start.12 = (bf16[560,768]{1,0:T(8,128)(2,1)S(1)}, bf16[560,768]{1,0:T(8,128)(2,1)S(1)}, u32[]{:S(2)}, u32[]{:S(2)}) collective-permute-start(bf16[560,768]{1,0:T(8,128)(2,1)S(1)} %get-tuple-element.65), channel_id=1, source_target_pairs={{0,1},{1,0},{2,3},{3,2},{4,5},{5,4},{6,7},{7,6},{8,9},{9,8},{10,11... | collective-permute-start | bytes 2580488 | tf_op jit(solution)/shard_map/ppermute | solution.py:639
  49.2 7.4 %collective-permute-start.13 = (bf16[48,768]{1,0:T(8,128)(2,1)S(1)}, bf16[48,768]{1,0:T(8,128)(2,1)S(1)}, u32[]{:S(2)}, u32[]{:S(2)}) collective-permute-start(bf16[48,768]{1,0:T(8,128)(2,1)S(1)} %get-tuple-element.68), channel_id=1, source_target_pairs={{0,6},{1,7},{2,4},{3,5},{4,2},{5,3},{6,0},{7,1},{8,14},{9,15},{10,... | collective-permute-start | bytes 221192 | tf_op jit(solution)/shard_map/ppermute | solution.py:639
  51.6 7.8 %collective-permute-start.14 = (bf16[48,768]{1,0:T(8,128)(2,1)S(1)}, bf16[48,768]{1,0:T(8,128)(2,1)S(1)}, u32[]{:S(2)}, u32[]{:S(2)}) collective-permute-start(bf16[48,768]{1,0:T(8,128)(2,1)S(1)} %get-tuple-element.69), channel_id=1, source_target_pairs={{0,4},{1,5},{2,6},{3,7},{4,0},{5,1},{6,2},{7,3},{8,12},{9,13},{10,... | collective-permute-start | bytes 221192 | tf_op jit(solution)/shard_map/ppermute | solution.py:639
  52.0 7.3 %collective-permute-start.15 = (bf16[48,768]{1,0:T(8,128)(2,1)S(1)}, bf16[48,768]{1,0:T(8,128)(2,1)S(1)}, u32[]{:S(2)}, u32[]{:S(2)}) collective-permute-start(bf16[48,768]{1,0:T(8,128)(2,1)S(1)} %get-tuple-element.70), channel_id=1, source_target_pairs={{0,24},{1,25},{2,26},{3,27},{4,28},{5,29},{6,30},{7,31},{8,16},{9,... | collective-permute-start | bytes 221192 | tf_op jit(solution)/shard_map/ppermute | solution.py:639
  53.6 5.8 %collective-permute-start.16 = (bf16[48,768]{1,0:T(8,128)(2,1)S(1)}, bf16[48,768]{1,0:T(8,128)(2,1)S(1)}, u32[]{:S(2)}, u32[]{:S(2)}) collective-permute-start(bf16[48,768]{1,0:T(8,128)(2,1)S(1)} %get-tuple-element.71), channel_id=1, source_target_pairs={{0,16},{1,17},{2,18},{3,19},{4,20},{5,21},{6,22},{7,23},{8,24},{9,... | collective-permute-start | bytes 221192 | tf_op jit(solution)/shard_map/ppermute | solution.py:639
  54.4 5.0 %collective-permute-start.17 = (bf16[48,768]{1,0:T(8,128)(2,1)S(1)}, bf16[48,768]{1,0:T(8,128)(2,1)S(1)}, u32[]{:S(2)}, u32[]{:S(2)}) collective-permute-start(bf16[48,768]{1,0:T(8,128)(2,1)S(1)} %get-tuple-element.72), channel_id=1, source_target_pairs={{0,8},{1,9},{2,10},{3,11},{4,12},{5,13},{6,14},{7,15},{8,0},{9,1},... | collective-permute-start | bytes 221192 | tf_op jit(solution)/shard_map/ppermute | solution.py:639
